TPU v7x, 32 devices: a whole 2x2x4 slice. The times are simulated.
32 devices in a mesh: blk: 16 (over z, y, core), inner: 2 (over x).
Axes of the slice: x: 2, y: 2, z: 4, core: 2. Of those that a mesh axis runs over, the one named last changes fastest.
Arguments:
- picture_vectors: bfloat16 [12288, 1152], P(('blk', 'inner')), may hold values from -0.29882812 to 0.29882812
- caption_vectors: bfloat16 [12288, 1152], P(('blk', 'inner')), may hold values from -0.29882812 to 0.29882812
- score_scaling: float32 [], replicated, may hold values from 5 to 20
- score_shift: float32 [], replicated, may hold values from -3 to 0
Outputs:
- loss_rows: float32 [12288], P(('blk', 'inner'))
- image_grad: bfloat16 [12288, 1152], P(('blk', 'inner'))
- text_grad: bfloat16 [12288, 1152], P(('blk', 'inner'))
All inputs are finite; a program needn't handle non-finite values.
Results may differ from a plain program's by a relative error of at most 0.0061.
Values may be sent and summed in bfloat16 or wider, within the bound.
No kernel may reach another device: no remote copies, remote signals or barrier semaphores. Data moves between devices by JAX's collectives and lax.ppermute only.
A program may use at most 64 MiB of HBM per device.

v0:
```python
import jax
import jax.numpy as jnp
from jax import lax
from jax.sharding import PartitionSpec as P

SPAN = 4


def from_behind(value, axis, steps):
    count = lax.axis_size(axis)
    pairs = [(source, (source + steps) % count) for source in range(count)]
    return lax.ppermute(value, axis, pairs)


def normalize(block):
    values = block.astype(jnp.float32)
    length = jnp.sqrt(jnp.sum(values * values, axis=-1, keepdims=True) + 1e-06)
    return (values / length, length)


def matrix_entries(
    picture_summed, caption_summed, score_scaling, score_shift, first_round_indicator
):
    match_scores = (
        score_scaling
        * lax.dot_general(
            picture_summed,
            caption_summed,
            (((1,), (1,)), ((), ())),
            preferred_element_type=jnp.float32,
        )
        + score_shift
    )
    rows = match_scores.shape[0]
    if first_round_indicator:
        same = jnp.arange(rows)[:, None] == jnp.arange(rows)[None, :]
        match_sign = jnp.where(same, jnp.float32(1.0), jnp.float32(-1.0))
    else:
        match_sign = jnp.float32(-1.0)
    objective_total = jnp.sum(jax.nn.softplus(-match_sign * match_scores), axis=1)
    score_multiplier = (
        -match_sign * jax.nn.sigmoid(-match_sign * match_scores) * score_scaling
    ).astype(jnp.bfloat16)
    return (objective_total, score_multiplier)


def project(unit, grad, length):
    return (grad - unit * jnp.sum(unit * grad, axis=-1, keepdims=True)) / length


def back_term(score_multiplier, picture_summed):
    return lax.dot_general(
        score_multiplier,
        picture_summed,
        (((0,), (0,)), ((), ())),
        preferred_element_type=jnp.float32,
    )


def local(picture_vectors, caption_vectors, score_scaling, score_shift):
    rows = picture_vectors.shape[0]
    image_unit, image_length = normalize(picture_vectors)
    text_unit, text_length = normalize(caption_vectors)
    picture_summed = image_unit.astype(jnp.bfloat16)
    caption_summed = text_unit.astype(jnp.bfloat16)
    loss_total = jnp.zeros((rows,), jnp.float32)
    grad_image = jnp.zeros(picture_vectors.shape, jnp.float32)
    current_tile = caption_summed
    running = jnp.zeros(picture_vectors.shape, jnp.float32)
    for peer_distance in range(SPAN):
        if peer_distance > 0:
            current_tile = from_behind(current_tile, ("blk", "inner"), 1)
        objective_total, score_multiplier = matrix_entries(
            picture_summed, current_tile, score_scaling, score_shift, peer_distance == 0
        )
        loss_total = loss_total + objective_total
        grad_image = grad_image + jnp.dot(
            score_multiplier, current_tile, preferred_element_type=jnp.float32
        )
        term = back_term(score_multiplier, picture_summed)
        if peer_distance == 0:
            running = term
        else:
            running = from_behind(running, ("blk", "inner"), 1) + term
    grad_text = from_behind(running, ("blk", "inner"), 1 - SPAN)
    loss_rows = loss_total / (SPAN * rows)
    image_grad = project(image_unit, grad_image, image_length).astype(jnp.bfloat16)
    text_grad = project(text_unit, grad_text, text_length).astype(jnp.bfloat16)
    return (loss_rows, image_grad, text_grad)


def solution(mesh):
    in_specs = (P(("blk", "inner"), None), P(("blk", "inner"), None), P(), P())
    out_specs = (P(("blk", "inner")), P(("blk", "inner"), None), P(("blk", "inner"), None))
    return jax.shard_map(local, mesh=mesh, in_specs=in_specs, out_specs=out_specs, check_vma=False)
```

profile of v0, /device:TPU:1, one launch (start us, length us, event | category | flops | bytes accessed | tf_op | source)
XLA Modules:
  0.0 234.8 jit_solution(18265482511876902524)
XLA Ops:
  0.6 0.0 copy-start
  1.4 1.4 fusion
  2.8 1.4 fusion.11
  4.2 0.0 copy-done
  4.3 0.3 fusion.1
  4.5 0.3 fusion.12
  5.4 1.0 fusion.7
  6.5 0.7 fusion.15
  7.1 2.1 collective-permute-start.3
  9.2 1.8 collective-permute-start
  11.0 56.0 %collective-permute-done = bf16[384,1152]{1,0:T(8,128)(2,1)S(1)} collective-permute-done((bf16[384,1152]{1,0:T(8,128)(2,1)S(1)}, bf16[384,1152]{1,0:T(8,128)(2,1)S(1)}, u32[]{:S(2)}, u32[]{:S(2)}) %collective-permute-start) | collective-permute-done | bytes 884768 | tf_op jit(solution)/shard_map/ppermute | solution.py:12
  67.0 1.0 fusion.8
  68.0 0.0 collective-permute-done.3
  68.0 0.7 convolution_add_fusion
  68.7 0.7 collective-permute-start.4
  69.4 3.2 %collective-permute-start.1 = (bf16[384,1152]{1,0:T(8,128)(2,1)S(1)}, bf16[384,1152]{1,0:T(8,128)(2,1)S(1)}, u32[]{:S(2)}, u32[]{:S(2)}) collective-permute-start(bf16[384,1152]{1,0:T(8,128)(2,1)S(1)} %collective-permute-done), channel_id=1, source_target_pairs={{0,1},{1,2},{2,3},{3,4},{4,5},{5,6},{6,7},{7,8},{8,9},{9,10},{10,1... | collective-permute-start | bytes 2654216 | tf_op jit(solution)/shard_map/ppermute | solution.py:12
  72.6 54.9 %collective-permute-done.1 = bf16[384,1152]{1,0:T(8,128)(2,1)S(1)} collective-permute-done((bf16[384,1152]{1,0:T(8,128)(2,1)S(1)}, bf16[384,1152]{1,0:T(8,128)(2,1)S(1)}, u32[]{:S(2)}, u32[]{:S(2)}) %collective-permute-start.1) | collective-permute-done | bytes 884768 | tf_op jit(solution)/shard_map/ppermute | solution.py:12
  127.4 1.0 fusion.9
  128.4 0.7 fusion.13
  129.0 0.0 collective-permute-done.4
  129.1 0.3 add.108
  129.3 1.1 collective-permute-start.5
  130.5 3.4 %collective-permute-start.2 = (bf16[384,1152]{1,0:T(8,128)(2,1)S(1)}, bf16[384,1152]{1,0:T(8,128)(2,1)S(1)}, u32[]{:S(2)}, u32[]{:S(2)}) collective-permute-start(bf16[384,1152]{1,0:T(8,128)(2,1)S(1)} %collective-permute-done.1), channel_id=1, source_target_pairs={{0,1},{1,2},{2,3},{3,4},{4,5},{5,6},{6,7},{7,8},{8,9},{9,10},{10,1... | collective-permute-start | bytes 2654216 | tf_op jit(solution)/shard_map/ppermute | solution.py:12
  133.8 0.7 fusion.16
  134.5 0.7 convolution_add_fusion.3
  135.3 51.7 %collective-permute-done.2 = bf16[384,1152]{1,0:T(8,128)(2,1)S(1)} collective-permute-done((bf16[384,1152]{1,0:T(8,128)(2,1)S(1)}, bf16[384,1152]{1,0:T(8,128)(2,1)S(1)}, u32[]{:S(2)}, u32[]{:S(2)}) %collective-permute-start.2) | collective-permute-done | bytes 884768 | tf_op jit(solution)/shard_map/ppermute | solution.py:12
  186.9 1.0 fusion.10
  187.9 0.7 fusion.14
  188.6 0.0 collective-permute-done.5
  188.6 0.2 add.109
  188.8 0.0 copy-start.1
  188.8 6.4 %collective-permute-start.6 = (f32[384,1152]{1,0:T(8,128)S(1)}, f32[384,1152]{1,0:T(8,128)S(1)}, u32[]{:S(2)}, u32[]{:S(2)}) collective-permute-start(f32[384,1152]{1,0:T(8,128)S(1)} %add.109), channel_id=1, source_target_pairs={{0,29},{1,30},{2,31},{3,0},{4,1},{5,2},{6,3},{7,4},{8,5},{9,6},{10... | collective-permute-start | bytes 5308424 | tf_op jit(solution)/shard_map/ppermute | solution.py:12
  195.1 0.7 convolution_add_fusion.2
  195.9 0.6 add_multiply_fusion
  196.4 0.0 copy-done.1
  196.4 1.0 multiply_reduce_fusion.1
  197.4 1.3 divide_convert_fusion.1
  198.8 34.3 %collective-permute-done.6 = f32[384,1152]{1,0:T(8,128)S(1)} collective-permute-done((f32[384,1152]{1,0:T(8,128)S(1)}, f32[384,1152]{1,0:T(8,128)S(1)}, u32[]{:S(2)}, u32[]{:S(2)}) %collective-permute-start.6) | collective-permute-done | bytes 1769504 | tf_op jit(solution)/shard_map/ppermute | solution.py:12
  233.0 0.4 multiply_reduce_fusion
  233.5 1.3 divide_convert_fusion
  (2 shorter events, 0.0 us)
Async XLA Ops:
  0.6 3.6 %copy-start = (bf16[384,1152]{1,0:T(8,128)(2,1)S(1)}, bf16[384,1152]{1,0:T(8,128)(2,1)}, u32[]{:S(2)}) copy-start(bf16[384,1152]{1,0:T(8,128)(2,1)} %param.5) | copy-start | bytes 2654212
  7.1 60.9 %collective-permute-start.3 = (f32[384,1152]{1,0:T(8,128)S(1)}, f32[384,1152]{1,0:T(8,128)S(1)}, u32[]{:S(2)}, u32[]{:S(2)}) collective-permute-start(f32[384,1152]{1,0:T(8,128)S(1)} %fusion.15), channel_id=1, source_target_pairs={{0,1},{1,2},{2,3},{3,4},{4,5},{5,6},{6,7},{7,8},{8,9},{9,10},{10,1... | collective-permute-start | bytes 5308424 | tf_op jit(solution)/shard_map/ppermute | solution.py:12
  9.2 57.8 %collective-permute-start = (bf16[384,1152]{1,0:T(8,128)(2,1)S(1)}, bf16[384,1152]{1,0:T(8,128)(2,1)S(1)}, u32[]{:S(2)}, u32[]{:S(2)}) collective-permute-start(bf16[384,1152]{1,0:T(8,128)(2,1)S(1)} %fusion.12), channel_id=1, source_target_pairs={{0,1},{1,2},{2,3},{3,4},{4,5},{5,6},{6,7},{7,8},{8,9},{9,10},{10,1... | collective-permute-start | bytes 2654216 | tf_op jit(solution)/shard_map/ppermute | solution.py:12
  68.7 60.4 %collective-permute-start.4 = (f32[384,1152]{1,0:T(8,128)S(1)}, f32[384,1152]{1,0:T(8,128)S(1)}, u32[]{:S(2)}, u32[]{:S(2)}) collective-permute-start(f32[384,1152]{1,0:T(8,128)S(1)} %convolution_add_fusion), channel_id=1, source_target_pairs={{0,1},{1,2},{2,3},{3,4},{4,5},{5,6},{6,7},{7,8},{8,9},{9,10},{10,1... | collective-permute-start | bytes 5308424 | tf_op jit(solution)/shard_map/ppermute | solution.py:12
  69.4 58.0 %collective-permute-start.1 = (bf16[384,1152]{1,0:T(8,128)(2,1)S(1)}, bf16[384,1152]{1,0:T(8,128)(2,1)S(1)}, u32[]{:S(2)}, u32[]{:S(2)}) collective-permute-start(bf16[384,1152]{1,0:T(8,128)(2,1)S(1)} %collective-permute-done), channel_id=1, source_target_pairs={{0,1},{1,2},{2,3},{3,4},{4,5},{5,6},{6,7},{7,8},{8,9},{9,10},{10,1... | collective-permute-start | bytes 2654216 | tf_op jit(solution)/shard_map/ppermute | solution.py:12
  129.3 59.3 %collective-permute-start.5 = (f32[384,1152]{1,0:T(8,128)S(1)}, f32[384,1152]{1,0:T(8,128)S(1)}, u32[]{:S(2)}, u32[]{:S(2)}) collective-permute-start(f32[384,1152]{1,0:T(8,128)S(1)} %add.108), channel_id=1, source_target_pairs={{0,1},{1,2},{2,3},{3,4},{4,5},{5,6},{6,7},{7,8},{8,9},{9,10},{10,1... | collective-permute-start | bytes 5308424 | tf_op jit(solution)/shard_map/ppermute | solution.py:12
  130.5 56.5 %collective-permute-start.2 = (bf16[384,1152]{1,0:T(8,128)(2,1)S(1)}, bf16[384,1152]{1,0:T(8,128)(2,1)S(1)}, u32[]{:S(2)}, u32[]{:S(2)}) collective-permute-start(bf16[384,1152]{1,0:T(8,128)(2,1)S(1)} %collective-permute-done.1), channel_id=1, source_target_pairs={{0,1},{1,2},{2,3},{3,4},{4,5},{5,6},{6,7},{7,8},{8,9},{9,10},{10,1... | collective-permute-start | bytes 2654216 | tf_op jit(solution)/shard_map/ppermute | solution.py:12
  188.8 7.7 %copy-start.1 = (bf16[384,1152]{1,0:T(8,128)(2,1)S(1)}, bf16[384,1152]{1,0:T(8,128)(2,1)}, u32[]{:S(2)}) copy-start(bf16[384,1152]{1,0:T(8,128)(2,1)} %param.4) | copy-start | bytes 2654212
  188.8 44.3 %collective-permute-start.6 = (f32[384,1152]{1,0:T(8,128)S(1)}, f32[384,1152]{1,0:T(8,128)S(1)}, u32[]{:S(2)}, u32[]{:S(2)}) collective-permute-start(f32[384,1152]{1,0:T(8,128)S(1)} %add.109), channel_id=1, source_target_pairs={{0,29},{1,30},{2,31},{3,0},{4,1},{5,2},{6,3},{7,4},{8,5},{9,6},{10... | collective-permute-start | bytes 5308424 | tf_op jit(solution)/shard_map/ppermute | solution.py:12
where the time goes:
time: 236 us; the launch traced here: 235 us
  waiting for transfers between devices  197 us (83%)
  starting transfers between devices  18.7 us (8%)
  matrix products  9.66 us (4%)
  other arithmetic  7.49 us (3%)
    ppermute x7, waiting for transfers between devices, from_behind(): return lax.ppermute(value, axis, pairs)  197 us
    ppermute x7, starting transfers between devices, from_behind(): return lax.ppermute(value, axis, pairs)  18.7 us
  transfers between devices with their start and end apart: 7, of which 4 were waited for; matrix products, arithmetic and copies ran while one was open for 4% of the time, Pallas kernels for 0%

commit v1 on v0

v1 whole, which is shorter than its diff:
```python
import jax
import jax.numpy as jnp
from jax import lax
from jax.experimental import pallas as pl
from jax.experimental.pallas import tpu as pltpu
from jax.sharding import PartitionSpec as P

SPAN = 4
GROUP = 4
AXES = ("blk", "inner")
F32 = jnp.float32
BF16 = jnp.bfloat16
VMEM_LIMIT = 48 * 1024 * 1024

CORE_SWAP = {0: (2, 0), 2: (0, 0), 1: (3, 0), 3: (1, 0)}
X_SWAP = {0: (1, 0), 1: (0, 0), 2: (3, 0), 3: (2, 0)}
GROUP_SHIFT = {0: (2, -1), 1: (3, -1), 2: (0, 1), 3: (1, 1)}


def send(value, moves):
    count = lax.axis_size(AXES)
    groups = count // GROUP
    pairs = [
        (g * GROUP + role, (g + step) % groups * GROUP + to)
        for g in range(groups)
        for role, (to, step) in moves.items()
    ]
    return lax.ppermute(value, AXES, pairs)


def unit_rows(raw):
    values = raw.astype(F32)
    length = jnp.sqrt(jnp.sum(values * values, axis=1, keepdims=True) + 1e-06)
    return values * (1.0 / length), length


def soft_terms(x):
    small = jnp.exp(-jnp.abs(x))
    below = small * (1.0 - small * (0.5 - small * (1.0 / 3.0)))
    log_part = jnp.where(small < 0.015625, below, jnp.log(1.0 + small))
    plus = jnp.maximum(x, 0.0) + log_part
    sigmoid = jnp.where(x >= 0.0, 1.0, small) / (1.0 + small)
    return plus, sigmoid


def dot_nt(a, b):
    return lax.dot_general(a, b, (((1,), (1,)), ((), ())), preferred_element_type=F32)


def dot_nn(a, b):
    return lax.dot_general(a, b, (((1,), (0,)), ((), ())), preferred_element_type=F32)


def dot_tn(a, b):
    return lax.dot_general(a, b, (((0,), (0,)), ((), ())), preferred_element_type=F32)


def lanes_sum(x):
    total = x[:, :128]
    for start in range(128, x.shape[1], 128):
        total = total + x[:, start : start + 128]
    return total


def pair_step(own, raw, scale, shift):
    block = unit_rows(raw)[0].astype(BF16)
    plus, sigmoid = soft_terms(scale * dot_nt(own, block) + shift)
    coef = (sigmoid * scale).astype(BF16)
    return dot_nn(coef, block), lanes_sum(plus)


def project(raw, grad):
    unit, length = unit_rows(raw)
    return ((grad - unit * jnp.sum(unit * grad, axis=1, keepdims=True)) / length).astype(BF16)


def own_kernel(flag, scal, image, text, z_u, z_w, grad_u, grad_w, loss):
    u_is_image = flag[0] == 1
    scale, shift = scal[0], scal[1]
    zi = unit_rows(image[...])[0].astype(BF16)
    zt = unit_rows(text[...])[0].astype(BF16)
    z_u[...] = jnp.where(u_is_image, zi, zt)
    z_w[...] = jnp.where(u_is_image, zt, zi)
    scores = scale * dot_nt(zi, zt) + shift
    rows = lax.broadcasted_iota(jnp.int32, scores.shape, 0)
    columns = lax.broadcasted_iota(jnp.int32, scores.shape, 1)
    sign = jnp.where(rows == columns, F32(-1.0), F32(1.0))
    plus, sigmoid = soft_terms(sign * scores)
    coef = (sign * sigmoid * scale).astype(BF16)
    loss[...] = lanes_sum(plus)
    grad_image = dot_nn(coef, zt)
    grad_text = dot_tn(coef, zi)
    grad_u[...] = jnp.where(u_is_image, grad_image, grad_text)
    grad_w[...] = jnp.where(u_is_image, grad_text, grad_image)


def near_kernel(flag, scal, b1, b2, b3, z_u, z_w, grad_u, grad_w, loss_in, out_u, out_w, loss):
    scale, shift = scal[0], scal[1]
    u_weight = flag[0].astype(F32)
    term1, loss1 = pair_step(z_w[...], b1[...], scale, shift)
    term2, loss2 = pair_step(z_u[...], b2[...], scale, shift)
    term3, loss3 = pair_step(z_w[...], b3[...], scale, shift)
    out_u[...] = grad_u[...] + term2
    out_w[...] = grad_w[...] + term1 + term3
    loss[...] = loss_in[...] + u_weight * loss2 + (1.0 - u_weight) * (loss1 + loss3)


def u_kernel(flag, scal, b4, b5, z_u, grad_u, loss_in, raw_u, out, loss):
    scale, shift = scal[0], scal[1]
    term4, loss4 = pair_step(z_u[...], b4[...], scale, shift)
    term5, loss5 = pair_step(z_u[...], b5[...], scale, shift)
    loss[...] = loss_in[...] + flag[0].astype(F32) * (loss4 + loss5)
    out[...] = project(raw_u[...], grad_u[...] + term4 + term5)


def w_kernel(flag, scal, b6, z_w, grad_w, loss_in, raw_w, done_u, image_grad, text_grad, loss_rows):
    u_is_image = flag[0] == 1
    scale, shift = scal[0], scal[1]
    term, row_loss = pair_step(z_w[...], b6[...], scale, shift)
    total = loss_in[...] + (1.0 - flag[0].astype(F32)) * row_loss
    per_row = jnp.sum(jnp.transpose(total), axis=0, keepdims=True)
    loss_rows[...] = per_row / (SPAN * total.shape[0])
    done_w = project(raw_w[...], grad_w[...] + term)
    image_grad[...] = jnp.where(u_is_image, done_u[...], done_w)
    text_grad[...] = jnp.where(u_is_image, done_w, done_u[...])


def call(kernel, args, outs, products, name):
    smem = pl.BlockSpec(memory_space=pltpu.SMEM)
    vmem = pl.BlockSpec(memory_space=pltpu.VMEM)
    rows, width = args[2].shape
    size = sum(a.size * a.dtype.itemsize for a in list(args) + list(outs))
    return pl.pallas_call(
        kernel,
        out_shape=outs,
        in_specs=[smem, smem] + [vmem] * (len(args) - 2),
        out_specs=[vmem] * len(outs),
        name=name,
        cost_estimate=pl.CostEstimate(
            flops=2 * rows * rows * width * products, bytes_accessed=size, transcendentals=0
        ),
        compiler_params=pltpu.CompilerParams(vmem_limit_bytes=VMEM_LIMIT),
    )(*args)


def local(image, text, score_scaling, score_shift):
    rows, width = image.shape
    role = lax.axis_index(AXES) % GROUP
    u_is_image = role < 2
    flag = u_is_image.astype(jnp.int32).reshape(1)
    scal = jnp.stack([score_scaling, score_shift])
    u = jnp.where(u_is_image, image, text)
    w = jnp.where(u_is_image, text, image)
    outer = (role == 0) | (role == 3)

    slot1 = send(w, CORE_SWAP)
    slot2 = send(u, GROUP_SHIFT)
    slot3 = send(jnp.where(outer, slot1, u), X_SWAP)
    slot4 = send(slot3, GROUP_SHIFT)
    slot5 = send(jnp.where(outer, w, slot2), X_SWAP)
    slot6 = send(slot5, CORE_SWAP)

    block = jax.ShapeDtypeStruct((rows, width), BF16)
    sums = jax.ShapeDtypeStruct((rows, width), F32)
    partial = jax.ShapeDtypeStruct((rows, 128), F32)
    line = jax.ShapeDtypeStruct((1, rows), F32)

    z_u, z_w, grad_u, grad_w, loss = call(
        own_kernel, (flag, scal, image, text), (block, block, sums, sums, partial), 3, "own_pair"
    )
    grad_u, grad_w, loss = call(
        near_kernel,
        (flag, scal, slot1, slot2, slot3, z_u, z_w, grad_u, grad_w, loss),
        (sums, sums, partial),
        6,
        "near_blocks",
    )
    done_u, loss = call(
        u_kernel, (flag, scal, slot4, slot5, z_u, grad_u, loss, u), (block, partial), 4, "finish_u"
    )
    image_grad, text_grad, loss_rows = call(
        w_kernel, (flag, scal, slot6, z_w, grad_w, loss, w, done_u), (block, block, line), 2, "finish_w"
    )
    return loss_rows.reshape(rows), image_grad, text_grad


def solution(mesh):
    in_specs = (P(AXES, None), P(AXES, None), P(), P())
    out_specs = (P(AXES), P(AXES, None), P(AXES, None))
    return jax.shard_map(local, mesh=mesh, in_specs=in_specs, out_specs=out_specs, check_vma=False)
```

time: 236 us -> 77.7 us (0.33)
  waiting for transfers between devices: 197 us -> 38.6 us
  Pallas kernels: 0 us -> 23.8 us
  starting transfers between devices: 18.7 us -> 6.92 us
  matrix products: 9.66 us -> 0 us
  other arithmetic: 7.49 us -> 2.33 us
  local copies, waits for them, and re-layouts: 0.01 us -> 3.35 us
    ppermute x7 -> x6, waiting for transfers between devices: 197 us -> 38.6 us  [send(): return lax.ppermute(value, AXES, pairs)]
    pallas_call x0 -> x4, Pallas kernels: none -> 23.8 us  [call(): pl.pallas_call(kernel, out_shape=outs, in_specs=[smem, smem] + [vmem] * (...]
    ppermute x7 -> x6, starting transfers between devices: 18.7 us -> 6.92 us  [send(): return lax.ppermute(value, AXES, pairs)]
    dot_general x12 -> x0, matrix products: 9.66 us -> none  [the longest x4 3.93 us: matrix_entries(): lax.dot_general(picture_summed, caption_summed, (((1,), (1,)), ((), ())),...]
    convert_element_type x4 -> x0, other arithmetic: 4.37 us -> none  [the longest x1 1.44 us: local(): picture_summed = image_unit.astype(jnp.bfloat16)]
    unnamed x4 -> x14, local copies, waits for them, and re-layouts: 0.01 us -> 3.35 us
  transfers between devices with their start and end apart: 7 -> 6, of which waited for: 4 -> 3; matrix products, arithmetic and copies ran while one was open for 4% -> 0% of each run, Pallas kernels for 0% -> 24%
where the time goes in v1:
time: 77.7 us; the launch traced here: 77 us
  waiting for transfers between devices  38.6 us (50%)
  Pallas kernels  23.8 us (31%)
  starting transfers between devices  6.92 us (9%)
  local copies, waits for them, and re-layouts  3.35 us (4%)
  other arithmetic  2.33 us (3%)
  between operations  2.01 us (3%)
    ppermute x6, waiting for transfers between devices, send(): return lax.ppermute(value, AXES, pairs)  38.6 us
    pallas_call x4, Pallas kernels, call(): pl.pallas_call(kernel, out_shape=outs, in_specs=[smem, smem] + [vmem] * (...  23.8 us
    ppermute x6, starting transfers between devices, send(): return lax.ppermute(value, AXES, pairs)  6.92 us
    unnamed x14, local copies, waits for them, and re-layouts  3.35 us
  transfers between devices with their start and end apart: 6, of which 3 were waited for; matrix products, arithmetic and copies ran while one was open for 0% of the time, Pallas kernels for 24%

profile of v1, /device:TPU:1, one launch (start us, length us, event | category | flops | bytes accessed | tf_op | source)
XLA Modules:
  0.0 77.0 jit_solution(573034036416165814)
XLA Ops:
  0.6 0.0 copy-start.1
  0.6 0.0 copy-start
  0.7 1.4 %broadcast_select_fusion.1.raw_w = bf16[384,1152]{1,0:T(8,128)(2,1)S(1)} fusion(bf16[384,1152]{1,0:T(8,128)(2,1)} %text.1, bf16[384,1152]{1,0:T(8,128)(2,1)} %image.1, pred[]{:T(512)S(6)} %lt.10), kind=kLoop, calls=%fused_computation.1 | loop fusion | flops 442368 | bytes 2654209 | tf_op jit(solution)/shard_map/jit(_where)/select_n | solution.py:153
  2.1 0.1 collective-permute-start.3
  2.2 2.4 %collective-permute-done.3.b1 = bf16[384,1152]{1,0:T(8,128)(2,1)S(1)} collective-permute-done((bf16[384,1152]{1,0:T(8,128)(2,1)S(1)}, bf16[384,1152]{1,0:T(8,128)(2,1)S(1)}, u32[]{:S(2)}, u32[]{:S(2)}) %collective-permute-start.3) | collective-permute-done | bytes 884768 | tf_op jit(solution)/shard_map/ppermute | solution.py:28
  4.6 0.0 copy-done.1
  4.6 0.0 copy-done
  4.6 0.2 broadcast_select_fusion.2
  4.7 2.7 %collective-permute-start = (bf16[384,1152]{1,0:T(8,128)(2,1)S(1)}, bf16[384,1152]{1,0:T(8,128)(2,1)S(1)}, u32[]{:S(2)}, u32[]{:S(2)}) collective-permute-start(bf16[384,1152]{1,0:T(8,128)(2,1)S(1)} %get-tuple-element.30.raw_u), channel_id=1, source_target_pairs={{0,30},{1,31},{2,4},{3,5},{4,2},{5,3},{6,8},{7,9},{8,6},{9,7},{10,... | collective-permute-start | bytes 2654216 | tf_op jit(solution)/shard_map/ppermute | solution.py:28
  7.4 0.0 copy-start.3
  7.4 0.9 %copy-done.3 = bf16[384,1152]{1,0:T(8,128)(2,1)} copy-done((bf16[384,1152]{1,0:T(8,128)(2,1)}, bf16[384,1152]{1,0:T(8,128)(2,1)S(1)}, u32[]{:S(2)}) %copy-start.3) | copy-done | bytes 884760
  8.3 1.2 %collective-permute-start.4 = (bf16[384,1152]{1,0:T(8,128)(2,1)S(1)}, bf16[384,1152]{1,0:T(8,128)(2,1)}, u32[]{:S(2)}, u32[]{:S(2)}) collective-permute-start(bf16[384,1152]{1,0:T(8,128)(2,1)S(1)} %get-tuple-element.29), channel_id=1, source_target_pairs={{0,1},{1,0},{2,3},{3,2},{4,5},{5,4},{6,7},{7,6},{8,9},{9,8},{10,11... | collective-permute-start | bytes 2654216 | tf_op jit(solution)/shard_map/ppermute | solution.py:28
  9.6 18.5 %collective-permute-done.b2 = bf16[384,1152]{1,0:T(8,128)(2,1)S(1)} collective-permute-done((bf16[384,1152]{1,0:T(8,128)(2,1)S(1)}, bf16[384,1152]{1,0:T(8,128)(2,1)S(1)}, u32[]{:S(2)}, u32[]{:S(2)}) %collective-permute-start) | collective-permute-done | bytes 884768 | tf_op jit(solution)/shard_map/ppermute | solution.py:28
  28.0 0.1 broadcast_select_fusion.3
  28.1 1.5 %collective-permute-start.1 = (bf16[384,1152]{1,0:T(8,128)(2,1)S(1)}, bf16[384,1152]{1,0:T(8,128)(2,1)}, u32[]{:S(2)}, u32[]{:S(2)}) collective-permute-start(bf16[384,1152]{1,0:T(8,128)(2,1)S(1)} %broadcast_select_fusion.3), channel_id=1, source_target_pairs={{0,1},{1,0},{2,3},{3,2},{4,5},{5,4},{6,7},{7,6},{8,9},{9,8},{10,11... | collective-permute-start | bytes 2654216 | tf_op jit(solution)/shard_map/ppermute | solution.py:28
  29.7 0.0 collective-permute-done.4.b3
  29.7 1.4 %collective-permute-start.5 = (bf16[384,1152]{1,0:T(8,128)(2,1)}, bf16[384,1152]{1,0:T(8,128)(2,1)}, u32[]{:S(2)}, u32[]{:S(2)}) collective-permute-start(bf16[384,1152]{1,0:T(8,128)(2,1)} %collective-permute-done.4.b3), channel_id=1, source_target_pairs={{0,30},{1,31},{2,4},{3,5},{4,2},{5,3},{6,8},{7,9},{8,6},{9,7},{10,... | collective-permute-start | bytes 2654216 | tf_op jit(solution)/shard_map/ppermute | solution.py:28
  31.0 17.7 %collective-permute-done.1.b5 = bf16[384,1152]{1,0:T(8,128)(2,1)} collective-permute-done((bf16[384,1152]{1,0:T(8,128)(2,1)S(1)}, bf16[384,1152]{1,0:T(8,128)(2,1)}, u32[]{:S(2)}, u32[]{:S(2)}) %collective-permute-start.1) | collective-permute-done | bytes 884768 | tf_op jit(solution)/shard_map/ppermute | solution.py:28
  48.8 0.0 collective-permute-start.2
  50.1 0.1 pad_maximum_fusion.scal
  50.2 0.0 copy-start.2
  50.2 1.2 %copy-done.2 = bf16[384,1152]{1,0:T(8,128)(2,1)S(1)} copy-done((bf16[384,1152]{1,0:T(8,128)(2,1)S(1)}, bf16[384,1152]{1,0:T(8,128)(2,1)}, u32[]{:S(2)}) %copy-start.2) | copy-done | bytes 884760
  51.3 4.4 %own_pair.1 = (bf16[384,1152]{1,0:T(8,128)(2,1)S(1)}, bf16[384,1152]{1,0:T(8,128)(2,1)S(1)}, f32[384,1152]{1,0:T(8,128)S(1)}, f32[384,1152]{1,0:T(8,128)}, f32[384,128]{1,0:T(8,128)S(1)}) custom-call(s32[1]{0:T(128)} %bitcast.flag, f32[2]{0:T(128)S(1)} %pad_maximum_fusion.scal, bf16[384,1152]{1,0:T(8,128)(2,1)S(1)} %copy-done.2, bf16[384,1152]{1,0:T(8,128)(2,1)S(1)} %copy-done), custom_call_target="tpu_custom_call" | custom-call | flops 1019215872 | bytes 7274508 | tf_op jit(solution)/shard_map/own_pair/pallas_call | solution.py:133
  55.8 0.0 copy-start.6
  55.8 1.3 %copy-done.6 = f32[384,1152]{1,0:T(8,128)} copy-done((f32[384,1152]{1,0:T(8,128)}, f32[384,1152]{1,0:T(8,128)S(1)}, u32[]{:S(2)}) %copy-start.6) | copy-done | bytes 1769496
  57.0 0.0 copy-start.4
  57.0 8.5 %near_blocks.1 = (f32[384,1152]{1,0:T(8,128)}, f32[384,1152]{1,0:T(8,128)}, f32[384,128]{1,0:T(8,128)S(1)}) custom-call(s32[1]{0:T(128)} %bitcast.flag, f32[2]{0:T(128)S(1)} %pad_maximum_fusion.scal, bf16[384,1152]{1,0:T(8,128)(2,1)S(1)} %collective-permute-done.3.b1, bf16[384,1152]{1,0:T(8,128)(2,1)S(1)} %collective-permute-done.b2, ...), custom_call_target="tpu_custom_call" | custom-call | flops 2038431744 | bytes 11894796 | tf_op jit(solution)/shard_map/near_blocks/pallas_call | solution.py:133
  65.5 0.0 collective-permute-done.5.b4
  65.5 0.0 copy-done.4
  65.5 0.0 copy-start.5
  65.5 5.9 %finish_u.1 = (bf16[384,1152]{1,0:T(8,128)(2,1)S(1)}, f32[384,128]{1,0:T(8,128)S(1)}) custom-call(s32[1]{0:T(128)} %bitcast.flag, f32[2]{0:T(128)S(1)} %pad_maximum_fusion.scal, bf16[384,1152]{1,0:T(8,128)(2,1)} %collective-permute-done.5.b4, bf16[384,1152]{1,0:T(8,128)(2,1)} %collective-permute-done.1.b5, bf16[384,1152]{1,0:T(8,128)(2,1)S(1)} %get-tuple-element.17.z_u, ...), custom_call_target="tpu_custom_call" | custom-call | flops 1358954496 | bytes 6586380 | tf_op jit(solution)/shard_map/finish_u/pallas_call | solution.py:133
  71.4 0.0 collective-permute-done.2.b6
  71.4 0.0 copy-done.5
  71.4 5.0 %finish_w.1 = (bf16[384,1152]{1,0:T(8,128)(2,1)}, bf16[384,1152]{1,0:T(8,128)(2,1)}, f32[1,384]{1,0:T(1,128)S(1)}) custom-call(s32[1]{0:T(128)} %bitcast.flag, f32[2]{0:T(128)S(1)} %pad_maximum_fusion.scal, bf16[384,1152]{1,0:T(8,128)(2,1)} %collective-permute-done.2.b6, bf16[384,1152]{1,0:T(8,128)(2,1)S(1)} %get-tuple-element.16.z_w, ...), custom_call_target="tpu_custom_call" | custom-call | flops 679477248 | bytes 7276044 | tf_op jit(solution)/shard_map/finish_w/pallas_call | solution.py:133
  76.4 0.6 reduce
Async XLA Ops:
  0.6 3.9 %copy-start.1 = (bf16[384,1152]{1,0:T(8,128)(2,1)S(1)}, bf16[384,1152]{1,0:T(8,128)(2,1)}, u32[]{:S(2)}) copy-start(bf16[384,1152]{1,0:T(8,128)(2,1)} %image.1) | copy-start | bytes 2654212
  0.6 3.9 %copy-start = (bf16[384,1152]{1,0:T(8,128)(2,1)S(1)}, bf16[384,1152]{1,0:T(8,128)(2,1)}, u32[]{:S(2)}) copy-start(bf16[384,1152]{1,0:T(8,128)(2,1)} %text.1) | copy-start | bytes 2654212
  2.1 2.5 %collective-permute-start.3 = (bf16[384,1152]{1,0:T(8,128)(2,1)S(1)}, bf16[384,1152]{1,0:T(8,128)(2,1)S(1)}, u32[]{:S(2)}, u32[]{:S(2)}) collective-permute-start(bf16[384,1152]{1,0:T(8,128)(2,1)S(1)} %broadcast_select_fusion.1.raw_w), channel_id=1, source_target_pairs={{0,2},{2,0},{1,3},{3,1},{4,6},{6,4},{5,7},{7,5},{8,10},{10,8},{9,1... | collective-permute-start | bytes 2654216 | tf_op jit(solution)/shard_map/ppermute | solution.py:28
  4.7 23.3 %collective-permute-start = (bf16[384,1152]{1,0:T(8,128)(2,1)S(1)}, bf16[384,1152]{1,0:T(8,128)(2,1)S(1)}, u32[]{:S(2)}, u32[]{:S(2)}) collective-permute-start(bf16[384,1152]{1,0:T(8,128)(2,1)S(1)} %get-tuple-element.30.raw_u), channel_id=1, source_target_pairs={{0,30},{1,31},{2,4},{3,5},{4,2},{5,3},{6,8},{7,9},{8,6},{9,7},{10,... | collective-permute-start | bytes 2654216 | tf_op jit(solution)/shard_map/ppermute | solution.py:28
  7.4 0.9 %copy-start.3 = (bf16[384,1152]{1,0:T(8,128)(2,1)}, bf16[384,1152]{1,0:T(8,128)(2,1)S(1)}, u32[]{:S(2)}) copy-start(bf16[384,1152]{1,0:T(8,128)(2,1)S(1)} %get-tuple-element.30.raw_u) | copy-start | bytes 2654212
  8.3 21.3 %collective-permute-start.4 = (bf16[384,1152]{1,0:T(8,128)(2,1)S(1)}, bf16[384,1152]{1,0:T(8,128)(2,1)}, u32[]{:S(2)}, u32[]{:S(2)}) collective-permute-start(bf16[384,1152]{1,0:T(8,128)(2,1)S(1)} %get-tuple-element.29), channel_id=1, source_target_pairs={{0,1},{1,0},{2,3},{3,2},{4,5},{5,4},{6,7},{7,6},{8,9},{9,8},{10,11... | collective-permute-start | bytes 2654216 | tf_op jit(solution)/shard_map/ppermute | solution.py:28
  28.1 20.6 %collective-permute-start.1 = (bf16[384,1152]{1,0:T(8,128)(2,1)S(1)}, bf16[384,1152]{1,0:T(8,128)(2,1)}, u32[]{:S(2)}, u32[]{:S(2)}) collective-permute-start(bf16[384,1152]{1,0:T(8,128)(2,1)S(1)} %broadcast_select_fusion.3), channel_id=1, source_target_pairs={{0,1},{1,0},{2,3},{3,2},{4,5},{5,4},{6,7},{7,6},{8,9},{9,8},{10,11... | collective-permute-start | bytes 2654216 | tf_op jit(solution)/shard_map/ppermute | solution.py:28
  29.7 35.8 %collective-permute-start.5 = (bf16[384,1152]{1,0:T(8,128)(2,1)}, bf16[384,1152]{1,0:T(8,128)(2,1)}, u32[]{:S(2)}, u32[]{:S(2)}) collective-permute-start(bf16[384,1152]{1,0:T(8,128)(2,1)} %collective-permute-done.4.b3), channel_id=1, source_target_pairs={{0,30},{1,31},{2,4},{3,5},{4,2},{5,3},{6,8},{7,9},{8,6},{9,7},{10,... | collective-permute-start | bytes 2654216 | tf_op jit(solution)/shard_map/ppermute | solution.py:28
  48.8 22.6 %collective-permute-start.2 = (bf16[384,1152]{1,0:T(8,128)(2,1)}, bf16[384,1152]{1,0:T(8,128)(2,1)}, u32[]{:S(2)}, u32[]{:S(2)}) collective-permute-start(bf16[384,1152]{1,0:T(8,128)(2,1)} %collective-permute-done.1.b5), channel_id=1, source_target_pairs={{0,2},{2,0},{1,3},{3,1},{4,6},{6,4},{5,7},{7,5},{8,10},{10,8},{9,1... | collective-permute-start | bytes 2654216 | tf_op jit(solution)/shard_map/ppermute | solution.py:28
  50.2 1.2 %copy-start.2 = (bf16[384,1152]{1,0:T(8,128)(2,1)S(1)}, bf16[384,1152]{1,0:T(8,128)(2,1)}, u32[]{:S(2)}) copy-start(bf16[384,1152]{1,0:T(8,128)(2,1)} %image.1) | copy-start | bytes 2654212
  55.8 1.3 %copy-start.6 = (f32[384,1152]{1,0:T(8,128)}, f32[384,1152]{1,0:T(8,128)S(1)}, u32[]{:S(2)}) copy-start(f32[384,1152]{1,0:T(8,128)S(1)} %get-tuple-element.18.grad_u) | copy-start | bytes 5308420
  57.0 8.5 %copy-start.4 = (bf16[384,1152]{1,0:T(8,128)(2,1)S(1)}, bf16[384,1152]{1,0:T(8,128)(2,1)}, u32[]{:S(2)}) copy-start(bf16[384,1152]{1,0:T(8,128)(2,1)} %copy-done.3) | copy-start | bytes 2654212
  65.5 5.9 %copy-start.5 = (f32[384,1152]{1,0:T(8,128)S(1)}, f32[384,1152]{1,0:T(8,128)}, u32[]{:S(2)}) copy-start(f32[384,1152]{1,0:T(8,128)} %get-tuple-element.21.grad_w) | copy-start | bytes 5308420

commit v2 on v1

--- a/solution.py
+++ b/solution.py
@@ -14,6 +14,8 @@
 
 CORE_SWAP = {0: (2, 0), 2: (0, 0), 1: (3, 0), 3: (1, 0)}
 X_SWAP = {0: (1, 0), 1: (0, 0), 2: (3, 0), 3: (2, 0)}
+IMAGE_BACK = {1: (0, 0), 2: (1, 0)}
+TEXT_ON = {1: (2, 0), 2: (3, 0)}
 GROUP_SHIFT = {0: (2, -1), 1: (3, -1), 2: (0, 1), 3: (1, 1)}
 
 
@@ -34,13 +36,28 @@
     return values * (1.0 / length), length
 
 
-def soft_terms(x):
-    small = jnp.exp(-jnp.abs(x))
-    below = small * (1.0 - small * (0.5 - small * (1.0 / 3.0)))
-    log_part = jnp.where(small < 0.015625, below, jnp.log(1.0 + small))
-    plus = jnp.maximum(x, 0.0) + log_part
-    sigmoid = jnp.where(x >= 0.0, 1.0, small) / (1.0 + small)
-    return plus, sigmoid
+def sigmoid_of(p):
+    whole = 1.0 + p
+    guess = pl.reciprocal(whole, approx=True)
+    guess = guess * (2.0 - whole * guess)
+    return p * (guess * (2.0 - whole * guess))
+
+
+def log1p_of(p):
+    below = p * (1.0 - p * (0.5 - p * (1.0 / 3.0)))
+    return jnp.where(p < 0.015625, below, jnp.log(1.0 + p))
+
+
+def softplus_lanes(p):
+    total = None
+    parts = [p[:, start : start + 128] for start in range(0, p.shape[1], 128)]
+    for first in range(0, len(parts), 3):
+        joint = parts[first]
+        for part in parts[first + 1 : first + 3]:
+            joint = joint + part + joint * part
+        value = log1p_of(joint)
+        total = value if total is None else total + value
+    return total
 
 
 def dot_nt(a, b):
@@ -55,18 +72,11 @@
     return lax.dot_general(a, b, (((0,), (0,)), ((), ())), preferred_element_type=F32)
 
 
-def lanes_sum(x):
-    total = x[:, :128]
-    for start in range(128, x.shape[1], 128):
-        total = total + x[:, start : start + 128]
-    return total
-
-
 def pair_step(own, raw, scale, shift):
     block = unit_rows(raw)[0].astype(BF16)
-    plus, sigmoid = soft_terms(scale * dot_nt(own, block) + shift)
-    coef = (sigmoid * scale).astype(BF16)
-    return dot_nn(coef, block), lanes_sum(plus)
+    p = jnp.exp(scale * dot_nt(own, block) + shift)
+    coef = (sigmoid_of(p) * scale).astype(BF16)
+    return dot_nn(coef, block), softplus_lanes(p)
 
 
 def project(raw, grad):
@@ -85,24 +95,30 @@
     rows = lax.broadcasted_iota(jnp.int32, scores.shape, 0)
     columns = lax.broadcasted_iota(jnp.int32, scores.shape, 1)
     sign = jnp.where(rows == columns, F32(-1.0), F32(1.0))
-    plus, sigmoid = soft_terms(sign * scores)
-    coef = (sign * sigmoid * scale).astype(BF16)
-    loss[...] = lanes_sum(plus)
+    p = jnp.exp(sign * scores)
+    coef = (sign * sigmoid_of(p) * scale).astype(BF16)
+    loss[...] = softplus_lanes(p)
     grad_image = dot_nn(coef, zt)
     grad_text = dot_tn(coef, zi)
     grad_u[...] = jnp.where(u_is_image, grad_image, grad_text)
     grad_w[...] = jnp.where(u_is_image, grad_text, grad_image)
 
 
-def near_kernel(flag, scal, b1, b2, b3, z_u, z_w, grad_u, grad_w, loss_in, out_u, out_w, loss):
+def first_kernel(flag, scal, b1, z_w, grad_w, loss_in, out_w, loss):
+    scale, shift = scal[0], scal[1]
+    term, row_loss = pair_step(z_w[...], b1[...], scale, shift)
+    out_w[...] = grad_w[...] + term
+    loss[...] = loss_in[...] + (1.0 - flag[0].astype(F32)) * row_loss
+
+
+def near_kernel(flag, scal, b2, b3, z_u, z_w, grad_u, grad_w, loss_in, out_u, out_w, loss):
     scale, shift = scal[0], scal[1]
     u_weight = flag[0].astype(F32)
-    term1, loss1 = pair_step(z_w[...], b1[...], scale, shift)
     term2, loss2 = pair_step(z_u[...], b2[...], scale, shift)
     term3, loss3 = pair_step(z_w[...], b3[...], scale, shift)
     out_u[...] = grad_u[...] + term2
-    out_w[...] = grad_w[...] + term1 + term3
-    loss[...] = loss_in[...] + u_weight * loss2 + (1.0 - u_weight) * (loss1 + loss3)
+    out_w[...] = grad_w[...] + term3
+    loss[...] = loss_in[...] + u_weight * loss2 + (1.0 - u_weight) * loss3
 
 
 def u_kernel(flag, scal, b4, b5, z_u, grad_u, loss_in, raw_u, out, loss):
@@ -153,28 +169,32 @@
     w = jnp.where(u_is_image, text, image)
     outer = (role == 0) | (role == 3)
 
-    slot1 = send(w, CORE_SWAP)
-    slot2 = send(u, GROUP_SHIFT)
-    slot3 = send(jnp.where(outer, slot1, u), X_SWAP)
-    slot4 = send(slot3, GROUP_SHIFT)
-    slot5 = send(jnp.where(outer, w, slot2), X_SWAP)
-    slot6 = send(slot5, CORE_SWAP)
-
     block = jax.ShapeDtypeStruct((rows, width), BF16)
     sums = jax.ShapeDtypeStruct((rows, width), F32)
     partial = jax.ShapeDtypeStruct((rows, 128), F32)
     line = jax.ShapeDtypeStruct((1, rows), F32)
 
+    slot1 = send(w, CORE_SWAP)
+    slot2 = send(u, GROUP_SHIFT)
+    slot3 = jnp.where(u_is_image, send(image, IMAGE_BACK), send(text, TEXT_ON))
     z_u, z_w, grad_u, grad_w, loss = call(
         own_kernel, (flag, scal, image, text), (block, block, sums, sums, partial), 3, "own_pair"
     )
+    grad_w, loss = call(
+        first_kernel, (flag, scal, slot1, z_w, grad_w, loss), (sums, partial), 2, "first_block"
+    )
+    w_sent, grad_w, loss = lax.optimization_barrier((w, grad_w, loss))
+    slot5 = send(jnp.where(outer, w_sent, slot2), X_SWAP)
+    slot4 = send(slot3, GROUP_SHIFT)
     grad_u, grad_w, loss = call(
         near_kernel,
-        (flag, scal, slot1, slot2, slot3, z_u, z_w, grad_u, grad_w, loss),
+        (flag, scal, slot2, slot3, z_u, z_w, grad_u, grad_w, loss),
         (sums, sums, partial),
-        6,
+        4,
         "near_blocks",
     )
+    slot5, grad_u, grad_w, loss = lax.optimization_barrier((slot5, grad_u, grad_w, loss))
+    slot6 = send(slot5, CORE_SWAP)
     done_u, loss = call(
         u_kernel, (flag, scal, slot4, slot5, z_u, grad_u, loss, u), (block, partial), 4, "finish_u"
     )

time: 77.7 us -> 67.9 us (0.87)
  waiting for transfers between devices: 38.6 us -> 19.7 us
  starting transfers between devices: 6.92 us -> 15.2 us
  other arithmetic: 2.33 us -> 3.65 us
    ppermute x6 -> x7, waiting for transfers between devices: 38.6 us -> 19.7 us  [send(): return lax.ppermute(value, AXES, pairs)]
    ppermute x6 -> x7, starting transfers between devices: 6.92 us -> 15.2 us  [send(): return lax.ppermute(value, AXES, pairs)]
    select_n x3, other arithmetic: 1.66 us -> 2.98 us  [the longest x1 1.6 us: local(): u = jnp.where(u_is_image, image, text)]
    pallas_call x4 -> x5, Pallas kernels: 23.8 us -> 23.1 us  [call(): pl.pallas_call(kernel, out_shape=outs, in_specs=[smem, smem] + [vmem] * (...]
    unnamed x14 -> x10, local copies, waits for them, and re-layouts: 3.35 us -> 3.96 us
  transfers between devices with their start and end apart: 6 -> 7, of which waited for: 3 -> 3; matrix products, arithmetic and copies ran while one was open for 0% -> 2% of each run, Pallas kernels for 24% -> 28%
where the time goes in v2:
time: 67.9 us; the launch traced here: 67.6 us
  Pallas kernels  23.1 us (34%)
  waiting for transfers between devices  19.7 us (29%)
  starting transfers between devices  15.2 us (22%)
  local copies, waits for them, and re-layouts  3.96 us (6%)
  other arithmetic  3.65 us (5%)
  between operations  2.05 us (3%)
    pallas_call x5, Pallas kernels, call(): pl.pallas_call(kernel, out_shape=outs, in_specs=[smem, smem] + [vmem] * (...  23.1 us
    ppermute x7, waiting for transfers between devices, send(): return lax.ppermute(value, AXES, pairs)  19.7 us
    ppermute x7, starting transfers between devices, send(): return lax.ppermute(value, AXES, pairs)  15.2 us
    unnamed x10, local copies, waits for them, and re-layouts  3.96 us
    select_n x1, other arithmetic, local(): u = jnp.where(u_is_image, image, text)  1.6 us
  transfers between devices with their start and end apart: 7, of which 3 were waited for; matrix products, arithmetic and copies ran while one was open for 2% of the time, Pallas kernels for 28%

profile of v2, /device:TPU:1, one launch (start us, length us, event | category | flops | bytes accessed | tf_op | source)
XLA Modules:
  0.0 67.6 jit_solution(7592588516154018327)
XLA Ops:
  0.6 1.6 %broadcast_select_fusion.1 = (bf16[384,1152]{1,0:T(8,128)(2,1)S(1)}, bf16[384,1152]{1,0:T(8,128)(2,1)S(1)}) fusion(bf16[384,1152]{1,0:T(8,128)(2,1)} %image.1, bf16[384,1152]{1,0:T(8,128)(2,1)} %text.1, pred[]{:T(512)S(6)} %lt.10), kind=kLoop, calls=%fused_computation.1 | loop fusion | flops 884736 | bytes 3538945 | tf_op jit(solution)/shard_map/jit(_where)/select_n | solution.py:168
  2.2 0.1 collective-permute-start
  2.4 2.7 %collective-permute-start.1 = (bf16[384,1152]{1,0:T(8,128)(2,1)S(1)}, bf16[384,1152]{1,0:T(8,128)(2,1)S(1)}, u32[]{:S(2)}, u32[]{:S(2)}) collective-permute-start(bf16[384,1152]{1,0:T(8,128)(2,1)S(1)} %get-tuple-element.47.raw_u), channel_id=1, source_target_pairs={{0,30},{1,31},{2,4},{3,5},{4,2},{5,3},{6,8},{7,9},{8,6},{9,7},{10,... | collective-permute-start | bytes 2654216 | tf_op jit(solution)/shard_map/ppermute | solution.py:30
  5.0 7.4 %collective-permute-start.3 = (bf16[384,1152]{1,0:T(8,128)(2,1)}, bf16[384,1152]{1,0:T(8,128)(2,1)}, u32[]{:S(2)}, u32[]{:S(2)}) collective-permute-start(bf16[384,1152]{1,0:T(8,128)(2,1)} %image.1), channel_id=1, source_target_pairs={{1,0},{2,1},{5,4},{6,5},{9,8},{10,9},{13,12},{14,13},{17,16},{18,1... | collective-permute-start | bytes 2654216 | tf_op jit(solution)/shard_map/ppermute | solution.py:30
  12.4 1.9 %collective-permute-start.4 = (bf16[384,1152]{1,0:T(8,128)(2,1)}, bf16[384,1152]{1,0:T(8,128)(2,1)}, u32[]{:S(2)}, u32[]{:S(2)}) collective-permute-start(bf16[384,1152]{1,0:T(8,128)(2,1)} %text.1), channel_id=1, source_target_pairs={{1,2},{2,3},{5,6},{6,7},{9,10},{10,11},{13,14},{14,15},{17,18},{18... | collective-permute-start | bytes 2654216 | tf_op jit(solution)/shard_map/ppermute | solution.py:30
  15.6 0.1 pad_maximum_fusion.scal
  15.7 5.2 %own_pair.1 = (bf16[384,1152]{1,0:T(8,128)(2,1)S(1)}, bf16[384,1152]{1,0:T(8,128)(2,1)S(1)}, f32[384,1152]{1,0:T(8,128)S(1)}, f32[384,1152]{1,0:T(8,128)}, f32[384,128]{1,0:T(8,128)S(1)}) custom-call(s32[1]{0:T(128)} %bitcast.flag, f32[2]{0:T(128)S(1)} %pad_maximum_fusion.scal, bf16[384,1152]{1,0:T(8,128)(2,1)} %image.1, bf16[384,1152]{1,0:T(8,128)(2,1)} %text.1), custom_call_target="tpu_custom_call" | custom-call | flops 1019215872 | bytes 7274508 | tf_op jit(solution)/shard_map/own_pair/pallas_call | solution.py:149
  20.9 0.0 copy-start.3
  20.9 1.2 %copy-done.3 = f32[384,1152]{1,0:T(8,128)} copy-done((f32[384,1152]{1,0:T(8,128)}, f32[384,1152]{1,0:T(8,128)S(1)}, u32[]{:S(2)}) %copy-start.3) | copy-done | bytes 1769496
  22.2 0.0 collective-permute-done.b1
  22.2 0.0 copy-start.2
  22.2 1.5 %copy-done.2 = f32[384,1152]{1,0:T(8,128)S(1)} copy-done((f32[384,1152]{1,0:T(8,128)S(1)}, f32[384,1152]{1,0:T(8,128)}, u32[]{:S(2)}) %copy-start.2) | copy-done | bytes 1769496
  23.7 2.3 %first_block.1 = (f32[384,1152]{1,0:T(8,128)S(1)}, f32[384,128]{1,0:T(8,128)S(1)}) custom-call(s32[1]{0:T(128)} %bitcast.flag, f32[2]{0:T(128)S(1)} %pad_maximum_fusion.scal, bf16[384,1152]{1,0:T(8,128)(2,1)S(1)} %collective-permute-done.b1, bf16[384,1152]{1,0:T(8,128)(2,1)S(1)} %get-tuple-element.25.z_w, f32[384,1152]{1,0:T(8,128)S(1)} %copy-done.2, ...), custom_call_target="tpu_custom_call" | custom-call | flops 679477248 | bytes 5701644 | tf_op jit(solution)/shard_map/first_block/pallas_call | solution.py:149
  25.9 0.0 copy-start.4
  26.0 0.0 collective-permute-done.1.b2
  26.0 0.1 broadcast_select_fusion.3
  26.1 1.1 %collective-permute-start.2 = (bf16[384,1152]{1,0:T(8,128)(2,1)S(1)}, bf16[384,1152]{1,0:T(8,128)(2,1)S(1)}, u32[]{:S(2)}, u32[]{:S(2)}) collective-permute-start(bf16[384,1152]{1,0:T(8,128)(2,1)S(1)} %broadcast_select_fusion.3), channel_id=1, source_target_pairs={{0,1},{1,0},{2,3},{3,2},{4,5},{5,4},{6,7},{7,6},{8,9},{9,8},{10,11... | collective-permute-start | bytes 2654216 | tf_op jit(solution)/shard_map/ppermute | solution.py:30
  27.1 0.0 collective-permute-done.3
  27.2 9.2 %collective-permute-done.4 = bf16[384,1152]{1,0:T(8,128)(2,1)} collective-permute-done((bf16[384,1152]{1,0:T(8,128)(2,1)}, bf16[384,1152]{1,0:T(8,128)(2,1)}, u32[]{:S(2)}, u32[]{:S(2)}) %collective-permute-start.4) | collective-permute-done | bytes 884768 | tf_op jit(solution)/shard_map/ppermute | solution.py:30
  36.3 1.3 %broadcast_select_fusion.b3 = bf16[384,1152]{1,0:T(8,128)(2,1)S(1)} fusion(bf16[384,1152]{1,0:T(8,128)(2,1)} %collective-permute-done.3, bf16[384,1152]{1,0:T(8,128)(2,1)} %collective-permute-done.4, pred[]{:T(512)S(6)} %lt.10), kind=kLoop, calls=%fused_computation | loop fusion | flops 442368 | bytes 2654209 | tf_op jit(solution)/shard_map/jit(_where)/select_n | solution.py:179
  37.6 0.0 copy-done.4
  37.6 0.1 collective-permute-start.6
  37.7 6.4 %near_blocks.1 = (f32[384,1152]{1,0:T(8,128)S(1)}, f32[384,1152]{1,0:T(8,128)}, f32[384,128]{1,0:T(8,128)S(1)}) custom-call(s32[1]{0:T(128)} %bitcast.flag, f32[2]{0:T(128)S(1)} %pad_maximum_fusion.scal, bf16[384,1152]{1,0:T(8,128)(2,1)S(1)} %collective-permute-done.1.b2, bf16[384,1152]{1,0:T(8,128)(2,1)S(1)} %broadcast_select_fusion.b3, ...), custom_call_target="tpu_custom_call" | custom-call | flops 1358954496 | bytes 11010060 | tf_op jit(solution)/shard_map/near_blocks/pallas_call | solution.py:149
  44.1 0.0 copy-start.1
  44.1 1.2 %copy-done.1 = f32[384,1152]{1,0:T(8,128)} copy-done((f32[384,1152]{1,0:T(8,128)}, f32[384,1152]{1,0:T(8,128)S(1)}, u32[]{:S(2)}) %copy-start.1) | copy-done | bytes 1769496
  45.3 4.8 %collective-permute-done.2.b5 = bf16[384,1152]{1,0:T(8,128)(2,1)S(1)} collective-permute-done((bf16[384,1152]{1,0:T(8,128)(2,1)S(1)}, bf16[384,1152]{1,0:T(8,128)(2,1)S(1)}, u32[]{:S(2)}, u32[]{:S(2)}) %collective-permute-start.2) | collective-permute-done | bytes 884768 | tf_op jit(solution)/shard_map/ppermute | solution.py:30
  50.1 0.0 copy-start
  50.1 2.0 %collective-permute-start.5 = (bf16[384,1152]{1,0:T(8,128)(2,1)S(1)}, bf16[384,1152]{1,0:T(8,128)(2,1)S(1)}, u32[]{:S(2)}, u32[]{:S(2)}) collective-permute-start(bf16[384,1152]{1,0:T(8,128)(2,1)S(1)} %collective-permute-done.2.b5), channel_id=1, source_target_pairs={{0,2},{2,0},{1,3},{3,1},{4,6},{6,4},{5,7},{7,5},{8,10},{10,8},{9,1... | collective-permute-start | bytes 2654216 | tf_op jit(solution)/shard_map/ppermute | solution.py:30
  52.1 5.7 %collective-permute-done.6.b4 = bf16[384,1152]{1,0:T(8,128)(2,1)S(1)} collective-permute-done((bf16[384,1152]{1,0:T(8,128)(2,1)S(1)}, bf16[384,1152]{1,0:T(8,128)(2,1)S(1)}, u32[]{:S(2)}, u32[]{:S(2)}) %collective-permute-start.6) | collective-permute-done | bytes 884768 | tf_op jit(solution)/shard_map/ppermute | solution.py:30
  57.8 5.0 %finish_u.1 = (bf16[384,1152]{1,0:T(8,128)(2,1)S(1)}, f32[384,128]{1,0:T(8,128)S(1)}) custom-call(s32[1]{0:T(128)} %bitcast.flag, f32[2]{0:T(128)S(1)} %pad_maximum_fusion.scal, bf16[384,1152]{1,0:T(8,128)(2,1)S(1)} %collective-permute-done.6.b4, bf16[384,1152]{1,0:T(8,128)(2,1)S(1)} %collective-permute-done.2.b5, ...), custom_call_target="tpu_custom_call" | custom-call | flops 1358954496 | bytes 6586380 | tf_op jit(solution)/shard_map/finish_u/pallas_call | solution.py:149
  62.8 0.0 collective-permute-done.5.b6
  62.8 0.0 copy-done
  62.8 4.2 %finish_w.1 = (bf16[384,1152]{1,0:T(8,128)(2,1)}, bf16[384,1152]{1,0:T(8,128)(2,1)}, f32[1,384]{1,0:T(1,128)S(1)}) custom-call(s32[1]{0:T(128)} %bitcast.flag, f32[2]{0:T(128)S(1)} %pad_maximum_fusion.scal, bf16[384,1152]{1,0:T(8,128)(2,1)S(1)} %collective-permute-done.5.b6, bf16[384,1152]{1,0:T(8,128)(2,1)S(1)} %get-tuple-element.25.z_w, ...), custom_call_target="tpu_custom_call" | custom-call | flops 679477248 | bytes 7276044 | tf_op jit(solution)/shard_map/finish_w/pallas_call | solution.py:149
  67.0 0.6 reduce
Async XLA Ops:
  2.2 19.9 %collective-permute-start = (bf16[384,1152]{1,0:T(8,128)(2,1)S(1)}, bf16[384,1152]{1,0:T(8,128)(2,1)S(1)}, u32[]{:S(2)}, u32[]{:S(2)}) collective-permute-start(bf16[384,1152]{1,0:T(8,128)(2,1)S(1)} %get-tuple-element.30.raw_w), channel_id=1, source_target_pairs={{0,2},{2,0},{1,3},{3,1},{4,6},{6,4},{5,7},{7,5},{8,10},{10,8},{9,1... | collective-permute-start | bytes 2654216 | tf_op jit(solution)/shard_map/ppermute | solution.py:30
  2.4 23.6 %collective-permute-start.1 = (bf16[384,1152]{1,0:T(8,128)(2,1)S(1)}, bf16[384,1152]{1,0:T(8,128)(2,1)S(1)}, u32[]{:S(2)}, u32[]{:S(2)}) collective-permute-start(bf16[384,1152]{1,0:T(8,128)(2,1)S(1)} %get-tuple-element.47.raw_u), channel_id=1, source_target_pairs={{0,30},{1,31},{2,4},{3,5},{4,2},{5,3},{6,8},{7,9},{8,6},{9,7},{10,... | collective-permute-start | bytes 2654216 | tf_op jit(solution)/shard_map/ppermute | solution.py:30
  5.0 22.1 %collective-permute-start.3 = (bf16[384,1152]{1,0:T(8,128)(2,1)}, bf16[384,1152]{1,0:T(8,128)(2,1)}, u32[]{:S(2)}, u32[]{:S(2)}) collective-permute-start(bf16[384,1152]{1,0:T(8,128)(2,1)} %image.1), channel_id=1, source_target_pairs={{1,0},{2,1},{5,4},{6,5},{9,8},{10,9},{13,12},{14,13},{17,16},{18,1... | collective-permute-start | bytes 2654216 | tf_op jit(solution)/shard_map/ppermute | solution.py:30
  12.4 23.9 %collective-permute-start.4 = (bf16[384,1152]{1,0:T(8,128)(2,1)}, bf16[384,1152]{1,0:T(8,128)(2,1)}, u32[]{:S(2)}, u32[]{:S(2)}) collective-permute-start(bf16[384,1152]{1,0:T(8,128)(2,1)} %text.1), channel_id=1, source_target_pairs={{1,2},{2,3},{5,6},{6,7},{9,10},{10,11},{13,14},{14,15},{17,18},{18... | collective-permute-start | bytes 2654216 | tf_op jit(solution)/shard_map/ppermute | solution.py:30
  20.9 1.2 %copy-start.3 = (f32[384,1152]{1,0:T(8,128)}, f32[384,1152]{1,0:T(8,128)S(1)}, u32[]{:S(2)}) copy-start(f32[384,1152]{1,0:T(8,128)S(1)} %get-tuple-element.32.grad_u) | copy-start | bytes 5308420
  22.2 1.5 %copy-start.2 = (f32[384,1152]{1,0:T(8,128)S(1)}, f32[384,1152]{1,0:T(8,128)}, u32[]{:S(2)}) copy-start(f32[384,1152]{1,0:T(8,128)} %get-tuple-element.26.grad_w) | copy-start | bytes 5308420
  25.9 11.6 %copy-start.4 = (f32[384,1152]{1,0:T(8,128)}, f32[384,1152]{1,0:T(8,128)S(1)}, u32[]{:S(2)}) copy-start(f32[384,1152]{1,0:T(8,128)S(1)} %get-tuple-element.33.grad_w) | copy-start | bytes 5308420
  26.1 24.0 %collective-permute-start.2 = (bf16[384,1152]{1,0:T(8,128)(2,1)S(1)}, bf16[384,1152]{1,0:T(8,128)(2,1)S(1)}, u32[]{:S(2)}, u32[]{:S(2)}) collective-permute-start(bf16[384,1152]{1,0:T(8,128)(2,1)S(1)} %broadcast_select_fusion.3), channel_id=1, source_target_pairs={{0,1},{1,0},{2,3},{3,2},{4,5},{5,4},{6,7},{7,6},{8,9},{9,8},{10,11... | collective-permute-start | bytes 2654216 | tf_op jit(solution)/shard_map/ppermute | solution.py:30
  37.6 20.2 %collective-permute-start.6 = (bf16[384,1152]{1,0:T(8,128)(2,1)S(1)}, bf16[384,1152]{1,0:T(8,128)(2,1)S(1)}, u32[]{:S(2)}, u32[]{:S(2)}) collective-permute-start(bf16[384,1152]{1,0:T(8,128)(2,1)S(1)} %broadcast_select_fusion.b3), channel_id=1, source_target_pairs={{0,30},{1,31},{2,4},{3,5},{4,2},{5,3},{6,8},{7,9},{8,6},{9,7},{10,... | collective-permute-start | bytes 2654216 | tf_op jit(solution)/shard_map/ppermute | solution.py:30
  44.1 1.2 %copy-start.1 = (f32[384,1152]{1,0:T(8,128)}, f32[384,1152]{1,0:T(8,128)S(1)}, u32[]{:S(2)}) copy-start(f32[384,1152]{1,0:T(8,128)S(1)} %get-tuple-element.40.grad_u) | copy-start | bytes 5308420
  50.1 12.7 %copy-start = (f32[384,1152]{1,0:T(8,128)S(1)}, f32[384,1152]{1,0:T(8,128)}, u32[]{:S(2)}) copy-start(f32[384,1152]{1,0:T(8,128)} %get-tuple-element.39.grad_w) | copy-start | bytes 5308420
  50.1 12.7 %collective-permute-start.5 = (bf16[384,1152]{1,0:T(8,128)(2,1)S(1)}, bf16[384,1152]{1,0:T(8,128)(2,1)S(1)}, u32[]{:S(2)}, u32[]{:S(2)}) collective-permute-start(bf16[384,1152]{1,0:T(8,128)(2,1)S(1)} %collective-permute-done.2.b5), channel_id=1, source_target_pairs={{0,2},{2,0},{1,3},{3,1},{4,6},{6,4},{5,7},{7,5},{8,10},{10,8},{9,1... | collective-permute-start | bytes 2654216 | tf_op jit(solution)/shard_map/ppermute | solution.py:30

commit v3 on v2

v3 whole, which is shorter than its diff:
```python
import jax
import jax.numpy as jnp
from jax import lax
from jax.experimental import pallas as pl
from jax.experimental.pallas import tpu as pltpu
from jax.sharding import PartitionSpec as P

SPAN = 4
GROUP = 4
AXES = ("blk", "inner")
F32 = jnp.float32
BF16 = jnp.bfloat16
VMEM_LIMIT = 24 * 1024 * 1024

TEXT_BY_TWO = {0: (2, 0), 1: (3, 0), 2: (0, 1), 3: (1, 1)}
IMAGE_BY_TWO = {0: (2, -1), 1: (3, -1), 2: (0, 0), 3: (1, 0)}
TEXT_X = {0: (0, 0), 1: (2, 0), 2: (3, 0), 3: (1, 0)}
IMAGE_X = {0: (2, 0), 1: (0, 0), 2: (1, 0), 3: (3, 0)}
X_SWAP = {0: (1, 0), 1: (0, 0), 2: (3, 0), 3: (2, 0)}
CORE_SWAP = {0: (2, 0), 1: (3, 0), 2: (0, 0), 3: (1, 0)}
RELAY = {0: (2, -1), 1: (3, -1), 2: (0, 1), 3: (1, 1)}


def send(value, moves):
    count = lax.axis_size(AXES)
    groups = count // GROUP
    pairs = [
        (g * GROUP + role, (g + step) % groups * GROUP + to)
        for g in range(groups)
        for role, (to, step) in moves.items()
    ]
    return lax.ppermute(value, AXES, pairs)


def unit_rows(raw):
    values = raw.astype(F32)
    length = jnp.sqrt(jnp.sum(values * values, axis=1, keepdims=True) + 1e-06)
    return values * (1.0 / length), length


def sigmoid_of(p):
    whole = 1.0 + p
    guess = pl.reciprocal(whole, approx=True)
    guess = guess * (2.0 - whole * guess)
    return p * (guess * (2.0 - whole * guess))


def log1p_of(p):
    below = p * (1.0 - p * (0.5 - p * (1.0 / 3.0)))
    return jnp.where(p < 0.015625, below, jnp.log(1.0 + p))


def softplus_lanes(p):
    total = None
    parts = [p[:, start : start + 128] for start in range(0, p.shape[1], 128)]
    for first in range(0, len(parts), 3):
        joint = parts[first]
        for part in parts[first + 1 : first + 3]:
            joint = joint + part + joint * part
        value = log1p_of(joint)
        total = value if total is None else total + value
    return total


def dot_nt(a, b):
    return lax.dot_general(a, b, (((1,), (1,)), ((), ())), preferred_element_type=F32)


def dot_nn(a, b):
    return lax.dot_general(a, b, (((1,), (0,)), ((), ())), preferred_element_type=F32)


def dot_tn(a, b):
    return lax.dot_general(a, b, (((0,), (0,)), ((), ())), preferred_element_type=F32)


def pair_step(own, blocks, scale, shift, work):
    rows = own.shape[0]
    for place, raw in enumerate(blocks):
        work[place * rows : (place + 1) * rows] = unit_rows(raw)[0].astype(BF16)
    others = work[: len(blocks) * rows]
    p = jnp.exp(scale * dot_nt(own, others) + shift)
    coef = (sigmoid_of(p) * scale).astype(BF16)
    return dot_nn(coef, others), softplus_lanes(p)


def project(raw, grad):
    unit, length = unit_rows(raw)
    return ((grad - unit * jnp.sum(unit * grad, axis=1, keepdims=True)) / length).astype(BF16)


def own_kernel(scal, image, text, z_image, z_text, grad_image, grad_text, loss):
    scale, shift = scal[0], scal[1]
    zi = unit_rows(image[...])[0].astype(BF16)
    zt = unit_rows(text[...])[0].astype(BF16)
    z_image[...] = zi
    z_text[...] = zt
    scores = scale * dot_nt(zi, zt) + shift
    rows = lax.broadcasted_iota(jnp.int32, scores.shape, 0)
    columns = lax.broadcasted_iota(jnp.int32, scores.shape, 1)
    sign = jnp.where(rows == columns, F32(-1.0), F32(1.0))
    p = jnp.exp(sign * scores)
    coef = (sign * sigmoid_of(p) * scale).astype(BF16)
    loss[...] = softplus_lanes(p)
    grad_image[...] = dot_nn(coef, zt)
    grad_text[...] = dot_tn(coef, zi)


def near_kernel(
    scal, flag, text, image, b3, z_image, z_text, grad_image, grad_text, loss_in,
    z_u, z_w, grad_u, grad_w, loss, work,
):
    u_is_image = flag[0] == 1
    u_weight = flag[0].astype(F32)
    scale, shift = scal[0], scal[1]
    z_u[...] = jnp.where(u_is_image, z_image[...], z_text[...])
    z_w[...] = jnp.where(u_is_image, z_text[...], z_image[...])
    for_u = jnp.where(u_is_image, text[...], image[...])
    for_w = jnp.where(u_is_image, image[...], text[...])
    term, row_loss = pair_step(z_u[...], (for_u,), scale, shift, work)
    grad_u[...] = jnp.where(u_is_image, grad_image[...], grad_text[...]) + term
    total = loss_in[...] + u_weight * row_loss
    term, row_loss = pair_step(z_w[...], (for_w, b3[...]), scale, shift, work)
    grad_w[...] = jnp.where(u_is_image, grad_text[...], grad_image[...]) + term
    loss[...] = total + (1.0 - u_weight) * row_loss


def u_kernel(scal, flag, b4, b5, z_u, grad_u, loss_in, image, text, out, loss, work):
    raw = jnp.where(flag[0] == 1, image[...], text[...])
    term, row_loss = pair_step(z_u[...], (b4[...], b5[...]), scal[0], scal[1], work)
    loss[...] = loss_in[...] + flag[0].astype(F32) * row_loss
    out[...] = project(raw, grad_u[...] + term)


def w_kernel(
    scal, flag, b6, z_w, grad_w, loss_in, image, text, done_u, image_grad, text_grad, loss_rows, work
):
    u_is_image = flag[0] == 1
    raw = jnp.where(u_is_image, text[...], image[...])
    term, row_loss = pair_step(z_w[...], (b6[...],), scal[0], scal[1], work)
    total = loss_in[...] + (1.0 - flag[0].astype(F32)) * row_loss
    per_row = jnp.sum(jnp.transpose(total), axis=0, keepdims=True)
    loss_rows[...] = per_row / (SPAN * total.shape[0])
    done_w = project(raw, grad_w[...] + term)
    image_grad[...] = jnp.where(u_is_image, done_u[...], done_w)
    text_grad[...] = jnp.where(u_is_image, done_w, done_u[...])


def call(kernel, scalars, args, outs, products, name, work_rows=0):
    smem = pl.BlockSpec(memory_space=pltpu.SMEM)
    vmem = pl.BlockSpec(memory_space=pltpu.VMEM)
    rows, width = args[0].shape
    size = sum(a.size * a.dtype.itemsize for a in list(args) + list(outs))
    return pl.pallas_call(
        kernel,
        out_shape=outs,
        in_specs=[smem] * len(scalars) + [vmem] * len(args),
        out_specs=[vmem] * len(outs),
        scratch_shapes=[pltpu.VMEM((work_rows, width), BF16)] if work_rows else [],
        name=name,
        cost_estimate=pl.CostEstimate(
            flops=2 * rows * rows * width * products, bytes_accessed=size, transcendentals=0
        ),
        compiler_params=pltpu.CompilerParams(vmem_limit_bytes=VMEM_LIMIT),
    )(*scalars, *args)


def local(image, text, score_scaling, score_shift):
    rows, width = image.shape
    role = lax.axis_index(AXES) % GROUP
    u_is_image = role < 2
    flag = u_is_image.astype(jnp.int32).reshape(1)
    scal = jnp.stack([score_scaling, score_shift])
    block = jax.ShapeDtypeStruct((rows, width), BF16)
    sums = jax.ShapeDtypeStruct((rows, width), F32)
    partial = jax.ShapeDtypeStruct((rows, 128), F32)
    line = jax.ShapeDtypeStruct((1, rows), F32)

    image_x = send(image, IMAGE_X)
    text_x = send(text, TEXT_X)
    text_two = send(text, TEXT_BY_TWO)
    image_two = send(image, IMAGE_BY_TWO)
    z_image, z_text, grad_image, grad_text, loss = call(
        own_kernel, (scal,), (image, text), (block, block, sums, sums, partial), 3, "own_pair"
    )
    text_kept, image_kept, loss = lax.optimization_barrier((text, image, loss))
    slot5 = send(
        jnp.where(
            u_is_image,
            jnp.where(role == 0, text_kept, text_two),
            jnp.where(role == 3, image_kept, image_two),
        ),
        X_SWAP,
    )
    slot3 = jnp.where(u_is_image, image_x, text_x)
    slot4 = send(slot3, RELAY)
    z_u, z_w, grad_u, grad_w, loss = call(
        near_kernel,
        (scal, flag),
        (text_two, image_two, slot3, z_image, z_text, grad_image, grad_text, loss),
        (block, block, sums, sums, partial),
        6,
        "near_blocks",
        2 * rows,
    )
    slot5, loss = lax.optimization_barrier((slot5, loss))
    slot6 = send(slot5, CORE_SWAP)
    done_u, loss = call(
        u_kernel,
        (scal, flag),
        (slot4, slot5, z_u, grad_u, loss, image, text),
        (block, partial),
        4,
        "finish_u",
        2 * rows,
    )
    image_grad, text_grad, loss_rows = call(
        w_kernel,
        (scal, flag),
        (slot6, z_w, grad_w, loss, image, text, done_u),
        (block, block, line),
        2,
        "finish_w",
        rows,
    )
    return loss_rows.reshape(rows), image_grad, text_grad


def solution(mesh):
    in_specs = (P(AXES, None), P(AXES, None), P(), P())
    out_specs = (P(AXES), P(AXES, None), P(AXES, None))
    return jax.shard_map(local, mesh=mesh, in_specs=in_specs, out_specs=out_specs, check_vma=False)
```

time: 67.9 us -> 66 us (0.972)
  Pallas kernels: 23.1 us -> 17.3 us
  waiting for transfers between devices: 19.7 us -> 21.7 us
  starting transfers between devices: 15.2 us -> 16.6 us
    pallas_call x5 -> x4, Pallas kernels: 23.1 us -> 17.3 us  [call(): pl.pallas_call(kernel, out_shape=outs, in_specs=[smem] * len(scalars) + [...]
    ppermute x7, waiting for transfers between devices: 19.7 us -> 21.7 us  [send(): return lax.ppermute(value, AXES, pairs)]
    ppermute x7, starting transfers between devices: 15.2 us -> 16.6 us  [send(): return lax.ppermute(value, AXES, pairs)]
    select_n x3 -> x2, other arithmetic: 2.98 us -> 2.37 us  [the longest x1 1.27 us: local(): slot3 = jnp.where(u_is_image, image_x, text_x)]
    unnamed x10 -> x24, local copies, waits for them, and re-layouts: 3.96 us -> 4.45 us
  transfers between devices with their start and end apart: 7 -> 7, of which waited for: 3 -> 5; matrix products, arithmetic and copies ran while one was open for 2% -> 4% of each run, Pallas kernels for 28% -> 20%
where the time goes in v3:
time: 66 us; the launch traced here: 65.1 us
  waiting for transfers between devices  21.7 us (33%)
  Pallas kernels  17.3 us (26%)
  starting transfers between devices  16.6 us (25%)
  local copies, waits for them, and re-layouts  4.45 us (7%)
  other arithmetic  3.05 us (5%)
  between operations  2.04 us (3%)
    ppermute x7, waiting for transfers between devices, send(): return lax.ppermute(value, AXES, pairs)  21.7 us
    pallas_call x4, Pallas kernels, call(): pl.pallas_call(kernel, out_shape=outs, in_specs=[smem] * len(scalars) + [...  17.3 us
    ppermute x7, starting transfers between devices, send(): return lax.ppermute(value, AXES, pairs)  16.6 us
    unnamed x24, local copies, waits for them, and re-layouts  4.45 us
  transfers between devices with their start and end apart: 7, of which 5 were waited for; matrix products, arithmetic and copies ran while one was open for 4% of the time, Pallas kernels for 20%

profile of v3, /device:TPU:1, one launch (start us, length us, event | category | flops | bytes accessed | tf_op | source)
XLA Modules:
  0.0 65.1 jit_solution(16827418809070565389)
XLA Ops:
  0.6 2.7 %collective-permute-start = (bf16[384,1152]{1,0:T(8,128)(2,1)}, bf16[384,1152]{1,0:T(8,128)(2,1)S(1)}, u32[]{:S(2)}, u32[]{:S(2)}) collective-permute-start(bf16[384,1152]{1,0:T(8,128)(2,1)} %text.5), channel_id=1, source_target_pairs={{0,2},{1,3},{2,4},{3,5},{4,6},{5,7},{6,8},{7,9},{8,10},{9,11},{10,... | collective-permute-start | bytes 2654216 | tf_op jit(solution)/shard_map/ppermute | solution.py:32
  3.3 0.0 collective-permute-start.1
  3.3 6.3 %collective-permute-start.3 = (bf16[384,1152]{1,0:T(8,128)(2,1)}, bf16[384,1152]{1,0:T(8,128)(2,1)}, u32[]{:S(2)}, u32[]{:S(2)}) collective-permute-start(bf16[384,1152]{1,0:T(8,128)(2,1)} %image.5), channel_id=1, source_target_pairs={{0,2},{1,0},{2,1},{3,3},{4,6},{5,4},{6,5},{7,7},{8,10},{9,8},{10,9... | collective-permute-start | bytes 2654216 | tf_op jit(solution)/shard_map/ppermute | solution.py:32
  9.6 5.0 %collective-permute-start.4 = (bf16[384,1152]{1,0:T(8,128)(2,1)}, bf16[384,1152]{1,0:T(8,128)(2,1)}, u32[]{:S(2)}, u32[]{:S(2)}) collective-permute-start(bf16[384,1152]{1,0:T(8,128)(2,1)} %text.5), channel_id=1, source_target_pairs={{0,0},{1,2},{2,3},{3,1},{4,4},{5,6},{6,7},{7,5},{8,8},{9,10},{10,1... | collective-permute-start | bytes 2654216 | tf_op jit(solution)/shard_map/ppermute | solution.py:32
  16.0 0.1 pad_maximum_fusion.scal
  16.0 0.0 copy-start
  16.0 1.2 %copy-done = bf16[384,1152]{1,0:T(8,128)(2,1)S(1)} copy-done((bf16[384,1152]{1,0:T(8,128)(2,1)S(1)}, bf16[384,1152]{1,0:T(8,128)(2,1)}, u32[]{:S(2)}) %copy-start) | copy-done | bytes 884760
  17.2 0.0 copy-start.2
  17.2 1.2 %copy-done.2 = bf16[384,1152]{1,0:T(8,128)(2,1)S(1)} copy-done((bf16[384,1152]{1,0:T(8,128)(2,1)S(1)}, bf16[384,1152]{1,0:T(8,128)(2,1)}, u32[]{:S(2)}) %copy-start.2) | copy-done | bytes 884760
  18.4 3.1 %own_pair.1 = (bf16[384,1152]{1,0:T(8,128)(2,1)S(1)}, bf16[384,1152]{1,0:T(8,128)(2,1)S(1)}, f32[384,1152]{1,0:T(8,128)S(1)}, f32[384,1152]{1,0:T(8,128)S(1)}, f32[384,128]{1,0:T(8,128)S(1)}) custom-call(f32[2]{0:T(128)S(1)} %pad_maximum_fusion.scal, bf16[384,1152]{1,0:T(8,128)(2,1)S(1)} %copy-done, bf16[384,1152]{1,0:T(8,128)(2,1)S(1)} %copy-done.2), custom_call_target="tpu_custom_call" | custom-call | flops 1019215872 | bytes 7274496 | tf_op jit(solution)/shard_map/own_pair/pallas_call | solution.py:154
  21.5 0.0 copy-start.4
  21.5 0.0 copy-start.6
  21.5 0.0 copy-start.8
  21.6 0.0 copy-start.10
  21.6 1.5 %collective-permute-done.text = bf16[384,1152]{1,0:T(8,128)(2,1)S(1)} collective-permute-done((bf16[384,1152]{1,0:T(8,128)(2,1)}, bf16[384,1152]{1,0:T(8,128)(2,1)S(1)}, u32[]{:S(2)}, u32[]{:S(2)}) %collective-permute-start) | collective-permute-done | bytes 884768 | tf_op jit(solution)/shard_map/ppermute | solution.py:32
  23.1 2.4 %collective-permute-done.1.image = bf16[384,1152]{1,0:T(8,128)(2,1)S(1)} collective-permute-done((bf16[384,1152]{1,0:T(8,128)(2,1)}, bf16[384,1152]{1,0:T(8,128)(2,1)S(1)}, u32[]{:S(2)}, u32[]{:S(2)}) %collective-permute-start.1) | collective-permute-done | bytes 884768 | tf_op jit(solution)/shard_map/ppermute | solution.py:32
  25.5 1.1 %select_select_fusion = bf16[384,1152]{1,0:T(8,128)(2,1)} fusion(bf16[384,1152]{1,0:T(8,128)(2,1)S(1)} %copy-done, bf16[384,1152]{1,0:T(8,128)(2,1)S(1)} %collective-permute-done.1.image, bf16[384,1152]{1,0:T(8,128)(2,1)S(1)} %copy-done.2, bf16[384,1152]{1,0:T(8,128)(2,1)S(1)} %collective-permute-done.text, pred[]{:T(512)S(6)} %eq.9, pred[]{:T(512)S(6)} %eq.8, ...), kind=kLoop, calls=%fused_computation | loop fusion | flops 1327104 | bytes 4423683 | tf_op jit(solution)/shard_map/jit(_where)/select_n | solution.py:188
  26.6 0.0 copy-done.4
  26.6 0.0 copy-done.6
  26.6 0.0 copy-done.8
  26.6 0.0 copy-done.10
  26.6 1.3 %collective-permute-start.2 = (bf16[384,1152]{1,0:T(8,128)(2,1)}, bf16[384,1152]{1,0:T(8,128)(2,1)}, u32[]{:S(2)}, u32[]{:S(2)}) collective-permute-start(bf16[384,1152]{1,0:T(8,128)(2,1)} %select_select_fusion), channel_id=1, source_target_pairs={{0,1},{1,0},{2,3},{3,2},{4,5},{5,4},{6,7},{7,6},{8,9},{9,8},{10,11... | collective-permute-start | bytes 2654216 | tf_op jit(solution)/shard_map/ppermute | solution.py:32
  27.9 0.0 copy-start.5
  27.9 0.0 copy-start.7
  27.9 0.0 collective-permute-done.3
  27.9 4.4 %collective-permute-done.4 = bf16[384,1152]{1,0:T(8,128)(2,1)} collective-permute-done((bf16[384,1152]{1,0:T(8,128)(2,1)}, bf16[384,1152]{1,0:T(8,128)(2,1)}, u32[]{:S(2)}, u32[]{:S(2)}) %collective-permute-start.4) | collective-permute-done | bytes 884768 | tf_op jit(solution)/shard_map/ppermute | solution.py:32
  32.3 1.3 %broadcast_select_fusion.b3 = bf16[384,1152]{1,0:T(8,128)(2,1)S(1)} fusion(bf16[384,1152]{1,0:T(8,128)(2,1)} %collective-permute-done.3, bf16[384,1152]{1,0:T(8,128)(2,1)} %collective-permute-done.4, pred[]{:T(512)S(6)} %lt.10), kind=kLoop, calls=%fused_computation.1 | loop fusion | flops 442368 | bytes 2654209 | tf_op jit(solution)/shard_map/jit(_where)/select_n | solution.py:195
  33.6 0.1 collective-permute-start.6
  33.7 0.0 copy-done.5
  33.7 0.0 copy-done.7
  33.7 0.0 copy-start.9
  33.7 1.2 %copy-done.9 = bf16[384,1152]{1,0:T(8,128)(2,1)S(1)} copy-done((bf16[384,1152]{1,0:T(8,128)(2,1)S(1)}, bf16[384,1152]{1,0:T(8,128)(2,1)}, u32[]{:S(2)}) %copy-start.9) | copy-done | bytes 884760
  34.8 0.0 copy-start.11
  34.8 0.9 %copy-done.11 = f32[384,128]{1,0:T(8,128)S(1)} copy-done((f32[384,128]{1,0:T(8,128)S(1)}, f32[384,128]{1,0:T(8,128)}, u32[]{:S(2)}) %copy-start.11) | copy-done | bytes 196632
  35.8 0.0 copy-start.1
  35.8 0.0 copy-start.3
  35.8 5.2 %near_blocks.1 = (bf16[384,1152]{1,0:T(8,128)(2,1)S(1)}, bf16[384,1152]{1,0:T(8,128)(2,1)S(1)}, f32[384,1152]{1,0:T(8,128)S(1)}, f32[384,1152]{1,0:T(8,128)S(1)}, f32[384,128]{1,0:T(8,128)S(1)}) custom-call(f32[2]{0:T(128)S(1)} %pad_maximum_fusion.scal, s32[1]{0:T(128)} %bitcast.2.flag, bf16[384,1152]{1,0:T(8,128)(2,1)S(1)} %collective-permute-done.text, ...), custom_call_target="tpu_custom_call" | custom-call | flops 2038431744 | bytes 13664256 | tf_op jit(solution)/shard_map/near_blocks/pallas_call | solution.py:154
  41.0 7.7 %collective-permute-done.2.b5 = bf16[384,1152]{1,0:T(8,128)(2,1)} collective-permute-done((bf16[384,1152]{1,0:T(8,128)(2,1)}, bf16[384,1152]{1,0:T(8,128)(2,1)}, u32[]{:S(2)}, u32[]{:S(2)}) %collective-permute-start.2) | collective-permute-done | bytes 884768 | tf_op jit(solution)/shard_map/ppermute | solution.py:32
  48.7 1.2 %collective-permute-start.5 = (bf16[384,1152]{1,0:T(8,128)(2,1)}, bf16[384,1152]{1,0:T(8,128)(2,1)S(1)}, u32[]{:S(2)}, u32[]{:S(2)}) collective-permute-start(bf16[384,1152]{1,0:T(8,128)(2,1)} %collective-permute-done.2.b5), channel_id=1, source_target_pairs={{0,2},{1,3},{2,0},{3,1},{4,6},{5,7},{6,4},{7,5},{8,10},{9,11},{10,... | collective-permute-start | bytes 2654216 | tf_op jit(solution)/shard_map/ppermute | solution.py:32
  49.9 5.7 %collective-permute-done.6.b4 = bf16[384,1152]{1,0:T(8,128)(2,1)S(1)} collective-permute-done((bf16[384,1152]{1,0:T(8,128)(2,1)S(1)}, bf16[384,1152]{1,0:T(8,128)(2,1)S(1)}, u32[]{:S(2)}, u32[]{:S(2)}) %collective-permute-start.6) | collective-permute-done | bytes 884768 | tf_op jit(solution)/shard_map/ppermute | solution.py:32
  55.6 0.0 copy-done.1
  55.6 0.0 copy-done.3
  55.6 4.7 %finish_u.1 = (bf16[384,1152]{1,0:T(8,128)(2,1)S(1)}, f32[384,128]{1,0:T(8,128)S(1)}) custom-call(f32[2]{0:T(128)S(1)} %pad_maximum_fusion.scal, s32[1]{0:T(128)} %bitcast.2.flag, bf16[384,1152]{1,0:T(8,128)(2,1)S(1)} %collective-permute-done.6.b4, bf16[384,1152]{1,0:T(8,128)(2,1)} %collective-permute-done.2.b5, ...), custom_call_target="tpu_custom_call" | custom-call | flops 1358954496 | bytes 7471104 | tf_op jit(solution)/shard_map/finish_u/pallas_call | solution.py:154
  60.3 0.0 collective-permute-done.5.b6
  60.3 4.2 %finish_w.1 = (bf16[384,1152]{1,0:T(8,128)(2,1)}, bf16[384,1152]{1,0:T(8,128)(2,1)}, f32[1,384]{1,0:T(1,128)S(1)}) custom-call(f32[2]{0:T(128)S(1)} %pad_maximum_fusion.scal, s32[1]{0:T(128)} %bitcast.2.flag, bf16[384,1152]{1,0:T(8,128)(2,1)S(1)} %collective-permute-done.5.b6, bf16[384,1152]{1,0:T(8,128)(2,1)S(1)} %get-tuple-element.33.z_w, ...), custom_call_target="tpu_custom_call" | custom-call | flops 679477248 | bytes 8160768 | tf_op jit(solution)/shard_map/finish_w/pallas_call | solution.py:154
  64.5 0.6 reduce
Async XLA Ops:
  0.6 22.5 %collective-permute-start = (bf16[384,1152]{1,0:T(8,128)(2,1)}, bf16[384,1152]{1,0:T(8,128)(2,1)S(1)}, u32[]{:S(2)}, u32[]{:S(2)}) collective-permute-start(bf16[384,1152]{1,0:T(8,128)(2,1)} %text.5), channel_id=1, source_target_pairs={{0,2},{1,3},{2,4},{3,5},{4,6},{5,7},{6,8},{7,9},{8,10},{9,11},{10,... | collective-permute-start | bytes 2654216 | tf_op jit(solution)/shard_map/ppermute | solution.py:32
  3.3 22.2 %collective-permute-start.1 = (bf16[384,1152]{1,0:T(8,128)(2,1)}, bf16[384,1152]{1,0:T(8,128)(2,1)S(1)}, u32[]{:S(2)}, u32[]{:S(2)}) collective-permute-start(bf16[384,1152]{1,0:T(8,128)(2,1)} %image.5), channel_id=1, source_target_pairs={{0,30},{1,31},{2,0},{3,1},{4,2},{5,3},{6,4},{7,5},{8,6},{9,7},{10,... | collective-permute-start | bytes 2654216 | tf_op jit(solution)/shard_map/ppermute | solution.py:32
  3.3 24.6 %collective-permute-start.3 = (bf16[384,1152]{1,0:T(8,128)(2,1)}, bf16[384,1152]{1,0:T(8,128)(2,1)}, u32[]{:S(2)}, u32[]{:S(2)}) collective-permute-start(bf16[384,1152]{1,0:T(8,128)(2,1)} %image.5), channel_id=1, source_target_pairs={{0,2},{1,0},{2,1},{3,3},{4,6},{5,4},{6,5},{7,7},{8,10},{9,8},{10,9... | collective-permute-start | bytes 2654216 | tf_op jit(solution)/shard_map/ppermute | solution.py:32
  9.6 22.7 %collective-permute-start.4 = (bf16[384,1152]{1,0:T(8,128)(2,1)}, bf16[384,1152]{1,0:T(8,128)(2,1)}, u32[]{:S(2)}, u32[]{:S(2)}) collective-permute-start(bf16[384,1152]{1,0:T(8,128)(2,1)} %text.5), channel_id=1, source_target_pairs={{0,0},{1,2},{2,3},{3,1},{4,4},{5,6},{6,7},{7,5},{8,8},{9,10},{10,1... | collective-permute-start | bytes 2654216 | tf_op jit(solution)/shard_map/ppermute | solution.py:32
  16.0 1.2 %copy-start = (bf16[384,1152]{1,0:T(8,128)(2,1)S(1)}, bf16[384,1152]{1,0:T(8,128)(2,1)}, u32[]{:S(2)}) copy-start(bf16[384,1152]{1,0:T(8,128)(2,1)} %image.5) | copy-start | bytes 2654212
  17.2 1.2 %copy-start.2 = (bf16[384,1152]{1,0:T(8,128)(2,1)S(1)}, bf16[384,1152]{1,0:T(8,128)(2,1)}, u32[]{:S(2)}) copy-start(bf16[384,1152]{1,0:T(8,128)(2,1)} %text.5) | copy-start | bytes 2654212
  21.5 5.1 %copy-start.4 = (f32[384,1152]{1,0:T(8,128)}, f32[384,1152]{1,0:T(8,128)S(1)}, u32[]{:S(2)}) copy-start(f32[384,1152]{1,0:T(8,128)S(1)} %get-tuple-element.29.grad_text) | copy-start | bytes 5308420
  21.5 5.1 %copy-start.6 = (bf16[384,1152]{1,0:T(8,128)(2,1)}, bf16[384,1152]{1,0:T(8,128)(2,1)S(1)}, u32[]{:S(2)}) copy-start(bf16[384,1152]{1,0:T(8,128)(2,1)S(1)} %get-tuple-element.26.z_image) | copy-start | bytes 2654212
  21.5 5.0 %copy-start.8 = (bf16[384,1152]{1,0:T(8,128)(2,1)}, bf16[384,1152]{1,0:T(8,128)(2,1)S(1)}, u32[]{:S(2)}) copy-start(bf16[384,1152]{1,0:T(8,128)(2,1)S(1)} %get-tuple-element.27.z_text) | copy-start | bytes 2654212
  21.6 5.0 %copy-start.10 = (f32[384,128]{1,0:T(8,128)}, f32[384,128]{1,0:T(8,128)S(1)}, u32[]{:S(2)}) copy-start(f32[384,128]{1,0:T(8,128)S(1)} %get-tuple-element.30.loss_in) | copy-start | bytes 589828
  26.6 22.1 %collective-permute-start.2 = (bf16[384,1152]{1,0:T(8,128)(2,1)}, bf16[384,1152]{1,0:T(8,128)(2,1)}, u32[]{:S(2)}, u32[]{:S(2)}) collective-permute-start(bf16[384,1152]{1,0:T(8,128)(2,1)} %select_select_fusion), channel_id=1, source_target_pairs={{0,1},{1,0},{2,3},{3,2},{4,5},{5,4},{6,7},{7,6},{8,9},{9,8},{10,11... | collective-permute-start | bytes 2654216 | tf_op jit(solution)/shard_map/ppermute | solution.py:32
  27.9 5.8 %copy-start.5 = (f32[384,1152]{1,0:T(8,128)S(1)}, f32[384,1152]{1,0:T(8,128)}, u32[]{:S(2)}) copy-start(f32[384,1152]{1,0:T(8,128)} %copy-done.4) | copy-start | bytes 5308420
  27.9 5.8 %copy-start.7 = (bf16[384,1152]{1,0:T(8,128)(2,1)S(1)}, bf16[384,1152]{1,0:T(8,128)(2,1)}, u32[]{:S(2)}) copy-start(bf16[384,1152]{1,0:T(8,128)(2,1)} %copy-done.6) | copy-start | bytes 2654212
  33.6 22.0 %collective-permute-start.6 = (bf16[384,1152]{1,0:T(8,128)(2,1)S(1)}, bf16[384,1152]{1,0:T(8,128)(2,1)S(1)}, u32[]{:S(2)}, u32[]{:S(2)}) collective-permute-start(bf16[384,1152]{1,0:T(8,128)(2,1)S(1)} %broadcast_select_fusion.b3), channel_id=1, source_target_pairs={{0,30},{1,31},{2,4},{3,5},{4,2},{5,3},{6,8},{7,9},{8,6},{9,7},{10,... | collective-permute-start | bytes 2654216 | tf_op jit(solution)/shard_map/ppermute | solution.py:32
  33.7 1.2 %copy-start.9 = (bf16[384,1152]{1,0:T(8,128)(2,1)S(1)}, bf16[384,1152]{1,0:T(8,128)(2,1)}, u32[]{:S(2)}) copy-start(bf16[384,1152]{1,0:T(8,128)(2,1)} %copy-done.8) | copy-start | bytes 2654212
  34.8 0.9 %copy-start.11 = (f32[384,128]{1,0:T(8,128)S(1)}, f32[384,128]{1,0:T(8,128)}, u32[]{:S(2)}) copy-start(f32[384,128]{1,0:T(8,128)} %copy-done.10) | copy-start | bytes 589828
  35.8 19.8 %copy-start.1 = (bf16[384,1152]{1,0:T(8,128)(2,1)S(1)}, bf16[384,1152]{1,0:T(8,128)(2,1)}, u32[]{:S(2)}) copy-start(bf16[384,1152]{1,0:T(8,128)(2,1)} %image.5) | copy-start | bytes 2654212
  35.8 19.8 %copy-start.3 = (bf16[384,1152]{1,0:T(8,128)(2,1)S(1)}, bf16[384,1152]{1,0:T(8,128)(2,1)}, u32[]{:S(2)}) copy-start(bf16[384,1152]{1,0:T(8,128)(2,1)} %text.5) | copy-start | bytes 2654212
  48.7 11.6 %collective-permute-start.5 = (bf16[384,1152]{1,0:T(8,128)(2,1)}, bf16[384,1152]{1,0:T(8,128)(2,1)S(1)}, u32[]{:S(2)}, u32[]{:S(2)}) collective-permute-start(bf16[384,1152]{1,0:T(8,128)(2,1)} %collective-permute-done.2.b5), channel_id=1, source_target_pairs={{0,2},{1,3},{2,0},{3,1},{4,6},{5,7},{6,4},{7,5},{8,10},{9,11},{10,... | collective-permute-start | bytes 2654216 | tf_op jit(solution)/shard_map/ppermute | solution.py:32

commit v4 on v3

--- a/solution.py
+++ b/solution.py
@@ -12,13 +12,9 @@
 BF16 = jnp.bfloat16
 VMEM_LIMIT = 24 * 1024 * 1024
 
-TEXT_BY_TWO = {0: (2, 0), 1: (3, 0), 2: (0, 1), 3: (1, 1)}
-IMAGE_BY_TWO = {0: (2, -1), 1: (3, -1), 2: (0, 0), 3: (1, 0)}
-TEXT_X = {0: (0, 0), 1: (2, 0), 2: (3, 0), 3: (1, 0)}
-IMAGE_X = {0: (2, 0), 1: (0, 0), 2: (1, 0), 3: (3, 0)}
 X_SWAP = {0: (1, 0), 1: (0, 0), 2: (3, 0), 3: (2, 0)}
 CORE_SWAP = {0: (2, 0), 1: (3, 0), 2: (0, 0), 3: (1, 0)}
-RELAY = {0: (2, -1), 1: (3, -1), 2: (0, 1), 3: (1, 1)}
+GROUP_SHIFT = {0: (2, -1), 1: (3, -1), 2: (0, 1), 3: (1, 1)}
 
 
 def send(value, moves):
@@ -107,7 +103,7 @@
 
 
 def near_kernel(
-    scal, flag, text, image, b3, z_image, z_text, grad_image, grad_text, loss_in,
+    scal, flag, b1, b2, b3, z_image, z_text, grad_image, grad_text, loss_in,
     z_u, z_w, grad_u, grad_w, loss, work,
 ):
     u_is_image = flag[0] == 1
@@ -115,33 +111,29 @@
     scale, shift = scal[0], scal[1]
     z_u[...] = jnp.where(u_is_image, z_image[...], z_text[...])
     z_w[...] = jnp.where(u_is_image, z_text[...], z_image[...])
-    for_u = jnp.where(u_is_image, text[...], image[...])
-    for_w = jnp.where(u_is_image, image[...], text[...])
-    term, row_loss = pair_step(z_u[...], (for_u,), scale, shift, work)
+    term, row_loss = pair_step(z_u[...], (b2[...],), scale, shift, work)
     grad_u[...] = jnp.where(u_is_image, grad_image[...], grad_text[...]) + term
     total = loss_in[...] + u_weight * row_loss
-    term, row_loss = pair_step(z_w[...], (for_w, b3[...]), scale, shift, work)
+    term, row_loss = pair_step(z_w[...], (b1[...], b3[...]), scale, shift, work)
     grad_w[...] = jnp.where(u_is_image, grad_text[...], grad_image[...]) + term
     loss[...] = total + (1.0 - u_weight) * row_loss
 
 
-def u_kernel(scal, flag, b4, b5, z_u, grad_u, loss_in, image, text, out, loss, work):
-    raw = jnp.where(flag[0] == 1, image[...], text[...])
+def u_kernel(scal, flag, b4, b5, z_u, grad_u, loss_in, raw, out, loss, work):
     term, row_loss = pair_step(z_u[...], (b4[...], b5[...]), scal[0], scal[1], work)
     loss[...] = loss_in[...] + flag[0].astype(F32) * row_loss
-    out[...] = project(raw, grad_u[...] + term)
+    out[...] = project(raw[...], grad_u[...] + term)
 
 
 def w_kernel(
-    scal, flag, b6, z_w, grad_w, loss_in, image, text, done_u, image_grad, text_grad, loss_rows, work
+    scal, flag, b6, z_w, grad_w, loss_in, raw, done_u, image_grad, text_grad, loss_rows, work
 ):
     u_is_image = flag[0] == 1
-    raw = jnp.where(u_is_image, text[...], image[...])
     term, row_loss = pair_step(z_w[...], (b6[...],), scal[0], scal[1], work)
     total = loss_in[...] + (1.0 - flag[0].astype(F32)) * row_loss
     per_row = jnp.sum(jnp.transpose(total), axis=0, keepdims=True)
     loss_rows[...] = per_row / (SPAN * total.shape[0])
-    done_w = project(raw, grad_w[...] + term)
+    done_w = project(raw[...], grad_w[...] + term)
     image_grad[...] = jnp.where(u_is_image, done_u[...], done_w)
     text_grad[...] = jnp.where(u_is_image, done_w, done_u[...])
 
@@ -176,28 +168,23 @@
     partial = jax.ShapeDtypeStruct((rows, 128), F32)
     line = jax.ShapeDtypeStruct((1, rows), F32)
 
-    image_x = send(image, IMAGE_X)
-    text_x = send(text, TEXT_X)
-    text_two = send(text, TEXT_BY_TWO)
-    image_two = send(image, IMAGE_BY_TWO)
+    u = jnp.where(u_is_image, image, text)
+    w = jnp.where(u_is_image, text, image)
+    outer = (role == 0) | (role == 3)
+
+    slot1 = send(w, CORE_SWAP)
+    slot2 = send(u, GROUP_SHIFT)
+    slot3 = send(jnp.where(outer, slot1, u), X_SWAP)
+    slot4 = send(slot3, GROUP_SHIFT)
+    slot5 = send(jnp.where(outer, w, slot2), X_SWAP)
+    slot3, own_image, own_text = lax.optimization_barrier((slot3, image, text))
     z_image, z_text, grad_image, grad_text, loss = call(
-        own_kernel, (scal,), (image, text), (block, block, sums, sums, partial), 3, "own_pair"
-    )
-    text_kept, image_kept, loss = lax.optimization_barrier((text, image, loss))
-    slot5 = send(
-        jnp.where(
-            u_is_image,
-            jnp.where(role == 0, text_kept, text_two),
-            jnp.where(role == 3, image_kept, image_two),
-        ),
-        X_SWAP,
-    )
-    slot3 = jnp.where(u_is_image, image_x, text_x)
-    slot4 = send(slot3, RELAY)
+        own_kernel, (scal,), (own_image, own_text), (block, block, sums, sums, partial), 3, "own_pair"
+    )
     z_u, z_w, grad_u, grad_w, loss = call(
         near_kernel,
         (scal, flag),
-        (text_two, image_two, slot3, z_image, z_text, grad_image, grad_text, loss),
+        (slot1, slot2, slot3, z_image, z_text, grad_image, grad_text, loss),
         (block, block, sums, sums, partial),
         6,
         "near_blocks",
@@ -208,7 +195,7 @@
     done_u, loss = call(
         u_kernel,
         (scal, flag),
-        (slot4, slot5, z_u, grad_u, loss, image, text),
+        (slot4, slot5, z_u, grad_u, loss, u),
         (block, partial),
         4,
         "finish_u",
@@ -217,7 +204,7 @@
     image_grad, text_grad, loss_rows = call(
         w_kernel,
         (scal, flag),
-        (slot6, z_w, grad_w, loss, image, text, done_u),
+        (slot6, z_w, grad_w, loss, w, done_u),
         (block, block, line),
         2,
         "finish_w",

time: 66 us -> 64.6 us (0.979)
  starting transfers between devices: 16.6 us -> 6.81 us
  waiting for transfers between devices: 21.7 us -> 31.4 us
  local copies, waits for them, and re-layouts: 4.45 us -> 2.1 us
  other arithmetic: 3.05 us -> 4.16 us
    ppermute x7 -> x6, starting transfers between devices: 16.6 us -> 6.81 us  [send(): return lax.ppermute(value, AXES, pairs)]
    ppermute x7 -> x6, waiting for transfers between devices: 21.7 us -> 31.4 us  [send(): return lax.ppermute(value, AXES, pairs)]
    unnamed x24 -> x10, local copies, waits for them, and re-layouts: 4.45 us -> 2.1 us
    select_n x2 -> x3, other arithmetic: 2.37 us -> 3.49 us  [the longest x1 1.4 us: local(): w = jnp.where(u_is_image, text, image)]
  transfers between devices with their start and end apart: 7 -> 6, of which waited for: 5 -> 4; matrix products, arithmetic and copies ran while one was open for 4% -> 2% of each run, Pallas kernels for 20% -> 21%
where the time goes in v4:
time: 64.6 us; the launch traced here: 64.4 us
  waiting for transfers between devices  31.4 us (49%)
  Pallas kernels  17.9 us (28%)
  starting transfers between devices  6.81 us (11%)
  other arithmetic  4.16 us (6%)
  local copies, waits for them, and re-layouts  2.1 us (3%)
  between operations  2.01 us (3%)
    ppermute x6, waiting for transfers between devices, send(): return lax.ppermute(value, AXES, pairs)  31.4 us
    pallas_call x4, Pallas kernels, call(): pl.pallas_call(kernel, out_shape=outs, in_specs=[smem] * len(scalars) + [...  17.9 us
    ppermute x6, starting transfers between devices, send(): return lax.ppermute(value, AXES, pairs)  6.81 us
    unnamed x10, local copies, waits for them, and re-layouts  2.1 us
    select_n x1, other arithmetic, local(): w = jnp.where(u_is_image, text, image)  1.4 us
  transfers between devices with their start and end apart: 6, of which 4 were waited for; matrix products, arithmetic and copies ran while one was open for 2% of the time, Pallas kernels for 21%

profile of v4, /device:TPU:1, one launch (start us, length us, event | category | flops | bytes accessed | tf_op | source)
XLA Modules:
  0.0 64.4 jit_solution(9430333649048626257)
XLA Ops:
  0.6 0.0 copy-start.1
  0.6 0.0 copy-start
  0.7 1.4 %broadcast_select_fusion.1.raw = bf16[384,1152]{1,0:T(8,128)(2,1)S(1)} fusion(bf16[384,1152]{1,0:T(8,128)(2,1)} %text, bf16[384,1152]{1,0:T(8,128)(2,1)} %image, pred[]{:T(512)S(6)} %lt.10), kind=kLoop, calls=%fused_computation.1 | loop fusion | flops 442368 | bytes 2654209 | tf_op jit(solution)/shard_map/jit(_where)/select_n | solution.py:172
  2.1 0.1 collective-permute-start.2
  2.2 2.4 %collective-permute-done.2.b1 = bf16[384,1152]{1,0:T(8,128)(2,1)S(1)} collective-permute-done((bf16[384,1152]{1,0:T(8,128)(2,1)S(1)}, bf16[384,1152]{1,0:T(8,128)(2,1)S(1)}, u32[]{:S(2)}, u32[]{:S(2)}) %collective-permute-start.2) | collective-permute-done | bytes 884768 | tf_op jit(solution)/shard_map/ppermute | solution.py:28
  4.6 0.0 copy-done.1
  4.6 0.0 copy-done
  4.6 1.1 %broadcast_select_fusion.2 = (bf16[384,1152]{1,0:T(8,128)(2,1)}, bf16[384,1152]{1,0:T(8,128)(2,1)S(1)}) fusion(bf16[384,1152]{1,0:T(8,128)(2,1)S(1)} %collective-permute-done.2.b1, pred[]{:T(512)S(6)} %or.3, bf16[384,1152]{1,0:T(8,128)(2,1)S(1)} %copy-done.1, bf16[384,1152]{1,0:T(8,128)(2,1)S(1)} %copy-done, pred[]{:T(512)S(6)} %lt.10), kind=kLoop, calls=%fused_computation.2 | loop fusion | flops 884736 | bytes 4423682 | tf_op jit(solution)/shard_map/jit(_where)/select_n | solution.py:177
  5.6 2.6 %collective-permute-start = (bf16[384,1152]{1,0:T(8,128)(2,1)S(1)}, bf16[384,1152]{1,0:T(8,128)(2,1)S(1)}, u32[]{:S(2)}, u32[]{:S(2)}) collective-permute-start(bf16[384,1152]{1,0:T(8,128)(2,1)S(1)} %get-tuple-element.44.raw), channel_id=1, source_target_pairs={{0,30},{1,31},{2,4},{3,5},{4,2},{5,3},{6,8},{7,9},{8,6},{9,7},{10,... | collective-permute-start | bytes 2654216 | tf_op jit(solution)/shard_map/ppermute | solution.py:28
  8.3 0.0 copy-start.3
  8.3 0.9 %copy-done.3 = bf16[384,1152]{1,0:T(8,128)(2,1)} copy-done((bf16[384,1152]{1,0:T(8,128)(2,1)}, bf16[384,1152]{1,0:T(8,128)(2,1)S(1)}, u32[]{:S(2)}) %copy-start.3) | copy-done | bytes 884760
  9.2 1.2 %collective-permute-start.3 = (bf16[384,1152]{1,0:T(8,128)(2,1)}, bf16[384,1152]{1,0:T(8,128)(2,1)}, u32[]{:S(2)}, u32[]{:S(2)}) collective-permute-start(bf16[384,1152]{1,0:T(8,128)(2,1)} %get-tuple-element.43), channel_id=1, source_target_pairs={{0,1},{1,0},{2,3},{3,2},{4,5},{5,4},{6,7},{7,6},{8,9},{9,8},{10,11... | collective-permute-start | bytes 2654216 | tf_op jit(solution)/shard_map/ppermute | solution.py:28
  10.4 18.5 %collective-permute-done.b2 = bf16[384,1152]{1,0:T(8,128)(2,1)S(1)} collective-permute-done((bf16[384,1152]{1,0:T(8,128)(2,1)S(1)}, bf16[384,1152]{1,0:T(8,128)(2,1)S(1)}, u32[]{:S(2)}, u32[]{:S(2)}) %collective-permute-start) | collective-permute-done | bytes 884768 | tf_op jit(solution)/shard_map/ppermute | solution.py:28
  28.9 1.0 %broadcast_select_fusion.3 = bf16[384,1152]{1,0:T(8,128)(2,1)} fusion(bf16[384,1152]{1,0:T(8,128)(2,1)S(1)} %broadcast_select_fusion.1.raw, bf16[384,1152]{1,0:T(8,128)(2,1)S(1)} %collective-permute-done.b2, pred[]{:T(512)S(6)} %or.3), kind=kLoop, calls=%fused_computation.3 | loop fusion | flops 442368 | bytes 2654209 | tf_op jit(solution)/shard_map/jit(_where)/select_n | solution.py:179
  29.9 1.5 %collective-permute-start.1 = (bf16[384,1152]{1,0:T(8,128)(2,1)}, bf16[384,1152]{1,0:T(8,128)(2,1)}, u32[]{:S(2)}, u32[]{:S(2)}) collective-permute-start(bf16[384,1152]{1,0:T(8,128)(2,1)} %broadcast_select_fusion.3), channel_id=1, source_target_pairs={{0,1},{1,0},{2,3},{3,2},{4,5},{5,4},{6,7},{7,6},{8,9},{9,8},{10,11... | collective-permute-start | bytes 2654216 | tf_op jit(solution)/shard_map/ppermute | solution.py:28
  32.6 0.1 pad_maximum_fusion.scal
  32.7 0.0 collective-permute-done.3.b3
  32.7 1.4 %collective-permute-start.5 = (bf16[384,1152]{1,0:T(8,128)(2,1)}, bf16[384,1152]{1,0:T(8,128)(2,1)S(1)}, u32[]{:S(2)}, u32[]{:S(2)}) collective-permute-start(bf16[384,1152]{1,0:T(8,128)(2,1)} %collective-permute-done.3.b3), channel_id=1, source_target_pairs={{0,30},{1,31},{2,4},{3,5},{4,2},{5,3},{6,8},{7,9},{8,6},{9,7},{10,... | collective-permute-start | bytes 2654216 | tf_op jit(solution)/shard_map/ppermute | solution.py:28
  34.1 0.0 copy-start.2
  34.1 1.2 %copy-done.2 = bf16[384,1152]{1,0:T(8,128)(2,1)S(1)} copy-done((bf16[384,1152]{1,0:T(8,128)(2,1)S(1)}, bf16[384,1152]{1,0:T(8,128)(2,1)}, u32[]{:S(2)}) %copy-start.2) | copy-done | bytes 884760
  35.3 3.1 %own_pair.1 = (bf16[384,1152]{1,0:T(8,128)(2,1)S(1)}, bf16[384,1152]{1,0:T(8,128)(2,1)S(1)}, f32[384,1152]{1,0:T(8,128)S(1)}, f32[384,1152]{1,0:T(8,128)S(1)}, f32[384,128]{1,0:T(8,128)S(1)}) custom-call(f32[2]{0:T(128)S(1)} %pad_maximum_fusion.scal, bf16[384,1152]{1,0:T(8,128)(2,1)S(1)} %copy-done.2, bf16[384,1152]{1,0:T(8,128)(2,1)S(1)} %copy-done), custom_call_target="tpu_custom_call" | custom-call | flops 1019215872 | bytes 7274496 | tf_op jit(solution)/shard_map/own_pair/pallas_call | solution.py:146
  38.4 0.0 copy-start.4
  38.4 5.9 %near_blocks.1 = (bf16[384,1152]{1,0:T(8,128)(2,1)S(1)}, bf16[384,1152]{1,0:T(8,128)(2,1)S(1)}, f32[384,1152]{1,0:T(8,128)S(1)}, f32[384,1152]{1,0:T(8,128)S(1)}, f32[384,128]{1,0:T(8,128)S(1)}) custom-call(f32[2]{0:T(128)S(1)} %pad_maximum_fusion.scal, s32[1]{0:T(128)} %bitcast.2.flag, bf16[384,1152]{1,0:T(8,128)(2,1)S(1)} %collective-permute-done.2.b1, ...), custom_call_target="tpu_custom_call" | custom-call | flops 2038431744 | bytes 13664256 | tf_op jit(solution)/shard_map/near_blocks/pallas_call | solution.py:146
  44.4 5.5 %collective-permute-done.1.b5 = bf16[384,1152]{1,0:T(8,128)(2,1)} collective-permute-done((bf16[384,1152]{1,0:T(8,128)(2,1)}, bf16[384,1152]{1,0:T(8,128)(2,1)}, u32[]{:S(2)}, u32[]{:S(2)}) %collective-permute-start.1) | collective-permute-done | bytes 884768 | tf_op jit(solution)/shard_map/ppermute | solution.py:28
  49.8 0.0 collective-permute-start.4
  49.8 5.1 %collective-permute-done.5.b4 = bf16[384,1152]{1,0:T(8,128)(2,1)S(1)} collective-permute-done((bf16[384,1152]{1,0:T(8,128)(2,1)}, bf16[384,1152]{1,0:T(8,128)(2,1)S(1)}, u32[]{:S(2)}, u32[]{:S(2)}) %collective-permute-start.5) | collective-permute-done | bytes 884768 | tf_op jit(solution)/shard_map/ppermute | solution.py:28
  54.9 0.0 copy-done.4
  54.9 4.6 %finish_u.1 = (bf16[384,1152]{1,0:T(8,128)(2,1)S(1)}, f32[384,128]{1,0:T(8,128)S(1)}) custom-call(f32[2]{0:T(128)S(1)} %pad_maximum_fusion.scal, s32[1]{0:T(128)} %bitcast.2.flag, bf16[384,1152]{1,0:T(8,128)(2,1)S(1)} %collective-permute-done.5.b4, bf16[384,1152]{1,0:T(8,128)(2,1)} %collective-permute-done.1.b5, ...), custom_call_target="tpu_custom_call" | custom-call | flops 1358954496 | bytes 6586368 | tf_op jit(solution)/shard_map/finish_u/pallas_call | solution.py:146
  59.5 0.0 collective-permute-done.4.b6
  59.6 4.2 %finish_w.1 = (bf16[384,1152]{1,0:T(8,128)(2,1)}, bf16[384,1152]{1,0:T(8,128)(2,1)}, f32[1,384]{1,0:T(1,128)S(1)}) custom-call(f32[2]{0:T(128)S(1)} %pad_maximum_fusion.scal, s32[1]{0:T(128)} %bitcast.2.flag, bf16[384,1152]{1,0:T(8,128)(2,1)S(1)} %collective-permute-done.4.b6, bf16[384,1152]{1,0:T(8,128)(2,1)S(1)} %get-tuple-element.33.z_w, ...), custom_call_target="tpu_custom_call" | custom-call | flops 679477248 | bytes 7276032 | tf_op jit(solution)/shard_map/finish_w/pallas_call | solution.py:146
  63.8 0.6 reduce
Async XLA Ops:
  0.6 3.9 %copy-start.1 = (bf16[384,1152]{1,0:T(8,128)(2,1)S(1)}, bf16[384,1152]{1,0:T(8,128)(2,1)}, u32[]{:S(2)}) copy-start(bf16[384,1152]{1,0:T(8,128)(2,1)} %image) | copy-start | bytes 2654212
  0.6 3.9 %copy-start = (bf16[384,1152]{1,0:T(8,128)(2,1)S(1)}, bf16[384,1152]{1,0:T(8,128)(2,1)}, u32[]{:S(2)}) copy-start(bf16[384,1152]{1,0:T(8,128)(2,1)} %text) | copy-start | bytes 2654212
  2.1 2.5 %collective-permute-start.2 = (bf16[384,1152]{1,0:T(8,128)(2,1)S(1)}, bf16[384,1152]{1,0:T(8,128)(2,1)S(1)}, u32[]{:S(2)}, u32[]{:S(2)}) collective-permute-start(bf16[384,1152]{1,0:T(8,128)(2,1)S(1)} %broadcast_select_fusion.1.raw), channel_id=1, source_target_pairs={{0,2},{1,3},{2,0},{3,1},{4,6},{5,7},{6,4},{7,5},{8,10},{9,11},{10,... | collective-permute-start | bytes 2654216 | tf_op jit(solution)/shard_map/ppermute | solution.py:28
  5.6 23.2 %collective-permute-start = (bf16[384,1152]{1,0:T(8,128)(2,1)S(1)}, bf16[384,1152]{1,0:T(8,128)(2,1)S(1)}, u32[]{:S(2)}, u32[]{:S(2)}) collective-permute-start(bf16[384,1152]{1,0:T(8,128)(2,1)S(1)} %get-tuple-element.44.raw), channel_id=1, source_target_pairs={{0,30},{1,31},{2,4},{3,5},{4,2},{5,3},{6,8},{7,9},{8,6},{9,7},{10,... | collective-permute-start | bytes 2654216 | tf_op jit(solution)/shard_map/ppermute | solution.py:28
  8.3 0.9 %copy-start.3 = (bf16[384,1152]{1,0:T(8,128)(2,1)}, bf16[384,1152]{1,0:T(8,128)(2,1)S(1)}, u32[]{:S(2)}) copy-start(bf16[384,1152]{1,0:T(8,128)(2,1)S(1)} %get-tuple-element.44.raw) | copy-start | bytes 2654212
  9.2 23.5 %collective-permute-start.3 = (bf16[384,1152]{1,0:T(8,128)(2,1)}, bf16[384,1152]{1,0:T(8,128)(2,1)}, u32[]{:S(2)}, u32[]{:S(2)}) collective-permute-start(bf16[384,1152]{1,0:T(8,128)(2,1)} %get-tuple-element.43), channel_id=1, source_target_pairs={{0,1},{1,0},{2,3},{3,2},{4,5},{5,4},{6,7},{7,6},{8,9},{9,8},{10,11... | collective-permute-start | bytes 2654216 | tf_op jit(solution)/shard_map/ppermute | solution.py:28
  29.9 19.9 %collective-permute-start.1 = (bf16[384,1152]{1,0:T(8,128)(2,1)}, bf16[384,1152]{1,0:T(8,128)(2,1)}, u32[]{:S(2)}, u32[]{:S(2)}) collective-permute-start(bf16[384,1152]{1,0:T(8,128)(2,1)} %broadcast_select_fusion.3), channel_id=1, source_target_pairs={{0,1},{1,0},{2,3},{3,2},{4,5},{5,4},{6,7},{7,6},{8,9},{9,8},{10,11... | collective-permute-start | bytes 2654216 | tf_op jit(solution)/shard_map/ppermute | solution.py:28
  32.7 22.2 %collective-permute-start.5 = (bf16[384,1152]{1,0:T(8,128)(2,1)}, bf16[384,1152]{1,0:T(8,128)(2,1)S(1)}, u32[]{:S(2)}, u32[]{:S(2)}) collective-permute-start(bf16[384,1152]{1,0:T(8,128)(2,1)} %collective-permute-done.3.b3), channel_id=1, source_target_pairs={{0,30},{1,31},{2,4},{3,5},{4,2},{5,3},{6,8},{7,9},{8,6},{9,7},{10,... | collective-permute-start | bytes 2654216 | tf_op jit(solution)/shard_map/ppermute | solution.py:28
  34.1 1.2 %copy-start.2 = (bf16[384,1152]{1,0:T(8,128)(2,1)S(1)}, bf16[384,1152]{1,0:T(8,128)(2,1)}, u32[]{:S(2)}) copy-start(bf16[384,1152]{1,0:T(8,128)(2,1)} %image) | copy-start | bytes 2654212
  38.4 16.5 %copy-start.4 = (bf16[384,1152]{1,0:T(8,128)(2,1)S(1)}, bf16[384,1152]{1,0:T(8,128)(2,1)}, u32[]{:S(2)}) copy-start(bf16[384,1152]{1,0:T(8,128)(2,1)} %copy-done.3) | copy-start | bytes 2654212
  49.8 9.7 %collective-permute-start.4 = (bf16[384,1152]{1,0:T(8,128)(2,1)}, bf16[384,1152]{1,0:T(8,128)(2,1)S(1)}, u32[]{:S(2)}, u32[]{:S(2)}) collective-permute-start(bf16[384,1152]{1,0:T(8,128)(2,1)} %collective-permute-done.1.b5), channel_id=1, source_target_pairs={{0,2},{1,3},{2,0},{3,1},{4,6},{5,7},{6,4},{7,5},{8,10},{9,11},{10,... | collective-permute-start | bytes 2654216 | tf_op jit(solution)/shard_map/ppermute | solution.py:28

commit v5 on v4

v5 whole, which is shorter than its diff:
```python
import jax
import jax.numpy as jnp
from jax import lax
from jax.experimental import pallas as pl
from jax.experimental.pallas import tpu as pltpu
from jax.sharding import PartitionSpec as P

SPAN = 4
GROUP = 4
AXES = ("blk", "inner")
F32 = jnp.float32
BF16 = jnp.bfloat16
VMEM_LIMIT = 16 * 1024 * 1024

X_SWAP = {0: (1, 0), 1: (0, 0), 2: (3, 0), 3: (2, 0)}
CORE_SWAP = {0: (2, 0), 1: (3, 0), 2: (0, 0), 3: (1, 0)}
GROUP_SHIFT = {0: (2, -1), 1: (3, -1), 2: (0, 1), 3: (1, 1)}


def send(value, moves):
    count = lax.axis_size(AXES)
    groups = count // GROUP
    pairs = [
        (g * GROUP + role, (g + step) % groups * GROUP + to)
        for g in range(groups)
        for role, (to, step) in moves.items()
    ]
    return lax.ppermute(value, AXES, pairs)


def unit_rows(raw):
    values = raw.astype(F32)
    length = jnp.sqrt(jnp.sum(values * values, axis=1, keepdims=True) + 1e-06)
    return values * (1.0 / length), length


def sigmoid_of(p):
    whole = 1.0 + p
    guess = pl.reciprocal(whole, approx=True)
    guess = guess * (2.0 - whole * guess)
    return p * (guess * (2.0 - whole * guess))


def log1p_of(p):
    below = p * (1.0 - p * (0.5 - p * (1.0 / 3.0)))
    return jnp.where(p < 0.015625, below, jnp.log(1.0 + p))


def softplus_lanes(p):
    total = None
    parts = [p[:, start : start + 128] for start in range(0, p.shape[1], 128)]
    for first in range(0, len(parts), 3):
        joint = parts[first]
        for part in parts[first + 1 : first + 3]:
            joint = joint + part + joint * part
        value = log1p_of(joint)
        total = value if total is None else total + value
    return total


def dot_nt(a, b):
    return lax.dot_general(a, b, (((1,), (1,)), ((), ())), preferred_element_type=F32)


def dot_nn(a, b):
    return lax.dot_general(a, b, (((1,), (0,)), ((), ())), preferred_element_type=F32)


def dot_tn(a, b):
    return lax.dot_general(a, b, (((0,), (0,)), ((), ())), preferred_element_type=F32)


def pair_step(own, blocks, scale, shift, work):
    rows = own.shape[0]
    for place, raw in enumerate(blocks):
        work[place * rows : (place + 1) * rows] = unit_rows(raw)[0].astype(BF16)
    others = work[: len(blocks) * rows]
    p = jnp.exp(scale * dot_nt(own, others) + shift)
    coef = (sigmoid_of(p) * scale).astype(BF16)
    return dot_nn(coef, others), softplus_lanes(p)


def project(raw, grad):
    unit, length = unit_rows(raw)
    return ((grad - unit * jnp.sum(unit * grad, axis=1, keepdims=True)) / length).astype(BF16)


def near_kernel(scal, flag, image, text, b1, b2, b3, z_u, z_w, grad_u, grad_w, loss, work):
    u_is_image = flag[0] == 1
    u_weight = flag[0].astype(F32)
    scale, shift = scal[0], scal[1]
    zi = unit_rows(image[...])[0].astype(BF16)
    zt = unit_rows(text[...])[0].astype(BF16)
    z_u[...] = jnp.where(u_is_image, zi, zt)
    z_w[...] = jnp.where(u_is_image, zt, zi)
    scores = scale * dot_nt(zi, zt) + shift
    rows = lax.broadcasted_iota(jnp.int32, scores.shape, 0)
    columns = lax.broadcasted_iota(jnp.int32, scores.shape, 1)
    sign = jnp.where(rows == columns, F32(-1.0), F32(1.0))
    p = jnp.exp(sign * scores)
    coef = (sign * sigmoid_of(p) * scale).astype(BF16)
    total = softplus_lanes(p)
    grad_image = dot_nn(coef, zt)
    grad_text = dot_tn(coef, zi)
    grad_u[...] = jnp.where(u_is_image, grad_image, grad_text)
    grad_w[...] = jnp.where(u_is_image, grad_text, grad_image)
    term, row_loss = pair_step(z_u[...], (b2[...],), scale, shift, work)
    grad_u[...] += term
    total = total + u_weight * row_loss
    term, row_loss = pair_step(z_w[...], (b1[...], b3[...]), scale, shift, work)
    grad_w[...] += term
    loss[...] = total + (1.0 - u_weight) * row_loss


def fifth_kernel(scal, flag, b5, z_u, grad_in, loss_in, grad_u, loss, work):
    term, row_loss = pair_step(z_u[...], (b5[...],), scal[0], scal[1], work)
    grad_u[...] = grad_in[...] + term
    loss[...] = loss_in[...] + flag[0].astype(F32) * row_loss


def u_kernel(scal, flag, b4, z_u, grad_u, loss_in, image, text, done_u, loss, work):
    raw = jnp.where(flag[0] == 1, image[...], text[...])
    term, row_loss = pair_step(z_u[...], (b4[...],), scal[0], scal[1], work)
    loss[...] = loss_in[...] + flag[0].astype(F32) * row_loss
    done_u[...] = project(raw, grad_u[...] + term)


def w_kernel(
    scal, flag, b6, z_w, grad_w, loss_in, image, text, done_u, image_grad, text_grad, loss_rows, work
):
    u_is_image = flag[0] == 1
    raw = jnp.where(u_is_image, text[...], image[...])
    term, row_loss = pair_step(z_w[...], (b6[...],), scal[0], scal[1], work)
    total = loss_in[...] + (1.0 - flag[0].astype(F32)) * row_loss
    loss_rows[...] = jnp.sum(jnp.transpose(total), axis=0) / (SPAN * total.shape[0])
    done_w = project(raw, grad_w[...] + term)
    image_grad[...] = jnp.where(u_is_image, done_u[...], done_w)
    text_grad[...] = jnp.where(u_is_image, done_w, done_u[...])


def call(kernel, scalars, args, outs, name, work_rows=0):
    smem = pl.BlockSpec(memory_space=pltpu.SMEM)
    vmem = pl.BlockSpec(memory_space=pltpu.VMEM)
    width = args[0].shape[1]
    return pl.pallas_call(
        kernel,
        out_shape=outs,
        in_specs=[smem] * len(scalars) + [vmem] * len(args),
        out_specs=[vmem] * len(outs),
        scratch_shapes=[pltpu.VMEM((work_rows, width), BF16)] if work_rows else [],
        name=name,
        cost_estimate=pl.CostEstimate(flops=1, bytes_accessed=1, transcendentals=0),
        compiler_params=pltpu.CompilerParams(vmem_limit_bytes=VMEM_LIMIT),
    )(*scalars, *args)


def local(image, text, score_scaling, score_shift):
    rows, width = image.shape
    role = lax.axis_index(AXES) % GROUP
    u_is_image = role < 2
    flag = u_is_image.astype(jnp.int32).reshape(1)
    scal = jnp.stack([score_scaling, score_shift])
    block = jax.ShapeDtypeStruct((rows, width), BF16)
    sums = jax.ShapeDtypeStruct((rows, width), F32)
    partial = jax.ShapeDtypeStruct((rows, 128), F32)
    line = jax.ShapeDtypeStruct((rows,), F32)

    u = jnp.where(u_is_image, image, text)
    w = jnp.where(u_is_image, text, image)
    u, w = lax.optimization_barrier((u, w))
    outer = (role == 0) | (role == 3)

    slot1 = send(w, CORE_SWAP)
    slot2 = send(u, GROUP_SHIFT)
    slot3 = send(jnp.where(outer, slot1, u), X_SWAP)
    slot4 = send(slot3, GROUP_SHIFT)
    slot5 = send(jnp.where(outer, w, slot2), X_SWAP)
    z_u, z_w, grad_u, grad_w, loss = call(
        near_kernel,
        (scal, flag),
        (image, text, slot1, slot2, slot3),
        (block, block, sums, sums, partial),
        "near_blocks",
        2 * rows,
    )
    slot5, loss = lax.optimization_barrier((slot5, loss))
    slot6 = send(slot5, CORE_SWAP)
    grad_u, loss = call(
        fifth_kernel, (scal, flag), (slot5, z_u, grad_u, loss), (sums, partial), "fifth_block", rows
    )
    done_u, loss = call(
        u_kernel,
        (scal, flag),
        (slot4, z_u, grad_u, loss, image, text),
        (block, partial),
        "finish_u",
        rows,
    )
    image_grad, text_grad, loss_rows = call(
        w_kernel,
        (scal, flag),
        (slot6, z_w, grad_w, loss, image, text, done_u),
        (block, block, line),
        "finish_w",
        rows,
    )
    return loss_rows, image_grad, text_grad


def solution(mesh):
    in_specs = (P(AXES, None), P(AXES, None), P(), P())
    out_specs = (P(AXES), P(AXES, None), P(AXES, None))
    return jax.shard_map(local, mesh=mesh, in_specs=in_specs, out_specs=out_specs, check_vma=False)
```

time: 64.6 us -> 61.5 us (0.952)
  waiting for transfers between devices: 31.4 us -> 28.2 us
  local copies, waits for them, and re-layouts: 2.1 us -> 0.01 us
  other arithmetic: 4.16 us -> 5.85 us
    ppermute x6, waiting for transfers between devices: 31.4 us -> 28.2 us  [send(): return lax.ppermute(value, AXES, pairs)]
    unnamed x10 -> x6, local copies, waits for them, and re-layouts: 2.1 us -> 0.01 us
    select_n x1, other arithmetic: 1.07 us -> 2.25 us  [local(): slot3 = send(jnp.where(outer, slot1, u), X_SWAP)]
    select_n x1, other arithmetic: 1.4 us -> 2.51 us  [local(): w = jnp.where(u_is_image, text, image)]
  transfers between devices with their start and end apart: 6 -> 6, of which waited for: 4 -> 3; matrix products, arithmetic and copies ran while one was open for 2% -> 5% of each run, Pallas kernels for 21% -> 22%
where the time goes in v5:
time: 61.5 us; the launch traced here: 61.2 us
  waiting for transfers between devices  28.2 us (46%)
  Pallas kernels  17.8 us (29%)
  starting transfers between devices  7.33 us (12%)
  other arithmetic  5.85 us (10%)
  between operations  1.98 us (3%)
    ppermute x6, waiting for transfers between devices, send(): return lax.ppermute(value, AXES, pairs)  28.2 us
    pallas_call x4, Pallas kernels, call(): pl.pallas_call(kernel, out_shape=outs, in_specs=[smem] * len(scalars) + [...  17.8 us
    ppermute x6, starting transfers between devices, send(): return lax.ppermute(value, AXES, pairs)  7.33 us
    select_n x1, other arithmetic, local(): w = jnp.where(u_is_image, text, image)  2.51 us
    select_n x1, other arithmetic, local(): slot3 = send(jnp.where(outer, slot1, u), X_SWAP)  2.25 us
  transfers between devices with their start and end apart: 6, of which 3 were waited for; matrix products, arithmetic and copies ran while one was open for 5% of the time, Pallas kernels for 22%

profile of v5, /device:TPU:1, one launch (start us, length us, event | category | flops | bytes accessed | tf_op | source)
XLA Modules:
  0.0 61.2 jit_solution(16390246790455367180)
XLA Ops:
  0.6 2.5 %broadcast_select_fusion = (bf16[384,1152]{1,0:T(8,128)(2,1)S(1)}, bf16[384,1152]{1,0:T(8,128)(2,1)}) fusion(bf16[384,1152]{1,0:T(8,128)(2,1)} %text.5, bf16[384,1152]{1,0:T(8,128)(2,1)} %image.5, pred[]{:T(512)S(6)} %lt.10), kind=kLoop, calls=%fused_computation | loop fusion | flops 884736 | bytes 3538945 | tf_op jit(solution)/shard_map/jit(_where)/select_n | solution.py:169
  3.2 0.0 copy-start.2
  3.2 0.1 collective-permute-start.2
  3.2 2.6 %collective-permute-start = (bf16[384,1152]{1,0:T(8,128)(2,1)}, bf16[384,1152]{1,0:T(8,128)(2,1)S(1)}, u32[]{:S(2)}, u32[]{:S(2)}) collective-permute-start(bf16[384,1152]{1,0:T(8,128)(2,1)} %get-tuple-element.20), channel_id=1, source_target_pairs={{0,30},{1,31},{2,4},{3,5},{4,2},{5,3},{6,8},{7,9},{8,6},{9,7},{10,... | collective-permute-start | bytes 2654216 | tf_op jit(solution)/shard_map/ppermute | solution.py:28
  5.8 0.0 collective-permute-done.2.b1
  5.8 0.0 copy-done.2
  5.8 2.3 %broadcast_select_fusion.2 = bf16[384,1152]{1,0:T(8,128)(2,1)} fusion(bf16[384,1152]{1,0:T(8,128)(2,1)S(1)} %collective-permute-done.2.b1, bf16[384,1152]{1,0:T(8,128)(2,1)} %get-tuple-element.20, pred[]{:T(512)S(6)} %or.3), kind=kLoop, calls=%fused_computation.2 | loop fusion | flops 442368 | bytes 2654209 | tf_op jit(solution)/shard_map/jit(_where)/select_n | solution.py:175
  8.1 0.0 copy-start
  8.1 0.0 copy-start.1
  8.1 0.9 %collective-permute-start.3 = (bf16[384,1152]{1,0:T(8,128)(2,1)}, bf16[384,1152]{1,0:T(8,128)(2,1)}, u32[]{:S(2)}, u32[]{:S(2)}) collective-permute-start(bf16[384,1152]{1,0:T(8,128)(2,1)} %broadcast_select_fusion.2), channel_id=1, source_target_pairs={{0,1},{1,0},{2,3},{3,2},{4,5},{5,4},{6,7},{7,6},{8,9},{9,8},{10,11... | collective-permute-start | bytes 2654216 | tf_op jit(solution)/shard_map/ppermute | solution.py:28
  9.0 17.6 %collective-permute-done.b2 = bf16[384,1152]{1,0:T(8,128)(2,1)S(1)} collective-permute-done((bf16[384,1152]{1,0:T(8,128)(2,1)}, bf16[384,1152]{1,0:T(8,128)(2,1)S(1)}, u32[]{:S(2)}, u32[]{:S(2)}) %collective-permute-start) | collective-permute-done | bytes 884768 | tf_op jit(solution)/shard_map/ppermute | solution.py:28
  26.6 1.0 %broadcast_select_fusion.3 = bf16[384,1152]{1,0:T(8,128)(2,1)} fusion(bf16[384,1152]{1,0:T(8,128)(2,1)} %copy-done.2, bf16[384,1152]{1,0:T(8,128)(2,1)S(1)} %collective-permute-done.b2, pred[]{:T(512)S(6)} %or.3), kind=kLoop, calls=%fused_computation.3 | loop fusion | flops 442368 | bytes 2654209 | tf_op jit(solution)/shard_map/jit(_where)/select_n | solution.py:177
  27.6 3.0 %collective-permute-start.1 = (bf16[384,1152]{1,0:T(8,128)(2,1)}, bf16[384,1152]{1,0:T(8,128)(2,1)}, u32[]{:S(2)}, u32[]{:S(2)}) collective-permute-start(bf16[384,1152]{1,0:T(8,128)(2,1)} %broadcast_select_fusion.3), channel_id=1, source_target_pairs={{0,1},{1,0},{2,3},{3,2},{4,5},{5,4},{6,7},{7,6},{8,9},{9,8},{10,11... | collective-permute-start | bytes 2654216 | tf_op jit(solution)/shard_map/ppermute | solution.py:28
  31.9 0.1 pad_maximum_fusion.scal
  32.0 0.0 collective-permute-done.3.b3
  32.0 0.8 %collective-permute-start.5 = (bf16[384,1152]{1,0:T(8,128)(2,1)}, bf16[384,1152]{1,0:T(8,128)(2,1)S(1)}, u32[]{:S(2)}, u32[]{:S(2)}) collective-permute-start(bf16[384,1152]{1,0:T(8,128)(2,1)} %collective-permute-done.3.b3), channel_id=1, source_target_pairs={{0,30},{1,31},{2,4},{3,5},{4,2},{5,3},{6,8},{7,9},{8,6},{9,7},{10,... | collective-permute-start | bytes 2654216 | tf_op jit(solution)/shard_map/ppermute | solution.py:28
  32.8 0.0 copy-done
  32.8 0.0 copy-done.1
  32.8 7.8 %near_blocks.1 = (bf16[384,1152]{1,0:T(8,128)(2,1)S(1)}, bf16[384,1152]{1,0:T(8,128)(2,1)S(1)}, f32[384,1152]{1,0:T(8,128)S(1)}, f32[384,1152]{1,0:T(8,128)S(1)}, f32[384,128]{1,0:T(8,128)S(1)}) custom-call(f32[2]{0:T(128)S(1)} %pad_maximum_fusion.scal, s32[1]{0:T(128)} %bitcast.2.flag, bf16[384,1152]{1,0:T(8,128)(2,1)S(1)} %copy-done.1, ...), custom_call_target="tpu_custom_call" | custom-call | flops 1 | bytes 1 | tf_op jit(solution)/shard_map/near_blocks/pallas_call | solution.py:145
  40.6 8.1 %collective-permute-done.1.b5 = bf16[384,1152]{1,0:T(8,128)(2,1)} collective-permute-done((bf16[384,1152]{1,0:T(8,128)(2,1)}, bf16[384,1152]{1,0:T(8,128)(2,1)}, u32[]{:S(2)}, u32[]{:S(2)}) %collective-permute-start.1) | collective-permute-done | bytes 884768 | tf_op jit(solution)/shard_map/ppermute | solution.py:28
  48.7 0.0 collective-permute-start.4
  48.7 2.9 %fifth_block.1 = (f32[384,1152]{1,0:T(8,128)S(1)}, f32[384,128]{1,0:T(8,128)S(1)}) custom-call(f32[2]{0:T(128)S(1)} %pad_maximum_fusion.scal, s32[1]{0:T(128)} %bitcast.2.flag, bf16[384,1152]{1,0:T(8,128)(2,1)} %collective-permute-done.1.b5, bf16[384,1152]{1,0:T(8,128)(2,1)S(1)} %get-tuple-element.25.z_u, f32[384,1152]{1,0:T(8,128)S(1)} %get-tuple-element.26.grad_in, ...), custom_call_target="tpu_custom_call" | custom-call | flops 1 | bytes 1 | tf_op jit(solution)/shard_map/fifth_block/pallas_call | solution.py:145
  51.7 2.5 %collective-permute-done.5.b4 = bf16[384,1152]{1,0:T(8,128)(2,1)S(1)} collective-permute-done((bf16[384,1152]{1,0:T(8,128)(2,1)}, bf16[384,1152]{1,0:T(8,128)(2,1)S(1)}, u32[]{:S(2)}, u32[]{:S(2)}) %collective-permute-start.5) | collective-permute-done | bytes 884768 | tf_op jit(solution)/shard_map/ppermute | solution.py:28
  54.2 2.8 %finish_u.1 = (bf16[384,1152]{1,0:T(8,128)(2,1)S(1)}, f32[384,128]{1,0:T(8,128)S(1)}) custom-call(f32[2]{0:T(128)S(1)} %pad_maximum_fusion.scal, s32[1]{0:T(128)} %bitcast.2.flag, bf16[384,1152]{1,0:T(8,128)(2,1)S(1)} %collective-permute-done.5.b4, bf16[384,1152]{1,0:T(8,128)(2,1)S(1)} %get-tuple-element.25.z_u, f32[384,1152]{1,0:T(8,128)S(1)} %get-tuple-element.28.grad_u, ...), custom_call_target="tpu_custom_call" | custom-call | flops 1 | bytes 1 | tf_op jit(solution)/shard_map/finish_u/pallas_call | solution.py:145
  57.0 0.0 collective-permute-done.4.b6
  57.0 4.2 %finish_w.1 = (bf16[384,1152]{1,0:T(8,128)(2,1)}, bf16[384,1152]{1,0:T(8,128)(2,1)}, f32[384]{0:T(512)}) custom-call(f32[2]{0:T(128)S(1)} %pad_maximum_fusion.scal, s32[1]{0:T(128)} %bitcast.2.flag, bf16[384,1152]{1,0:T(8,128)(2,1)S(1)} %collective-permute-done.4.b6, bf16[384,1152]{1,0:T(8,128)(2,1)S(1)} %get-tuple-element.23.z_w, ...), custom_call_target="tpu_custom_call" | custom-call | flops 1 | bytes 1 | tf_op jit(solution)/shard_map/finish_w/pallas_call | solution.py:145
Async XLA Ops:
  3.2 2.6 %copy-start.2 = (bf16[384,1152]{1,0:T(8,128)(2,1)}, bf16[384,1152]{1,0:T(8,128)(2,1)S(1)}, u32[]{:S(2)}) copy-start(bf16[384,1152]{1,0:T(8,128)(2,1)S(1)} %get-tuple-element.19) | copy-start | bytes 2654212
  3.2 2.6 %collective-permute-start.2 = (bf16[384,1152]{1,0:T(8,128)(2,1)S(1)}, bf16[384,1152]{1,0:T(8,128)(2,1)S(1)}, u32[]{:S(2)}, u32[]{:S(2)}) collective-permute-start(bf16[384,1152]{1,0:T(8,128)(2,1)S(1)} %get-tuple-element.19), channel_id=1, source_target_pairs={{0,2},{1,3},{2,0},{3,1},{4,6},{5,7},{6,4},{7,5},{8,10},{9,11},{10,... | collective-permute-start | bytes 2654216 | tf_op jit(solution)/shard_map/ppermute | solution.py:28
  3.2 23.4 %collective-permute-start = (bf16[384,1152]{1,0:T(8,128)(2,1)}, bf16[384,1152]{1,0:T(8,128)(2,1)S(1)}, u32[]{:S(2)}, u32[]{:S(2)}) collective-permute-start(bf16[384,1152]{1,0:T(8,128)(2,1)} %get-tuple-element.20), channel_id=1, source_target_pairs={{0,30},{1,31},{2,4},{3,5},{4,2},{5,3},{6,8},{7,9},{8,6},{9,7},{10,... | collective-permute-start | bytes 2654216 | tf_op jit(solution)/shard_map/ppermute | solution.py:28
  8.1 24.7 %copy-start = (bf16[384,1152]{1,0:T(8,128)(2,1)S(1)}, bf16[384,1152]{1,0:T(8,128)(2,1)}, u32[]{:S(2)}) copy-start(bf16[384,1152]{1,0:T(8,128)(2,1)} %text.5) | copy-start | bytes 2654212
  8.1 24.7 %copy-start.1 = (bf16[384,1152]{1,0:T(8,128)(2,1)S(1)}, bf16[384,1152]{1,0:T(8,128)(2,1)}, u32[]{:S(2)}) copy-start(bf16[384,1152]{1,0:T(8,128)(2,1)} %image.5) | copy-start | bytes 2654212
  8.1 23.9 %collective-permute-start.3 = (bf16[384,1152]{1,0:T(8,128)(2,1)}, bf16[384,1152]{1,0:T(8,128)(2,1)}, u32[]{:S(2)}, u32[]{:S(2)}) collective-permute-start(bf16[384,1152]{1,0:T(8,128)(2,1)} %broadcast_select_fusion.2), channel_id=1, source_target_pairs={{0,1},{1,0},{2,3},{3,2},{4,5},{5,4},{6,7},{7,6},{8,9},{9,8},{10,11... | collective-permute-start | bytes 2654216 | tf_op jit(solution)/shard_map/ppermute | solution.py:28
  27.6 21.1 %collective-permute-start.1 = (bf16[384,1152]{1,0:T(8,128)(2,1)}, bf16[384,1152]{1,0:T(8,128)(2,1)}, u32[]{:S(2)}, u32[]{:S(2)}) collective-permute-start(bf16[384,1152]{1,0:T(8,128)(2,1)} %broadcast_select_fusion.3), channel_id=1, source_target_pairs={{0,1},{1,0},{2,3},{3,2},{4,5},{5,4},{6,7},{7,6},{8,9},{9,8},{10,11... | collective-permute-start | bytes 2654216 | tf_op jit(solution)/shard_map/ppermute | solution.py:28
  32.0 22.2 %collective-permute-start.5 = (bf16[384,1152]{1,0:T(8,128)(2,1)}, bf16[384,1152]{1,0:T(8,128)(2,1)S(1)}, u32[]{:S(2)}, u32[]{:S(2)}) collective-permute-start(bf16[384,1152]{1,0:T(8,128)(2,1)} %collective-permute-done.3.b3), channel_id=1, source_target_pairs={{0,30},{1,31},{2,4},{3,5},{4,2},{5,3},{6,8},{7,9},{8,6},{9,7},{10,... | collective-permute-start | bytes 2654216 | tf_op jit(solution)/shard_map/ppermute | solution.py:28
  48.7 8.3 %collective-permute-start.4 = (bf16[384,1152]{1,0:T(8,128)(2,1)}, bf16[384,1152]{1,0:T(8,128)(2,1)S(1)}, u32[]{:S(2)}, u32[]{:S(2)}) collective-permute-start(bf16[384,1152]{1,0:T(8,128)(2,1)} %collective-permute-done.1.b5), channel_id=1, source_target_pairs={{0,2},{1,3},{2,0},{3,1},{4,6},{5,7},{6,4},{7,5},{8,10},{9,11},{10,... | collective-permute-start | bytes 2654216 | tf_op jit(solution)/shard_map/ppermute | solution.py:28

commit v6 on v5

--- a/solution.py
+++ b/solution.py
@@ -85,10 +85,48 @@
     return ((grad - unit * jnp.sum(unit * grad, axis=1, keepdims=True)) / length).astype(BF16)
 
 
-def near_kernel(scal, flag, image, text, b1, b2, b3, z_u, z_w, grad_u, grad_w, loss, work):
-    u_is_image = flag[0] == 1
-    u_weight = flag[0].astype(F32)
-    scale, shift = scal[0], scal[1]
+def scalar_pair(scalars):
+    return scalars[0:1, 0:1], scalars[1:2, 0:1]
+
+
+def image_is_u():
+    return lax.rem(lax.axis_index("blk"), 2) == 0
+
+
+def is_outer():
+    return lax.rem(lax.axis_index("blk"), 2) == lax.axis_index("inner")
+
+
+def sort_kernel(image, text, u, w, sems):
+    def move(image_to, text_to):
+        copies = [
+            pltpu.make_async_copy(image, image_to, sems.at[0]),
+            pltpu.make_async_copy(text, text_to, sems.at[1]),
+        ]
+        for copy in copies:
+            copy.start()
+        for copy in copies:
+            copy.wait()
+
+    u_is_image = image_is_u()
+
+    @pl.when(u_is_image)
+    def _():
+        move(u, w)
+
+    @pl.when(jnp.logical_not(u_is_image))
+    def _():
+        move(w, u)
+
+
+def pick_kernel(when_outer, when_inner, picked):
+    picked[...] = jnp.where(is_outer(), when_outer[...], when_inner[...])
+
+
+def near_kernel(scalars, image, text, b1, b2, b3, z_u, z_w, grad_u, grad_w, loss, work):
+    u_is_image = image_is_u()
+    u_weight = u_is_image.astype(F32)
+    scale, shift = scalar_pair(scalars)
     zi = unit_rows(image[...])[0].astype(BF16)
     zt = unit_rows(text[...])[0].astype(BF16)
     z_u[...] = jnp.where(u_is_image, zi, zt)
@@ -112,97 +150,93 @@
     loss[...] = total + (1.0 - u_weight) * row_loss
 
 
-def fifth_kernel(scal, flag, b5, z_u, grad_in, loss_in, grad_u, loss, work):
-    term, row_loss = pair_step(z_u[...], (b5[...],), scal[0], scal[1], work)
+def fifth_kernel(scalars, b5, z_u, grad_in, loss_in, grad_u, loss, work):
+    term, row_loss = pair_step(z_u[...], (b5[...],), *scalar_pair(scalars), work)
     grad_u[...] = grad_in[...] + term
-    loss[...] = loss_in[...] + flag[0].astype(F32) * row_loss
-
-
-def u_kernel(scal, flag, b4, z_u, grad_u, loss_in, image, text, done_u, loss, work):
-    raw = jnp.where(flag[0] == 1, image[...], text[...])
-    term, row_loss = pair_step(z_u[...], (b4[...],), scal[0], scal[1], work)
-    loss[...] = loss_in[...] + flag[0].astype(F32) * row_loss
+    loss[...] = loss_in[...] + image_is_u().astype(F32) * row_loss
+
+
+def u_kernel(scalars, b4, z_u, grad_u, loss_in, image, text, done_u, loss, work):
+    raw = jnp.where(image_is_u(), image[...], text[...])
+    term, row_loss = pair_step(z_u[...], (b4[...],), *scalar_pair(scalars), work)
+    loss[...] = loss_in[...] + image_is_u().astype(F32) * row_loss
     done_u[...] = project(raw, grad_u[...] + term)
 
 
 def w_kernel(
-    scal, flag, b6, z_w, grad_w, loss_in, image, text, done_u, image_grad, text_grad, loss_rows, work
+    scalars, b6, z_w, grad_w, loss_in, image, text, done_u, image_grad, text_grad, loss_rows, work
 ):
-    u_is_image = flag[0] == 1
+    u_is_image = image_is_u()
     raw = jnp.where(u_is_image, text[...], image[...])
-    term, row_loss = pair_step(z_w[...], (b6[...],), scal[0], scal[1], work)
-    total = loss_in[...] + (1.0 - flag[0].astype(F32)) * row_loss
+    term, row_loss = pair_step(z_w[...], (b6[...],), *scalar_pair(scalars), work)
+    total = loss_in[...] + (1.0 - image_is_u().astype(F32)) * row_loss
     loss_rows[...] = jnp.sum(jnp.transpose(total), axis=0) / (SPAN * total.shape[0])
     done_w = project(raw, grad_w[...] + term)
     image_grad[...] = jnp.where(u_is_image, done_u[...], done_w)
     text_grad[...] = jnp.where(u_is_image, done_w, done_u[...])
 
 
-def call(kernel, scalars, args, outs, name, work_rows=0):
-    smem = pl.BlockSpec(memory_space=pltpu.SMEM)
-    vmem = pl.BlockSpec(memory_space=pltpu.VMEM)
-    width = args[0].shape[1]
+VMEM = pl.BlockSpec(memory_space=pltpu.VMEM)
+ANY = pl.BlockSpec(memory_space=pl.ANY)
+
+
+def call(kernel, in_specs, args, outs, name, scratch=()):
     return pl.pallas_call(
         kernel,
         out_shape=outs,
-        in_specs=[smem] * len(scalars) + [vmem] * len(args),
-        out_specs=[vmem] * len(outs),
-        scratch_shapes=[pltpu.VMEM((work_rows, width), BF16)] if work_rows else [],
+        in_specs=in_specs,
+        out_specs=[VMEM] * len(outs),
+        scratch_shapes=list(scratch),
         name=name,
         cost_estimate=pl.CostEstimate(flops=1, bytes_accessed=1, transcendentals=0),
         compiler_params=pltpu.CompilerParams(vmem_limit_bytes=VMEM_LIMIT),
-    )(*scalars, *args)
+    )(*args)
 
 
 def local(image, text, score_scaling, score_shift):
     rows, width = image.shape
-    role = lax.axis_index(AXES) % GROUP
-    u_is_image = role < 2
-    flag = u_is_image.astype(jnp.int32).reshape(1)
-    scal = jnp.stack([score_scaling, score_shift])
     block = jax.ShapeDtypeStruct((rows, width), BF16)
     sums = jax.ShapeDtypeStruct((rows, width), F32)
     partial = jax.ShapeDtypeStruct((rows, 128), F32)
     line = jax.ShapeDtypeStruct((rows,), F32)
-
-    u = jnp.where(u_is_image, image, text)
-    w = jnp.where(u_is_image, text, image)
-    u, w = lax.optimization_barrier((u, w))
-    outer = (role == 0) | (role == 3)
-
+    def pick(when_outer, when_inner):
+        return call(pick_kernel, [VMEM] * 2, (when_outer, when_inner), (block,), "pick")[0]
+
+    def compute(kernel, args, outs, name, places):
+        work = pltpu.VMEM((places * rows, width), BF16)
+        return call(kernel, [VMEM] * (1 + len(args)), (scalars, *args), outs, name, (work,))
+
+    u, w = call(
+        sort_kernel,
+        [ANY] * 2,
+        [pltpu.with_memory_space_constraint(x, pltpu.HBM) for x in (image, text)],
+        (block, block),
+        "sort",
+        (pltpu.SemaphoreType.DMA((2,)),),
+    )
     slot1 = send(w, CORE_SWAP)
     slot2 = send(u, GROUP_SHIFT)
-    slot3 = send(jnp.where(outer, slot1, u), X_SWAP)
+    slot3 = send(pick(slot1, u), X_SWAP)
     slot4 = send(slot3, GROUP_SHIFT)
-    slot5 = send(jnp.where(outer, w, slot2), X_SWAP)
-    z_u, z_w, grad_u, grad_w, loss = call(
+    slot5 = send(pick(w, slot2), X_SWAP)
+    slot3, score_scaling, score_shift = lax.optimization_barrier((slot3, score_scaling, score_shift))
+    first = lax.broadcasted_iota(jnp.int32, (8, 128), 0) == 0
+    scalars = jnp.where(first, score_scaling, score_shift)
+    z_u, z_w, grad_u, grad_w, loss = compute(
         near_kernel,
-        (scal, flag),
         (image, text, slot1, slot2, slot3),
         (block, block, sums, sums, partial),
         "near_blocks",
-        2 * rows,
+        2,
     )
     slot5, loss = lax.optimization_barrier((slot5, loss))
     slot6 = send(slot5, CORE_SWAP)
-    grad_u, loss = call(
-        fifth_kernel, (scal, flag), (slot5, z_u, grad_u, loss), (sums, partial), "fifth_block", rows
-    )
-    done_u, loss = call(
-        u_kernel,
-        (scal, flag),
-        (slot4, z_u, grad_u, loss, image, text),
-        (block, partial),
-        "finish_u",
-        rows,
-    )
-    image_grad, text_grad, loss_rows = call(
-        w_kernel,
-        (scal, flag),
-        (slot6, z_w, grad_w, loss, image, text, done_u),
-        (block, block, line),
-        "finish_w",
-        rows,
+    grad_u, loss = compute(fifth_kernel, (slot5, z_u, grad_u, loss), (sums, partial), "fifth_block", 1)
+    done_u, loss = compute(
+        u_kernel, (slot4, z_u, grad_u, loss, image, text), (block, partial), "finish_u", 1
+    )
+    image_grad, text_grad, loss_rows = compute(
+        w_kernel, (slot6, z_w, grad_w, loss, image, text, done_u), (block, block, line), "finish_w", 1
     )
     return loss_rows, image_grad, text_grad
 

time: 61.5 us -> 58.1 us (0.945)
  other arithmetic: 5.85 us -> 0.01 us
  Pallas kernels: 17.8 us -> 20.2 us
  starting transfers between devices: 7.33 us -> 8.06 us
  waiting for transfers between devices: 28.2 us -> 27.5 us
    select_n x3 -> x1, other arithmetic: 5.78 us -> 0.01 us  [local(): scalars = jnp.where(first, score_scaling, score_shift)]
    pallas_call x4 -> x7, Pallas kernels: 17.8 us -> 20.2 us  [call(): pl.pallas_call(kernel, out_shape=outs, in_specs=in_specs, out_specs=[VMEM...]
    ppermute x6, waiting for transfers between devices: 28.2 us -> 27.5 us  [send(): return lax.ppermute(value, AXES, pairs)]
    ppermute x6, starting transfers between devices: 7.33 us -> 8.06 us  [send(): return lax.ppermute(value, AXES, pairs)]
  transfers between devices with their start and end apart: 6 -> 6, of which waited for: 3 -> 3; matrix products, arithmetic and copies ran while one was open for 5% -> 0% of each run, Pallas kernels for 22% -> 26%
where the time goes in v6:
time: 58.1 us; the launch traced here: 57.8 us
  waiting for transfers between devices  27.5 us (47%)
  Pallas kernels  20.2 us (35%)
  starting transfers between devices  8.06 us (14%)
  between operations  1.99 us (3%)
    ppermute x6, waiting for transfers between devices, send(): return lax.ppermute(value, AXES, pairs)  27.5 us
    pallas_call x7, Pallas kernels, call(): pl.pallas_call(kernel, out_shape=outs, in_specs=in_specs, out_specs=[VMEM...  20.2 us
    ppermute x6, starting transfers between devices, send(): return lax.ppermute(value, AXES, pairs)  8.06 us
  transfers between devices with their start and end apart: 6, of which 3 were waited for; matrix products, arithmetic and copies ran while one was open for 0% of the time, Pallas kernels for 26%

profile of v6, /device:TPU:1, one launch (start us, length us, event | category | flops | bytes accessed | tf_op | source)
XLA Modules:
  0.0 57.8 jit_solution(4205213824397304301)
XLA Ops:
  0.6 1.5 %sort.1 = (bf16[384,1152]{1,0:T(8,128)(2,1)S(1)}, bf16[384,1152]{1,0:T(8,128)(2,1)S(1)}) custom-call(bf16[384,1152]{1,0:T(8,128)(2,1)} %image.7, bf16[384,1152]{1,0:T(8,128)(2,1)} %text.7), custom_call_target="tpu_custom_call" | custom-call | flops 1 | bytes 1 | tf_op jit(solution)/shard_map/sort/pallas_call | solution.py:184
  2.1 0.1 collective-permute-start
  2.2 2.7 %collective-permute-start.2 = (bf16[384,1152]{1,0:T(8,128)(2,1)S(1)}, bf16[384,1152]{1,0:T(8,128)(2,1)S(1)}, u32[]{:S(2)}, u32[]{:S(2)}) collective-permute-start(bf16[384,1152]{1,0:T(8,128)(2,1)S(1)} %get-tuple-element.23.when_inner), channel_id=1, source_target_pairs={{0,30},{1,31},{2,4},{3,5},{4,2},{5,3},{6,8},{7,9},{8,6},{9,7},{10,... | collective-permute-start | bytes 2654216 | tf_op jit(solution)/shard_map/ppermute | solution.py:28
  4.9 0.0 collective-permute-done.when_outer.b1
  4.9 1.0 %pick.2 = bf16[384,1152]{1,0:T(8,128)(2,1)} custom-call(bf16[384,1152]{1,0:T(8,128)(2,1)S(1)} %collective-permute-done.when_outer.b1, bf16[384,1152]{1,0:T(8,128)(2,1)S(1)} %get-tuple-element.23.when_inner), custom_call_target="tpu_custom_call" | custom-call | flops 1 | bytes 1 | tf_op jit(solution)/shard_map/pick/pallas_call | solution.py:184
  5.9 0.0 copy-start
  5.9 0.0 copy-start.1
  5.9 2.1 %collective-permute-start.1 = (bf16[384,1152]{1,0:T(8,128)(2,1)}, bf16[384,1152]{1,0:T(8,128)(2,1)}, u32[]{:S(2)}, u32[]{:S(2)}) collective-permute-start(bf16[384,1152]{1,0:T(8,128)(2,1)} %pick.2), channel_id=1, source_target_pairs={{0,1},{1,0},{2,3},{3,2},{4,5},{5,4},{6,7},{7,6},{8,9},{9,8},{10,11... | collective-permute-start | bytes 2654216 | tf_op jit(solution)/shard_map/ppermute | solution.py:28
  8.0 17.5 %collective-permute-done.2.when_inner.b2 = bf16[384,1152]{1,0:T(8,128)(2,1)S(1)} collective-permute-done((bf16[384,1152]{1,0:T(8,128)(2,1)S(1)}, bf16[384,1152]{1,0:T(8,128)(2,1)S(1)}, u32[]{:S(2)}, u32[]{:S(2)}) %collective-permute-start.2) | collective-permute-done | bytes 884768 | tf_op jit(solution)/shard_map/ppermute | solution.py:28
  25.5 1.0 %pick.3 = bf16[384,1152]{1,0:T(8,128)(2,1)} custom-call(bf16[384,1152]{1,0:T(8,128)(2,1)S(1)} %get-tuple-element.22.when_outer, bf16[384,1152]{1,0:T(8,128)(2,1)S(1)} %collective-permute-done.2.when_inner.b2), custom_call_target="tpu_custom_call" | custom-call | flops 1 | bytes 1 | tf_op jit(solution)/shard_map/pick/pallas_call | solution.py:184
  26.5 1.7 %collective-permute-start.3 = (bf16[384,1152]{1,0:T(8,128)(2,1)}, bf16[384,1152]{1,0:T(8,128)(2,1)}, u32[]{:S(2)}, u32[]{:S(2)}) collective-permute-start(bf16[384,1152]{1,0:T(8,128)(2,1)} %pick.3), channel_id=1, source_target_pairs={{0,1},{1,0},{2,3},{3,2},{4,5},{5,4},{6,7},{7,6},{8,9},{9,8},{10,11... | collective-permute-start | bytes 2654216 | tf_op jit(solution)/shard_map/ppermute | solution.py:28
  29.6 0.0 collective-permute-done.1.b3
  29.6 1.5 %collective-permute-start.5 = (bf16[384,1152]{1,0:T(8,128)(2,1)}, bf16[384,1152]{1,0:T(8,128)(2,1)S(1)}, u32[]{:S(2)}, u32[]{:S(2)}) collective-permute-start(bf16[384,1152]{1,0:T(8,128)(2,1)} %collective-permute-done.1.b3), channel_id=1, source_target_pairs={{0,30},{1,31},{2,4},{3,5},{4,2},{5,3},{6,8},{7,9},{8,6},{9,7},{10,... | collective-permute-start | bytes 2654216 | tf_op jit(solution)/shard_map/ppermute | solution.py:28
  31.1 0.1 iota.7.scalars
  31.1 0.0 copy-done
  31.1 0.0 copy-done.1
  31.1 7.8 %near_blocks.1 = (bf16[384,1152]{1,0:T(8,128)(2,1)S(1)}, bf16[384,1152]{1,0:T(8,128)(2,1)S(1)}, f32[384,1152]{1,0:T(8,128)S(1)}, f32[384,1152]{1,0:T(8,128)S(1)}, f32[384,128]{1,0:T(8,128)S(1)}) custom-call(f32[8,128]{1,0:T(8,128)S(1)} %iota.7.scalars, bf16[384,1152]{1,0:T(8,128)(2,1)S(1)} %copy-done, bf16[384,1152]{1,0:T(8,128)(2,1)S(1)} %copy-done.1, ...), custom_call_target="tpu_custom_call" | custom-call | flops 1 | bytes 1 | tf_op jit(solution)/shard_map/near_blocks/pallas_call | solution.py:184
  38.9 8.2 %collective-permute-done.3.b5 = bf16[384,1152]{1,0:T(8,128)(2,1)} collective-permute-done((bf16[384,1152]{1,0:T(8,128)(2,1)}, bf16[384,1152]{1,0:T(8,128)(2,1)}, u32[]{:S(2)}, u32[]{:S(2)}) %collective-permute-start.3) | collective-permute-done | bytes 884768 | tf_op jit(solution)/shard_map/ppermute | solution.py:28
  47.1 0.0 collective-permute-start.4
  47.1 2.9 %fifth_block.1 = (f32[384,1152]{1,0:T(8,128)S(1)}, f32[384,128]{1,0:T(8,128)S(1)}) custom-call(f32[8,128]{1,0:T(8,128)S(1)} %iota.7.scalars, bf16[384,1152]{1,0:T(8,128)(2,1)} %collective-permute-done.3.b5, bf16[384,1152]{1,0:T(8,128)(2,1)S(1)} %get-tuple-element.31.z_u, f32[384,1152]{1,0:T(8,128)S(1)} %get-tuple-element.32.grad_in, ...), custom_call_target="tpu_custom_call" | custom-call | flops 1 | bytes 1 | tf_op jit(solution)/shard_map/fifth_block/pallas_call | solution.py:184
  50.1 1.7 %collective-permute-done.5.b4 = bf16[384,1152]{1,0:T(8,128)(2,1)S(1)} collective-permute-done((bf16[384,1152]{1,0:T(8,128)(2,1)}, bf16[384,1152]{1,0:T(8,128)(2,1)S(1)}, u32[]{:S(2)}, u32[]{:S(2)}) %collective-permute-start.5) | collective-permute-done | bytes 884768 | tf_op jit(solution)/shard_map/ppermute | solution.py:28
  51.8 2.3 %finish_u.1 = (bf16[384,1152]{1,0:T(8,128)(2,1)S(1)}, f32[384,128]{1,0:T(8,128)S(1)}) custom-call(f32[8,128]{1,0:T(8,128)S(1)} %iota.7.scalars, bf16[384,1152]{1,0:T(8,128)(2,1)S(1)} %collective-permute-done.5.b4, bf16[384,1152]{1,0:T(8,128)(2,1)S(1)} %get-tuple-element.31.z_u, f32[384,1152]{1,0:T(8,128)S(1)} %get-tuple-element.34.grad_u, ...), custom_call_target="tpu_custom_call" | custom-call | flops 1 | bytes 1 | tf_op jit(solution)/shard_map/finish_u/pallas_call | solution.py:184
  54.1 0.0 collective-permute-done.4.b6
  54.1 3.7 %finish_w.1 = (bf16[384,1152]{1,0:T(8,128)(2,1)}, bf16[384,1152]{1,0:T(8,128)(2,1)}, f32[384]{0:T(512)}) custom-call(f32[8,128]{1,0:T(8,128)S(1)} %iota.7.scalars, bf16[384,1152]{1,0:T(8,128)(2,1)S(1)} %collective-permute-done.4.b6, bf16[384,1152]{1,0:T(8,128)(2,1)S(1)} %get-tuple-element.29.z_w, f32[384,1152]{1,0:T(8,128)S(1)} %get-tuple-element.30.grad_w, ...), custom_call_target="tpu_custom_call" | custom-call | flops 1 | bytes 1 | tf_op jit(solution)/shard_map/finish_w/pallas_call | solution.py:184
  (1 shorter events, 0.0 us)
Async XLA Ops:
  2.1 2.8 %collective-permute-start = (bf16[384,1152]{1,0:T(8,128)(2,1)S(1)}, bf16[384,1152]{1,0:T(8,128)(2,1)S(1)}, u32[]{:S(2)}, u32[]{:S(2)}) collective-permute-start(bf16[384,1152]{1,0:T(8,128)(2,1)S(1)} %get-tuple-element.22.when_outer), channel_id=1, source_target_pairs={{0,2},{1,3},{2,0},{3,1},{4,6},{5,7},{6,4},{7,5},{8,10},{9,11},{10,... | collective-permute-start | bytes 2654216 | tf_op jit(solution)/shard_map/ppermute | solution.py:28
  2.2 23.3 %collective-permute-start.2 = (bf16[384,1152]{1,0:T(8,128)(2,1)S(1)}, bf16[384,1152]{1,0:T(8,128)(2,1)S(1)}, u32[]{:S(2)}, u32[]{:S(2)}) collective-permute-start(bf16[384,1152]{1,0:T(8,128)(2,1)S(1)} %get-tuple-element.23.when_inner), channel_id=1, source_target_pairs={{0,30},{1,31},{2,4},{3,5},{4,2},{5,3},{6,8},{7,9},{8,6},{9,7},{10,... | collective-permute-start | bytes 2654216 | tf_op jit(solution)/shard_map/ppermute | solution.py:28
  5.9 25.2 %copy-start = (bf16[384,1152]{1,0:T(8,128)(2,1)S(1)}, bf16[384,1152]{1,0:T(8,128)(2,1)}, u32[]{:S(2)}) copy-start(bf16[384,1152]{1,0:T(8,128)(2,1)} %image.7) | copy-start | bytes 2654212
  5.9 25.2 %copy-start.1 = (bf16[384,1152]{1,0:T(8,128)(2,1)S(1)}, bf16[384,1152]{1,0:T(8,128)(2,1)}, u32[]{:S(2)}) copy-start(bf16[384,1152]{1,0:T(8,128)(2,1)} %text.7) | copy-start | bytes 2654212
  5.9 23.7 %collective-permute-start.1 = (bf16[384,1152]{1,0:T(8,128)(2,1)}, bf16[384,1152]{1,0:T(8,128)(2,1)}, u32[]{:S(2)}, u32[]{:S(2)}) collective-permute-start(bf16[384,1152]{1,0:T(8,128)(2,1)} %pick.2), channel_id=1, source_target_pairs={{0,1},{1,0},{2,3},{3,2},{4,5},{5,4},{6,7},{7,6},{8,9},{9,8},{10,11... | collective-permute-start | bytes 2654216 | tf_op jit(solution)/shard_map/ppermute | solution.py:28
  26.5 20.6 %collective-permute-start.3 = (bf16[384,1152]{1,0:T(8,128)(2,1)}, bf16[384,1152]{1,0:T(8,128)(2,1)}, u32[]{:S(2)}, u32[]{:S(2)}) collective-permute-start(bf16[384,1152]{1,0:T(8,128)(2,1)} %pick.3), channel_id=1, source_target_pairs={{0,1},{1,0},{2,3},{3,2},{4,5},{5,4},{6,7},{7,6},{8,9},{9,8},{10,11... | collective-permute-start | bytes 2654216 | tf_op jit(solution)/shard_map/ppermute | solution.py:28
  29.6 22.2 %collective-permute-start.5 = (bf16[384,1152]{1,0:T(8,128)(2,1)}, bf16[384,1152]{1,0:T(8,128)(2,1)S(1)}, u32[]{:S(2)}, u32[]{:S(2)}) collective-permute-start(bf16[384,1152]{1,0:T(8,128)(2,1)} %collective-permute-done.1.b3), channel_id=1, source_target_pairs={{0,30},{1,31},{2,4},{3,5},{4,2},{5,3},{6,8},{7,9},{8,6},{9,7},{10,... | collective-permute-start | bytes 2654216 | tf_op jit(solution)/shard_map/ppermute | solution.py:28
  47.1 7.0 %collective-permute-start.4 = (bf16[384,1152]{1,0:T(8,128)(2,1)}, bf16[384,1152]{1,0:T(8,128)(2,1)S(1)}, u32[]{:S(2)}, u32[]{:S(2)}) collective-permute-start(bf16[384,1152]{1,0:T(8,128)(2,1)} %collective-permute-done.3.b5), channel_id=1, source_target_pairs={{0,2},{1,3},{2,0},{3,1},{4,6},{5,7},{6,4},{7,5},{8,10},{9,11},{10,... | collective-permute-start | bytes 2654216 | tf_op jit(solution)/shard_map/ppermute | solution.py:28

commit v7 on v6

--- a/solution.py
+++ b/solution.py
@@ -30,8 +30,8 @@
 
 def unit_rows(raw):
     values = raw.astype(F32)
-    length = jnp.sqrt(jnp.sum(values * values, axis=1, keepdims=True) + 1e-06)
-    return values * (1.0 / length), length
+    inverse = 1.0 / jnp.sqrt(jnp.sum(values * values, axis=1, keepdims=True) + 1e-06)
+    return values * inverse, inverse
 
 
 def sigmoid_of(p):
@@ -74,15 +74,22 @@
     rows = own.shape[0]
     for place, raw in enumerate(blocks):
         work[place * rows : (place + 1) * rows] = unit_rows(raw)[0].astype(BF16)
-    others = work[: len(blocks) * rows]
+    return terms(own, work[: len(blocks) * rows], scale, shift)
+
+
+def terms(own, others, scale, shift):
     p = jnp.exp(scale * dot_nt(own, others) + shift)
     coef = (sigmoid_of(p) * scale).astype(BF16)
     return dot_nn(coef, others), softplus_lanes(p)
 
 
-def project(raw, grad):
-    unit, length = unit_rows(raw)
-    return ((grad - unit * jnp.sum(unit * grad, axis=1, keepdims=True)) / length).astype(BF16)
+def project(unit, inverse, grad):
+    return ((grad - unit * jnp.sum(unit * grad, axis=1, keepdims=True)) * inverse).astype(BF16)
+
+
+def row_parts(rows):
+    count = 3 if rows % 48 == 0 else 1
+    return [pl.ds(place * (rows // count), rows // count) for place in range(count)]
 
 
 def scalar_pair(scalars):
@@ -119,16 +126,31 @@
         move(w, u)
 
 
-def pick_kernel(when_outer, when_inner, picked):
-    picked[...] = jnp.where(is_outer(), when_outer[...], when_inner[...])
-
-
-def near_kernel(scalars, image, text, b1, b2, b3, z_u, z_w, grad_u, grad_w, loss, work):
+def pick_kernel(when_outer, when_inner, picked, sem):
+    @pl.when(is_outer())
+    def _():
+        pltpu.async_copy(when_outer, picked, sem).wait()
+
+    @pl.when(jnp.logical_not(is_outer()))
+    def _():
+        pltpu.async_copy(when_inner, picked, sem).wait()
+
+
+def near_kernel(
+    scalars, image, text, b1, b2, b3,
+    z_u, z_w, unit_u, unit_w, inverse_u, inverse_w, grad_u, grad_w, loss, work,
+):
     u_is_image = image_is_u()
     u_weight = u_is_image.astype(F32)
     scale, shift = scalar_pair(scalars)
-    zi = unit_rows(image[...])[0].astype(BF16)
-    zt = unit_rows(text[...])[0].astype(BF16)
+    image_unit, image_inverse = unit_rows(image[...])
+    text_unit, text_inverse = unit_rows(text[...])
+    unit_u[...] = jnp.where(u_is_image, image_unit, text_unit)
+    unit_w[...] = jnp.where(u_is_image, text_unit, image_unit)
+    inverse_u[...] = jnp.where(u_is_image, image_inverse, text_inverse)
+    inverse_w[...] = jnp.where(u_is_image, text_inverse, image_inverse)
+    zi = image_unit.astype(BF16)
+    zt = text_unit.astype(BF16)
     z_u[...] = jnp.where(u_is_image, zi, zt)
     z_w[...] = jnp.where(u_is_image, zt, zi)
     scores = scale * dot_nt(zi, zt) + shift
@@ -150,42 +172,67 @@
     loss[...] = total + (1.0 - u_weight) * row_loss
 
 
-def fifth_kernel(scalars, b5, z_u, grad_in, loss_in, grad_u, loss, work):
-    term, row_loss = pair_step(z_u[...], (b5[...],), *scalar_pair(scalars), work)
+def fifth_kernel(scalars, b5, z_u, grad_in, loss_in, grad_u, loss, raw, work, sems):
+    copies = []
+    for place, part in enumerate(row_parts(raw.shape[0])):
+        copy = pltpu.make_async_copy(b5.at[part], raw.at[part], sems.at[place])
+        copy.start()
+        copies.append((copy, part))
+    for copy, part in copies:
+        copy.wait()
+        work[part] = unit_rows(raw[part])[0].astype(BF16)
+    term, row_loss = terms(z_u[...], work[...], *scalar_pair(scalars))
     grad_u[...] = grad_in[...] + term
     loss[...] = loss_in[...] + image_is_u().astype(F32) * row_loss
 
 
-def u_kernel(scalars, b4, z_u, grad_u, loss_in, image, text, done_u, loss, work):
-    raw = jnp.where(image_is_u(), image[...], text[...])
+def u_kernel(scalars, b4, z_u, grad_u, loss_in, unit, inverse, done_u, loss, work):
     term, row_loss = pair_step(z_u[...], (b4[...],), *scalar_pair(scalars), work)
     loss[...] = loss_in[...] + image_is_u().astype(F32) * row_loss
-    done_u[...] = project(raw, grad_u[...] + term)
+    done_u[...] = project(unit[...], inverse[...], grad_u[...] + term)
 
 
 def w_kernel(
-    scalars, b6, z_w, grad_w, loss_in, image, text, done_u, image_grad, text_grad, loss_rows, work
+    scalars, b6, z_w, grad_w, loss_in, unit, inverse, done_u,
+    image_grad, text_grad, loss_rows, done_w, work, sems,
 ):
     u_is_image = image_is_u()
-    raw = jnp.where(u_is_image, text[...], image[...])
+    parts = row_parts(done_w.shape[0])
+
+    def output(action, source, part, to_image, sem):
+        @pl.when(to_image)
+        def _():
+            action(pltpu.make_async_copy(source.at[part], image_grad.at[part], sem))
+
+        @pl.when(jnp.logical_not(to_image))
+        def _():
+            action(pltpu.make_async_copy(source.at[part], text_grad.at[part], sem))
+
+    whole = pl.ds(0, done_w.shape[0])
+    output(lambda copy: copy.start(), done_u, whole, u_is_image, sems.at[0])
     term, row_loss = pair_step(z_w[...], (b6[...],), *scalar_pair(scalars), work)
-    total = loss_in[...] + (1.0 - image_is_u().astype(F32)) * row_loss
+    for place, part in enumerate(parts):
+        start = place * (done_w.shape[0] // len(parts))
+        rows = slice(start, start + done_w.shape[0] // len(parts))
+        done_w[part] = project(unit[part], inverse[part], grad_w[part] + term[rows])
+        output(lambda copy: copy.start(), done_w, part, jnp.logical_not(u_is_image), sems.at[1 + place])
+    total = loss_in[...] + (1.0 - u_is_image.astype(F32)) * row_loss
     loss_rows[...] = jnp.sum(jnp.transpose(total), axis=0) / (SPAN * total.shape[0])
-    done_w = project(raw, grad_w[...] + term)
-    image_grad[...] = jnp.where(u_is_image, done_u[...], done_w)
-    text_grad[...] = jnp.where(u_is_image, done_w, done_u[...])
+    output(lambda copy: copy.wait(), done_u, whole, u_is_image, sems.at[0])
+    for place, part in enumerate(parts):
+        output(lambda copy: copy.wait(), done_w, part, jnp.logical_not(u_is_image), sems.at[1 + place])
 
 
 VMEM = pl.BlockSpec(memory_space=pltpu.VMEM)
 ANY = pl.BlockSpec(memory_space=pl.ANY)
 
 
-def call(kernel, in_specs, args, outs, name, scratch=()):
+def call(kernel, in_specs, args, out_specs, outs, name, scratch=()):
     return pl.pallas_call(
         kernel,
         out_shape=outs,
         in_specs=in_specs,
-        out_specs=[VMEM] * len(outs),
+        out_specs=out_specs,
         scratch_shapes=list(scratch),
         name=name,
         cost_estimate=pl.CostEstimate(flops=1, bytes_accessed=1, transcendentals=0),
@@ -197,22 +244,30 @@
     rows, width = image.shape
     block = jax.ShapeDtypeStruct((rows, width), BF16)
     sums = jax.ShapeDtypeStruct((rows, width), F32)
+    column = jax.ShapeDtypeStruct((rows, 1), F32)
     partial = jax.ShapeDtypeStruct((rows, 128), F32)
     line = jax.ShapeDtypeStruct((rows,), F32)
+    raw = pltpu.VMEM((rows, width), BF16)
+    copies = pltpu.SemaphoreType.DMA((4,))
+
     def pick(when_outer, when_inner):
-        return call(pick_kernel, [VMEM] * 2, (when_outer, when_inner), (block,), "pick")[0]
-
-    def compute(kernel, args, outs, name, places):
-        work = pltpu.VMEM((places * rows, width), BF16)
-        return call(kernel, [VMEM] * (1 + len(args)), (scalars, *args), outs, name, (work,))
+        sem = pltpu.SemaphoreType.DMA
+        return call(
+            pick_kernel, [ANY] * 2, (when_outer, when_inner), [ANY], (block,), "pick", (sem,)
+        )[0]
+
+    def compute(kernel, args, outs, name, scratch):
+        in_specs = [VMEM] * (1 + len(args))
+        return call(kernel, in_specs, (scalars, *args), [VMEM] * len(outs), outs, name, scratch)
 
     u, w = call(
         sort_kernel,
         [ANY] * 2,
         [pltpu.with_memory_space_constraint(x, pltpu.HBM) for x in (image, text)],
+        [VMEM] * 2,
         (block, block),
         "sort",
-        (pltpu.SemaphoreType.DMA((2,)),),
+        (copies,),
     )
     slot1 = send(w, CORE_SWAP)
     slot2 = send(u, GROUP_SHIFT)
@@ -222,21 +277,39 @@
     slot3, score_scaling, score_shift = lax.optimization_barrier((slot3, score_scaling, score_shift))
     first = lax.broadcasted_iota(jnp.int32, (8, 128), 0) == 0
     scalars = jnp.where(first, score_scaling, score_shift)
-    z_u, z_w, grad_u, grad_w, loss = compute(
+    z_u, z_w, unit_u, unit_w, inverse_u, inverse_w, grad_u, grad_w, loss = compute(
         near_kernel,
         (image, text, slot1, slot2, slot3),
-        (block, block, sums, sums, partial),
+        (block, block, sums, sums, column, column, sums, sums, partial),
         "near_blocks",
-        2,
+        (pltpu.VMEM((2 * rows, width), BF16),),
     )
     slot5, loss = lax.optimization_barrier((slot5, loss))
     slot6 = send(slot5, CORE_SWAP)
-    grad_u, loss = compute(fifth_kernel, (slot5, z_u, grad_u, loss), (sums, partial), "fifth_block", 1)
+    grad_u, loss = call(
+        fifth_kernel,
+        [VMEM, ANY, VMEM, VMEM, VMEM],
+        (scalars, slot5, z_u, grad_u, loss),
+        [VMEM] * 2,
+        (sums, partial),
+        "fifth_block",
+        (raw, raw, copies),
+    )
     done_u, loss = compute(
-        u_kernel, (slot4, z_u, grad_u, loss, image, text), (block, partial), "finish_u", 1
-    )
-    image_grad, text_grad, loss_rows = compute(
-        w_kernel, (slot6, z_w, grad_w, loss, image, text, done_u), (block, block, line), "finish_w", 1
+        u_kernel,
+        (slot4, z_u, grad_u, loss, unit_u, inverse_u),
+        (block, partial),
+        "finish_u",
+        (raw,),
+    )
+    image_grad, text_grad, loss_rows = call(
+        w_kernel,
+        [VMEM] * 8,
+        (scalars, slot6, z_w, grad_w, loss, unit_w, inverse_w, done_u),
+        [ANY, ANY, VMEM],
+        (block, block, line),
+        "finish_w",
+        (raw, raw, copies),
     )
     return loss_rows, image_grad, text_grad
 

time: 58.1 us -> 57.6 us (level)
  no operation moved by 1% of the time
where the time goes in v7:
time: 57.6 us; the launch traced here: 57.4 us
  waiting for transfers between devices  27.3 us (47%)
  Pallas kernels  19.8 us (34%)
  starting transfers between devices  8.21 us (14%)
  between operations  2.02 us (4%)
    ppermute x6, waiting for transfers between devices, send(): return lax.ppermute(value, AXES, pairs)  27.3 us
    pallas_call x7, Pallas kernels, call(): pl.pallas_call(kernel, out_shape=outs, in_specs=in_specs, out_specs=out_s...  19.8 us
    ppermute x6, starting transfers between devices, send(): return lax.ppermute(value, AXES, pairs)  8.21 us
  transfers between devices with their start and end apart: 6, of which 3 were waited for; matrix products, arithmetic and copies ran while one was open for 0% of the time, Pallas kernels for 26%

profile of v7, /device:TPU:1, one launch (start us, length us, event | category | flops | bytes accessed | tf_op | source)
XLA Modules:
  0.0 57.4 jit_solution(11784946119819785312)
XLA Ops:
  0.6 1.5 %sort.1 = (bf16[384,1152]{1,0:T(8,128)(2,1)S(1)}, bf16[384,1152]{1,0:T(8,128)(2,1)S(1)}) custom-call(bf16[384,1152]{1,0:T(8,128)(2,1)} %image.3, bf16[384,1152]{1,0:T(8,128)(2,1)} %text.3), custom_call_target="tpu_custom_call" | custom-call | flops 1 | bytes 1 | tf_op jit(solution)/shard_map/sort/pallas_call | solution.py:231
  2.1 0.1 collective-permute-start
  2.2 2.7 %collective-permute-start.2 = (bf16[384,1152]{1,0:T(8,128)(2,1)S(1)}, bf16[384,1152]{1,0:T(8,128)(2,1)S(1)}, u32[]{:S(2)}, u32[]{:S(2)}) collective-permute-start(bf16[384,1152]{1,0:T(8,128)(2,1)S(1)} %get-tuple-element.27.when_inner), channel_id=1, source_target_pairs={{0,30},{1,31},{2,4},{3,5},{4,2},{5,3},{6,8},{7,9},{8,6},{9,7},{10,... | collective-permute-start | bytes 2654216 | tf_op jit(solution)/shard_map/ppermute | solution.py:28
  4.9 0.0 collective-permute-done.when_outer.b1
  4.9 0.9 %pick.2 = bf16[384,1152]{1,0:T(8,128)(2,1)} custom-call(bf16[384,1152]{1,0:T(8,128)(2,1)S(1)} %collective-permute-done.when_outer.b1, bf16[384,1152]{1,0:T(8,128)(2,1)S(1)} %get-tuple-element.27.when_inner), custom_call_target="tpu_custom_call" | custom-call | flops 1 | bytes 1 | tf_op jit(solution)/shard_map/pick/pallas_call | solution.py:231
  5.8 0.0 copy-start
  5.8 0.0 copy-start.1
  5.8 2.1 %collective-permute-start.1 = (bf16[384,1152]{1,0:T(8,128)(2,1)}, bf16[384,1152]{1,0:T(8,128)(2,1)}, u32[]{:S(2)}, u32[]{:S(2)}) collective-permute-start(bf16[384,1152]{1,0:T(8,128)(2,1)} %pick.2), channel_id=1, source_target_pairs={{0,1},{1,0},{2,3},{3,2},{4,5},{5,4},{6,7},{7,6},{8,9},{9,8},{10,11... | collective-permute-start | bytes 2654216 | tf_op jit(solution)/shard_map/ppermute | solution.py:28
  8.0 17.5 %collective-permute-done.2.when_inner.b2 = bf16[384,1152]{1,0:T(8,128)(2,1)S(1)} collective-permute-done((bf16[384,1152]{1,0:T(8,128)(2,1)S(1)}, bf16[384,1152]{1,0:T(8,128)(2,1)S(1)}, u32[]{:S(2)}, u32[]{:S(2)}) %collective-permute-start.2) | collective-permute-done | bytes 884768 | tf_op jit(solution)/shard_map/ppermute | solution.py:28
  25.5 0.9 %pick.3 = bf16[384,1152]{1,0:T(8,128)(2,1)} custom-call(bf16[384,1152]{1,0:T(8,128)(2,1)S(1)} %get-tuple-element.26.when_outer, bf16[384,1152]{1,0:T(8,128)(2,1)S(1)} %collective-permute-done.2.when_inner.b2), custom_call_target="tpu_custom_call" | custom-call | flops 1 | bytes 1 | tf_op jit(solution)/shard_map/pick/pallas_call | solution.py:231
  26.4 1.8 %collective-permute-start.3 = (bf16[384,1152]{1,0:T(8,128)(2,1)}, bf16[384,1152]{1,0:T(8,128)(2,1)}, u32[]{:S(2)}, u32[]{:S(2)}) collective-permute-start(bf16[384,1152]{1,0:T(8,128)(2,1)} %pick.3), channel_id=1, source_target_pairs={{0,1},{1,0},{2,3},{3,2},{4,5},{5,4},{6,7},{7,6},{8,9},{9,8},{10,11... | collective-permute-start | bytes 2654216 | tf_op jit(solution)/shard_map/ppermute | solution.py:28
  29.6 0.0 collective-permute-done.1.b3
  29.6 1.5 %collective-permute-start.5 = (bf16[384,1152]{1,0:T(8,128)(2,1)}, bf16[384,1152]{1,0:T(8,128)(2,1)S(1)}, u32[]{:S(2)}, u32[]{:S(2)}) collective-permute-start(bf16[384,1152]{1,0:T(8,128)(2,1)} %collective-permute-done.1.b3), channel_id=1, source_target_pairs={{0,30},{1,31},{2,4},{3,5},{4,2},{5,3},{6,8},{7,9},{8,6},{9,7},{10,... | collective-permute-start | bytes 2654216 | tf_op jit(solution)/shard_map/ppermute | solution.py:28
  31.1 0.1 iota.7.scalars
  31.1 0.0 copy-done
  31.1 0.0 copy-done.1
  31.1 8.0 %near_blocks.1 = (bf16[384,1152]{1,0:T(8,128)(2,1)S(1)}, bf16[384,1152]{1,0:T(8,128)(2,1)S(1)}, f32[384,1152]{1,0:T(8,128)S(1)}, f32[384,1152]{1,0:T(8,128)S(1)}...) custom-call(f32[8,128]{1,0:T(8,128)S(1)} %iota.7.scalars, ...), custom_call_target="tpu_custom_call" | custom-call | flops 1 | bytes 1 | tf_op jit(solution)/shard_map/near_blocks/pallas_call | solution.py:231
  39.1 8.0 %collective-permute-done.3.b5 = bf16[384,1152]{1,0:T(8,128)(2,1)} collective-permute-done((bf16[384,1152]{1,0:T(8,128)(2,1)}, bf16[384,1152]{1,0:T(8,128)(2,1)}, u32[]{:S(2)}, u32[]{:S(2)}) %collective-permute-start.3) | collective-permute-done | bytes 884768 | tf_op jit(solution)/shard_map/ppermute | solution.py:28
  47.2 0.0 collective-permute-start.4
  47.2 2.9 %fifth_block.1 = (f32[384,1152]{1,0:T(8,128)S(1)}, f32[384,128]{1,0:T(8,128)S(1)}) custom-call(f32[8,128]{1,0:T(8,128)S(1)} %iota.7.scalars, bf16[384,1152]{1,0:T(8,128)(2,1)} %collective-permute-done.3.b5, bf16[384,1152]{1,0:T(8,128)(2,1)S(1)} %get-tuple-element.35.z_u, f32[384,1152]{1,0:T(8,128)S(1)} %get-tuple-element.36.grad_in, ...), custom_call_target="tpu_custom_call" | custom-call | flops 1 | bytes 1 | tf_op jit(solution)/shard_map/fifth_block/pallas_call | solution.py:231
  50.0 1.7 %collective-permute-done.5.b4 = bf16[384,1152]{1,0:T(8,128)(2,1)S(1)} collective-permute-done((bf16[384,1152]{1,0:T(8,128)(2,1)}, bf16[384,1152]{1,0:T(8,128)(2,1)S(1)}, u32[]{:S(2)}, u32[]{:S(2)}) %collective-permute-start.5) | collective-permute-done | bytes 884768 | tf_op jit(solution)/shard_map/ppermute | solution.py:28
  51.8 2.2 %finish_u.1 = (bf16[384,1152]{1,0:T(8,128)(2,1)S(1)}, f32[384,128]{1,0:T(8,128)S(1)}) custom-call(f32[8,128]{1,0:T(8,128)S(1)} %iota.7.scalars, bf16[384,1152]{1,0:T(8,128)(2,1)S(1)} %collective-permute-done.5.b4, bf16[384,1152]{1,0:T(8,128)(2,1)S(1)} %get-tuple-element.35.z_u, f32[384,1152]{1,0:T(8,128)S(1)} %get-tuple-element.38.grad_u, ...), custom_call_target="tpu_custom_call" | custom-call | flops 1 | bytes 1 | tf_op jit(solution)/shard_map/finish_u/pallas_call | solution.py:231
  54.0 0.0 collective-permute-done.4.b6
  54.0 3.4 %finish_w.1 = (bf16[384,1152]{1,0:T(8,128)(2,1)}, bf16[384,1152]{1,0:T(8,128)(2,1)}, f32[384]{0:T(512)}) custom-call(f32[8,128]{1,0:T(8,128)S(1)} %iota.7.scalars, bf16[384,1152]{1,0:T(8,128)(2,1)S(1)} %collective-permute-done.4.b6, bf16[384,1152]{1,0:T(8,128)(2,1)S(1)} %get-tuple-element.33.z_w, f32[384,1152]{1,0:T(8,128)S(1)} %get-tuple-element.34.grad_w, ...), custom_call_target="tpu_custom_call" | custom-call | flops 1 | bytes 1 | tf_op jit(solution)/shard_map/finish_w/pallas_call | solution.py:231
  (1 shorter events, 0.0 us)
Async XLA Ops:
  2.1 2.8 %collective-permute-start = (bf16[384,1152]{1,0:T(8,128)(2,1)S(1)}, bf16[384,1152]{1,0:T(8,128)(2,1)S(1)}, u32[]{:S(2)}, u32[]{:S(2)}) collective-permute-start(bf16[384,1152]{1,0:T(8,128)(2,1)S(1)} %get-tuple-element.26.when_outer), channel_id=1, source_target_pairs={{0,2},{1,3},{2,0},{3,1},{4,6},{5,7},{6,4},{7,5},{8,10},{9,11},{10,... | collective-permute-start | bytes 2654216 | tf_op jit(solution)/shard_map/ppermute | solution.py:28
  2.2 23.3 %collective-permute-start.2 = (bf16[384,1152]{1,0:T(8,128)(2,1)S(1)}, bf16[384,1152]{1,0:T(8,128)(2,1)S(1)}, u32[]{:S(2)}, u32[]{:S(2)}) collective-permute-start(bf16[384,1152]{1,0:T(8,128)(2,1)S(1)} %get-tuple-element.27.when_inner), channel_id=1, source_target_pairs={{0,30},{1,31},{2,4},{3,5},{4,2},{5,3},{6,8},{7,9},{8,6},{9,7},{10,... | collective-permute-start | bytes 2654216 | tf_op jit(solution)/shard_map/ppermute | solution.py:28
  5.8 25.3 %copy-start = (bf16[384,1152]{1,0:T(8,128)(2,1)S(1)}, bf16[384,1152]{1,0:T(8,128)(2,1)}, u32[]{:S(2)}) copy-start(bf16[384,1152]{1,0:T(8,128)(2,1)} %image.3) | copy-start | bytes 2654212
  5.8 25.3 %copy-start.1 = (bf16[384,1152]{1,0:T(8,128)(2,1)S(1)}, bf16[384,1152]{1,0:T(8,128)(2,1)}, u32[]{:S(2)}) copy-start(bf16[384,1152]{1,0:T(8,128)(2,1)} %text.3) | copy-start | bytes 2654212
  5.8 23.7 %collective-permute-start.1 = (bf16[384,1152]{1,0:T(8,128)(2,1)}, bf16[384,1152]{1,0:T(8,128)(2,1)}, u32[]{:S(2)}, u32[]{:S(2)}) collective-permute-start(bf16[384,1152]{1,0:T(8,128)(2,1)} %pick.2), channel_id=1, source_target_pairs={{0,1},{1,0},{2,3},{3,2},{4,5},{5,4},{6,7},{7,6},{8,9},{9,8},{10,11... | collective-permute-start | bytes 2654216 | tf_op jit(solution)/shard_map/ppermute | solution.py:28
  26.4 20.7 %collective-permute-start.3 = (bf16[384,1152]{1,0:T(8,128)(2,1)}, bf16[384,1152]{1,0:T(8,128)(2,1)}, u32[]{:S(2)}, u32[]{:S(2)}) collective-permute-start(bf16[384,1152]{1,0:T(8,128)(2,1)} %pick.3), channel_id=1, source_target_pairs={{0,1},{1,0},{2,3},{3,2},{4,5},{5,4},{6,7},{7,6},{8,9},{9,8},{10,11... | collective-permute-start | bytes 2654216 | tf_op jit(solution)/shard_map/ppermute | solution.py:28
  29.6 22.2 %collective-permute-start.5 = (bf16[384,1152]{1,0:T(8,128)(2,1)}, bf16[384,1152]{1,0:T(8,128)(2,1)S(1)}, u32[]{:S(2)}, u32[]{:S(2)}) collective-permute-start(bf16[384,1152]{1,0:T(8,128)(2,1)} %collective-permute-done.1.b3), channel_id=1, source_target_pairs={{0,30},{1,31},{2,4},{3,5},{4,2},{5,3},{6,8},{7,9},{8,6},{9,7},{10,... | collective-permute-start | bytes 2654216 | tf_op jit(solution)/shard_map/ppermute | solution.py:28
  47.2 6.8 %collective-permute-start.4 = (bf16[384,1152]{1,0:T(8,128)(2,1)}, bf16[384,1152]{1,0:T(8,128)(2,1)S(1)}, u32[]{:S(2)}, u32[]{:S(2)}) collective-permute-start(bf16[384,1152]{1,0:T(8,128)(2,1)} %collective-permute-done.3.b5), channel_id=1, source_target_pairs={{0,2},{1,3},{2,0},{3,1},{4,6},{5,7},{6,4},{7,5},{8,10},{9,11},{10,... | collective-permute-start | bytes 2654216 | tf_op jit(solution)/shard_map/ppermute | solution.py:28

commit v8 on v7

--- a/solution.py
+++ b/solution.py
@@ -138,7 +138,7 @@
 
 def near_kernel(
     scalars, image, text, b1, b2, b3,
-    z_u, z_w, unit_u, unit_w, inverse_u, inverse_w, grad_u, grad_w, loss, work,
+    z_pair, unit_u, unit_w, inverse_u, inverse_w, grad_u, grad_w, loss, work, z_w,
 ):
     u_is_image = image_is_u()
     u_weight = u_is_image.astype(F32)
@@ -151,7 +151,8 @@
     inverse_w[...] = jnp.where(u_is_image, text_inverse, image_inverse)
     zi = image_unit.astype(BF16)
     zt = text_unit.astype(BF16)
-    z_u[...] = jnp.where(u_is_image, zi, zt)
+    z_u = jnp.where(u_is_image, zi, zt)
+    z_pair[: zi.shape[0]] = z_u
     z_w[...] = jnp.where(u_is_image, zt, zi)
     scores = scale * dot_nt(zi, zt) + shift
     rows = lax.broadcasted_iota(jnp.int32, scores.shape, 0)
@@ -164,37 +165,41 @@
     grad_text = dot_tn(coef, zi)
     grad_u[...] = jnp.where(u_is_image, grad_image, grad_text)
     grad_w[...] = jnp.where(u_is_image, grad_text, grad_image)
-    term, row_loss = pair_step(z_u[...], (b2[...],), scale, shift, work)
+    term, row_loss = pair_step(z_u, (b2[...],), scale, shift, work)
     grad_u[...] += term
     total = total + u_weight * row_loss
     term, row_loss = pair_step(z_w[...], (b1[...], b3[...]), scale, shift, work)
+    z_pair[zi.shape[0] :] = work[: zi.shape[0]]
     grad_w[...] += term
     loss[...] = total + (1.0 - u_weight) * row_loss
 
 
-def fifth_kernel(scalars, b5, z_u, grad_in, loss_in, grad_u, loss, raw, work, sems):
+def fifth_kernel(scalars, b5, z_pair, grad_in, loss_in, grad_u, loss, for_partner, raw, work, sems):
     copies = []
-    for place, part in enumerate(row_parts(raw.shape[0])):
+    rows, width = raw.shape
+    for place, part in enumerate(row_parts(rows)):
         copy = pltpu.make_async_copy(b5.at[part], raw.at[part], sems.at[place])
         copy.start()
         copies.append((copy, part))
     for copy, part in copies:
         copy.wait()
         work[part] = unit_rows(raw[part])[0].astype(BF16)
-    term, row_loss = terms(z_u[...], work[...], *scalar_pair(scalars))
-    grad_u[...] = grad_in[...] + term
-    loss[...] = loss_in[...] + image_is_u().astype(F32) * row_loss
-
-
-def u_kernel(scalars, b4, z_u, grad_u, loss_in, unit, inverse, done_u, loss, work):
-    term, row_loss = pair_step(z_u[...], (b4[...],), *scalar_pair(scalars), work)
+    term, row_loss = terms(z_pair[...], work[...], *scalar_pair(scalars))
+    for_partner[:, :width] = term[rows:].astype(BF16)
+    for_partner[:, width:] = row_loss[rows:].astype(BF16)
+    grad_u[...] = grad_in[...] + term[:rows]
+    loss[...] = loss_in[...] + image_is_u().astype(F32) * row_loss[:rows]
+
+
+def u_kernel(scalars, b4, z_pair, grad_u, loss_in, unit, inverse, done_u, loss, work):
+    rows = done_u.shape[0]
+    term, row_loss = pair_step(z_pair[:rows], (b4[...],), *scalar_pair(scalars), work)
     loss[...] = loss_in[...] + image_is_u().astype(F32) * row_loss
     done_u[...] = project(unit[...], inverse[...], grad_u[...] + term)
 
 
 def w_kernel(
-    scalars, b6, z_w, grad_w, loss_in, unit, inverse, done_u,
-    image_grad, text_grad, loss_rows, done_w, work, sems,
+    last, grad_w, loss_in, unit, inverse, done_u, image_grad, text_grad, loss_rows, done_w, sems
 ):
     u_is_image = image_is_u()
     parts = row_parts(done_w.shape[0])
@@ -210,13 +215,12 @@
 
     whole = pl.ds(0, done_w.shape[0])
     output(lambda copy: copy.start(), done_u, whole, u_is_image, sems.at[0])
-    term, row_loss = pair_step(z_w[...], (b6[...],), *scalar_pair(scalars), work)
+    width = done_w.shape[1]
     for place, part in enumerate(parts):
-        start = place * (done_w.shape[0] // len(parts))
-        rows = slice(start, start + done_w.shape[0] // len(parts))
-        done_w[part] = project(unit[part], inverse[part], grad_w[part] + term[rows])
+        grad = grad_w[part] + last[part, :width].astype(F32)
+        done_w[part] = project(unit[part], inverse[part], grad)
         output(lambda copy: copy.start(), done_w, part, jnp.logical_not(u_is_image), sems.at[1 + place])
-    total = loss_in[...] + (1.0 - u_is_image.astype(F32)) * row_loss
+    total = loss_in[...] + (1.0 - u_is_image.astype(F32)) * last[:, width:].astype(F32)
     loss_rows[...] = jnp.sum(jnp.transpose(total), axis=0) / (SPAN * total.shape[0])
     output(lambda copy: copy.wait(), done_u, whole, u_is_image, sems.at[0])
     for place, part in enumerate(parts):
@@ -227,7 +231,7 @@
 ANY = pl.BlockSpec(memory_space=pl.ANY)
 
 
-def call(kernel, in_specs, args, out_specs, outs, name, scratch=()):
+def call(kernel, in_specs, args, out_specs, outs, name, scratch=(), flops=1):
     return pl.pallas_call(
         kernel,
         out_shape=outs,
@@ -235,7 +239,7 @@
         out_specs=out_specs,
         scratch_shapes=list(scratch),
         name=name,
-        cost_estimate=pl.CostEstimate(flops=1, bytes_accessed=1, transcendentals=0),
+        cost_estimate=pl.CostEstimate(flops=flops, bytes_accessed=1, transcendentals=0),
         compiler_params=pltpu.CompilerParams(vmem_limit_bytes=VMEM_LIMIT),
     )(*args)
 
@@ -243,6 +247,7 @@
 def local(image, text, score_scaling, score_shift):
     rows, width = image.shape
     block = jax.ShapeDtypeStruct((rows, width), BF16)
+    pair = jax.ShapeDtypeStruct((2 * rows, width), BF16)
     sums = jax.ShapeDtypeStruct((rows, width), F32)
     column = jax.ShapeDtypeStruct((rows, 1), F32)
     partial = jax.ShapeDtypeStruct((rows, 128), F32)
@@ -256,9 +261,10 @@
             pick_kernel, [ANY] * 2, (when_outer, when_inner), [ANY], (block,), "pick", (sem,)
         )[0]
 
-    def compute(kernel, args, outs, name, scratch):
+    def compute(kernel, args, outs, name, scratch, flops=1):
         in_specs = [VMEM] * (1 + len(args))
-        return call(kernel, in_specs, (scalars, *args), [VMEM] * len(outs), outs, name, scratch)
+        out_specs = [VMEM] * len(outs)
+        return call(kernel, in_specs, (scalars, *args), out_specs, outs, name, scratch, flops)
 
     u, w = call(
         sort_kernel,
@@ -277,39 +283,39 @@
     slot3, score_scaling, score_shift = lax.optimization_barrier((slot3, score_scaling, score_shift))
     first = lax.broadcasted_iota(jnp.int32, (8, 128), 0) == 0
     scalars = jnp.where(first, score_scaling, score_shift)
-    z_u, z_w, unit_u, unit_w, inverse_u, inverse_w, grad_u, grad_w, loss = compute(
+    z_pair, unit_u, unit_w, inverse_u, inverse_w, grad_u, grad_w, loss = compute(
         near_kernel,
         (image, text, slot1, slot2, slot3),
-        (block, block, sums, sums, column, column, sums, sums, partial),
+        (pair, sums, sums, column, column, sums, sums, partial),
         "near_blocks",
-        (pltpu.VMEM((2 * rows, width), BF16),),
-    )
-    slot5, loss = lax.optimization_barrier((slot5, loss))
-    slot6 = send(slot5, CORE_SWAP)
-    grad_u, loss = call(
+        (pltpu.VMEM((2 * rows, width), BF16), raw),
+    )
+    grad_u, loss, for_partner = call(
         fifth_kernel,
         [VMEM, ANY, VMEM, VMEM, VMEM],
-        (scalars, slot5, z_u, grad_u, loss),
-        [VMEM] * 2,
-        (sums, partial),
+        (scalars, slot5, z_pair, grad_u, loss),
+        [VMEM] * 3,
+        (sums, partial, jax.ShapeDtypeStruct((rows, width + 128), BF16)),
         "fifth_block",
         (raw, raw, copies),
     )
+    last = send(for_partner, CORE_SWAP)
     done_u, loss = compute(
         u_kernel,
-        (slot4, z_u, grad_u, loss, unit_u, inverse_u),
+        (slot4, z_pair, grad_u, loss, unit_u, inverse_u),
         (block, partial),
         "finish_u",
         (raw,),
+        10**10,
     )
     image_grad, text_grad, loss_rows = call(
         w_kernel,
-        [VMEM] * 8,
-        (scalars, slot6, z_w, grad_w, loss, unit_w, inverse_w, done_u),
+        [VMEM] * 6,
+        (last, grad_w, loss, unit_w, inverse_w, done_u),
         [ANY, ANY, VMEM],
         (block, block, line),
         "finish_w",
-        (raw, raw, copies),
+        (raw, copies),
     )
     return loss_rows, image_grad, text_grad
 

time: 57.6 us -> 56.6 us (0.983)
  waiting for transfers between devices: 27.3 us -> 25.2 us
    ppermute x6, waiting for transfers between devices: 27.3 us -> 25.2 us  [send(): return lax.ppermute(value, AXES, pairs)]
  transfers between devices with their start and end apart: 6 -> 6, of which waited for: 3 -> 3; matrix products, arithmetic and copies ran while one was open for 0% -> 0% of each run, Pallas kernels for 26% -> 30%
where the time goes in v8:
time: 56.6 us; the launch traced here: 56.1 us
  waiting for transfers between devices  25.2 us (45%)
  Pallas kernels  20.1 us (36%)
  starting transfers between devices  8.66 us (15%)
  between operations  2.02 us (4%)
    ppermute x6, waiting for transfers between devices, send(): return lax.ppermute(value, AXES, pairs)  25.2 us
    pallas_call x7, Pallas kernels, call(): pl.pallas_call(kernel, out_shape=outs, in_specs=in_specs, out_specs=out_s...  20.1 us
    ppermute x6, starting transfers between devices, send(): return lax.ppermute(value, AXES, pairs)  8.66 us
  transfers between devices with their start and end apart: 6, of which 3 were waited for; matrix products, arithmetic and copies ran while one was open for 0% of the time, Pallas kernels for 30%

profile of v8, /device:TPU:1, one launch (start us, length us, event | category | flops | bytes accessed | tf_op | source)
XLA Modules:
  0.0 56.1 jit_solution(16628263323324077839)
XLA Ops:
  0.6 1.5 %sort.1 = (bf16[384,1152]{1,0:T(8,128)(2,1)S(1)}, bf16[384,1152]{1,0:T(8,128)(2,1)S(1)}) custom-call(bf16[384,1152]{1,0:T(8,128)(2,1)} %image.3, bf16[384,1152]{1,0:T(8,128)(2,1)} %text.3), custom_call_target="tpu_custom_call" | custom-call | flops 1 | bytes 1 | tf_op jit(solution)/shard_map/sort/pallas_call | solution.py:235
  2.1 0.1 collective-permute-start
  2.2 2.7 %collective-permute-start.2 = (bf16[384,1152]{1,0:T(8,128)(2,1)S(1)}, bf16[384,1152]{1,0:T(8,128)(2,1)S(1)}, u32[]{:S(2)}, u32[]{:S(2)}) collective-permute-start(bf16[384,1152]{1,0:T(8,128)(2,1)S(1)} %get-tuple-element.25.when_inner), channel_id=1, source_target_pairs={{0,30},{1,31},{2,4},{3,5},{4,2},{5,3},{6,8},{7,9},{8,6},{9,7},{10,... | collective-permute-start | bytes 2654216 | tf_op jit(solution)/shard_map/ppermute | solution.py:28
  4.9 0.0 collective-permute-done.when_outer.b1
  4.9 0.2 pick.2
  5.1 0.0 copy-start
  5.1 0.0 copy-start.1
  5.1 2.1 %collective-permute-start.1 = (bf16[384,1152]{1,0:T(8,128)(2,1)S(1)}, bf16[384,1152]{1,0:T(8,128)(2,1)}, u32[]{:S(2)}, u32[]{:S(2)}) collective-permute-start(bf16[384,1152]{1,0:T(8,128)(2,1)S(1)} %pick.2), channel_id=1, source_target_pairs={{0,1},{1,0},{2,3},{3,2},{4,5},{5,4},{6,7},{7,6},{8,9},{9,8},{10,11... | collective-permute-start | bytes 2654216 | tf_op jit(solution)/shard_map/ppermute | solution.py:28
  7.2 18.3 %collective-permute-done.2.when_inner.b2 = bf16[384,1152]{1,0:T(8,128)(2,1)S(1)} collective-permute-done((bf16[384,1152]{1,0:T(8,128)(2,1)S(1)}, bf16[384,1152]{1,0:T(8,128)(2,1)S(1)}, u32[]{:S(2)}, u32[]{:S(2)}) %collective-permute-start.2) | collective-permute-done | bytes 884768 | tf_op jit(solution)/shard_map/ppermute | solution.py:28
  25.5 0.9 %pick.3 = bf16[384,1152]{1,0:T(8,128)(2,1)} custom-call(bf16[384,1152]{1,0:T(8,128)(2,1)S(1)} %get-tuple-element.24.when_outer, bf16[384,1152]{1,0:T(8,128)(2,1)S(1)} %collective-permute-done.2.when_inner.b2), custom_call_target="tpu_custom_call" | custom-call | flops 1 | bytes 1 | tf_op jit(solution)/shard_map/pick/pallas_call | solution.py:235
  26.4 1.8 %collective-permute-start.3 = (bf16[384,1152]{1,0:T(8,128)(2,1)}, bf16[384,1152]{1,0:T(8,128)(2,1)}, u32[]{:S(2)}, u32[]{:S(2)}) collective-permute-start(bf16[384,1152]{1,0:T(8,128)(2,1)} %pick.3), channel_id=1, source_target_pairs={{0,1},{1,0},{2,3},{3,2},{4,5},{5,4},{6,7},{7,6},{8,9},{9,8},{10,11... | collective-permute-start | bytes 2654216 | tf_op jit(solution)/shard_map/ppermute | solution.py:28
  28.2 0.0 collective-permute-done.1.b3
  28.2 1.9 %collective-permute-start.5 = (bf16[384,1152]{1,0:T(8,128)(2,1)}, bf16[384,1152]{1,0:T(8,128)(2,1)}, u32[]{:S(2)}, u32[]{:S(2)}) collective-permute-start(bf16[384,1152]{1,0:T(8,128)(2,1)} %collective-permute-done.1.b3), channel_id=1, source_target_pairs={{0,30},{1,31},{2,4},{3,5},{4,2},{5,3},{6,8},{7,9},{8,6},{9,7},{10,... | collective-permute-start | bytes 2654216 | tf_op jit(solution)/shard_map/ppermute | solution.py:28
  31.4 0.1 iota.7.scalars
  31.5 0.0 copy-done
  31.5 0.0 copy-done.1
  31.5 8.0 %near_blocks.1 = (bf16[768,1152]{1,0:T(8,128)(2,1)S(1)}, f32[384,1152]{1,0:T(8,128)S(1)}, f32[384,1152]{1,0:T(8,128)S(1)}, f32[384,1]{1,0:T(8,128)S(1)}, f32[384...) custom-call(f32[8,128]{1,0:T(8,128)S(1)} %iota.7.scalars, ...), custom_call_target="tpu_custom_call" | custom-call | flops 1 | bytes 1 | tf_op jit(solution)/shard_map/near_blocks/pallas_call | solution.py:235
  39.5 6.7 %collective-permute-done.3.b5 = bf16[384,1152]{1,0:T(8,128)(2,1)} collective-permute-done((bf16[384,1152]{1,0:T(8,128)(2,1)}, bf16[384,1152]{1,0:T(8,128)(2,1)}, u32[]{:S(2)}, u32[]{:S(2)}) %collective-permute-start.3) | collective-permute-done | bytes 884768 | tf_op jit(solution)/shard_map/ppermute | solution.py:28
  46.2 4.1 %fifth_block.1 = (f32[384,1152]{1,0:T(8,128)S(1)}, f32[384,128]{1,0:T(8,128)S(1)}, bf16[384,1280]{1,0:T(8,128)(2,1)S(1)}) custom-call(f32[8,128]{1,0:T(8,128)S(1)} %iota.7.scalars, bf16[384,1152]{1,0:T(8,128)(2,1)} %collective-permute-done.3.b5, bf16[768,1152]{1,0:T(8,128)(2,1)S(1)} %get-tuple-element.29.z_pair, f32[384,1152]{1,0:T(8,128)S(1)} %get-tuple-element.30.grad_in, ...), custom_call_target="tpu_custom_call" | custom-call | flops 1 | bytes 1 | tf_op jit(solution)/shard_map/fifth_block/pallas_call | solution.py:235
  50.3 0.1 collective-permute-start.4
  50.4 0.3 collective-permute-done.5.b4
  50.6 3.4 %finish_u.1 = (bf16[384,1152]{1,0:T(8,128)(2,1)S(1)}, f32[384,128]{1,0:T(8,128)S(1)}) custom-call(f32[8,128]{1,0:T(8,128)S(1)} %iota.7.scalars, bf16[384,1152]{1,0:T(8,128)(2,1)} %collective-permute-done.5.b4, bf16[768,1152]{1,0:T(8,128)(2,1)S(1)} %get-tuple-element.29.z_pair, f32[384,1152]{1,0:T(8,128)S(1)} %get-tuple-element.34.grad_u, ...), custom_call_target="tpu_custom_call" | custom-call | flops 10000000000 | bytes 1 | tf_op jit(solution)/shard_map/finish_u/pallas_call | solution.py:235
  54.0 0.0 collective-permute-done.4.last
  54.1 2.1 %finish_w.1 = (bf16[384,1152]{1,0:T(8,128)(2,1)}, bf16[384,1152]{1,0:T(8,128)(2,1)}, f32[384]{0:T(512)}) custom-call(bf16[384,1280]{1,0:T(8,128)(2,1)S(1)} %collective-permute-done.4.last, f32[384,1152]{1,0:T(8,128)S(1)} %get-tuple-element.33.grad_w, f32[384,128]{1,0:T(8,128)S(1)} %get-tuple-element.38.loss_in, f32[384,1152]{1,0:T(8,128)S(1)} %get-tuple-element.39.unit, ...), custom_call_target="tpu_custom_call" | custom-call | flops 1 | bytes 1 | tf_op jit(solution)/shard_map/finish_w/pallas_call | solution.py:235
  (1 shorter events, 0.0 us)
Async XLA Ops:
  2.1 2.8 %collective-permute-start = (bf16[384,1152]{1,0:T(8,128)(2,1)S(1)}, bf16[384,1152]{1,0:T(8,128)(2,1)S(1)}, u32[]{:S(2)}, u32[]{:S(2)}) collective-permute-start(bf16[384,1152]{1,0:T(8,128)(2,1)S(1)} %get-tuple-element.24.when_outer), channel_id=1, source_target_pairs={{0,2},{1,3},{2,0},{3,1},{4,6},{5,7},{6,4},{7,5},{8,10},{9,11},{10,... | collective-permute-start | bytes 2654216 | tf_op jit(solution)/shard_map/ppermute | solution.py:28
  2.2 23.3 %collective-permute-start.2 = (bf16[384,1152]{1,0:T(8,128)(2,1)S(1)}, bf16[384,1152]{1,0:T(8,128)(2,1)S(1)}, u32[]{:S(2)}, u32[]{:S(2)}) collective-permute-start(bf16[384,1152]{1,0:T(8,128)(2,1)S(1)} %get-tuple-element.25.when_inner), channel_id=1, source_target_pairs={{0,30},{1,31},{2,4},{3,5},{4,2},{5,3},{6,8},{7,9},{8,6},{9,7},{10,... | collective-permute-start | bytes 2654216 | tf_op jit(solution)/shard_map/ppermute | solution.py:28
  5.1 26.4 %copy-start = (bf16[384,1152]{1,0:T(8,128)(2,1)S(1)}, bf16[384,1152]{1,0:T(8,128)(2,1)}, u32[]{:S(2)}) copy-start(bf16[384,1152]{1,0:T(8,128)(2,1)} %image.3) | copy-start | bytes 2654212
  5.1 26.4 %copy-start.1 = (bf16[384,1152]{1,0:T(8,128)(2,1)S(1)}, bf16[384,1152]{1,0:T(8,128)(2,1)}, u32[]{:S(2)}) copy-start(bf16[384,1152]{1,0:T(8,128)(2,1)} %text.3) | copy-start | bytes 2654212
  5.1 23.1 %collective-permute-start.1 = (bf16[384,1152]{1,0:T(8,128)(2,1)S(1)}, bf16[384,1152]{1,0:T(8,128)(2,1)}, u32[]{:S(2)}, u32[]{:S(2)}) collective-permute-start(bf16[384,1152]{1,0:T(8,128)(2,1)S(1)} %pick.2), channel_id=1, source_target_pairs={{0,1},{1,0},{2,3},{3,2},{4,5},{5,4},{6,7},{7,6},{8,9},{9,8},{10,11... | collective-permute-start | bytes 2654216 | tf_op jit(solution)/shard_map/ppermute | solution.py:28
  26.4 19.8 %collective-permute-start.3 = (bf16[384,1152]{1,0:T(8,128)(2,1)}, bf16[384,1152]{1,0:T(8,128)(2,1)}, u32[]{:S(2)}, u32[]{:S(2)}) collective-permute-start(bf16[384,1152]{1,0:T(8,128)(2,1)} %pick.3), channel_id=1, source_target_pairs={{0,1},{1,0},{2,3},{3,2},{4,5},{5,4},{6,7},{7,6},{8,9},{9,8},{10,11... | collective-permute-start | bytes 2654216 | tf_op jit(solution)/shard_map/ppermute | solution.py:28
  28.2 22.4 %collective-permute-start.5 = (bf16[384,1152]{1,0:T(8,128)(2,1)}, bf16[384,1152]{1,0:T(8,128)(2,1)}, u32[]{:S(2)}, u32[]{:S(2)}) collective-permute-start(bf16[384,1152]{1,0:T(8,128)(2,1)} %collective-permute-done.1.b3), channel_id=1, source_target_pairs={{0,30},{1,31},{2,4},{3,5},{4,2},{5,3},{6,8},{7,9},{8,6},{9,7},{10,... | collective-permute-start | bytes 2654216 | tf_op jit(solution)/shard_map/ppermute | solution.py:28
  50.3 3.7 %collective-permute-start.4 = (bf16[384,1280]{1,0:T(8,128)(2,1)S(1)}, bf16[384,1280]{1,0:T(8,128)(2,1)S(1)}, u32[]{:S(2)}, u32[]{:S(2)}) collective-permute-start(bf16[384,1280]{1,0:T(8,128)(2,1)S(1)} %get-tuple-element.32), channel_id=1, source_target_pairs={{0,2},{1,3},{2,0},{3,1},{4,6},{5,7},{6,4},{7,5},{8,10},{9,11},{10,... | collective-permute-start | bytes 2949128 | tf_op jit(solution)/shard_map/ppermute | solution.py:28

commit v9 on v8

--- a/solution.py
+++ b/solution.py
@@ -71,7 +71,7 @@
 
 
 def pair_step(own, blocks, scale, shift, work):
-    rows = own.shape[0]
+    rows = blocks[0].shape[0]
     for place, raw in enumerate(blocks):
         work[place * rows : (place + 1) * rows] = unit_rows(raw)[0].astype(BF16)
     return terms(own, work[: len(blocks) * rows], scale, shift)
@@ -174,17 +174,9 @@
     loss[...] = total + (1.0 - u_weight) * row_loss
 
 
-def fifth_kernel(scalars, b5, z_pair, grad_in, loss_in, grad_u, loss, for_partner, raw, work, sems):
-    copies = []
-    rows, width = raw.shape
-    for place, part in enumerate(row_parts(rows)):
-        copy = pltpu.make_async_copy(b5.at[part], raw.at[part], sems.at[place])
-        copy.start()
-        copies.append((copy, part))
-    for copy, part in copies:
-        copy.wait()
-        work[part] = unit_rows(raw[part])[0].astype(BF16)
-    term, row_loss = terms(z_pair[...], work[...], *scalar_pair(scalars))
+def fifth_kernel(scalars, b5, z_pair, grad_in, loss_in, grad_u, loss, for_partner, work):
+    rows, width = b5.shape
+    term, row_loss = pair_step(z_pair[...], (b5[...],), *scalar_pair(scalars), work)
     for_partner[:, :width] = term[rows:].astype(BF16)
     for_partner[:, width:] = row_loss[rows:].astype(BF16)
     grad_u[...] = grad_in[...] + term[:rows]
@@ -254,6 +246,7 @@
     line = jax.ShapeDtypeStruct((rows,), F32)
     raw = pltpu.VMEM((rows, width), BF16)
     copies = pltpu.SemaphoreType.DMA((4,))
+    in_hbm = [pltpu.with_memory_space_constraint(x, pltpu.HBM) for x in (image, text)]
 
     def pick(when_outer, when_inner):
         sem = pltpu.SemaphoreType.DMA
@@ -269,7 +262,7 @@
     u, w = call(
         sort_kernel,
         [ANY] * 2,
-        [pltpu.with_memory_space_constraint(x, pltpu.HBM) for x in (image, text)],
+        in_hbm,
         [VMEM] * 2,
         (block, block),
         "sort",
@@ -285,24 +278,22 @@
     scalars = jnp.where(first, score_scaling, score_shift)
     z_pair, unit_u, unit_w, inverse_u, inverse_w, grad_u, grad_w, loss = compute(
         near_kernel,
-        (image, text, slot1, slot2, slot3),
+        (*in_hbm, slot1, slot2, slot3),
         (pair, sums, sums, column, column, sums, sums, partial),
         "near_blocks",
         (pltpu.VMEM((2 * rows, width), BF16), raw),
     )
-    grad_u, loss, for_partner = call(
+    grad_u, loss, for_partner = compute(
         fifth_kernel,
-        [VMEM, ANY, VMEM, VMEM, VMEM],
-        (scalars, slot5, z_pair, grad_u, loss),
-        [VMEM] * 3,
+        (pltpu.with_memory_space_constraint(slot5, pltpu.VMEM), z_pair, grad_u, loss),
         (sums, partial, jax.ShapeDtypeStruct((rows, width + 128), BF16)),
         "fifth_block",
-        (raw, raw, copies),
+        (raw,),
     )
     last = send(for_partner, CORE_SWAP)
     done_u, loss = compute(
         u_kernel,
-        (slot4, z_pair, grad_u, loss, unit_u, inverse_u),
+        (pltpu.with_memory_space_constraint(slot4, pltpu.VMEM), z_pair, grad_u, loss, unit_u, inverse_u),
         (block, partial),
         "finish_u",
         (raw,),

time: 56.6 us -> 56.5 us (level)
  starting transfers between devices: 8.66 us -> 9.37 us
    ppermute x6, starting transfers between devices: 8.66 us -> 9.37 us  [send(): return lax.ppermute(value, AXES, pairs)]
  transfers between devices with their start and end apart: 6 -> 6, of which waited for: 3 -> 2; matrix products, arithmetic and copies ran while one was open for 0% -> 0% of each run, Pallas kernels for 30% -> 29%
where the time goes in v9:
time: 56.5 us; the launch traced here: 55.8 us
  waiting for transfers between devices  24.7 us (44%)
  Pallas kernels  19.6 us (35%)
  starting transfers between devices  9.37 us (17%)
  between operations  2.01 us (4%)
    ppermute x6, waiting for transfers between devices, send(): return lax.ppermute(value, AXES, pairs)  24.7 us
    pallas_call x7, Pallas kernels, call(): pl.pallas_call(kernel, out_shape=outs, in_specs=in_specs, out_specs=out_s...  19.6 us
    ppermute x6, starting transfers between devices, send(): return lax.ppermute(value, AXES, pairs)  9.37 us
  transfers between devices with their start and end apart: 6, of which 2 were waited for; matrix products, arithmetic and copies ran while one was open for 0% of the time, Pallas kernels for 29%

profile of v9, /device:TPU:1, one launch (start us, length us, event | category | flops | bytes accessed | tf_op | source)
XLA Modules:
  0.0 55.8 jit_solution(6152728278693748760)
XLA Ops:
  0.6 1.5 %sort.1 = (bf16[384,1152]{1,0:T(8,128)(2,1)S(1)}, bf16[384,1152]{1,0:T(8,128)(2,1)S(1)}) custom-call(bf16[384,1152]{1,0:T(8,128)(2,1)} %image.3, bf16[384,1152]{1,0:T(8,128)(2,1)} %text.3), custom_call_target="tpu_custom_call" | custom-call | flops 1 | bytes 1 | tf_op jit(solution)/shard_map/sort/pallas_call | solution.py:227
  2.1 0.1 collective-permute-start
  2.2 2.7 %collective-permute-start.2 = (bf16[384,1152]{1,0:T(8,128)(2,1)S(1)}, bf16[384,1152]{1,0:T(8,128)(2,1)S(1)}, u32[]{:S(2)}, u32[]{:S(2)}) collective-permute-start(bf16[384,1152]{1,0:T(8,128)(2,1)S(1)} %get-tuple-element.25.when_inner), channel_id=1, source_target_pairs={{0,30},{1,31},{2,4},{3,5},{4,2},{5,3},{6,8},{7,9},{8,6},{9,7},{10,... | collective-permute-start | bytes 2654216 | tf_op jit(solution)/shard_map/ppermute | solution.py:28
  4.9 0.0 collective-permute-done.when_outer.b1
  4.9 0.2 pick.2
  5.1 2.1 %collective-permute-start.1 = (bf16[384,1152]{1,0:T(8,128)(2,1)S(1)}, bf16[384,1152]{1,0:T(8,128)(2,1)S(1)}, u32[]{:S(2)}, u32[]{:S(2)}) collective-permute-start(bf16[384,1152]{1,0:T(8,128)(2,1)S(1)} %pick.2), channel_id=1, source_target_pairs={{0,1},{1,0},{2,3},{3,2},{4,5},{5,4},{6,7},{7,6},{8,9},{9,8},{10,11... | collective-permute-start | bytes 2654216 | tf_op jit(solution)/shard_map/ppermute | solution.py:28
  7.2 18.2 %collective-permute-done.2.when_inner.b2 = bf16[384,1152]{1,0:T(8,128)(2,1)S(1)} collective-permute-done((bf16[384,1152]{1,0:T(8,128)(2,1)S(1)}, bf16[384,1152]{1,0:T(8,128)(2,1)S(1)}, u32[]{:S(2)}, u32[]{:S(2)}) %collective-permute-start.2) | collective-permute-done | bytes 884768 | tf_op jit(solution)/shard_map/ppermute | solution.py:28
  25.4 0.2 pick.3
  25.6 1.8 %collective-permute-start.3 = (bf16[384,1152]{1,0:T(8,128)(2,1)S(1)}, bf16[384,1152]{1,0:T(8,128)(2,1)}, u32[]{:S(2)}, u32[]{:S(2)}) collective-permute-start(bf16[384,1152]{1,0:T(8,128)(2,1)S(1)} %pick.3), channel_id=1, source_target_pairs={{0,1},{1,0},{2,3},{3,2},{4,5},{5,4},{6,7},{7,6},{8,9},{9,8},{10,11... | collective-permute-start | bytes 2654216 | tf_op jit(solution)/shard_map/ppermute | solution.py:28
  27.4 0.0 collective-permute-done.1.b3
  27.4 2.6 %collective-permute-start.5 = (bf16[384,1152]{1,0:T(8,128)(2,1)S(1)}, bf16[384,1152]{1,0:T(8,128)(2,1)}, u32[]{:S(2)}, u32[]{:S(2)}) collective-permute-start(bf16[384,1152]{1,0:T(8,128)(2,1)S(1)} %collective-permute-done.1.b3), channel_id=1, source_target_pairs={{0,30},{1,31},{2,4},{3,5},{4,2},{5,3},{6,8},{7,9},{8,6},{9,7},{10,... | collective-permute-start | bytes 2654216 | tf_op jit(solution)/shard_map/ppermute | solution.py:28
  31.3 0.1 iota.7.scalars
  31.4 8.3 %near_blocks.1 = (bf16[768,1152]{1,0:T(8,128)(2,1)S(1)}, f32[384,1152]{1,0:T(8,128)S(1)}, f32[384,1152]{1,0:T(8,128)S(1)}, f32[384,1]{1,0:T(8,128)S(1)}, f32[384...) custom-call(f32[8,128]{1,0:T(8,128)S(1)} %iota.7.scalars, ...), custom_call_target="tpu_custom_call" | custom-call | flops 1 | bytes 1 | tf_op jit(solution)/shard_map/near_blocks/pallas_call | solution.py:227
  39.6 6.6 %collective-permute-done.3.b5 = bf16[384,1152]{1,0:T(8,128)(2,1)} collective-permute-done((bf16[384,1152]{1,0:T(8,128)(2,1)S(1)}, bf16[384,1152]{1,0:T(8,128)(2,1)}, u32[]{:S(2)}, u32[]{:S(2)}) %collective-permute-start.3) | collective-permute-done | bytes 884768 | tf_op jit(solution)/shard_map/ppermute | solution.py:28
  46.2 4.1 %fifth_block.1 = (f32[384,1152]{1,0:T(8,128)S(1)}, f32[384,128]{1,0:T(8,128)S(1)}, bf16[384,1280]{1,0:T(8,128)(2,1)S(1)}) custom-call(f32[8,128]{1,0:T(8,128)S(1)} %iota.7.scalars, bf16[384,1152]{1,0:T(8,128)(2,1)} %collective-permute-done.3.b5, bf16[768,1152]{1,0:T(8,128)(2,1)S(1)} %get-tuple-element.29.z_pair, f32[384,1152]{1,0:T(8,128)S(1)} %get-tuple-element.30.grad_in, ...), custom_call_target="tpu_custom_call" | custom-call | flops 1 | bytes 1 | tf_op jit(solution)/shard_map/fifth_block/pallas_call | solution.py:227
  50.3 0.1 collective-permute-start.4
  50.4 0.0 collective-permute-done.5.b4
  50.4 3.3 %finish_u.1 = (bf16[384,1152]{1,0:T(8,128)(2,1)S(1)}, f32[384,128]{1,0:T(8,128)S(1)}) custom-call(f32[8,128]{1,0:T(8,128)S(1)} %iota.7.scalars, bf16[384,1152]{1,0:T(8,128)(2,1)} %collective-permute-done.5.b4, bf16[768,1152]{1,0:T(8,128)(2,1)S(1)} %get-tuple-element.29.z_pair, f32[384,1152]{1,0:T(8,128)S(1)} %get-tuple-element.34.grad_u, ...), custom_call_target="tpu_custom_call" | custom-call | flops 10000000000 | bytes 1 | tf_op jit(solution)/shard_map/finish_u/pallas_call | solution.py:227
  53.7 0.0 collective-permute-done.4.last
  53.8 2.1 %finish_w.1 = (bf16[384,1152]{1,0:T(8,128)(2,1)}, bf16[384,1152]{1,0:T(8,128)(2,1)}, f32[384]{0:T(512)}) custom-call(bf16[384,1280]{1,0:T(8,128)(2,1)S(1)} %collective-permute-done.4.last, f32[384,1152]{1,0:T(8,128)S(1)} %get-tuple-element.33.grad_w, f32[384,128]{1,0:T(8,128)S(1)} %get-tuple-element.38.loss_in, f32[384,1152]{1,0:T(8,128)S(1)} %get-tuple-element.39.unit, ...), custom_call_target="tpu_custom_call" | custom-call | flops 1 | bytes 1 | tf_op jit(solution)/shard_map/finish_w/pallas_call | solution.py:227
  (1 shorter events, 0.0 us)
Async XLA Ops:
  2.1 2.8 %collective-permute-start = (bf16[384,1152]{1,0:T(8,128)(2,1)S(1)}, bf16[384,1152]{1,0:T(8,128)(2,1)S(1)}, u32[]{:S(2)}, u32[]{:S(2)}) collective-permute-start(bf16[384,1152]{1,0:T(8,128)(2,1)S(1)} %get-tuple-element.24.when_outer), channel_id=1, source_target_pairs={{0,2},{1,3},{2,0},{3,1},{4,6},{5,7},{6,4},{7,5},{8,10},{9,11},{10,... | collective-permute-start | bytes 2654216 | tf_op jit(solution)/shard_map/ppermute | solution.py:28
  2.2 23.2 %collective-permute-start.2 = (bf16[384,1152]{1,0:T(8,128)(2,1)S(1)}, bf16[384,1152]{1,0:T(8,128)(2,1)S(1)}, u32[]{:S(2)}, u32[]{:S(2)}) collective-permute-start(bf16[384,1152]{1,0:T(8,128)(2,1)S(1)} %get-tuple-element.25.when_inner), channel_id=1, source_target_pairs={{0,30},{1,31},{2,4},{3,5},{4,2},{5,3},{6,8},{7,9},{8,6},{9,7},{10,... | collective-permute-start | bytes 2654216 | tf_op jit(solution)/shard_map/ppermute | solution.py:28
  5.1 22.3 %collective-permute-start.1 = (bf16[384,1152]{1,0:T(8,128)(2,1)S(1)}, bf16[384,1152]{1,0:T(8,128)(2,1)S(1)}, u32[]{:S(2)}, u32[]{:S(2)}) collective-permute-start(bf16[384,1152]{1,0:T(8,128)(2,1)S(1)} %pick.2), channel_id=1, source_target_pairs={{0,1},{1,0},{2,3},{3,2},{4,5},{5,4},{6,7},{7,6},{8,9},{9,8},{10,11... | collective-permute-start | bytes 2654216 | tf_op jit(solution)/shard_map/ppermute | solution.py:28
  25.6 20.6 %collective-permute-start.3 = (bf16[384,1152]{1,0:T(8,128)(2,1)S(1)}, bf16[384,1152]{1,0:T(8,128)(2,1)}, u32[]{:S(2)}, u32[]{:S(2)}) collective-permute-start(bf16[384,1152]{1,0:T(8,128)(2,1)S(1)} %pick.3), channel_id=1, source_target_pairs={{0,1},{1,0},{2,3},{3,2},{4,5},{5,4},{6,7},{7,6},{8,9},{9,8},{10,11... | collective-permute-start | bytes 2654216 | tf_op jit(solution)/shard_map/ppermute | solution.py:28
  27.4 23.0 %collective-permute-start.5 = (bf16[384,1152]{1,0:T(8,128)(2,1)S(1)}, bf16[384,1152]{1,0:T(8,128)(2,1)}, u32[]{:S(2)}, u32[]{:S(2)}) collective-permute-start(bf16[384,1152]{1,0:T(8,128)(2,1)S(1)} %collective-permute-done.1.b3), channel_id=1, source_target_pairs={{0,30},{1,31},{2,4},{3,5},{4,2},{5,3},{6,8},{7,9},{8,6},{9,7},{10,... | collective-permute-start | bytes 2654216 | tf_op jit(solution)/shard_map/ppermute | solution.py:28
  50.3 3.4 %collective-permute-start.4 = (bf16[384,1280]{1,0:T(8,128)(2,1)S(1)}, bf16[384,1280]{1,0:T(8,128)(2,1)S(1)}, u32[]{:S(2)}, u32[]{:S(2)}) collective-permute-start(bf16[384,1280]{1,0:T(8,128)(2,1)S(1)} %get-tuple-element.32), channel_id=1, source_target_pairs={{0,2},{1,3},{2,0},{3,1},{4,6},{5,7},{6,4},{7,5},{8,10},{9,11},{10,... | collective-permute-start | bytes 2949128 | tf_op jit(solution)/shard_map/ppermute | solution.py:28

commit v10 on v9

--- a/solution.py
+++ b/solution.py
@@ -246,12 +246,15 @@
     line = jax.ShapeDtypeStruct((rows,), F32)
     raw = pltpu.VMEM((rows, width), BF16)
     copies = pltpu.SemaphoreType.DMA((4,))
-    in_hbm = [pltpu.with_memory_space_constraint(x, pltpu.HBM) for x in (image, text)]
-
-    def pick(when_outer, when_inner):
+
+    def in_hbm(*arrays):
+        return [pltpu.with_memory_space_constraint(x, pltpu.HBM) for x in arrays]
+
+
+    def pick(when_outer, when_inner, out):
         sem = pltpu.SemaphoreType.DMA
         return call(
-            pick_kernel, [ANY] * 2, (when_outer, when_inner), [ANY], (block,), "pick", (sem,)
+            pick_kernel, [ANY] * 2, (when_outer, when_inner), [ANY], (out,), "pick", (sem,)
         )[0]
 
     def compute(kernel, args, outs, name, scratch, flops=1):
@@ -262,7 +265,7 @@
     u, w = call(
         sort_kernel,
         [ANY] * 2,
-        in_hbm,
+        in_hbm(image, text),
         [VMEM] * 2,
         (block, block),
         "sort",
@@ -270,15 +273,15 @@
     )
     slot1 = send(w, CORE_SWAP)
     slot2 = send(u, GROUP_SHIFT)
-    slot3 = send(pick(slot1, u), X_SWAP)
+    slot3 = send(pick(slot1, u, block), X_SWAP)
     slot4 = send(slot3, GROUP_SHIFT)
-    slot5 = send(pick(w, slot2), X_SWAP)
+    slot5 = send(pick(w, slot2, pltpu.HBM((rows, width), BF16)), X_SWAP)
     slot3, score_scaling, score_shift = lax.optimization_barrier((slot3, score_scaling, score_shift))
     first = lax.broadcasted_iota(jnp.int32, (8, 128), 0) == 0
     scalars = jnp.where(first, score_scaling, score_shift)
     z_pair, unit_u, unit_w, inverse_u, inverse_w, grad_u, grad_w, loss = compute(
         near_kernel,
-        (*in_hbm, slot1, slot2, slot3),
+        (*in_hbm(image, text), slot1, *in_hbm(slot2, slot3)),
         (pair, sums, sums, column, column, sums, sums, partial),
         "near_blocks",
         (pltpu.VMEM((2 * rows, width), BF16), raw),

time: 56.5 us -> 55 us (0.973)
  Pallas kernels: 19.6 us -> 18.6 us
  waiting for transfers between devices: 24.7 us -> 25.5 us
  starting transfers between devices: 9.37 us -> 8.62 us
    pallas_call x7, Pallas kernels: 19.6 us -> 18.6 us  [call(): pl.pallas_call(kernel, out_shape=outs, in_specs=in_specs, out_specs=out_s...]
    ppermute x6, waiting for transfers between devices: 24.7 us -> 25.5 us  [send(): return lax.ppermute(value, AXES, pairs)]
    ppermute x6, starting transfers between devices: 9.37 us -> 8.62 us  [send(): return lax.ppermute(value, AXES, pairs)]
  transfers between devices with their start and end apart: 6 -> 6, of which waited for: 2 -> 3; matrix products, arithmetic and copies ran while one was open for 0% -> 0% of each run, Pallas kernels for 29% -> 27%
where the time goes in v10:
time: 55 us; the launch traced here: 54.8 us
  waiting for transfers between devices  25.5 us (46%)
  Pallas kernels  18.6 us (34%)
  starting transfers between devices  8.62 us (16%)
  between operations  2 us (4%)
    ppermute x6, waiting for transfers between devices, send(): return lax.ppermute(value, AXES, pairs)  25.5 us
    pallas_call x7, Pallas kernels, call(): pl.pallas_call(kernel, out_shape=outs, in_specs=in_specs, out_specs=out_s...  18.6 us
    ppermute x6, starting transfers between devices, send(): return lax.ppermute(value, AXES, pairs)  8.62 us
  transfers between devices with their start and end apart: 6, of which 3 were waited for; matrix products, arithmetic and copies ran while one was open for 0% of the time, Pallas kernels for 27%

profile of v10, /device:TPU:1, one launch (start us, length us, event | category | flops | bytes accessed | tf_op | source)
XLA Modules:
  0.0 54.8 jit_solution(16728108770986165510)
XLA Ops:
  0.6 1.5 %sort.1 = (bf16[384,1152]{1,0:T(8,128)(2,1)S(1)}, bf16[384,1152]{1,0:T(8,128)(2,1)S(1)}) custom-call(bf16[384,1152]{1,0:T(8,128)(2,1)} %image.3, bf16[384,1152]{1,0:T(8,128)(2,1)} %text.3), custom_call_target="tpu_custom_call" | custom-call | flops 1 | bytes 1 | tf_op jit(solution)/shard_map/sort/pallas_call | solution.py:227
  2.1 0.1 collective-permute-start
  2.2 2.7 %collective-permute-start.2 = (bf16[384,1152]{1,0:T(8,128)(2,1)S(1)}, bf16[384,1152]{1,0:T(8,128)(2,1)S(1)}, u32[]{:S(2)}, u32[]{:S(2)}) collective-permute-start(bf16[384,1152]{1,0:T(8,128)(2,1)S(1)} %get-tuple-element.25.when_inner), channel_id=1, source_target_pairs={{0,30},{1,31},{2,4},{3,5},{4,2},{5,3},{6,8},{7,9},{8,6},{9,7},{10,... | collective-permute-start | bytes 2654216 | tf_op jit(solution)/shard_map/ppermute | solution.py:28
  4.9 0.0 collective-permute-done.when_outer.b1
  4.9 0.2 pick.2
  5.1 2.1 %collective-permute-start.1 = (bf16[384,1152]{1,0:T(8,128)(2,1)S(1)}, bf16[384,1152]{1,0:T(8,128)(2,1)}, u32[]{:S(2)}, u32[]{:S(2)}) collective-permute-start(bf16[384,1152]{1,0:T(8,128)(2,1)S(1)} %pick.2), channel_id=1, source_target_pairs={{0,1},{1,0},{2,3},{3,2},{4,5},{5,4},{6,7},{7,6},{8,9},{9,8},{10,11... | collective-permute-start | bytes 2654216 | tf_op jit(solution)/shard_map/ppermute | solution.py:28
  7.2 18.3 %collective-permute-done.2.when_inner.b2 = bf16[384,1152]{1,0:T(8,128)(2,1)S(1)} collective-permute-done((bf16[384,1152]{1,0:T(8,128)(2,1)S(1)}, bf16[384,1152]{1,0:T(8,128)(2,1)S(1)}, u32[]{:S(2)}, u32[]{:S(2)}) %collective-permute-start.2) | collective-permute-done | bytes 884768 | tf_op jit(solution)/shard_map/ppermute | solution.py:28
  25.5 0.0 copy-start
  25.5 0.9 %pick.3 = bf16[384,1152]{1,0:T(8,128)(2,1)} custom-call(bf16[384,1152]{1,0:T(8,128)(2,1)S(1)} %get-tuple-element.24.when_outer, bf16[384,1152]{1,0:T(8,128)(2,1)S(1)} %collective-permute-done.2.when_inner.b2), custom_call_target="tpu_custom_call" | custom-call | flops 1 | bytes 1 | tf_op jit(solution)/shard_map/pick/pallas_call | solution.py:227
  26.4 1.8 %collective-permute-start.3 = (bf16[384,1152]{1,0:T(8,128)(2,1)}, bf16[384,1152]{1,0:T(8,128)(2,1)S(1)}, u32[]{:S(2)}, u32[]{:S(2)}) collective-permute-start(bf16[384,1152]{1,0:T(8,128)(2,1)} %pick.3), channel_id=1, source_target_pairs={{0,1},{1,0},{2,3},{3,2},{4,5},{5,4},{6,7},{7,6},{8,9},{9,8},{10,11... | collective-permute-start | bytes 2654216 | tf_op jit(solution)/shard_map/ppermute | solution.py:28
  28.3 0.0 collective-permute-done.1.b3
  28.3 1.8 %collective-permute-start.5 = (bf16[384,1152]{1,0:T(8,128)(2,1)}, bf16[384,1152]{1,0:T(8,128)(2,1)S(1)}, u32[]{:S(2)}, u32[]{:S(2)}) collective-permute-start(bf16[384,1152]{1,0:T(8,128)(2,1)} %collective-permute-done.1.b3), channel_id=1, source_target_pairs={{0,30},{1,31},{2,4},{3,5},{4,2},{5,3},{6,8},{7,9},{8,6},{9,7},{10,... | collective-permute-start | bytes 2654216 | tf_op jit(solution)/shard_map/ppermute | solution.py:28
  31.4 0.1 iota.7.scalars
  31.5 0.0 copy-done
  31.5 8.8 %near_blocks.1 = (bf16[768,1152]{1,0:T(8,128)(2,1)S(1)}, f32[384,1152]{1,0:T(8,128)S(1)}, f32[384,1152]{1,0:T(8,128)S(1)}, f32[384,1]{1,0:T(8,128)S(1)}, f32[384...) custom-call(f32[8,128]{1,0:T(8,128)S(1)} %iota.7.scalars, ...), custom_call_target="tpu_custom_call" | custom-call | flops 1 | bytes 1 | tf_op jit(solution)/shard_map/near_blocks/pallas_call | solution.py:227
  40.3 5.8 %collective-permute-done.3.b5 = bf16[384,1152]{1,0:T(8,128)(2,1)S(1)} collective-permute-done((bf16[384,1152]{1,0:T(8,128)(2,1)}, bf16[384,1152]{1,0:T(8,128)(2,1)S(1)}, u32[]{:S(2)}, u32[]{:S(2)}) %collective-permute-start.3) | collective-permute-done | bytes 884768 | tf_op jit(solution)/shard_map/ppermute | solution.py:28
  46.1 3.0 %fifth_block.1 = (f32[384,1152]{1,0:T(8,128)S(1)}, f32[384,128]{1,0:T(8,128)S(1)}, bf16[384,1280]{1,0:T(8,128)(2,1)S(1)}) custom-call(f32[8,128]{1,0:T(8,128)S(1)} %iota.7.scalars, bf16[384,1152]{1,0:T(8,128)(2,1)S(1)} %collective-permute-done.3.b5, bf16[768,1152]{1,0:T(8,128)(2,1)S(1)} %get-tuple-element.29.z_pair, ...), custom_call_target="tpu_custom_call" | custom-call | flops 1 | bytes 1 | tf_op jit(solution)/shard_map/fifth_block/pallas_call | solution.py:227
  49.0 0.1 collective-permute-start.4
  49.1 1.4 %collective-permute-done.5.b4 = bf16[384,1152]{1,0:T(8,128)(2,1)S(1)} collective-permute-done((bf16[384,1152]{1,0:T(8,128)(2,1)}, bf16[384,1152]{1,0:T(8,128)(2,1)S(1)}, u32[]{:S(2)}, u32[]{:S(2)}) %collective-permute-start.5) | collective-permute-done | bytes 884768 | tf_op jit(solution)/shard_map/ppermute | solution.py:28
  50.5 2.2 %finish_u.1 = (bf16[384,1152]{1,0:T(8,128)(2,1)S(1)}, f32[384,128]{1,0:T(8,128)S(1)}) custom-call(f32[8,128]{1,0:T(8,128)S(1)} %iota.7.scalars, bf16[384,1152]{1,0:T(8,128)(2,1)S(1)} %collective-permute-done.5.b4, bf16[768,1152]{1,0:T(8,128)(2,1)S(1)} %get-tuple-element.29.z_pair, f32[384,1152]{1,0:T(8,128)S(1)} %get-tuple-element.34.grad_u, ...), custom_call_target="tpu_custom_call" | custom-call | flops 10000000000 | bytes 1 | tf_op jit(solution)/shard_map/finish_u/pallas_call | solution.py:227
  52.7 0.0 collective-permute-done.4.last
  52.7 2.1 %finish_w.1 = (bf16[384,1152]{1,0:T(8,128)(2,1)}, bf16[384,1152]{1,0:T(8,128)(2,1)}, f32[384]{0:T(512)}) custom-call(bf16[384,1280]{1,0:T(8,128)(2,1)S(1)} %collective-permute-done.4.last, f32[384,1152]{1,0:T(8,128)S(1)} %get-tuple-element.33.grad_w, f32[384,128]{1,0:T(8,128)S(1)} %get-tuple-element.38.loss_in, f32[384,1152]{1,0:T(8,128)S(1)} %get-tuple-element.39.unit, ...), custom_call_target="tpu_custom_call" | custom-call | flops 1 | bytes 1 | tf_op jit(solution)/shard_map/finish_w/pallas_call | solution.py:227
  (1 shorter events, 0.0 us)
Async XLA Ops:
  2.1 2.8 %collective-permute-start = (bf16[384,1152]{1,0:T(8,128)(2,1)S(1)}, bf16[384,1152]{1,0:T(8,128)(2,1)S(1)}, u32[]{:S(2)}, u32[]{:S(2)}) collective-permute-start(bf16[384,1152]{1,0:T(8,128)(2,1)S(1)} %get-tuple-element.24.when_outer), channel_id=1, source_target_pairs={{0,2},{1,3},{2,0},{3,1},{4,6},{5,7},{6,4},{7,5},{8,10},{9,11},{10,... | collective-permute-start | bytes 2654216 | tf_op jit(solution)/shard_map/ppermute | solution.py:28
  2.2 23.3 %collective-permute-start.2 = (bf16[384,1152]{1,0:T(8,128)(2,1)S(1)}, bf16[384,1152]{1,0:T(8,128)(2,1)S(1)}, u32[]{:S(2)}, u32[]{:S(2)}) collective-permute-start(bf16[384,1152]{1,0:T(8,128)(2,1)S(1)} %get-tuple-element.25.when_inner), channel_id=1, source_target_pairs={{0,30},{1,31},{2,4},{3,5},{4,2},{5,3},{6,8},{7,9},{8,6},{9,7},{10,... | collective-permute-start | bytes 2654216 | tf_op jit(solution)/shard_map/ppermute | solution.py:28
  5.1 23.2 %collective-permute-start.1 = (bf16[384,1152]{1,0:T(8,128)(2,1)S(1)}, bf16[384,1152]{1,0:T(8,128)(2,1)}, u32[]{:S(2)}, u32[]{:S(2)}) collective-permute-start(bf16[384,1152]{1,0:T(8,128)(2,1)S(1)} %pick.2), channel_id=1, source_target_pairs={{0,1},{1,0},{2,3},{3,2},{4,5},{5,4},{6,7},{7,6},{8,9},{9,8},{10,11... | collective-permute-start | bytes 2654216 | tf_op jit(solution)/shard_map/ppermute | solution.py:28
  25.5 6.0 %copy-start = (bf16[384,1152]{1,0:T(8,128)(2,1)}, bf16[384,1152]{1,0:T(8,128)(2,1)S(1)}, u32[]{:S(2)}) copy-start(bf16[384,1152]{1,0:T(8,128)(2,1)S(1)} %collective-permute-done.2.when_inner.b2) | copy-start | bytes 2654212
  26.4 19.6 %collective-permute-start.3 = (bf16[384,1152]{1,0:T(8,128)(2,1)}, bf16[384,1152]{1,0:T(8,128)(2,1)S(1)}, u32[]{:S(2)}, u32[]{:S(2)}) collective-permute-start(bf16[384,1152]{1,0:T(8,128)(2,1)} %pick.3), channel_id=1, source_target_pairs={{0,1},{1,0},{2,3},{3,2},{4,5},{5,4},{6,7},{7,6},{8,9},{9,8},{10,11... | collective-permute-start | bytes 2654216 | tf_op jit(solution)/shard_map/ppermute | solution.py:28
  28.3 22.3 %collective-permute-start.5 = (bf16[384,1152]{1,0:T(8,128)(2,1)}, bf16[384,1152]{1,0:T(8,128)(2,1)S(1)}, u32[]{:S(2)}, u32[]{:S(2)}) collective-permute-start(bf16[384,1152]{1,0:T(8,128)(2,1)} %collective-permute-done.1.b3), channel_id=1, source_target_pairs={{0,30},{1,31},{2,4},{3,5},{4,2},{5,3},{6,8},{7,9},{8,6},{9,7},{10,... | collective-permute-start | bytes 2654216 | tf_op jit(solution)/shard_map/ppermute | solution.py:28
  49.0 3.6 %collective-permute-start.4 = (bf16[384,1280]{1,0:T(8,128)(2,1)S(1)}, bf16[384,1280]{1,0:T(8,128)(2,1)S(1)}, u32[]{:S(2)}, u32[]{:S(2)}) collective-permute-start(bf16[384,1280]{1,0:T(8,128)(2,1)S(1)} %get-tuple-element.32), channel_id=1, source_target_pairs={{0,2},{1,3},{2,0},{3,1},{4,6},{5,7},{6,4},{7,5},{8,10},{9,11},{10,... | collective-permute-start | bytes 2949128 | tf_op jit(solution)/shard_map/ppermute | solution.py:28

commit v11 on v10

--- a/solution.py
+++ b/solution.py
@@ -12,9 +12,13 @@
 BF16 = jnp.bfloat16
 VMEM_LIMIT = 16 * 1024 * 1024
 
+CYCLE = {0: (2, 0), 1: (0, 0), 2: (3, 0), 3: (1, 0)}
+TEXT_BY_TWO = {0: (2, 0), 1: (3, 0), 2: (0, 1), 3: (1, 1)}
+IMAGE_BY_TWO = {0: (2, -1), 1: (3, -1), 2: (0, 0), 3: (1, 0)}
 X_SWAP = {0: (1, 0), 1: (0, 0), 2: (3, 0), 3: (2, 0)}
 CORE_SWAP = {0: (2, 0), 1: (3, 0), 2: (0, 0), 3: (1, 0)}
-GROUP_SHIFT = {0: (2, -1), 1: (3, -1), 2: (0, 1), 3: (1, 1)}
+OUTER_RELAY = {0: (2, -1), 1: (3, 0), 2: (0, 0), 3: (1, 1)}
+INNER_RELAY = {0: (2, 0), 1: (3, -1), 2: (0, 1), 3: (1, 0)}
 
 
 def send(value, moves):
@@ -104,6 +108,10 @@
     return lax.rem(lax.axis_index("blk"), 2) == lax.axis_index("inner")
 
 
+def when(condition, then):
+    pl.when(condition)(then)
+
+
 def sort_kernel(image, text, u, w, sems):
     def move(image_to, text_to):
         copies = [
@@ -115,29 +123,24 @@
         for copy in copies:
             copy.wait()
 
-    u_is_image = image_is_u()
-
-    @pl.when(u_is_image)
-    def _():
-        move(u, w)
-
-    @pl.when(jnp.logical_not(u_is_image))
-    def _():
-        move(w, u)
-
-
-def pick_kernel(when_outer, when_inner, picked, sem):
-    @pl.when(is_outer())
-    def _():
-        pltpu.async_copy(when_outer, picked, sem).wait()
-
-    @pl.when(jnp.logical_not(is_outer()))
-    def _():
-        pltpu.async_copy(when_inner, picked, sem).wait()
+    when(image_is_u(), lambda: move(u, w))
+    when(jnp.logical_not(image_is_u()), lambda: move(w, u))
+
+
+def pick_kernel(outer_u, outer_w, inner_u, inner_w, picked, sem):
+    def move(source):
+        pltpu.async_copy(source, picked, sem).wait()
+
+    u_is_image, outer = image_is_u(), is_outer()
+    inner, w_is_image = jnp.logical_not(outer), jnp.logical_not(u_is_image)
+    when(jnp.logical_and(outer, u_is_image), lambda: move(outer_u))
+    when(jnp.logical_and(outer, w_is_image), lambda: move(outer_w))
+    when(jnp.logical_and(inner, u_is_image), lambda: move(inner_u))
+    when(jnp.logical_and(inner, w_is_image), lambda: move(inner_w))
 
 
 def near_kernel(
-    scalars, image, text, b1, b2, b3,
+    scalars, image, text, image_two, text_two, outer_b3, inner_b3,
     z_pair, unit_u, unit_w, inverse_u, inverse_w, grad_u, grad_w, loss, work, z_w,
 ):
     u_is_image = image_is_u()
@@ -153,6 +156,9 @@
     zt = text_unit.astype(BF16)
     z_u = jnp.where(u_is_image, zi, zt)
     z_pair[: zi.shape[0]] = z_u
+    b1 = jnp.where(u_is_image, image_two[...], text_two[...])
+    b2 = jnp.where(u_is_image, text_two[...], image_two[...])
+    b3 = jnp.where(is_outer(), outer_b3[...], inner_b3[...])
     z_w[...] = jnp.where(u_is_image, zt, zi)
     scores = scale * dot_nt(zi, zt) + shift
     rows = lax.broadcasted_iota(jnp.int32, scores.shape, 0)
@@ -165,10 +171,10 @@
     grad_text = dot_tn(coef, zi)
     grad_u[...] = jnp.where(u_is_image, grad_image, grad_text)
     grad_w[...] = jnp.where(u_is_image, grad_text, grad_image)
-    term, row_loss = pair_step(z_u, (b2[...],), scale, shift, work)
+    term, row_loss = pair_step(z_u, (b2,), scale, shift, work)
     grad_u[...] += term
     total = total + u_weight * row_loss
-    term, row_loss = pair_step(z_w[...], (b1[...], b3[...]), scale, shift, work)
+    term, row_loss = pair_step(z_w[...], (b1, b3), scale, shift, work)
     z_pair[zi.shape[0] :] = work[: zi.shape[0]]
     grad_w[...] += term
     loss[...] = total + (1.0 - u_weight) * row_loss
@@ -183,9 +189,10 @@
     loss[...] = loss_in[...] + image_is_u().astype(F32) * row_loss[:rows]
 
 
-def u_kernel(scalars, b4, z_pair, grad_u, loss_in, unit, inverse, done_u, loss, work):
+def u_kernel(scalars, outer_b4, inner_b4, z_pair, grad_u, loss_in, unit, inverse, done_u, loss, work):
     rows = done_u.shape[0]
-    term, row_loss = pair_step(z_pair[:rows], (b4[...],), *scalar_pair(scalars), work)
+    b4 = jnp.where(is_outer(), outer_b4[...], inner_b4[...])
+    term, row_loss = pair_step(z_pair[:rows], (b4,), *scalar_pair(scalars), work)
     loss[...] = loss_in[...] + image_is_u().astype(F32) * row_loss
     done_u[...] = project(unit[...], inverse[...], grad_u[...] + term)
 
@@ -251,44 +258,48 @@
         return [pltpu.with_memory_space_constraint(x, pltpu.HBM) for x in arrays]
 
 
-    def pick(when_outer, when_inner, out):
-        sem = pltpu.SemaphoreType.DMA
-        return call(
-            pick_kernel, [ANY] * 2, (when_outer, when_inner), [ANY], (out,), "pick", (sem,)
-        )[0]
+    def in_vmem(*arrays):
+        return [pltpu.with_memory_space_constraint(x, pltpu.VMEM) for x in arrays]
 
     def compute(kernel, args, outs, name, scratch, flops=1):
         in_specs = [VMEM] * (1 + len(args))
         out_specs = [VMEM] * len(outs)
         return call(kernel, in_specs, (scalars, *args), out_specs, outs, name, scratch, flops)
 
-    u, w = call(
-        sort_kernel,
-        [ANY] * 2,
-        in_hbm(image, text),
-        [VMEM] * 2,
-        (block, block),
-        "sort",
-        (copies,),
-    )
-    slot1 = send(w, CORE_SWAP)
-    slot2 = send(u, GROUP_SHIFT)
-    slot3 = send(pick(slot1, u, block), X_SWAP)
-    slot4 = send(slot3, GROUP_SHIFT)
-    slot5 = send(pick(w, slot2, pltpu.HBM((rows, width), BF16)), X_SWAP)
-    slot3, score_scaling, score_shift = lax.optimization_barrier((slot3, score_scaling, score_shift))
+    text_cycle = send(text, CYCLE)
+    image_cycle = send(image, CYCLE)
+    text_two = send(text, TEXT_BY_TWO)
+    image_two = send(image, IMAGE_BY_TWO)
+    slot5 = send(
+        call(
+            pick_kernel,
+            [ANY] * 4,
+            (text, image, text_two, image_two),
+            [ANY],
+            (pltpu.HBM((rows, width), BF16),),
+            "pick",
+            (pltpu.SemaphoreType.DMA,),
+        )[0],
+        X_SWAP,
+    )
+    outer_b3, crossing = call(
+        sort_kernel, [ANY] * 2, (image_cycle, text_cycle), [ANY] * 2, (block, block), "sort", (copies,)
+    )
+    inner_b4 = send(outer_b3, OUTER_RELAY)
+    inner_b3 = send(crossing, CORE_SWAP)
+    outer_b4 = send(inner_b3, INNER_RELAY)
     first = lax.broadcasted_iota(jnp.int32, (8, 128), 0) == 0
     scalars = jnp.where(first, score_scaling, score_shift)
     z_pair, unit_u, unit_w, inverse_u, inverse_w, grad_u, grad_w, loss = compute(
         near_kernel,
-        (*in_hbm(image, text), slot1, *in_hbm(slot2, slot3)),
+        in_hbm(image, text, image_two, text_two, outer_b3, inner_b3),
         (pair, sums, sums, column, column, sums, sums, partial),
         "near_blocks",
         (pltpu.VMEM((2 * rows, width), BF16), raw),
     )
     grad_u, loss, for_partner = compute(
         fifth_kernel,
-        (pltpu.with_memory_space_constraint(slot5, pltpu.VMEM), z_pair, grad_u, loss),
+        (*in_vmem(slot5), z_pair, grad_u, loss),
         (sums, partial, jax.ShapeDtypeStruct((rows, width + 128), BF16)),
         "fifth_block",
         (raw,),
@@ -296,7 +307,7 @@
     last = send(for_partner, CORE_SWAP)
     done_u, loss = compute(
         u_kernel,
-        (pltpu.with_memory_space_constraint(slot4, pltpu.VMEM), z_pair, grad_u, loss, unit_u, inverse_u),
+        (*in_vmem(outer_b4, inner_b4), z_pair, grad_u, loss, unit_u, inverse_u),
         (block, partial),
         "finish_u",
         (raw,),

time: 55 us -> 57.2 us (1.040)
  waiting for transfers between devices: 25.5 us -> 27.2 us
    ppermute x6 -> x9, waiting for transfers between devices: 25.5 us -> 27.2 us  [send(): return lax.ppermute(value, AXES, pairs)]
    ppermute x6 -> x9, starting transfers between devices: 8.62 us -> 8.44 us  [send(): return lax.ppermute(value, AXES, pairs)]
    pallas_call x7 -> x6, Pallas kernels: 18.6 us -> 18.7 us  [call(): pl.pallas_call(kernel, out_shape=outs, in_specs=in_specs, out_specs=out_s...]
  transfers between devices with their start and end apart: 6 -> 9, of which waited for: 3 -> 4; matrix products, arithmetic and copies ran while one was open for 0% -> 0% of each run, Pallas kernels for 27% -> 29%
where the time goes in v11:
time: 57.2 us; the launch traced here: 56.7 us
  waiting for transfers between devices  27.2 us (48%)
  Pallas kernels  18.7 us (33%)
  starting transfers between devices  8.44 us (15%)
  between operations  2.01 us (4%)
    ppermute x9, waiting for transfers between devices, send(): return lax.ppermute(value, AXES, pairs)  27.2 us
    pallas_call x6, Pallas kernels, call(): pl.pallas_call(kernel, out_shape=outs, in_specs=in_specs, out_specs=out_s...  18.7 us
    ppermute x9, starting transfers between devices, send(): return lax.ppermute(value, AXES, pairs)  8.44 us
  transfers between devices with their start and end apart: 9, of which 4 were waited for; matrix products, arithmetic and copies ran while one was open for 0% of the time, Pallas kernels for 29%

profile of v11, /device:TPU:1, one launch (start us, length us, event | category | flops | bytes accessed | tf_op | source)
XLA Modules:
  0.0 56.7 jit_solution(15216898482632712783)
XLA Ops:
  0.6 0.0 copy-start.1
  0.6 0.0 copy-start
  0.7 2.1 %collective-permute-start.3 = (bf16[384,1152]{1,0:T(8,128)(2,1)}, bf16[384,1152]{1,0:T(8,128)(2,1)S(1)}, u32[]{:S(2)}, u32[]{:S(2)}) collective-permute-start(bf16[384,1152]{1,0:T(8,128)(2,1)} %image.1), channel_id=1, source_target_pairs={{0,2},{1,0},{2,3},{3,1},{4,6},{5,4},{6,7},{7,5},{8,10},{9,8},{10,1... | collective-permute-start | bytes 2654216 | tf_op jit(solution)/shard_map/ppermute | solution.py:32
  2.7 0.7 %collective-permute-start.4 = (bf16[384,1152]{1,0:T(8,128)(2,1)}, bf16[384,1152]{1,0:T(8,128)(2,1)S(1)}, u32[]{:S(2)}, u32[]{:S(2)}) collective-permute-start(bf16[384,1152]{1,0:T(8,128)(2,1)} %text.1), channel_id=1, source_target_pairs={{0,2},{1,0},{2,3},{3,1},{4,6},{5,4},{6,7},{7,5},{8,10},{9,8},{10,1... | collective-permute-start | bytes 2654216 | tf_op jit(solution)/shard_map/ppermute | solution.py:32
  3.4 1.0 %collective-permute-start = (bf16[384,1152]{1,0:T(8,128)(2,1)}, bf16[384,1152]{1,0:T(8,128)(2,1)S(1)}, u32[]{:S(2)}, u32[]{:S(2)}) collective-permute-start(bf16[384,1152]{1,0:T(8,128)(2,1)} %text.1), channel_id=1, source_target_pairs={{0,2},{1,3},{2,4},{3,5},{4,6},{5,7},{6,8},{7,9},{8,10},{9,11},{10,... | collective-permute-start | bytes 2654216 | tf_op jit(solution)/shard_map/ppermute | solution.py:32
  4.3 0.0 collective-permute-start.1
  4.3 8.7 %collective-permute-done.3.image = bf16[384,1152]{1,0:T(8,128)(2,1)S(1)} collective-permute-done((bf16[384,1152]{1,0:T(8,128)(2,1)}, bf16[384,1152]{1,0:T(8,128)(2,1)S(1)}, u32[]{:S(2)}, u32[]{:S(2)}) %collective-permute-start.3) | collective-permute-done | bytes 884768 | tf_op jit(solution)/shard_map/ppermute | solution.py:32
  13.0 9.5 %collective-permute-done.4.text = bf16[384,1152]{1,0:T(8,128)(2,1)S(1)} collective-permute-done((bf16[384,1152]{1,0:T(8,128)(2,1)}, bf16[384,1152]{1,0:T(8,128)(2,1)S(1)}, u32[]{:S(2)}, u32[]{:S(2)}) %collective-permute-start.4) | collective-permute-done | bytes 884768 | tf_op jit(solution)/shard_map/ppermute | solution.py:32
  22.5 1.1 %sort.1 = (bf16[384,1152]{1,0:T(8,128)(2,1)}, bf16[384,1152]{1,0:T(8,128)(2,1)S(1)}) custom-call(bf16[384,1152]{1,0:T(8,128)(2,1)S(1)} %collective-permute-done.3.image, bf16[384,1152]{1,0:T(8,128)(2,1)S(1)} %collective-permute-done.4.text), custom_call_target="tpu_custom_call" | custom-call | flops 1 | bytes 1 | tf_op jit(solution)/shard_map/sort/pallas_call | solution.py:234
  23.6 1.8 %collective-permute-start.5 = (bf16[384,1152]{1,0:T(8,128)(2,1)S(1)}, bf16[384,1152]{1,0:T(8,128)(2,1)}, u32[]{:S(2)}, u32[]{:S(2)}) collective-permute-start(bf16[384,1152]{1,0:T(8,128)(2,1)S(1)} %get-tuple-element.22), channel_id=1, source_target_pairs={{0,2},{1,3},{2,0},{3,1},{4,6},{5,7},{6,4},{7,5},{8,10},{9,11},{10,... | collective-permute-start | bytes 2654216 | tf_op jit(solution)/shard_map/ppermute | solution.py:32
  25.4 0.0 collective-permute-done.inner_u.text_two
  25.4 0.0 copy-start.2
  25.4 1.1 %collective-permute-done.1.inner_w.image_two = bf16[384,1152]{1,0:T(8,128)(2,1)S(1)} collective-permute-done((bf16[384,1152]{1,0:T(8,128)(2,1)}, bf16[384,1152]{1,0:T(8,128)(2,1)S(1)}, u32[]{:S(2)}, u32[]{:S(2)}) %collective-permute-start.1) | collective-permute-done | bytes 884768 | tf_op jit(solution)/shard_map/ppermute | solution.py:32
  26.5 0.0 copy-done.1
  26.5 0.0 copy-done
  26.5 0.0 copy-start.3
  26.5 1.0 %pick.1 = bf16[384,1152]{1,0:T(8,128)(2,1)} custom-call(bf16[384,1152]{1,0:T(8,128)(2,1)S(1)} %copy-done, bf16[384,1152]{1,0:T(8,128)(2,1)S(1)} %copy-done.1, bf16[384,1152]{1,0:T(8,128)(2,1)S(1)} %collective-permute-done.inner_u.text_two, bf16[384,1152]{1,0:T(8,128)(2,1)S(1)} %collective-permute-done.1.inner_w.image_two), custom_call_target="tpu_custom_call" | custom-call | flops 1 | bytes 1 | tf_op jit(solution)/shard_map/pick/pallas_call | solution.py:234
  27.5 0.0 copy-done.2
  27.5 0.2 copy-done.3
  27.7 0.7 %collective-permute-start.2 = (bf16[384,1152]{1,0:T(8,128)(2,1)}, bf16[384,1152]{1,0:T(8,128)(2,1)S(1)}, u32[]{:S(2)}, u32[]{:S(2)}) collective-permute-start(bf16[384,1152]{1,0:T(8,128)(2,1)} %pick.1), channel_id=1, source_target_pairs={{0,1},{1,0},{2,3},{3,2},{4,5},{5,4},{6,7},{7,6},{8,9},{9,8},{10,11... | collective-permute-start | bytes 2654216 | tf_op jit(solution)/shard_map/ppermute | solution.py:32
  28.5 0.0 collective-permute-start.8
  28.5 0.0 collective-permute-done.5.inner_b3
  28.5 1.7 %collective-permute-start.7 = (bf16[384,1152]{1,0:T(8,128)(2,1)}, bf16[384,1152]{1,0:T(8,128)(2,1)S(1)}, u32[]{:S(2)}, u32[]{:S(2)}) collective-permute-start(bf16[384,1152]{1,0:T(8,128)(2,1)} %collective-permute-done.5.inner_b3), channel_id=1, source_target_pairs={{0,2},{1,31},{2,4},{3,1},{4,6},{5,3},{6,8},{7,5},{8,10},{9,7},{10,... | collective-permute-start | bytes 2654216 | tf_op jit(solution)/shard_map/ppermute | solution.py:32
  31.5 0.1 iota.7.scalars
  31.6 9.4 %near_blocks.1 = (bf16[768,1152]{1,0:T(8,128)(2,1)S(1)}, f32[384,1152]{1,0:T(8,128)S(1)}, f32[384,1152]{1,0:T(8,128)S(1)}, f32[384,1]{1,0:T(8,128)S(1)}, f32[384...) custom-call(f32[8,128]{1,0:T(8,128)S(1)} %iota.7.scalars, ...), custom_call_target="tpu_custom_call" | custom-call | flops 1 | bytes 1 | tf_op jit(solution)/shard_map/near_blocks/pallas_call | solution.py:234
  41.0 8.0 %collective-permute-done.2.b5 = bf16[384,1152]{1,0:T(8,128)(2,1)S(1)} collective-permute-done((bf16[384,1152]{1,0:T(8,128)(2,1)}, bf16[384,1152]{1,0:T(8,128)(2,1)S(1)}, u32[]{:S(2)}, u32[]{:S(2)}) %collective-permute-start.2) | collective-permute-done | bytes 884768 | tf_op jit(solution)/shard_map/ppermute | solution.py:32
  49.0 2.9 %fifth_block.1 = (f32[384,1152]{1,0:T(8,128)S(1)}, f32[384,128]{1,0:T(8,128)S(1)}, bf16[384,1280]{1,0:T(8,128)(2,1)S(1)}) custom-call(f32[8,128]{1,0:T(8,128)S(1)} %iota.7.scalars, bf16[384,1152]{1,0:T(8,128)(2,1)S(1)} %collective-permute-done.2.b5, bf16[768,1152]{1,0:T(8,128)(2,1)S(1)} %get-tuple-element.23.z_pair, ...), custom_call_target="tpu_custom_call" | custom-call | flops 1 | bytes 1 | tf_op jit(solution)/shard_map/fifth_block/pallas_call | solution.py:234
  52.0 0.5 collective-permute-start.6
  52.4 0.0 collective-permute-done.8.inner_b4
  52.4 0.0 collective-permute-done.7.outer_b4
  52.4 2.2 %finish_u.1 = (bf16[384,1152]{1,0:T(8,128)(2,1)S(1)}, f32[384,128]{1,0:T(8,128)S(1)}) custom-call(f32[8,128]{1,0:T(8,128)S(1)} %iota.7.scalars, bf16[384,1152]{1,0:T(8,128)(2,1)S(1)} %collective-permute-done.7.outer_b4, bf16[384,1152]{1,0:T(8,128)(2,1)S(1)} %collective-permute-done.8.inner_b4, bf16[768,1152]{1,0:T(8,128)(2,1)S(1)} %get-tuple-element.23.z_pair, ...), custom_call_target="tpu_custom_call" | custom-call | flops 10000000000 | bytes 1 | tf_op jit(solution)/shard_map/finish_u/pallas_call | solution.py:234
  54.6 0.0 collective-permute-done.6.last
  54.6 2.1 %finish_w.1 = (bf16[384,1152]{1,0:T(8,128)(2,1)}, bf16[384,1152]{1,0:T(8,128)(2,1)}, f32[384]{0:T(512)}) custom-call(bf16[384,1280]{1,0:T(8,128)(2,1)S(1)} %collective-permute-done.6.last, f32[384,1152]{1,0:T(8,128)S(1)} %get-tuple-element.27.grad_w, f32[384,128]{1,0:T(8,128)S(1)} %get-tuple-element.32.loss_in, f32[384,1152]{1,0:T(8,128)S(1)} %get-tuple-element.33.unit, ...), custom_call_target="tpu_custom_call" | custom-call | flops 1 | bytes 1 | tf_op jit(solution)/shard_map/finish_w/pallas_call | solution.py:234
  (1 shorter events, 0.0 us)
Async XLA Ops:
  0.6 25.9 %copy-start.1 = (bf16[384,1152]{1,0:T(8,128)(2,1)S(1)}, bf16[384,1152]{1,0:T(8,128)(2,1)}, u32[]{:S(2)}) copy-start(bf16[384,1152]{1,0:T(8,128)(2,1)} %image.1) | copy-start | bytes 2654212
  0.6 25.9 %copy-start = (bf16[384,1152]{1,0:T(8,128)(2,1)S(1)}, bf16[384,1152]{1,0:T(8,128)(2,1)}, u32[]{:S(2)}) copy-start(bf16[384,1152]{1,0:T(8,128)(2,1)} %text.1) | copy-start | bytes 2654212
  0.7 12.4 %collective-permute-start.3 = (bf16[384,1152]{1,0:T(8,128)(2,1)}, bf16[384,1152]{1,0:T(8,128)(2,1)S(1)}, u32[]{:S(2)}, u32[]{:S(2)}) collective-permute-start(bf16[384,1152]{1,0:T(8,128)(2,1)} %image.1), channel_id=1, source_target_pairs={{0,2},{1,0},{2,3},{3,1},{4,6},{5,4},{6,7},{7,5},{8,10},{9,8},{10,1... | collective-permute-start | bytes 2654216 | tf_op jit(solution)/shard_map/ppermute | solution.py:32
  2.7 19.8 %collective-permute-start.4 = (bf16[384,1152]{1,0:T(8,128)(2,1)}, bf16[384,1152]{1,0:T(8,128)(2,1)S(1)}, u32[]{:S(2)}, u32[]{:S(2)}) collective-permute-start(bf16[384,1152]{1,0:T(8,128)(2,1)} %text.1), channel_id=1, source_target_pairs={{0,2},{1,0},{2,3},{3,1},{4,6},{5,4},{6,7},{7,5},{8,10},{9,8},{10,1... | collective-permute-start | bytes 2654216 | tf_op jit(solution)/shard_map/ppermute | solution.py:32
  3.4 22.1 %collective-permute-start = (bf16[384,1152]{1,0:T(8,128)(2,1)}, bf16[384,1152]{1,0:T(8,128)(2,1)S(1)}, u32[]{:S(2)}, u32[]{:S(2)}) collective-permute-start(bf16[384,1152]{1,0:T(8,128)(2,1)} %text.1), channel_id=1, source_target_pairs={{0,2},{1,3},{2,4},{3,5},{4,6},{5,7},{6,8},{7,9},{8,10},{9,11},{10,... | collective-permute-start | bytes 2654216 | tf_op jit(solution)/shard_map/ppermute | solution.py:32
  4.3 22.2 %collective-permute-start.1 = (bf16[384,1152]{1,0:T(8,128)(2,1)}, bf16[384,1152]{1,0:T(8,128)(2,1)S(1)}, u32[]{:S(2)}, u32[]{:S(2)}) collective-permute-start(bf16[384,1152]{1,0:T(8,128)(2,1)} %image.1), channel_id=1, source_target_pairs={{0,30},{1,31},{2,0},{3,1},{4,2},{5,3},{6,4},{7,5},{8,6},{9,7},{10,... | collective-permute-start | bytes 2654216 | tf_op jit(solution)/shard_map/ppermute | solution.py:32
  23.6 4.8 %collective-permute-start.5 = (bf16[384,1152]{1,0:T(8,128)(2,1)S(1)}, bf16[384,1152]{1,0:T(8,128)(2,1)}, u32[]{:S(2)}, u32[]{:S(2)}) collective-permute-start(bf16[384,1152]{1,0:T(8,128)(2,1)S(1)} %get-tuple-element.22), channel_id=1, source_target_pairs={{0,2},{1,3},{2,0},{3,1},{4,6},{5,7},{6,4},{7,5},{8,10},{9,11},{10,... | collective-permute-start | bytes 2654216 | tf_op jit(solution)/shard_map/ppermute | solution.py:32
  25.4 2.0 %copy-start.2 = (bf16[384,1152]{1,0:T(8,128)(2,1)}, bf16[384,1152]{1,0:T(8,128)(2,1)S(1)}, u32[]{:S(2)}) copy-start(bf16[384,1152]{1,0:T(8,128)(2,1)S(1)} %collective-permute-done.inner_u.text_two) | copy-start | bytes 2654212
  26.5 1.2 %copy-start.3 = (bf16[384,1152]{1,0:T(8,128)(2,1)}, bf16[384,1152]{1,0:T(8,128)(2,1)S(1)}, u32[]{:S(2)}) copy-start(bf16[384,1152]{1,0:T(8,128)(2,1)S(1)} %collective-permute-done.1.inner_w.image_two) | copy-start | bytes 2654212
  27.7 21.3 %collective-permute-start.2 = (bf16[384,1152]{1,0:T(8,128)(2,1)}, bf16[384,1152]{1,0:T(8,128)(2,1)S(1)}, u32[]{:S(2)}, u32[]{:S(2)}) collective-permute-start(bf16[384,1152]{1,0:T(8,128)(2,1)} %pick.1), channel_id=1, source_target_pairs={{0,1},{1,0},{2,3},{3,2},{4,5},{5,4},{6,7},{7,6},{8,9},{9,8},{10,11... | collective-permute-start | bytes 2654216 | tf_op jit(solution)/shard_map/ppermute | solution.py:32
  28.5 24.0 %collective-permute-start.8 = (bf16[384,1152]{1,0:T(8,128)(2,1)}, bf16[384,1152]{1,0:T(8,128)(2,1)S(1)}, u32[]{:S(2)}, u32[]{:S(2)}) collective-permute-start(bf16[384,1152]{1,0:T(8,128)(2,1)} %get-tuple-element.21.outer_b3), channel_id=1, source_target_pairs={{0,30},{1,3},{2,0},{3,5},{4,2},{5,7},{6,4},{7,9},{8,6},{9,11},{10,... | collective-permute-start | bytes 2654216 | tf_op jit(solution)/shard_map/ppermute | solution.py:32
  28.5 24.0 %collective-permute-start.7 = (bf16[384,1152]{1,0:T(8,128)(2,1)}, bf16[384,1152]{1,0:T(8,128)(2,1)S(1)}, u32[]{:S(2)}, u32[]{:S(2)}) collective-permute-start(bf16[384,1152]{1,0:T(8,128)(2,1)} %collective-permute-done.5.inner_b3), channel_id=1, source_target_pairs={{0,2},{1,31},{2,4},{3,1},{4,6},{5,3},{6,8},{7,5},{8,10},{9,7},{10,... | collective-permute-start | bytes 2654216 | tf_op jit(solution)/shard_map/ppermute | solution.py:32
  52.0 2.6 %collective-permute-start.6 = (bf16[384,1280]{1,0:T(8,128)(2,1)S(1)}, bf16[384,1280]{1,0:T(8,128)(2,1)S(1)}, u32[]{:S(2)}, u32[]{:S(2)}) collective-permute-start(bf16[384,1280]{1,0:T(8,128)(2,1)S(1)} %get-tuple-element.26), channel_id=1, source_target_pairs={{0,2},{1,3},{2,0},{3,1},{4,6},{5,7},{6,4},{7,5},{8,10},{9,11},{10,... | collective-permute-start | bytes 2949128 | tf_op jit(solution)/shard_map/ppermute | solution.py:32

commit v12 on v10

--- a/solution.py
+++ b/solution.py
@@ -11,6 +11,8 @@
 F32 = jnp.float32
 BF16 = jnp.bfloat16
 VMEM_LIMIT = 16 * 1024 * 1024
+
+HIDES = 10**10
 
 X_SWAP = {0: (1, 0), 1: (0, 0), 2: (3, 0), 3: (2, 0)}
 CORE_SWAP = {0: (2, 0), 1: (3, 0), 2: (0, 0), 3: (1, 0)}
@@ -47,6 +49,8 @@
 
 
 def softplus_lanes(p):
+    if p.shape[1] % 128:
+        p = jnp.pad(p, ((0, 0), (0, -p.shape[1] % 128)))
     total = None
     parts = [p[:, start : start + 128] for start in range(0, p.shape[1], 128)]
     for first in range(0, len(parts), 3):
@@ -71,10 +75,11 @@
 
 
 def pair_step(own, blocks, scale, shift, work):
-    rows = blocks[0].shape[0]
-    for place, raw in enumerate(blocks):
-        work[place * rows : (place + 1) * rows] = unit_rows(raw)[0].astype(BF16)
-    return terms(own, work[: len(blocks) * rows], scale, shift)
+    end = 0
+    for raw in blocks:
+        start, end = end, end + raw.shape[0]
+        work[start:end] = unit_rows(raw)[0].astype(BF16)
+    return terms(own, work[:end], scale, shift)
 
 
 def terms(own, others, scale, shift):
@@ -92,6 +97,11 @@
     return [pl.ds(place * (rows // count), rows // count) for place in range(count)]
 
 
+def chunk_rows(rows, sixths):
+    first = sixths * rows // 6 // 16 * 16
+    return first, rows - first
+
+
 def scalar_pair(scalars):
     return scalars[0:1, 0:1], scalars[1:2, 0:1]
 
@@ -106,38 +116,50 @@
 
 def sort_kernel(image, text, u, w, sems):
     def move(image_to, text_to):
+        copies = []
+        for source, target in ((image, image_to), (text, text_to)):
+            for part in row_parts(image.shape[0]):
+                sem = sems.at[len(copies)]
+                copies.append(pltpu.make_async_copy(source.at[part], target.at[part], sem))
+        for copy in copies:
+            copy.start()
+        for copy in copies:
+            copy.wait()
+
+    u_is_image = image_is_u()
+
+    @pl.when(u_is_image)
+    def _():
+        move(u, w)
+
+    @pl.when(jnp.logical_not(u_is_image))
+    def _():
+        move(w, u)
+
+
+def pick_kernel(when_outer, when_inner, first, second, sems):
+    def move(source):
+        split = first.shape[0]
         copies = [
-            pltpu.make_async_copy(image, image_to, sems.at[0]),
-            pltpu.make_async_copy(text, text_to, sems.at[1]),
+            pltpu.make_async_copy(source.at[pl.ds(0, split)], first, sems.at[0]),
+            pltpu.make_async_copy(source.at[pl.ds(split, second.shape[0])], second, sems.at[1]),
         ]
         for copy in copies:
             copy.start()
         for copy in copies:
             copy.wait()
 
-    u_is_image = image_is_u()
-
-    @pl.when(u_is_image)
-    def _():
-        move(u, w)
-
-    @pl.when(jnp.logical_not(u_is_image))
-    def _():
-        move(w, u)
-
-
-def pick_kernel(when_outer, when_inner, picked, sem):
     @pl.when(is_outer())
     def _():
-        pltpu.async_copy(when_outer, picked, sem).wait()
+        move(when_outer)
 
     @pl.when(jnp.logical_not(is_outer()))
     def _():
-        pltpu.async_copy(when_inner, picked, sem).wait()
+        move(when_inner)
 
 
 def near_kernel(
-    scalars, image, text, b1, b2, b3,
+    scalars, image, text, b1, b2, b3_first, b3_second,
     z_pair, unit_u, unit_w, inverse_u, inverse_w, grad_u, grad_w, loss, work, z_w,
 ):
     u_is_image = image_is_u()
@@ -168,17 +190,35 @@
     term, row_loss = pair_step(z_u, (b2[...],), scale, shift, work)
     grad_u[...] += term
     total = total + u_weight * row_loss
-    term, row_loss = pair_step(z_w[...], (b1[...], b3[...]), scale, shift, work)
+    term, row_loss = pair_step(z_w[...], (b1[...], b3_first[...], b3_second[...]), scale, shift, work)
     z_pair[zi.shape[0] :] = work[: zi.shape[0]]
     grad_w[...] += term
     loss[...] = total + (1.0 - u_weight) * row_loss
 
 
-def fifth_kernel(scalars, b5, z_pair, grad_in, loss_in, grad_u, loss, for_partner, work):
-    rows, width = b5.shape
+def fifth_first_kernel(scalars, b5, z_pair, grad_in, loss_in, grad_u, loss, for_partner, work):
+    rows, width = grad_u.shape
     term, row_loss = pair_step(z_pair[...], (b5[...],), *scalar_pair(scalars), work)
-    for_partner[:, :width] = term[rows:].astype(BF16)
-    for_partner[:, width:] = row_loss[rows:].astype(BF16)
+    for_partner[:, :width] = term[rows:]
+    for_partner[:, width:] = row_loss[rows:]
+    grad_u[...] = grad_in[...] + term[:rows]
+    loss[...] = loss_in[...] + image_is_u().astype(F32) * row_loss[:rows]
+
+
+def fourth_first_kernel(scalars, b4, z_pair, grad_in, loss_in, grad_u, loss, work):
+    rows = grad_u.shape[0]
+    term, row_loss = pair_step(z_pair[:rows], (b4[...],), *scalar_pair(scalars), work)
+    grad_u[...] = grad_in[...] + term
+    loss[...] = loss_in[...] + image_is_u().astype(F32) * row_loss
+
+
+def fifth_second_kernel(
+    scalars, b5, z_pair, grad_in, loss_in, partner_in, grad_u, loss, for_partner, work
+):
+    rows, width = grad_u.shape
+    term, row_loss = pair_step(z_pair[...], (b5[...],), *scalar_pair(scalars), work)
+    for_partner[:, :width] = (partner_in[:, :width] + term[rows:]).astype(BF16)
+    for_partner[:, width:] = (partner_in[:, width:] + row_loss[rows:]).astype(BF16)
     grad_u[...] = grad_in[...] + term[:rows]
     loss[...] = loss_in[...] + image_is_u().astype(F32) * row_loss[:rows]
 
@@ -245,17 +285,20 @@
     partial = jax.ShapeDtypeStruct((rows, 128), F32)
     line = jax.ShapeDtypeStruct((rows,), F32)
     raw = pltpu.VMEM((rows, width), BF16)
-    copies = pltpu.SemaphoreType.DMA((4,))
+    copies = pltpu.SemaphoreType.DMA((6,))
 
     def in_hbm(*arrays):
         return [pltpu.with_memory_space_constraint(x, pltpu.HBM) for x in arrays]
 
 
-    def pick(when_outer, when_inner, out):
-        sem = pltpu.SemaphoreType.DMA
+    def pick(when_outer, when_inner, space, sixths):
+        outs = [space((size, width), BF16) for size in chunk_rows(rows, sixths)]
         return call(
-            pick_kernel, [ANY] * 2, (when_outer, when_inner), [ANY], (out,), "pick", (sem,)
-        )[0]
+            pick_kernel, [ANY] * 2, (when_outer, when_inner), [ANY] * 2, outs, "pick", (copies,)
+        )
+
+    def in_vmem(*arrays):
+        return [pltpu.with_memory_space_constraint(x, pltpu.VMEM) for x in arrays]
 
     def compute(kernel, args, outs, name, scratch, flops=1):
         in_specs = [VMEM] * (1 + len(args))
@@ -273,34 +316,45 @@
     )
     slot1 = send(w, CORE_SWAP)
     slot2 = send(u, GROUP_SHIFT)
-    slot3 = send(pick(slot1, u, block), X_SWAP)
-    slot4 = send(slot3, GROUP_SHIFT)
-    slot5 = send(pick(w, slot2, pltpu.HBM((rows, width), BF16)), X_SWAP)
-    slot3, score_scaling, score_shift = lax.optimization_barrier((slot3, score_scaling, score_shift))
+    slot3 = [send(chunk, X_SWAP) for chunk in pick(slot1, u, jax.ShapeDtypeStruct, 3)]
+    slot4 = in_vmem(*[send(chunk, GROUP_SHIFT) for chunk in slot3])
+    slot5 = in_vmem(*[send(chunk, X_SWAP) for chunk in pick(w, slot2, pltpu.HBM, 4)])
     first = lax.broadcasted_iota(jnp.int32, (8, 128), 0) == 0
     scalars = jnp.where(first, score_scaling, score_shift)
     z_pair, unit_u, unit_w, inverse_u, inverse_w, grad_u, grad_w, loss = compute(
         near_kernel,
-        (*in_hbm(image, text), slot1, *in_hbm(slot2, slot3)),
+        (*in_hbm(image, text), slot1, *in_hbm(slot2, *slot3)),
         (pair, sums, sums, column, column, sums, sums, partial),
         "near_blocks",
         (pltpu.VMEM((2 * rows, width), BF16), raw),
-    )
+        HIDES // 5,
+    )
+    both = width + 128
     grad_u, loss, for_partner = compute(
-        fifth_kernel,
-        (pltpu.with_memory_space_constraint(slot5, pltpu.VMEM), z_pair, grad_u, loss),
-        (sums, partial, jax.ShapeDtypeStruct((rows, width + 128), BF16)),
-        "fifth_block",
+        fifth_first_kernel,
+        (slot5[0], z_pair, grad_u, loss),
+        (sums, partial, jax.ShapeDtypeStruct((rows, both), F32)),
+        "fifth_first",
+        (raw,),
+    )
+    grad_u, loss = compute(
+        fourth_first_kernel, (slot4[0], z_pair, grad_u, loss), (sums, partial), "fourth_first", (raw,)
+    )
+    grad_u, loss, for_partner = compute(
+        fifth_second_kernel,
+        (slot5[1], z_pair, grad_u, loss, for_partner),
+        (sums, partial, jax.ShapeDtypeStruct((rows, both), BF16)),
+        "fifth_second",
         (raw,),
     )
     last = send(for_partner, CORE_SWAP)
     done_u, loss = compute(
         u_kernel,
-        (pltpu.with_memory_space_constraint(slot4, pltpu.VMEM), z_pair, grad_u, loss, unit_u, inverse_u),
+        (slot4[1], z_pair, grad_u, loss, unit_u, inverse_u),
         (block, partial),
         "finish_u",
         (raw,),
-        10**10,
+        HIDES,
     )
     image_grad, text_grad, loss_rows = call(
         w_kernel,

time: 55 us -> 56 us (1.018)
  Pallas kernels: 18.6 us -> 22.1 us
  waiting for transfers between devices: 25.5 us -> 22 us
  starting transfers between devices: 8.62 us -> 9.47 us
    pallas_call x7 -> x9, Pallas kernels: 18.6 us -> 22.1 us  [call(): pl.pallas_call(kernel, out_shape=outs, in_specs=in_specs, out_specs=out_s...]
    ppermute x6 -> x9, waiting for transfers between devices: 25.5 us -> 22 us  [send(): return lax.ppermute(value, AXES, pairs)]
    ppermute x6 -> x9, starting transfers between devices: 8.62 us -> 9.47 us  [send(): return lax.ppermute(value, AXES, pairs)]
  transfers between devices with their start and end apart: 6 -> 9, of which waited for: 3 -> 2; matrix products, arithmetic and copies ran while one was open for 0% -> 0% of each run, Pallas kernels for 27% -> 33%
where the time goes in v12:
time: 56 us; the launch traced here: 55.7 us
  Pallas kernels  22.1 us (39%)
  waiting for transfers between devices  22 us (39%)
  starting transfers between devices  9.47 us (17%)
  between operations  2.03 us (4%)
    pallas_call x9, Pallas kernels, call(): pl.pallas_call(kernel, out_shape=outs, in_specs=in_specs, out_specs=out_s...  22.1 us
    ppermute x9, waiting for transfers between devices, send(): return lax.ppermute(value, AXES, pairs)  22 us
    ppermute x9, starting transfers between devices, send(): return lax.ppermute(value, AXES, pairs)  9.47 us
  transfers between devices with their start and end apart: 9, of which 2 were waited for; matrix products, arithmetic and copies ran while one was open for 0% of the time, Pallas kernels for 33%

profile of v12, /device:TPU:1, one launch (start us, length us, event | category | flops | bytes accessed | tf_op | source)
XLA Modules:
  0.0 55.7 jit_solution(11393898033749201395)
XLA Ops:
  0.6 1.5 %sort.1 = (bf16[384,1152]{1,0:T(8,128)(2,1)S(1)}, bf16[384,1152]{1,0:T(8,128)(2,1)S(1)}) custom-call(bf16[384,1152]{1,0:T(8,128)(2,1)} %image.3, bf16[384,1152]{1,0:T(8,128)(2,1)} %text.3), custom_call_target="tpu_custom_call" | custom-call | flops 1 | bytes 1 | tf_op jit(solution)/shard_map/sort/pallas_call | solution.py:267
  2.1 0.1 collective-permute-start.2
  2.2 2.7 %collective-permute-start = (bf16[384,1152]{1,0:T(8,128)(2,1)S(1)}, bf16[384,1152]{1,0:T(8,128)(2,1)S(1)}, u32[]{:S(2)}, u32[]{:S(2)}) collective-permute-start(bf16[384,1152]{1,0:T(8,128)(2,1)S(1)} %get-tuple-element.31.when_inner), channel_id=1, source_target_pairs={{0,30},{1,31},{2,4},{3,5},{4,2},{5,3},{6,8},{7,9},{8,6},{9,7},{10,... | collective-permute-start | bytes 2654216 | tf_op jit(solution)/shard_map/ppermute | solution.py:30
  4.9 0.0 collective-permute-done.2.when_outer.b1
  4.9 0.6 pick.3
  5.4 2.1 %collective-permute-start.3 = (bf16[192,1152]{1,0:T(8,128)(2,1)S(1)}, bf16[192,1152]{1,0:T(8,128)(2,1)}, u32[]{:S(2)}, u32[]{:S(2)}) collective-permute-start(bf16[192,1152]{1,0:T(8,128)(2,1)S(1)} %get-tuple-element.33), channel_id=1, source_target_pairs={{0,1},{1,0},{2,3},{3,2},{4,5},{5,4},{6,7},{7,6},{8,9},{9,8},{10,11... | collective-permute-start | bytes 1327112 | tf_op jit(solution)/shard_map/ppermute | solution.py:30
  7.6 0.1 collective-permute-start.4
  7.7 21.4 %collective-permute-done.when_inner.b2 = bf16[384,1152]{1,0:T(8,128)(2,1)S(1)} collective-permute-done((bf16[384,1152]{1,0:T(8,128)(2,1)S(1)}, bf16[384,1152]{1,0:T(8,128)(2,1)S(1)}, u32[]{:S(2)}, u32[]{:S(2)}) %collective-permute-start) | collective-permute-done | bytes 884768 | tf_op jit(solution)/shard_map/ppermute | solution.py:30
  29.1 0.0 copy-start
  29.1 1.0 %pick.2 = (bf16[256,1152]{1,0:T(8,128)(2,1)}, bf16[128,1152]{1,0:T(8,128)(2,1)}) custom-call(bf16[384,1152]{1,0:T(8,128)(2,1)S(1)} %get-tuple-element.30.when_outer, bf16[384,1152]{1,0:T(8,128)(2,1)S(1)} %collective-permute-done.when_inner.b2), custom_call_target="tpu_custom_call" | custom-call | flops 1 | bytes 1 | tf_op jit(solution)/shard_map/pick/pallas_call | solution.py:267
  30.1 1.3 %collective-permute-start.6 = (bf16[256,1152]{1,0:T(8,128)(2,1)}, bf16[256,1152]{1,0:T(8,128)(2,1)S(1)}, u32[]{:S(2)}, u32[]{:S(2)}) collective-permute-start(bf16[256,1152]{1,0:T(8,128)(2,1)} %get-tuple-element.36), channel_id=1, source_target_pairs={{0,1},{1,0},{2,3},{3,2},{4,5},{5,4},{6,7},{7,6},{8,9},{9,8},{10,11... | collective-permute-start | bytes 1769480 | tf_op jit(solution)/shard_map/ppermute | solution.py:30
  31.4 0.0 collective-permute-done.3.b3_first
  31.4 2.8 %collective-permute-start.5 = (bf16[192,1152]{1,0:T(8,128)(2,1)}, bf16[192,1152]{1,0:T(8,128)(2,1)S(1)}, u32[]{:S(2)}, u32[]{:S(2)}) collective-permute-start(bf16[192,1152]{1,0:T(8,128)(2,1)} %collective-permute-done.3.b3_first), channel_id=1, source_target_pairs={{0,30},{1,31},{2,4},{3,5},{4,2},{5,3},{6,8},{7,9},{8,6},{9,7},{10,... | collective-permute-start | bytes 1327112 | tf_op jit(solution)/shard_map/ppermute | solution.py:30
  34.1 0.0 collective-permute-done.4.b3_second
  34.1 0.1 collective-permute-start.8
  35.5 0.3 collective-permute-start.1
  35.8 0.1 iota.7.scalars
  35.9 0.0 copy-done
  35.9 8.8 %near_blocks.1 = (bf16[768,1152]{1,0:T(8,128)(2,1)S(1)}, f32[384,1152]{1,0:T(8,128)S(1)}, f32[384,1152]{1,0:T(8,128)S(1)}, f32[384,1]{1,0:T(8,128)S(1)}, f32[384...) custom-call(f32[8,128]{1,0:T(8,128)S(1)} %iota.7.scalars, ...), custom_call_target="tpu_custom_call" | custom-call | flops 2000000000 | bytes 1 | tf_op jit(solution)/shard_map/near_blocks/pallas_call | solution.py:267
  44.7 0.0 collective-permute-done.6.b5
  44.7 2.7 %fifth_first.1 = (f32[384,1152]{1,0:T(8,128)S(1)}, f32[384,128]{1,0:T(8,128)S(1)}, f32[384,1280]{1,0:T(8,128)S(1)}) custom-call(f32[8,128]{1,0:T(8,128)S(1)} %iota.7.scalars, bf16[256,1152]{1,0:T(8,128)(2,1)S(1)} %collective-permute-done.6.b5, bf16[768,1152]{1,0:T(8,128)(2,1)S(1)} %get-tuple-element.35.z_pair, f32[384,1152]{1,0:T(8,128)S(1)} %get-tuple-element.37.grad_in, ...), custom_call_target="tpu_custom_call" | custom-call | flops 1 | bytes 1 | tf_op jit(solution)/shard_map/fifth_first/pallas_call | solution.py:267
  47.4 0.0 collective-permute-done.5.b4
  47.4 1.6 %fourth_first.1 = (f32[384,1152]{1,0:T(8,128)S(1)}, f32[384,128]{1,0:T(8,128)S(1)}) custom-call(f32[8,128]{1,0:T(8,128)S(1)} %iota.7.scalars, bf16[192,1152]{1,0:T(8,128)(2,1)S(1)} %collective-permute-done.5.b4, bf16[768,1152]{1,0:T(8,128)(2,1)S(1)} %get-tuple-element.35.z_pair, f32[384,1152]{1,0:T(8,128)S(1)} %get-tuple-element.39.grad_in, ...), custom_call_target="tpu_custom_call" | custom-call | flops 1 | bytes 1 | tf_op jit(solution)/shard_map/fourth_first/pallas_call | solution.py:267
  49.0 0.0 collective-permute-done.1.b5
  49.0 2.1 %fifth_second.1 = (f32[384,1152]{1,0:T(8,128)S(1)}, f32[384,128]{1,0:T(8,128)S(1)}, bf16[384,1280]{1,0:T(8,128)(2,1)S(1)}) custom-call(f32[8,128]{1,0:T(8,128)S(1)} %iota.7.scalars, bf16[128,1152]{1,0:T(8,128)(2,1)S(1)} %collective-permute-done.1.b5, bf16[768,1152]{1,0:T(8,128)(2,1)S(1)} %get-tuple-element.35.z_pair, ...), custom_call_target="tpu_custom_call" | custom-call | flops 1 | bytes 1 | tf_op jit(solution)/shard_map/fifth_second/pallas_call | solution.py:267
  51.0 0.1 collective-permute-start.7
  51.1 0.0 collective-permute-done.8.b4
  51.1 1.9 %finish_u.1 = (bf16[384,1152]{1,0:T(8,128)(2,1)S(1)}, f32[384,128]{1,0:T(8,128)S(1)}) custom-call(f32[8,128]{1,0:T(8,128)S(1)} %iota.7.scalars, bf16[192,1152]{1,0:T(8,128)(2,1)S(1)} %collective-permute-done.8.b4, bf16[768,1152]{1,0:T(8,128)(2,1)S(1)} %get-tuple-element.35.z_pair, f32[384,1152]{1,0:T(8,128)S(1)} %get-tuple-element.46.grad_u, ...), custom_call_target="tpu_custom_call" | custom-call | flops 10000000000 | bytes 1 | tf_op jit(solution)/shard_map/finish_u/pallas_call | solution.py:267
  53.1 0.6 %collective-permute-done.7.last = bf16[384,1280]{1,0:T(8,128)(2,1)S(1)} collective-permute-done((bf16[384,1280]{1,0:T(8,128)(2,1)S(1)}, bf16[384,1280]{1,0:T(8,128)(2,1)S(1)}, u32[]{:S(2)}, u32[]{:S(2)}) %collective-permute-start.7) | collective-permute-done | bytes 983072 | tf_op jit(solution)/shard_map/ppermute | solution.py:30
  53.7 2.1 %finish_w.1 = (bf16[384,1152]{1,0:T(8,128)(2,1)}, bf16[384,1152]{1,0:T(8,128)(2,1)}, f32[384]{0:T(512)}) custom-call(bf16[384,1280]{1,0:T(8,128)(2,1)S(1)} %collective-permute-done.7.last, f32[384,1152]{1,0:T(8,128)S(1)} %get-tuple-element.45.grad_w, f32[384,128]{1,0:T(8,128)S(1)} %get-tuple-element.50.loss_in, f32[384,1152]{1,0:T(8,128)S(1)} %get-tuple-element.51.unit, ...), custom_call_target="tpu_custom_call" | custom-call | flops 1 | bytes 1 | tf_op jit(solution)/shard_map/finish_w/pallas_call | solution.py:267
  (1 shorter events, 0.0 us)
Async XLA Ops:
  2.1 2.8 %collective-permute-start.2 = (bf16[384,1152]{1,0:T(8,128)(2,1)S(1)}, bf16[384,1152]{1,0:T(8,128)(2,1)S(1)}, u32[]{:S(2)}, u32[]{:S(2)}) collective-permute-start(bf16[384,1152]{1,0:T(8,128)(2,1)S(1)} %get-tuple-element.30.when_outer), channel_id=1, source_target_pairs={{0,2},{1,3},{2,0},{3,1},{4,6},{5,7},{6,4},{7,5},{8,10},{9,11},{10,... | collective-permute-start | bytes 2654216 | tf_op jit(solution)/shard_map/ppermute | solution.py:30
  2.2 26.9 %collective-permute-start = (bf16[384,1152]{1,0:T(8,128)(2,1)S(1)}, bf16[384,1152]{1,0:T(8,128)(2,1)S(1)}, u32[]{:S(2)}, u32[]{:S(2)}) collective-permute-start(bf16[384,1152]{1,0:T(8,128)(2,1)S(1)} %get-tuple-element.31.when_inner), channel_id=1, source_target_pairs={{0,30},{1,31},{2,4},{3,5},{4,2},{5,3},{6,8},{7,9},{8,6},{9,7},{10,... | collective-permute-start | bytes 2654216 | tf_op jit(solution)/shard_map/ppermute | solution.py:30
  5.4 25.9 %collective-permute-start.3 = (bf16[192,1152]{1,0:T(8,128)(2,1)S(1)}, bf16[192,1152]{1,0:T(8,128)(2,1)}, u32[]{:S(2)}, u32[]{:S(2)}) collective-permute-start(bf16[192,1152]{1,0:T(8,128)(2,1)S(1)} %get-tuple-element.33), channel_id=1, source_target_pairs={{0,1},{1,0},{2,3},{3,2},{4,5},{5,4},{6,7},{7,6},{8,9},{9,8},{10,11... | collective-permute-start | bytes 1327112 | tf_op jit(solution)/shard_map/ppermute | solution.py:30
  7.6 26.6 %collective-permute-start.4 = (bf16[192,1152]{1,0:T(8,128)(2,1)S(1)}, bf16[192,1152]{1,0:T(8,128)(2,1)}, u32[]{:S(2)}, u32[]{:S(2)}) collective-permute-start(bf16[192,1152]{1,0:T(8,128)(2,1)S(1)} %get-tuple-element.34), channel_id=1, source_target_pairs={{0,1},{1,0},{2,3},{3,2},{4,5},{5,4},{6,7},{7,6},{8,9},{9,8},{10,11... | collective-permute-start | bytes 1327112 | tf_op jit(solution)/shard_map/ppermute | solution.py:30
  29.1 6.8 %copy-start = (bf16[384,1152]{1,0:T(8,128)(2,1)}, bf16[384,1152]{1,0:T(8,128)(2,1)S(1)}, u32[]{:S(2)}) copy-start(bf16[384,1152]{1,0:T(8,128)(2,1)S(1)} %collective-permute-done.when_inner.b2) | copy-start | bytes 2654212
  30.1 14.6 %collective-permute-start.6 = (bf16[256,1152]{1,0:T(8,128)(2,1)}, bf16[256,1152]{1,0:T(8,128)(2,1)S(1)}, u32[]{:S(2)}, u32[]{:S(2)}) collective-permute-start(bf16[256,1152]{1,0:T(8,128)(2,1)} %get-tuple-element.36), channel_id=1, source_target_pairs={{0,1},{1,0},{2,3},{3,2},{4,5},{5,4},{6,7},{7,6},{8,9},{9,8},{10,11... | collective-permute-start | bytes 1769480 | tf_op jit(solution)/shard_map/ppermute | solution.py:30
  31.4 16.0 %collective-permute-start.5 = (bf16[192,1152]{1,0:T(8,128)(2,1)}, bf16[192,1152]{1,0:T(8,128)(2,1)S(1)}, u32[]{:S(2)}, u32[]{:S(2)}) collective-permute-start(bf16[192,1152]{1,0:T(8,128)(2,1)} %collective-permute-done.3.b3_first), channel_id=1, source_target_pairs={{0,30},{1,31},{2,4},{3,5},{4,2},{5,3},{6,8},{7,9},{8,6},{9,7},{10,... | collective-permute-start | bytes 1327112 | tf_op jit(solution)/shard_map/ppermute | solution.py:30
  34.1 17.0 %collective-permute-start.8 = (bf16[192,1152]{1,0:T(8,128)(2,1)}, bf16[192,1152]{1,0:T(8,128)(2,1)S(1)}, u32[]{:S(2)}, u32[]{:S(2)}) collective-permute-start(bf16[192,1152]{1,0:T(8,128)(2,1)} %collective-permute-done.4.b3_second), channel_id=1, source_target_pairs={{0,30},{1,31},{2,4},{3,5},{4,2},{5,3},{6,8},{7,9},{8,6},{9,7},{10,... | collective-permute-start | bytes 1327112 | tf_op jit(solution)/shard_map/ppermute | solution.py:30
  35.5 13.5 %collective-permute-start.1 = (bf16[128,1152]{1,0:T(8,128)(2,1)}, bf16[128,1152]{1,0:T(8,128)(2,1)S(1)}, u32[]{:S(2)}, u32[]{:S(2)}) collective-permute-start(bf16[128,1152]{1,0:T(8,128)(2,1)} %get-tuple-element.32), channel_id=1, source_target_pairs={{0,1},{1,0},{2,3},{3,2},{4,5},{5,4},{6,7},{7,6},{8,9},{9,8},{10,11... | collective-permute-start | bytes 884744 | tf_op jit(solution)/shard_map/ppermute | solution.py:30
  51.0 2.6 %collective-permute-start.7 = (bf16[384,1280]{1,0:T(8,128)(2,1)S(1)}, bf16[384,1280]{1,0:T(8,128)(2,1)S(1)}, u32[]{:S(2)}, u32[]{:S(2)}) collective-permute-start(bf16[384,1280]{1,0:T(8,128)(2,1)S(1)} %get-tuple-element.44), channel_id=1, source_target_pairs={{0,2},{1,3},{2,0},{3,1},{4,6},{5,7},{6,4},{7,5},{8,10},{9,11},{10,... | collective-permute-start | bytes 2949128 | tf_op jit(solution)/shard_map/ppermute | solution.py:30

commit v13 on v10

--- a/solution.py
+++ b/solution.py
@@ -1,3 +1,5 @@
+import functools
+
 import jax
 import jax.numpy as jnp
 from jax import lax
@@ -78,17 +80,23 @@
 
 
 def terms(own, others, scale, shift):
-    p = jnp.exp(scale * dot_nt(own, others) + shift)
-    coef = (sigmoid_of(p) * scale).astype(BF16)
-    return dot_nn(coef, others), softplus_lanes(p)
+    half = own.shape[0] // 2
+    scores = [dot_nt(own[:half], others), dot_nt(own[half:], others)]
+    products, losses = [], []
+    for score in scores:
+        p = jnp.exp(scale * score + shift)
+        coef = (sigmoid_of(p) * scale).astype(BF16)
+        products.append(dot_nn(coef, others))
+        losses.append(softplus_lanes(p))
+    return jnp.concatenate(products), jnp.concatenate(losses)
 
 
 def project(unit, inverse, grad):
     return ((grad - unit * jnp.sum(unit * grad, axis=1, keepdims=True)) * inverse).astype(BF16)
 
 
-def row_parts(rows):
-    count = 3 if rows % 48 == 0 else 1
+def row_parts(rows, wanted):
+    count = wanted if rows % (16 * wanted) == 0 else 1
     return [pl.ds(place * (rows // count), rows // count) for place in range(count)]
 
 
@@ -104,26 +112,25 @@
     return lax.rem(lax.axis_index("blk"), 2) == lax.axis_index("inner")
 
 
-def sort_kernel(image, text, u, w, sems):
-    def move(image_to, text_to):
-        copies = [
-            pltpu.make_async_copy(image, image_to, sems.at[0]),
-            pltpu.make_async_copy(text, text_to, sems.at[1]),
-        ]
+def own_kernel(image_core, image, text, block, sems):
+    def move(source):
+        copies = []
+        for place, part in enumerate(row_parts(block.shape[0], 3)):
+            copies.append(pltpu.make_async_copy(source.at[part], block.at[part], sems.at[place]))
         for copy in copies:
             copy.start()
         for copy in copies:
             copy.wait()
 
-    u_is_image = image_is_u()
-
-    @pl.when(u_is_image)
+    wants_image = lax.rem(lax.axis_index("blk"), 2) == image_core
+
+    @pl.when(wants_image)
     def _():
-        move(u, w)
-
-    @pl.when(jnp.logical_not(u_is_image))
+        move(image)
+
+    @pl.when(jnp.logical_not(wants_image))
     def _():
-        move(w, u)
+        move(text)
 
 
 def pick_kernel(when_outer, when_inner, picked, sem):
@@ -194,7 +201,7 @@
     last, grad_w, loss_in, unit, inverse, done_u, image_grad, text_grad, loss_rows, done_w, sems
 ):
     u_is_image = image_is_u()
-    parts = row_parts(done_w.shape[0])
+    parts = row_parts(done_w.shape[0], 6)
 
     def output(action, source, part, to_image, sem):
         @pl.when(to_image)
@@ -245,7 +252,7 @@
     partial = jax.ShapeDtypeStruct((rows, 128), F32)
     line = jax.ShapeDtypeStruct((rows,), F32)
     raw = pltpu.VMEM((rows, width), BF16)
-    copies = pltpu.SemaphoreType.DMA((4,))
+    copies = pltpu.SemaphoreType.DMA((7,))
 
     def in_hbm(*arrays):
         return [pltpu.with_memory_space_constraint(x, pltpu.HBM) for x in arrays]
@@ -262,16 +269,13 @@
         out_specs = [VMEM] * len(outs)
         return call(kernel, in_specs, (scalars, *args), out_specs, outs, name, scratch, flops)
 
-    u, w = call(
-        sort_kernel,
-        [ANY] * 2,
-        in_hbm(image, text),
-        [VMEM] * 2,
-        (block, block),
-        "sort",
-        (copies,),
-    )
+    def own(image_core):
+        kernel = functools.partial(own_kernel, image_core)
+        return call(kernel, [ANY] * 2, in_hbm(image, text), [VMEM], (block,), "own", (copies,))[0]
+
+    w = own(1)
     slot1 = send(w, CORE_SWAP)
+    u = own(0)
     slot2 = send(u, GROUP_SHIFT)
     slot3 = send(pick(slot1, u, block), X_SWAP)
     slot4 = send(slot3, GROUP_SHIFT)

time: 55 us -> 55.6 us (1.011)
  waiting for transfers between devices: 25.5 us -> 27.8 us
  starting transfers between devices: 8.62 us -> 7.04 us
    ppermute x6, waiting for transfers between devices: 25.5 us -> 27.8 us  [send(): return lax.ppermute(value, AXES, pairs)]
    ppermute x6, starting transfers between devices: 8.62 us -> 7.04 us  [send(): return lax.ppermute(value, AXES, pairs)]
    pallas_call x7 -> x8, Pallas kernels: 18.6 us -> 18.5 us  [call(): pl.pallas_call(kernel, out_shape=outs, in_specs=in_specs, out_specs=out_s...]
where the time goes in v13:
time: 55.6 us; the launch traced here: 55.4 us
  waiting for transfers between devices  27.8 us (50%)
  Pallas kernels  18.5 us (33%)
  starting transfers between devices  7.04 us (13%)
  between operations  2.01 us (4%)
    ppermute x6, waiting for transfers between devices, send(): return lax.ppermute(value, AXES, pairs)  27.8 us
    pallas_call x8, Pallas kernels, call(): pl.pallas_call(kernel, out_shape=outs, in_specs=in_specs, out_specs=out_s...  18.5 us
    ppermute x6, starting transfers between devices, send(): return lax.ppermute(value, AXES, pairs)  7.04 us
  transfers between devices with their start and end apart: 6, of which 3 were waited for; matrix products, arithmetic and copies ran while one was open for 0% of the time, Pallas kernels for 27%

profile of v13, /device:TPU:1, one launch (start us, length us, event | category | flops | bytes accessed | tf_op | source)
XLA Modules:
  0.0 55.4 jit_solution(4264227538580505600)
XLA Ops:
  0.6 1.2 %own.2.when_outer = bf16[384,1152]{1,0:T(8,128)(2,1)S(1)} custom-call(bf16[384,1152]{1,0:T(8,128)(2,1)} %image.5, bf16[384,1152]{1,0:T(8,128)(2,1)} %text.5), custom_call_target="tpu_custom_call" | custom-call | flops 1 | bytes 1 | tf_op jit(solution)/shard_map/own/pallas_call | solution.py:234
  1.9 0.1 collective-permute-start
  2.0 1.2 %own.3.when_inner = bf16[384,1152]{1,0:T(8,128)(2,1)S(1)} custom-call(bf16[384,1152]{1,0:T(8,128)(2,1)} %image.5, bf16[384,1152]{1,0:T(8,128)(2,1)} %text.5), custom_call_target="tpu_custom_call" | custom-call | flops 1 | bytes 1 | tf_op jit(solution)/shard_map/own/pallas_call | solution.py:234
  3.2 2.7 %collective-permute-start.2 = (bf16[384,1152]{1,0:T(8,128)(2,1)S(1)}, bf16[384,1152]{1,0:T(8,128)(2,1)S(1)}, u32[]{:S(2)}, u32[]{:S(2)}) collective-permute-start(bf16[384,1152]{1,0:T(8,128)(2,1)S(1)} %own.3.when_inner), channel_id=1, source_target_pairs={{0,30},{1,31},{2,4},{3,5},{4,2},{5,3},{6,8},{7,9},{8,6},{9,7},{10,... | collective-permute-start | bytes 2654216 | tf_op jit(solution)/shard_map/ppermute | solution.py:30
  5.9 0.0 collective-permute-done.when_outer.b1
  5.9 0.2 pick.2
  6.0 1.3 %collective-permute-start.1 = (bf16[384,1152]{1,0:T(8,128)(2,1)S(1)}, bf16[384,1152]{1,0:T(8,128)(2,1)}, u32[]{:S(2)}, u32[]{:S(2)}) collective-permute-start(bf16[384,1152]{1,0:T(8,128)(2,1)S(1)} %pick.2), channel_id=1, source_target_pairs={{0,1},{1,0},{2,3},{3,2},{4,5},{5,4},{6,7},{7,6},{8,9},{9,8},{10,11... | collective-permute-start | bytes 2654216 | tf_op jit(solution)/shard_map/ppermute | solution.py:30
  7.3 19.1 %collective-permute-done.2.when_inner.b2 = bf16[384,1152]{1,0:T(8,128)(2,1)S(1)} collective-permute-done((bf16[384,1152]{1,0:T(8,128)(2,1)S(1)}, bf16[384,1152]{1,0:T(8,128)(2,1)S(1)}, u32[]{:S(2)}, u32[]{:S(2)}) %collective-permute-start.2) | collective-permute-done | bytes 884768 | tf_op jit(solution)/shard_map/ppermute | solution.py:30
  26.5 0.0 copy-start
  26.5 0.9 %pick.3 = bf16[384,1152]{1,0:T(8,128)(2,1)} custom-call(bf16[384,1152]{1,0:T(8,128)(2,1)S(1)} %own.2.when_outer, bf16[384,1152]{1,0:T(8,128)(2,1)S(1)} %collective-permute-done.2.when_inner.b2), custom_call_target="tpu_custom_call" | custom-call | flops 1 | bytes 1 | tf_op jit(solution)/shard_map/pick/pallas_call | solution.py:234
  27.4 1.9 %collective-permute-start.3 = (bf16[384,1152]{1,0:T(8,128)(2,1)}, bf16[384,1152]{1,0:T(8,128)(2,1)S(1)}, u32[]{:S(2)}, u32[]{:S(2)}) collective-permute-start(bf16[384,1152]{1,0:T(8,128)(2,1)} %pick.3), channel_id=1, source_target_pairs={{0,1},{1,0},{2,3},{3,2},{4,5},{5,4},{6,7},{7,6},{8,9},{9,8},{10,11... | collective-permute-start | bytes 2654216 | tf_op jit(solution)/shard_map/ppermute | solution.py:30
  29.3 0.0 collective-permute-done.1.b3
  29.3 1.0 %collective-permute-start.5 = (bf16[384,1152]{1,0:T(8,128)(2,1)}, bf16[384,1152]{1,0:T(8,128)(2,1)S(1)}, u32[]{:S(2)}, u32[]{:S(2)}) collective-permute-start(bf16[384,1152]{1,0:T(8,128)(2,1)} %collective-permute-done.1.b3), channel_id=1, source_target_pairs={{0,30},{1,31},{2,4},{3,5},{4,2},{5,3},{6,8},{7,9},{8,6},{9,7},{10,... | collective-permute-start | bytes 2654216 | tf_op jit(solution)/shard_map/ppermute | solution.py:30
  31.6 0.1 iota.7.scalars
  31.7 0.0 copy-done
  31.7 8.5 %near_blocks.1 = (bf16[768,1152]{1,0:T(8,128)(2,1)S(1)}, f32[384,1152]{1,0:T(8,128)S(1)}, f32[384,1152]{1,0:T(8,128)S(1)}, f32[384,1]{1,0:T(8,128)S(1)}, f32[384...) custom-call(f32[8,128]{1,0:T(8,128)S(1)} %iota.7.scalars, ...), custom_call_target="tpu_custom_call" | custom-call | flops 1 | bytes 1 | tf_op jit(solution)/shard_map/near_blocks/pallas_call | solution.py:234
  40.1 6.3 %collective-permute-done.3.b5 = bf16[384,1152]{1,0:T(8,128)(2,1)S(1)} collective-permute-done((bf16[384,1152]{1,0:T(8,128)(2,1)}, bf16[384,1152]{1,0:T(8,128)(2,1)S(1)}, u32[]{:S(2)}, u32[]{:S(2)}) %collective-permute-start.3) | collective-permute-done | bytes 884768 | tf_op jit(solution)/shard_map/ppermute | solution.py:30
  46.4 2.6 %fifth_block.1 = (f32[384,1152]{1,0:T(8,128)S(1)}, f32[384,128]{1,0:T(8,128)S(1)}, bf16[384,1280]{1,0:T(8,128)(2,1)S(1)}) custom-call(f32[8,128]{1,0:T(8,128)S(1)} %iota.7.scalars, bf16[384,1152]{1,0:T(8,128)(2,1)S(1)} %collective-permute-done.3.b5, bf16[768,1152]{1,0:T(8,128)(2,1)S(1)} %get-tuple-element.25.z_pair, ...), custom_call_target="tpu_custom_call" | custom-call | flops 1 | bytes 1 | tf_op jit(solution)/shard_map/fifth_block/pallas_call | solution.py:234
  49.0 0.1 collective-permute-start.4
  49.1 2.3 %collective-permute-done.5.b4 = bf16[384,1152]{1,0:T(8,128)(2,1)S(1)} collective-permute-done((bf16[384,1152]{1,0:T(8,128)(2,1)}, bf16[384,1152]{1,0:T(8,128)(2,1)S(1)}, u32[]{:S(2)}, u32[]{:S(2)}) %collective-permute-start.5) | collective-permute-done | bytes 884768 | tf_op jit(solution)/shard_map/ppermute | solution.py:30
  51.4 1.8 %finish_u.1 = (bf16[384,1152]{1,0:T(8,128)(2,1)S(1)}, f32[384,128]{1,0:T(8,128)S(1)}) custom-call(f32[8,128]{1,0:T(8,128)S(1)} %iota.7.scalars, bf16[384,1152]{1,0:T(8,128)(2,1)S(1)} %collective-permute-done.5.b4, bf16[768,1152]{1,0:T(8,128)(2,1)S(1)} %get-tuple-element.25.z_pair, f32[384,1152]{1,0:T(8,128)S(1)} %get-tuple-element.30.grad_u, ...), custom_call_target="tpu_custom_call" | custom-call | flops 10000000000 | bytes 1 | tf_op jit(solution)/shard_map/finish_u/pallas_call | solution.py:234
  53.3 0.0 collective-permute-done.4.last
  53.3 2.1 %finish_w.1 = (bf16[384,1152]{1,0:T(8,128)(2,1)}, bf16[384,1152]{1,0:T(8,128)(2,1)}, f32[384]{0:T(512)}) custom-call(bf16[384,1280]{1,0:T(8,128)(2,1)S(1)} %collective-permute-done.4.last, f32[384,1152]{1,0:T(8,128)S(1)} %get-tuple-element.29.grad_w, f32[384,128]{1,0:T(8,128)S(1)} %get-tuple-element.34.loss_in, f32[384,1152]{1,0:T(8,128)S(1)} %get-tuple-element.35.unit, ...), custom_call_target="tpu_custom_call" | custom-call | flops 1 | bytes 1 | tf_op jit(solution)/shard_map/finish_w/pallas_call | solution.py:234
  (1 shorter events, 0.0 us)
Async XLA Ops:
  1.9 4.0 %collective-permute-start = (bf16[384,1152]{1,0:T(8,128)(2,1)S(1)}, bf16[384,1152]{1,0:T(8,128)(2,1)S(1)}, u32[]{:S(2)}, u32[]{:S(2)}) collective-permute-start(bf16[384,1152]{1,0:T(8,128)(2,1)S(1)} %own.2.when_outer), channel_id=1, source_target_pairs={{0,2},{1,3},{2,0},{3,1},{4,6},{5,7},{6,4},{7,5},{8,10},{9,11},{10,... | collective-permute-start | bytes 2654216 | tf_op jit(solution)/shard_map/ppermute | solution.py:30
  3.2 23.3 %collective-permute-start.2 = (bf16[384,1152]{1,0:T(8,128)(2,1)S(1)}, bf16[384,1152]{1,0:T(8,128)(2,1)S(1)}, u32[]{:S(2)}, u32[]{:S(2)}) collective-permute-start(bf16[384,1152]{1,0:T(8,128)(2,1)S(1)} %own.3.when_inner), channel_id=1, source_target_pairs={{0,30},{1,31},{2,4},{3,5},{4,2},{5,3},{6,8},{7,9},{8,6},{9,7},{10,... | collective-permute-start | bytes 2654216 | tf_op jit(solution)/shard_map/ppermute | solution.py:30
  6.0 23.2 %collective-permute-start.1 = (bf16[384,1152]{1,0:T(8,128)(2,1)S(1)}, bf16[384,1152]{1,0:T(8,128)(2,1)}, u32[]{:S(2)}, u32[]{:S(2)}) collective-permute-start(bf16[384,1152]{1,0:T(8,128)(2,1)S(1)} %pick.2), channel_id=1, source_target_pairs={{0,1},{1,0},{2,3},{3,2},{4,5},{5,4},{6,7},{7,6},{8,9},{9,8},{10,11... | collective-permute-start | bytes 2654216 | tf_op jit(solution)/shard_map/ppermute | solution.py:30
  26.5 5.2 %copy-start = (bf16[384,1152]{1,0:T(8,128)(2,1)}, bf16[384,1152]{1,0:T(8,128)(2,1)S(1)}, u32[]{:S(2)}) copy-start(bf16[384,1152]{1,0:T(8,128)(2,1)S(1)} %collective-permute-done.2.when_inner.b2) | copy-start | bytes 2654212
  27.4 19.0 %collective-permute-start.3 = (bf16[384,1152]{1,0:T(8,128)(2,1)}, bf16[384,1152]{1,0:T(8,128)(2,1)S(1)}, u32[]{:S(2)}, u32[]{:S(2)}) collective-permute-start(bf16[384,1152]{1,0:T(8,128)(2,1)} %pick.3), channel_id=1, source_target_pairs={{0,1},{1,0},{2,3},{3,2},{4,5},{5,4},{6,7},{7,6},{8,9},{9,8},{10,11... | collective-permute-start | bytes 2654216 | tf_op jit(solution)/shard_map/ppermute | solution.py:30
  29.3 22.2 %collective-permute-start.5 = (bf16[384,1152]{1,0:T(8,128)(2,1)}, bf16[384,1152]{1,0:T(8,128)(2,1)S(1)}, u32[]{:S(2)}, u32[]{:S(2)}) collective-permute-start(bf16[384,1152]{1,0:T(8,128)(2,1)} %collective-permute-done.1.b3), channel_id=1, source_target_pairs={{0,30},{1,31},{2,4},{3,5},{4,2},{5,3},{6,8},{7,9},{8,6},{9,7},{10,... | collective-permute-start | bytes 2654216 | tf_op jit(solution)/shard_map/ppermute | solution.py:30
  49.0 4.2 %collective-permute-start.4 = (bf16[384,1280]{1,0:T(8,128)(2,1)S(1)}, bf16[384,1280]{1,0:T(8,128)(2,1)S(1)}, u32[]{:S(2)}, u32[]{:S(2)}) collective-permute-start(bf16[384,1280]{1,0:T(8,128)(2,1)S(1)} %get-tuple-element.28), channel_id=1, source_target_pairs={{0,2},{1,3},{2,0},{3,1},{4,6},{5,7},{6,4},{7,5},{8,10},{9,11},{10,... | collective-permute-start | bytes 2949128 | tf_op jit(solution)/shard_map/ppermute | solution.py:30

commit v14 on v13

--- a/solution.py
+++ b/solution.py
@@ -1,5 +1,3 @@
-import functools
-
 import jax
 import jax.numpy as jnp
 from jax import lax
@@ -12,7 +10,7 @@
 AXES = ("blk", "inner")
 F32 = jnp.float32
 BF16 = jnp.bfloat16
-VMEM_LIMIT = 16 * 1024 * 1024
+VMEM_LIMIT = 28 * 1024 * 1024
 
 X_SWAP = {0: (1, 0), 1: (0, 0), 2: (3, 0), 3: (2, 0)}
 CORE_SWAP = {0: (2, 0), 1: (3, 0), 2: (0, 0), 3: (1, 0)}
@@ -92,7 +90,7 @@
 
 
 def project(unit, inverse, grad):
-    return ((grad - unit * jnp.sum(unit * grad, axis=1, keepdims=True)) * inverse).astype(BF16)
+    return (grad - unit * jnp.sum(unit * grad, axis=1, keepdims=True)) * inverse
 
 
 def row_parts(rows, wanted):
@@ -112,25 +110,27 @@
     return lax.rem(lax.axis_index("blk"), 2) == lax.axis_index("inner")
 
 
-def own_kernel(image_core, image, text, block, sems):
-    def move(source):
+def sort_kernel(image, text, u, w, sems):
+    def move(image_to, text_to):
         copies = []
-        for place, part in enumerate(row_parts(block.shape[0], 3)):
-            copies.append(pltpu.make_async_copy(source.at[part], block.at[part], sems.at[place]))
+        for source, target in ((image, image_to), (text, text_to)):
+            for part in row_parts(image.shape[0], 3):
+                sem = sems.at[len(copies)]
+                copies.append(pltpu.make_async_copy(source.at[part], target.at[part], sem))
         for copy in copies:
             copy.start()
         for copy in copies:
             copy.wait()
 
-    wants_image = lax.rem(lax.axis_index("blk"), 2) == image_core
-
-    @pl.when(wants_image)
+    u_is_image = image_is_u()
+
+    @pl.when(u_is_image)
     def _():
-        move(image)
-
-    @pl.when(jnp.logical_not(wants_image))
+        move(u, w)
+
+    @pl.when(jnp.logical_not(u_is_image))
     def _():
-        move(text)
+        move(w, u)
 
 
 def pick_kernel(when_outer, when_inner, picked, sem):
@@ -145,7 +145,7 @@
 
 def near_kernel(
     scalars, image, text, b1, b2, b3,
-    z_pair, unit_u, unit_w, inverse_u, inverse_w, grad_u, grad_w, loss, work, z_w,
+    z_pair, unit_u, unit_other, inverse_u, inverse_other, grad_u, part_w, loss, work, z_w, grad_w, unit_w,
 ):
     u_is_image = image_is_u()
     u_weight = u_is_image.astype(F32)
@@ -155,7 +155,8 @@
     unit_u[...] = jnp.where(u_is_image, image_unit, text_unit)
     unit_w[...] = jnp.where(u_is_image, text_unit, image_unit)
     inverse_u[...] = jnp.where(u_is_image, image_inverse, text_inverse)
-    inverse_w[...] = jnp.where(u_is_image, text_inverse, image_inverse)
+    inverse_w = jnp.where(u_is_image, text_inverse, image_inverse)
+    unit_other[...], inverse_other[...] = unit_rows(b1[...])
     zi = image_unit.astype(BF16)
     zt = text_unit.astype(BF16)
     z_u = jnp.where(u_is_image, zi, zt)
@@ -177,14 +178,16 @@
     total = total + u_weight * row_loss
     term, row_loss = pair_step(z_w[...], (b1[...], b3[...]), scale, shift, work)
     z_pair[zi.shape[0] :] = work[: zi.shape[0]]
-    grad_w[...] += term
+    part_w[...] = project(unit_w[...], inverse_w, grad_w[...] + term)
     loss[...] = total + (1.0 - u_weight) * row_loss
 
 
-def fifth_kernel(scalars, b5, z_pair, grad_in, loss_in, grad_u, loss, for_partner, work):
+def fifth_kernel(
+    scalars, b5, z_pair, unit_other, inverse_other, grad_in, loss_in, grad_u, loss, for_partner, work
+):
     rows, width = b5.shape
     term, row_loss = pair_step(z_pair[...], (b5[...],), *scalar_pair(scalars), work)
-    for_partner[:, :width] = term[rows:].astype(BF16)
+    for_partner[:, :width] = project(unit_other[...], inverse_other[...], term[rows:]).astype(BF16)
     for_partner[:, width:] = row_loss[rows:].astype(BF16)
     grad_u[...] = grad_in[...] + term[:rows]
     loss[...] = loss_in[...] + image_is_u().astype(F32) * row_loss[:rows]
@@ -194,11 +197,11 @@
     rows = done_u.shape[0]
     term, row_loss = pair_step(z_pair[:rows], (b4[...],), *scalar_pair(scalars), work)
     loss[...] = loss_in[...] + image_is_u().astype(F32) * row_loss
-    done_u[...] = project(unit[...], inverse[...], grad_u[...] + term)
+    done_u[...] = project(unit[...], inverse[...], grad_u[...] + term).astype(BF16)
 
 
 def w_kernel(
-    last, grad_w, loss_in, unit, inverse, done_u, image_grad, text_grad, loss_rows, done_w, sems
+    last, part_w, loss_in, done_u, image_grad, text_grad, loss_rows, done_w, sems
 ):
     u_is_image = image_is_u()
     parts = row_parts(done_w.shape[0], 6)
@@ -216,8 +219,7 @@
     output(lambda copy: copy.start(), done_u, whole, u_is_image, sems.at[0])
     width = done_w.shape[1]
     for place, part in enumerate(parts):
-        grad = grad_w[part] + last[part, :width].astype(F32)
-        done_w[part] = project(unit[part], inverse[part], grad)
+        done_w[part] = (part_w[part] + last[part, :width].astype(F32)).astype(BF16)
         output(lambda copy: copy.start(), done_w, part, jnp.logical_not(u_is_image), sems.at[1 + place])
     total = loss_in[...] + (1.0 - u_is_image.astype(F32)) * last[:, width:].astype(F32)
     loss_rows[...] = jnp.sum(jnp.transpose(total), axis=0) / (SPAN * total.shape[0])
@@ -269,13 +271,10 @@
         out_specs = [VMEM] * len(outs)
         return call(kernel, in_specs, (scalars, *args), out_specs, outs, name, scratch, flops)
 
-    def own(image_core):
-        kernel = functools.partial(own_kernel, image_core)
-        return call(kernel, [ANY] * 2, in_hbm(image, text), [VMEM], (block,), "own", (copies,))[0]
-
-    w = own(1)
+    u, w = call(
+        sort_kernel, [ANY] * 2, in_hbm(image, text), [VMEM] * 2, (block, block), "sort", (copies,)
+    )
     slot1 = send(w, CORE_SWAP)
-    u = own(0)
     slot2 = send(u, GROUP_SHIFT)
     slot3 = send(pick(slot1, u, block), X_SWAP)
     slot4 = send(slot3, GROUP_SHIFT)
@@ -283,16 +282,16 @@
     slot3, score_scaling, score_shift = lax.optimization_barrier((slot3, score_scaling, score_shift))
     first = lax.broadcasted_iota(jnp.int32, (8, 128), 0) == 0
     scalars = jnp.where(first, score_scaling, score_shift)
-    z_pair, unit_u, unit_w, inverse_u, inverse_w, grad_u, grad_w, loss = compute(
+    z_pair, unit_u, unit_other, inverse_u, inverse_other, grad_u, part_w, loss = compute(
         near_kernel,
         (*in_hbm(image, text), slot1, *in_hbm(slot2, slot3)),
         (pair, sums, sums, column, column, sums, sums, partial),
         "near_blocks",
-        (pltpu.VMEM((2 * rows, width), BF16), raw),
+        (pltpu.VMEM((2 * rows, width), BF16), raw) + (pltpu.VMEM((rows, width), F32),) * 2,
     )
     grad_u, loss, for_partner = compute(
         fifth_kernel,
-        (pltpu.with_memory_space_constraint(slot5, pltpu.VMEM), z_pair, grad_u, loss),
+        (pltpu.with_memory_space_constraint(slot5, pltpu.VMEM), z_pair, unit_other, inverse_other, grad_u, loss),
         (sums, partial, jax.ShapeDtypeStruct((rows, width + 128), BF16)),
         "fifth_block",
         (raw,),
@@ -308,8 +307,8 @@
     )
     image_grad, text_grad, loss_rows = call(
         w_kernel,
-        [VMEM] * 6,
-        (last, grad_w, loss, unit_w, inverse_w, done_u),
+        [VMEM] * 4,
+        (last, part_w, loss, done_u),
         [ANY, ANY, VMEM],
         (block, block, line),
         "finish_w",

time: 55.6 us -> 54.4 us (0.978)
  waiting for transfers between devices: 27.8 us -> 25.4 us
  starting transfers between devices: 7.04 us -> 8.62 us
    ppermute x6, waiting for transfers between devices: 27.8 us -> 25.4 us  [send(): return lax.ppermute(value, AXES, pairs)]
    ppermute x6, starting transfers between devices: 7.04 us -> 8.62 us  [send(): return lax.ppermute(value, AXES, pairs)]
    pallas_call x8 -> x7, Pallas kernels: 18.5 us -> 18.1 us  [call(): pl.pallas_call(kernel, out_shape=outs, in_specs=in_specs, out_specs=out_s...]
where the time goes in v14:
time: 54.4 us; the launch traced here: 54.2 us
  waiting for transfers between devices  25.4 us (47%)
  Pallas kernels  18.1 us (33%)
  starting transfers between devices  8.62 us (16%)
  between operations  2 us (4%)
    ppermute x6, waiting for transfers between devices, send(): return lax.ppermute(value, AXES, pairs)  25.4 us
    pallas_call x7, Pallas kernels, call(): pl.pallas_call(kernel, out_shape=outs, in_specs=in_specs, out_specs=out_s...  18.1 us
    ppermute x6, starting transfers between devices, send(): return lax.ppermute(value, AXES, pairs)  8.62 us
  transfers between devices with their start and end apart: 6, of which 3 were waited for; matrix products, arithmetic and copies ran while one was open for 0% of the time, Pallas kernels for 27%

profile of v14, /device:TPU:1, one launch (start us, length us, event | category | flops | bytes accessed | tf_op | source)
XLA Modules:
  0.0 54.2 jit_solution(11629590656922364469)
XLA Ops:
  0.6 1.5 %sort.1 = (bf16[384,1152]{1,0:T(8,128)(2,1)S(1)}, bf16[384,1152]{1,0:T(8,128)(2,1)S(1)}) custom-call(bf16[384,1152]{1,0:T(8,128)(2,1)} %image.3, bf16[384,1152]{1,0:T(8,128)(2,1)} %text.3), custom_call_target="tpu_custom_call" | custom-call | flops 1 | bytes 1 | tf_op jit(solution)/shard_map/sort/pallas_call | solution.py:236
  2.1 0.1 collective-permute-start
  2.2 2.7 %collective-permute-start.2 = (bf16[384,1152]{1,0:T(8,128)(2,1)S(1)}, bf16[384,1152]{1,0:T(8,128)(2,1)S(1)}, u32[]{:S(2)}, u32[]{:S(2)}) collective-permute-start(bf16[384,1152]{1,0:T(8,128)(2,1)S(1)} %get-tuple-element.25.when_inner), channel_id=1, source_target_pairs={{0,30},{1,31},{2,4},{3,5},{4,2},{5,3},{6,8},{7,9},{8,6},{9,7},{10,... | collective-permute-start | bytes 2654216 | tf_op jit(solution)/shard_map/ppermute | solution.py:28
  4.9 0.0 collective-permute-done.when_outer.b1
  4.9 0.2 pick.2
  5.1 2.1 %collective-permute-start.1 = (bf16[384,1152]{1,0:T(8,128)(2,1)S(1)}, bf16[384,1152]{1,0:T(8,128)(2,1)}, u32[]{:S(2)}, u32[]{:S(2)}) collective-permute-start(bf16[384,1152]{1,0:T(8,128)(2,1)S(1)} %pick.2), channel_id=1, source_target_pairs={{0,1},{1,0},{2,3},{3,2},{4,5},{5,4},{6,7},{7,6},{8,9},{9,8},{10,11... | collective-permute-start | bytes 2654216 | tf_op jit(solution)/shard_map/ppermute | solution.py:28
  7.2 18.3 %collective-permute-done.2.when_inner.b2 = bf16[384,1152]{1,0:T(8,128)(2,1)S(1)} collective-permute-done((bf16[384,1152]{1,0:T(8,128)(2,1)S(1)}, bf16[384,1152]{1,0:T(8,128)(2,1)S(1)}, u32[]{:S(2)}, u32[]{:S(2)}) %collective-permute-start.2) | collective-permute-done | bytes 884768 | tf_op jit(solution)/shard_map/ppermute | solution.py:28
  25.5 0.0 copy-start
  25.5 0.9 %pick.3 = bf16[384,1152]{1,0:T(8,128)(2,1)} custom-call(bf16[384,1152]{1,0:T(8,128)(2,1)S(1)} %get-tuple-element.24.when_outer, bf16[384,1152]{1,0:T(8,128)(2,1)S(1)} %collective-permute-done.2.when_inner.b2), custom_call_target="tpu_custom_call" | custom-call | flops 1 | bytes 1 | tf_op jit(solution)/shard_map/pick/pallas_call | solution.py:236
  26.4 1.8 %collective-permute-start.3 = (bf16[384,1152]{1,0:T(8,128)(2,1)}, bf16[384,1152]{1,0:T(8,128)(2,1)S(1)}, u32[]{:S(2)}, u32[]{:S(2)}) collective-permute-start(bf16[384,1152]{1,0:T(8,128)(2,1)} %pick.3), channel_id=1, source_target_pairs={{0,1},{1,0},{2,3},{3,2},{4,5},{5,4},{6,7},{7,6},{8,9},{9,8},{10,11... | collective-permute-start | bytes 2654216 | tf_op jit(solution)/shard_map/ppermute | solution.py:28
  28.3 0.0 collective-permute-done.1.b3
  28.3 1.8 %collective-permute-start.5 = (bf16[384,1152]{1,0:T(8,128)(2,1)}, bf16[384,1152]{1,0:T(8,128)(2,1)S(1)}, u32[]{:S(2)}, u32[]{:S(2)}) collective-permute-start(bf16[384,1152]{1,0:T(8,128)(2,1)} %collective-permute-done.1.b3), channel_id=1, source_target_pairs={{0,30},{1,31},{2,4},{3,5},{4,2},{5,3},{6,8},{7,9},{8,6},{9,7},{10,... | collective-permute-start | bytes 2654216 | tf_op jit(solution)/shard_map/ppermute | solution.py:28
  31.4 0.1 iota.7.scalars
  31.5 0.0 copy-done
  31.5 9.1 %near_blocks.1 = (bf16[768,1152]{1,0:T(8,128)(2,1)S(1)}, f32[384,1152]{1,0:T(8,128)S(1)}, f32[384,1152]{1,0:T(8,128)S(1)}, f32[384,1]{1,0:T(8,128)S(1)}, f32[384...) custom-call(f32[8,128]{1,0:T(8,128)S(1)} %iota.7.scalars, ...), custom_call_target="tpu_custom_call" | custom-call | flops 1 | bytes 1 | tf_op jit(solution)/shard_map/near_blocks/pallas_call | solution.py:236
  40.5 5.5 %collective-permute-done.3.b5 = bf16[384,1152]{1,0:T(8,128)(2,1)S(1)} collective-permute-done((bf16[384,1152]{1,0:T(8,128)(2,1)}, bf16[384,1152]{1,0:T(8,128)(2,1)S(1)}, u32[]{:S(2)}, u32[]{:S(2)}) %collective-permute-start.3) | collective-permute-done | bytes 884768 | tf_op jit(solution)/shard_map/ppermute | solution.py:28
  46.1 2.8 %fifth_block.1 = (f32[384,1152]{1,0:T(8,128)S(1)}, f32[384,128]{1,0:T(8,128)S(1)}, bf16[384,1280]{1,0:T(8,128)(2,1)S(1)}) custom-call(f32[8,128]{1,0:T(8,128)S(1)} %iota.7.scalars, bf16[384,1152]{1,0:T(8,128)(2,1)S(1)} %collective-permute-done.3.b5, bf16[768,1152]{1,0:T(8,128)(2,1)S(1)} %get-tuple-element.29.z_pair, ...), custom_call_target="tpu_custom_call" | custom-call | flops 1 | bytes 1 | tf_op jit(solution)/shard_map/fifth_block/pallas_call | solution.py:236
  48.9 0.1 collective-permute-start.4
  49.0 1.5 %collective-permute-done.5.b4 = bf16[384,1152]{1,0:T(8,128)(2,1)S(1)} collective-permute-done((bf16[384,1152]{1,0:T(8,128)(2,1)}, bf16[384,1152]{1,0:T(8,128)(2,1)S(1)}, u32[]{:S(2)}, u32[]{:S(2)}) %collective-permute-start.5) | collective-permute-done | bytes 884768 | tf_op jit(solution)/shard_map/ppermute | solution.py:28
  50.5 1.8 %finish_u.1 = (bf16[384,1152]{1,0:T(8,128)(2,1)S(1)}, f32[384,128]{1,0:T(8,128)S(1)}) custom-call(f32[8,128]{1,0:T(8,128)S(1)} %iota.7.scalars, bf16[384,1152]{1,0:T(8,128)(2,1)S(1)} %collective-permute-done.5.b4, bf16[768,1152]{1,0:T(8,128)(2,1)S(1)} %get-tuple-element.29.z_pair, f32[384,1152]{1,0:T(8,128)S(1)} %get-tuple-element.36.grad_u, ...), custom_call_target="tpu_custom_call" | custom-call | flops 10000000000 | bytes 1 | tf_op jit(solution)/shard_map/finish_u/pallas_call | solution.py:236
  52.3 0.0 collective-permute-done.4.last
  52.4 1.8 %finish_w.1 = (bf16[384,1152]{1,0:T(8,128)(2,1)}, bf16[384,1152]{1,0:T(8,128)(2,1)}, f32[384]{0:T(512)}) custom-call(bf16[384,1280]{1,0:T(8,128)(2,1)S(1)} %collective-permute-done.4.last, f32[384,1152]{1,0:T(8,128)S(1)} %get-tuple-element.35.part_w, f32[384,128]{1,0:T(8,128)S(1)} %get-tuple-element.40.loss_in, bf16[384,1152]{1,0:T(8,128)(2,1)S(1)} %get-tuple-element.41.done_u), custom_call_target="tpu_custom_call" | custom-call | flops 1 | bytes 1 | tf_op jit(solution)/shard_map/finish_w/pallas_call | solution.py:236
  (1 shorter events, 0.0 us)
Async XLA Ops:
  2.1 2.8 %collective-permute-start = (bf16[384,1152]{1,0:T(8,128)(2,1)S(1)}, bf16[384,1152]{1,0:T(8,128)(2,1)S(1)}, u32[]{:S(2)}, u32[]{:S(2)}) collective-permute-start(bf16[384,1152]{1,0:T(8,128)(2,1)S(1)} %get-tuple-element.24.when_outer), channel_id=1, source_target_pairs={{0,2},{1,3},{2,0},{3,1},{4,6},{5,7},{6,4},{7,5},{8,10},{9,11},{10,... | collective-permute-start | bytes 2654216 | tf_op jit(solution)/shard_map/ppermute | solution.py:28
  2.2 23.3 %collective-permute-start.2 = (bf16[384,1152]{1,0:T(8,128)(2,1)S(1)}, bf16[384,1152]{1,0:T(8,128)(2,1)S(1)}, u32[]{:S(2)}, u32[]{:S(2)}) collective-permute-start(bf16[384,1152]{1,0:T(8,128)(2,1)S(1)} %get-tuple-element.25.when_inner), channel_id=1, source_target_pairs={{0,30},{1,31},{2,4},{3,5},{4,2},{5,3},{6,8},{7,9},{8,6},{9,7},{10,... | collective-permute-start | bytes 2654216 | tf_op jit(solution)/shard_map/ppermute | solution.py:28
  5.1 23.2 %collective-permute-start.1 = (bf16[384,1152]{1,0:T(8,128)(2,1)S(1)}, bf16[384,1152]{1,0:T(8,128)(2,1)}, u32[]{:S(2)}, u32[]{:S(2)}) collective-permute-start(bf16[384,1152]{1,0:T(8,128)(2,1)S(1)} %pick.2), channel_id=1, source_target_pairs={{0,1},{1,0},{2,3},{3,2},{4,5},{5,4},{6,7},{7,6},{8,9},{9,8},{10,11... | collective-permute-start | bytes 2654216 | tf_op jit(solution)/shard_map/ppermute | solution.py:28
  25.5 6.0 %copy-start = (bf16[384,1152]{1,0:T(8,128)(2,1)}, bf16[384,1152]{1,0:T(8,128)(2,1)S(1)}, u32[]{:S(2)}) copy-start(bf16[384,1152]{1,0:T(8,128)(2,1)S(1)} %collective-permute-done.2.when_inner.b2) | copy-start | bytes 2654212
  26.4 19.6 %collective-permute-start.3 = (bf16[384,1152]{1,0:T(8,128)(2,1)}, bf16[384,1152]{1,0:T(8,128)(2,1)S(1)}, u32[]{:S(2)}, u32[]{:S(2)}) collective-permute-start(bf16[384,1152]{1,0:T(8,128)(2,1)} %pick.3), channel_id=1, source_target_pairs={{0,1},{1,0},{2,3},{3,2},{4,5},{5,4},{6,7},{7,6},{8,9},{9,8},{10,11... | collective-permute-start | bytes 2654216 | tf_op jit(solution)/shard_map/ppermute | solution.py:28
  28.3 22.3 %collective-permute-start.5 = (bf16[384,1152]{1,0:T(8,128)(2,1)}, bf16[384,1152]{1,0:T(8,128)(2,1)S(1)}, u32[]{:S(2)}, u32[]{:S(2)}) collective-permute-start(bf16[384,1152]{1,0:T(8,128)(2,1)} %collective-permute-done.1.b3), channel_id=1, source_target_pairs={{0,30},{1,31},{2,4},{3,5},{4,2},{5,3},{6,8},{7,9},{8,6},{9,7},{10,... | collective-permute-start | bytes 2654216 | tf_op jit(solution)/shard_map/ppermute | solution.py:28
  48.9 3.4 %collective-permute-start.4 = (bf16[384,1280]{1,0:T(8,128)(2,1)S(1)}, bf16[384,1280]{1,0:T(8,128)(2,1)S(1)}, u32[]{:S(2)}, u32[]{:S(2)}) collective-permute-start(bf16[384,1280]{1,0:T(8,128)(2,1)S(1)} %get-tuple-element.34), channel_id=1, source_target_pairs={{0,2},{1,3},{2,0},{3,1},{4,6},{5,7},{6,4},{7,5},{8,10},{9,11},{10,... | collective-permute-start | bytes 2949128 | tf_op jit(solution)/shard_map/ppermute | solution.py:28

commit v15 on v14

--- a/solution.py
+++ b/solution.py
@@ -141,6 +141,10 @@
     @pl.when(jnp.logical_not(is_outer()))
     def _():
         pltpu.async_copy(when_inner, picked, sem).wait()
+
+
+def other_kernel(both, block, sem):
+    pltpu.async_copy(both.at[1 - lax.axis_index("inner")], block, sem).wait()
 
 
 def near_kernel(
@@ -266,6 +270,10 @@
             pick_kernel, [ANY] * 2, (when_outer, when_inner), [ANY], (out,), "pick", (sem,)
         )[0]
 
+    def across_x(both):
+        sem = pltpu.SemaphoreType.DMA
+        return call(other_kernel, [ANY], in_hbm(both), [ANY], (block,), "other", (sem,))[0]
+
     def compute(kernel, args, outs, name, scratch, flops=1):
         in_specs = [VMEM] * (1 + len(args))
         out_specs = [VMEM] * len(outs)
@@ -276,9 +284,9 @@
     )
     slot1 = send(w, CORE_SWAP)
     slot2 = send(u, GROUP_SHIFT)
-    slot3 = send(pick(slot1, u, block), X_SWAP)
+    slot3 = across_x(lax.all_gather(pick(slot1, u, block), "inner"))
     slot4 = send(slot3, GROUP_SHIFT)
-    slot5 = send(pick(w, slot2, pltpu.HBM((rows, width), BF16)), X_SWAP)
+    both5 = lax.all_gather(pick(w, slot2, pltpu.HBM((rows, width), BF16)), "inner")
     slot3, score_scaling, score_shift = lax.optimization_barrier((slot3, score_scaling, score_shift))
     first = lax.broadcasted_iota(jnp.int32, (8, 128), 0) == 0
     scalars = jnp.where(first, score_scaling, score_shift)
@@ -289,6 +297,8 @@
         "near_blocks",
         (pltpu.VMEM((2 * rows, width), BF16), raw) + (pltpu.VMEM((rows, width), F32),) * 2,
     )
+    both5, loss = lax.optimization_barrier((both5, loss))
+    slot5 = across_x(both5)
     grad_u, loss, for_partner = compute(
         fifth_kernel,
         (pltpu.with_memory_space_constraint(slot5, pltpu.VMEM), z_pair, unit_other, inverse_other, grad_u, loss),

time: 54.4 us -> 94.4 us (1.74)
  waiting for transfers between devices: 25.4 us -> 41.2 us
  between operations: 2 us -> 15.5 us
  local copies, waits for them, and re-layouts: 0.07 us -> 9.25 us
  Pallas kernels: 18.1 us -> 22.6 us
  starting transfers between devices: 8.62 us -> 5.44 us
    all_gather x0 -> x2, waiting for transfers between devices: none -> 18.2 us  [the longest x1 11.1 us: local(): lax.all_gather(pick(w, slot2, pltpu.HBM((rows, width), BF16)), 'inner')]
    unnamed x2 -> x32, local copies, waits for them, and re-layouts: 0.01 us -> 9.18 us
    pallas_call x7 -> x9, Pallas kernels: 18.1 us -> 22.6 us  [call(): pl.pallas_call(kernel, out_shape=outs, in_specs=in_specs, out_specs=out_s...]
    ppermute x6 -> x4, starting transfers between devices: 8.62 us -> 5.36 us  [send(): return lax.ppermute(value, AXES, pairs)]
    ppermute x6 -> x4, waiting for transfers between devices: 25.4 us -> 23 us  [send(): return lax.ppermute(value, AXES, pairs)]
  transfers between devices with their start and end apart: 6 -> 6, of which waited for: 3 -> 4; matrix products, arithmetic and copies ran while one was open for 0% -> 0% of each run, Pallas kernels for 27% -> 20%
where the time goes in v15:
time: 94.4 us; the launch traced here: 94.1 us
  waiting for transfers between devices  41.2 us (44%)
  Pallas kernels  22.6 us (24%)
  between operations  15.5 us (16%)
  local copies, waits for them, and re-layouts  9.25 us (10%)
  starting transfers between devices  5.44 us (6%)
    ppermute x4, waiting for transfers between devices, send(): return lax.ppermute(value, AXES, pairs)  23 us
    pallas_call x9, Pallas kernels, call(): pl.pallas_call(kernel, out_shape=outs, in_specs=in_specs, out_specs=out_s...  22.6 us
    all_gather x1, waiting for transfers between devices, local(): lax.all_gather(pick(w, slot2, pltpu.HBM((rows, width), BF16)), 'inner')  11.1 us
    unnamed x32, local copies, waits for them, and re-layouts  9.18 us
    all_gather x1, waiting for transfers between devices, local(): slot3 = across_x(lax.all_gather(pick(slot1, u, block), 'inner'))  7.1 us
    ppermute x4, starting transfers between devices, send(): return lax.ppermute(value, AXES, pairs)  5.36 us
  transfers between devices with their start and end apart: 6, of which 4 were waited for; matrix products, arithmetic and copies ran while one was open for 0% of the time, Pallas kernels for 20%

profile of v15, /device:TPU:1, one launch (start us, length us, event | category | flops | bytes accessed | tf_op | source)
XLA Modules:
  0.0 94.1 jit_solution(3280447766178803699)
XLA Ops:
  7.2 0.0 all-gather.5.cloned.1.call-start
  7.2 1.5 %sort.1 = (bf16[384,1152]{1,0:T(8,128)(2,1)S(1)}, bf16[384,1152]{1,0:T(8,128)(2,1)S(1)}) custom-call(bf16[384,1152]{1,0:T(8,128)(2,1)} %image.3, bf16[384,1152]{1,0:T(8,128)(2,1)} %text.3), custom_call_target="tpu_custom_call" | custom-call | flops 1 | bytes 1 | tf_op jit(solution)/shard_map/sort/pallas_call | solution.py:240
  8.7 0.1 collective-permute-start
  8.8 2.4 %collective-permute-done.when_outer.b1 = bf16[384,1152]{1,0:T(8,128)(2,1)S(1)} collective-permute-done((bf16[384,1152]{1,0:T(8,128)(2,1)S(1)}, bf16[384,1152]{1,0:T(8,128)(2,1)S(1)}, u32[]{:S(2)}, u32[]{:S(2)}) %collective-permute-start) | collective-permute-done | bytes 884768 | tf_op jit(solution)/shard_map/ppermute | solution.py:28
  11.2 0.9 pick.2
  12.1 0.0 all-gather.5.cloned.1.call-update
  12.2 0.0 all-gather.7.cloned.1.call-start
  12.2 2.7 %collective-permute-start.1 = (bf16[384,1152]{1,0:T(8,128)(2,1)S(1)}, bf16[384,1152]{1,0:T(8,128)(2,1)S(1)}, u32[]{:S(2)}, u32[]{:S(2)}) collective-permute-start(bf16[384,1152]{1,0:T(8,128)(2,1)S(1)} %get-tuple-element.27.when_inner), channel_id=1, source_target_pairs={{0,30},{1,31},{2,4},{3,5},{4,2},{5,3},{6,8},{7,9},{8,6},{9,7},{10,... | collective-permute-start | bytes 2654216 | tf_op jit(solution)/shard_map/ppermute | solution.py:28
  14.9 20.6 %collective-permute-done.1.when_inner.b2 = bf16[384,1152]{1,0:T(8,128)(2,1)S(1)} collective-permute-done((bf16[384,1152]{1,0:T(8,128)(2,1)S(1)}, bf16[384,1152]{1,0:T(8,128)(2,1)S(1)}, u32[]{:S(2)}, u32[]{:S(2)}) %collective-permute-start.1) | collective-permute-done | bytes 884768 | tf_op jit(solution)/shard_map/ppermute | solution.py:28
  35.5 0.0 copy-start.1
  35.5 0.9 pick.3
  36.4 0.0 all-gather.7.cloned.1.call-update
  36.5 0.2 copy-done.1
  36.7 7.1 %all-gather.5.cloned.1.call-done = bf16[768,1152]{1,0:T(8,128)(2,1)} async-done(((bf16[384,1152]{1,0:T(8,128)(2,1)}), bf16[768,1152]{1,0:T(8,128)(2,1)}) %all-gather.5.cloned.1.call-update) | async-done | bytes 1769488 | tf_op jit(solution)/shard_map/all_gather | solution.py:287
  43.8 1.2 %other.2.b3 = bf16[384,1152]{1,0:T(8,128)(2,1)S(1)} custom-call(bf16[2,384,1152]{2,1,0:T(8,128)(2,1)} %bitcast.3), custom_call_target="tpu_custom_call" | custom-call | flops 1 | bytes 1 | tf_op jit(solution)/shard_map/other/pallas_call | solution.py:240
  45.0 0.0 copy-start
  45.0 1.8 %collective-permute-start.3 = (bf16[384,1152]{1,0:T(8,128)(2,1)S(1)}, bf16[384,1152]{1,0:T(8,128)(2,1)}, u32[]{:S(2)}, u32[]{:S(2)}) collective-permute-start(bf16[384,1152]{1,0:T(8,128)(2,1)S(1)} %other.2.b3), channel_id=1, source_target_pairs={{0,30},{1,31},{2,4},{3,5},{4,2},{5,3},{6,8},{7,9},{8,6},{9,7},{10,... | collective-permute-start | bytes 2654216 | tf_op jit(solution)/shard_map/ppermute | solution.py:28
  48.1 0.1 iota.7.scalars
  48.2 0.0 copy-done
  48.2 9.0 %near_blocks.1 = (bf16[768,1152]{1,0:T(8,128)(2,1)S(1)}, f32[384,1152]{1,0:T(8,128)S(1)}, f32[384,1152]{1,0:T(8,128)S(1)}, f32[384,1]{1,0:T(8,128)S(1)}, f32[384...) custom-call(f32[8,128]{1,0:T(8,128)S(1)} %iota.7.scalars, ...), custom_call_target="tpu_custom_call" | custom-call | flops 1 | bytes 1 | tf_op jit(solution)/shard_map/near_blocks/pallas_call | solution.py:240
  57.3 0.0 copy-start.2
  57.3 1.2 %copy-done.2 = f32[384,1152]{1,0:T(8,128)} copy-done((f32[384,1152]{1,0:T(8,128)}, f32[384,1152]{1,0:T(8,128)S(1)}, u32[]{:S(2)}) %copy-start.2) | copy-done | bytes 1769496
  58.5 0.0 copy-start.4
  58.5 1.3 %copy-done.4 = f32[384,1152]{1,0:T(8,128)} copy-done((f32[384,1152]{1,0:T(8,128)}, f32[384,1152]{1,0:T(8,128)S(1)}, u32[]{:S(2)}) %copy-start.4) | copy-done | bytes 1769496
  59.7 0.0 copy-start.6
  59.7 1.2 %copy-done.6 = f32[384,1152]{1,0:T(8,128)} copy-done((f32[384,1152]{1,0:T(8,128)}, f32[384,1152]{1,0:T(8,128)S(1)}, u32[]{:S(2)}) %copy-start.6) | copy-done | bytes 1769496
  60.9 0.0 copy-start.8
  61.0 0.7 copy-done.8
  61.6 0.0 copy-start.10
  61.6 0.7 copy-done.10
  62.3 0.0 copy-start.12
  62.3 1.3 %copy-done.12 = f32[384,1152]{1,0:T(8,128)} copy-done((f32[384,1152]{1,0:T(8,128)}, f32[384,1152]{1,0:T(8,128)S(1)}, u32[]{:S(2)}) %copy-start.12) | copy-done | bytes 1769496
  63.6 0.0 copy-start.14
  63.6 0.7 copy-done.14
  64.3 11.1 %all-gather.7.cloned.1.call-done = bf16[768,1152]{1,0:T(8,128)(2,1)} async-done(((bf16[384,1152]{1,0:T(8,128)(2,1)}), bf16[768,1152]{1,0:T(8,128)(2,1)}) %all-gather.7.cloned.1.call-update) | async-done | bytes 1769488 | tf_op jit(solution)/shard_map/all_gather | solution.py:289
  75.4 0.0 copy-start.3
  75.4 0.0 copy-start.9
  75.4 0.0 copy-start.11
  75.4 1.3 %other.3.b5 = bf16[384,1152]{1,0:T(8,128)(2,1)S(1)} custom-call(bf16[2,384,1152]{2,1,0:T(8,128)(2,1)} %bitcast.2), custom_call_target="tpu_custom_call" | custom-call | flops 1 | bytes 1 | tf_op jit(solution)/shard_map/other/pallas_call | solution.py:240
  76.7 0.4 copy-done.3
  77.1 0.0 copy-done.9
  77.1 0.0 copy-done.11
  77.2 0.0 copy-start.5
  77.2 1.5 %copy-done.5 = f32[384,1152]{1,0:T(8,128)S(1)} copy-done((f32[384,1152]{1,0:T(8,128)S(1)}, f32[384,1152]{1,0:T(8,128)}, u32[]{:S(2)}) %copy-start.5) | copy-done | bytes 1769496
  78.6 0.0 copy-start.13
  78.6 0.0 copy-start.15
  78.6 2.8 %fifth_block.1 = (f32[384,1152]{1,0:T(8,128)S(1)}, f32[384,128]{1,0:T(8,128)S(1)}, bf16[384,1280]{1,0:T(8,128)(2,1)S(1)}) custom-call(f32[8,128]{1,0:T(8,128)S(1)} %iota.7.scalars, bf16[384,1152]{1,0:T(8,128)(2,1)S(1)} %other.3.b5, bf16[768,1152]{1,0:T(8,128)(2,1)S(1)} %get-tuple-element.33.z_pair, f32[384,1152]{1,0:T(8,128)S(1)} %copy-done.3, ...), custom_call_target="tpu_custom_call" | custom-call | flops 1 | bytes 1 | tf_op jit(solution)/shard_map/fifth_block/pallas_call | solution.py:240
  81.5 0.7 collective-permute-start.2
  82.2 0.0 collective-permute-done.3.b4
  82.2 0.0 copy-done.13
  82.2 0.0 copy-done.15
  82.2 0.0 copy-start.7
  82.2 3.1 %finish_u.1 = (bf16[384,1152]{1,0:T(8,128)(2,1)S(1)}, f32[384,128]{1,0:T(8,128)S(1)}) custom-call(f32[8,128]{1,0:T(8,128)S(1)} %iota.7.scalars, bf16[384,1152]{1,0:T(8,128)(2,1)} %collective-permute-done.3.b4, bf16[768,1152]{1,0:T(8,128)(2,1)S(1)} %get-tuple-element.33.z_pair, f32[384,1152]{1,0:T(8,128)S(1)} %get-tuple-element.40.grad_u, ...), custom_call_target="tpu_custom_call" | custom-call | flops 10000000000 | bytes 1 | tf_op jit(solution)/shard_map/finish_u/pallas_call | solution.py:240
  85.3 0.0 collective-permute-done.2.last
  85.4 0.0 copy-done.7
  85.4 1.8 %finish_w.1 = (bf16[384,1152]{1,0:T(8,128)(2,1)}, bf16[384,1152]{1,0:T(8,128)(2,1)}, f32[384]{0:T(512)}) custom-call(bf16[384,1280]{1,0:T(8,128)(2,1)S(1)} %collective-permute-done.2.last, f32[384,1152]{1,0:T(8,128)S(1)} %copy-done.7, f32[384,128]{1,0:T(8,128)S(1)} %get-tuple-element.44.loss_in, bf16[384,1152]{1,0:T(8,128)(2,1)S(1)} %get-tuple-element.45.done_u), custom_call_target="tpu_custom_call" | custom-call | flops 1 | bytes 1 | tf_op jit(solution)/shard_map/finish_w/pallas_call | solution.py:240
  (1 shorter events, 0.0 us)
Async XLA Ops:
  7.2 36.6 %all-gather.5.cloned.1.call-start = ((), (), s32[]{:S(2)}) async-start(), calls=%async_computation | async-start | bytes 2654208 | tf_op jit(solution)/shard_map/all_gather | solution.py:287
  8.7 2.5 %collective-permute-start = (bf16[384,1152]{1,0:T(8,128)(2,1)S(1)}, bf16[384,1152]{1,0:T(8,128)(2,1)S(1)}, u32[]{:S(2)}, u32[]{:S(2)}) collective-permute-start(bf16[384,1152]{1,0:T(8,128)(2,1)S(1)} %get-tuple-element.26.when_outer), channel_id=1, source_target_pairs={{0,2},{1,3},{2,0},{3,1},{4,6},{5,7},{6,4},{7,5},{8,10},{9,11},{10,... | collective-permute-start | bytes 2654216 | tf_op jit(solution)/shard_map/ppermute | solution.py:28
  12.2 63.2 %all-gather.7.cloned.1.call-start = ((), (), s32[]{:S(2)}) async-start(), calls=%async_computation.1 | async-start | bytes 2654208 | tf_op jit(solution)/shard_map/all_gather | solution.py:289
  12.2 23.3 %collective-permute-start.1 = (bf16[384,1152]{1,0:T(8,128)(2,1)S(1)}, bf16[384,1152]{1,0:T(8,128)(2,1)S(1)}, u32[]{:S(2)}, u32[]{:S(2)}) collective-permute-start(bf16[384,1152]{1,0:T(8,128)(2,1)S(1)} %get-tuple-element.27.when_inner), channel_id=1, source_target_pairs={{0,30},{1,31},{2,4},{3,5},{4,2},{5,3},{6,8},{7,9},{8,6},{9,7},{10,... | collective-permute-start | bytes 2654216 | tf_op jit(solution)/shard_map/ppermute | solution.py:28
  35.5 1.2 %copy-start.1 = (bf16[384,1152]{1,0:T(8,128)(2,1)}, bf16[384,1152]{1,0:T(8,128)(2,1)S(1)}, u32[]{:S(2)}) copy-start(bf16[384,1152]{1,0:T(8,128)(2,1)S(1)} %collective-permute-done.1.when_inner.b2) | copy-start | bytes 2654212
  45.0 3.2 %copy-start = (bf16[384,1152]{1,0:T(8,128)(2,1)}, bf16[384,1152]{1,0:T(8,128)(2,1)S(1)}, u32[]{:S(2)}) copy-start(bf16[384,1152]{1,0:T(8,128)(2,1)S(1)} %other.2.b3) | copy-start | bytes 2654212
  45.0 37.2 %collective-permute-start.3 = (bf16[384,1152]{1,0:T(8,128)(2,1)S(1)}, bf16[384,1152]{1,0:T(8,128)(2,1)}, u32[]{:S(2)}, u32[]{:S(2)}) collective-permute-start(bf16[384,1152]{1,0:T(8,128)(2,1)S(1)} %other.2.b3), channel_id=1, source_target_pairs={{0,30},{1,31},{2,4},{3,5},{4,2},{5,3},{6,8},{7,9},{8,6},{9,7},{10,... | collective-permute-start | bytes 2654216 | tf_op jit(solution)/shard_map/ppermute | solution.py:28
  57.3 1.2 %copy-start.2 = (f32[384,1152]{1,0:T(8,128)}, f32[384,1152]{1,0:T(8,128)S(1)}, u32[]{:S(2)}) copy-start(f32[384,1152]{1,0:T(8,128)S(1)} %get-tuple-element.34.unit_other) | copy-start | bytes 5308420
  58.5 1.3 %copy-start.4 = (f32[384,1152]{1,0:T(8,128)}, f32[384,1152]{1,0:T(8,128)S(1)}, u32[]{:S(2)}) copy-start(f32[384,1152]{1,0:T(8,128)S(1)} %get-tuple-element.36.grad_in) | copy-start | bytes 5308420
  59.7 1.2 %copy-start.6 = (f32[384,1152]{1,0:T(8,128)}, f32[384,1152]{1,0:T(8,128)S(1)}, u32[]{:S(2)}) copy-start(f32[384,1152]{1,0:T(8,128)S(1)} %get-tuple-element.39.part_w) | copy-start | bytes 5308420
  60.9 0.7 copy-start.8
  61.6 0.7 copy-start.10
  62.3 1.3 %copy-start.12 = (f32[384,1152]{1,0:T(8,128)}, f32[384,1152]{1,0:T(8,128)S(1)}, u32[]{:S(2)}) copy-start(f32[384,1152]{1,0:T(8,128)S(1)} %get-tuple-element.42.unit) | copy-start | bytes 5308420
  63.6 0.7 copy-start.14
  75.4 1.7 %copy-start.3 = (f32[384,1152]{1,0:T(8,128)S(1)}, f32[384,1152]{1,0:T(8,128)}, u32[]{:S(2)}) copy-start(f32[384,1152]{1,0:T(8,128)} %copy-done.2) | copy-start | bytes 5308420
  75.4 1.7 %copy-start.9 = (f32[384,1]{1,0:T(8,128)S(1)}, f32[384,1]{1,0:T(8,128)}, u32[]{:S(2)}) copy-start(f32[384,1]{1,0:T(8,128)} %copy-done.8) | copy-start | bytes 4612
  75.4 1.8 %copy-start.11 = (f32[384,128]{1,0:T(8,128)S(1)}, f32[384,128]{1,0:T(8,128)}, u32[]{:S(2)}) copy-start(f32[384,128]{1,0:T(8,128)} %copy-done.10) | copy-start | bytes 589828
  77.2 1.5 %copy-start.5 = (f32[384,1152]{1,0:T(8,128)S(1)}, f32[384,1152]{1,0:T(8,128)}, u32[]{:S(2)}) copy-start(f32[384,1152]{1,0:T(8,128)} %copy-done.4) | copy-start | bytes 5308420
  78.6 3.6 %copy-start.13 = (f32[384,1152]{1,0:T(8,128)S(1)}, f32[384,1152]{1,0:T(8,128)}, u32[]{:S(2)}) copy-start(f32[384,1152]{1,0:T(8,128)} %copy-done.12) | copy-start | bytes 5308420
  78.6 3.6 %copy-start.15 = (f32[384,1]{1,0:T(8,128)S(1)}, f32[384,1]{1,0:T(8,128)}, u32[]{:S(2)}) copy-start(f32[384,1]{1,0:T(8,128)} %copy-done.14) | copy-start | bytes 4612
  81.5 3.9 %collective-permute-start.2 = (bf16[384,1280]{1,0:T(8,128)(2,1)S(1)}, bf16[384,1280]{1,0:T(8,128)(2,1)S(1)}, u32[]{:S(2)}, u32[]{:S(2)}) collective-permute-start(bf16[384,1280]{1,0:T(8,128)(2,1)S(1)} %get-tuple-element.38), channel_id=1, source_target_pairs={{0,2},{1,3},{2,0},{3,1},{4,6},{5,7},{6,4},{7,5},{8,10},{9,11},{10,... | collective-permute-start | bytes 2949128 | tf_op jit(solution)/shard_map/ppermute | solution.py:28
  82.2 3.1 %copy-start.7 = (f32[384,1152]{1,0:T(8,128)S(1)}, f32[384,1152]{1,0:T(8,128)}, u32[]{:S(2)}) copy-start(f32[384,1152]{1,0:T(8,128)} %copy-done.6) | copy-start | bytes 5308420
Sparse Core Ops, SparseCore 0:
  12.3 31.4 all-gather.4
  45.9 29.4 all-gather.6

commit v16 on v14

--- a/solution.py
+++ b/solution.py
@@ -284,7 +284,7 @@
     scalars = jnp.where(first, score_scaling, score_shift)
     z_pair, unit_u, unit_other, inverse_u, inverse_other, grad_u, part_w, loss = compute(
         near_kernel,
-        (*in_hbm(image, text), slot1, *in_hbm(slot2, slot3)),
+        (*in_hbm(image, text, slot1, slot2), slot3),
         (pair, sums, sums, column, column, sums, sums, partial),
         "near_blocks",
         (pltpu.VMEM((2 * rows, width), BF16), raw) + (pltpu.VMEM((rows, width), F32),) * 2,

time: 54.4 us -> 54 us (level)
  no operation moved by 1% of the time
where the time goes in v16:
time: 54 us; the launch traced here: 53.9 us
  waiting for transfers between devices  25.1 us (46%)
  Pallas kernels  18.1 us (34%)
  starting transfers between devices  8.61 us (16%)
  between operations  2.01 us (4%)
    ppermute x6, waiting for transfers between devices, send(): return lax.ppermute(value, AXES, pairs)  25.1 us
    pallas_call x7, Pallas kernels, call(): pl.pallas_call(kernel, out_shape=outs, in_specs=in_specs, out_specs=out_s...  18.1 us
    ppermute x6, starting transfers between devices, send(): return lax.ppermute(value, AXES, pairs)  8.61 us
  transfers between devices with their start and end apart: 6, of which 3 were waited for; matrix products, arithmetic and copies ran while one was open for 0% of the time, Pallas kernels for 27%

profile of v16, /device:TPU:1, one launch (start us, length us, event | category | flops | bytes accessed | tf_op | source)
XLA Modules:
  0.0 53.9 jit_solution(17580184114283346050)
XLA Ops:
  0.6 1.5 %sort.1 = (bf16[384,1152]{1,0:T(8,128)(2,1)S(1)}, bf16[384,1152]{1,0:T(8,128)(2,1)S(1)}) custom-call(bf16[384,1152]{1,0:T(8,128)(2,1)} %image.3, bf16[384,1152]{1,0:T(8,128)(2,1)} %text.3), custom_call_target="tpu_custom_call" | custom-call | flops 1 | bytes 1 | tf_op jit(solution)/shard_map/sort/pallas_call | solution.py:236
  2.1 0.1 collective-permute-start
  2.2 2.7 %collective-permute-start.2 = (bf16[384,1152]{1,0:T(8,128)(2,1)S(1)}, bf16[384,1152]{1,0:T(8,128)(2,1)S(1)}, u32[]{:S(2)}, u32[]{:S(2)}) collective-permute-start(bf16[384,1152]{1,0:T(8,128)(2,1)S(1)} %get-tuple-element.25.when_inner), channel_id=1, source_target_pairs={{0,30},{1,31},{2,4},{3,5},{4,2},{5,3},{6,8},{7,9},{8,6},{9,7},{10,... | collective-permute-start | bytes 2654216 | tf_op jit(solution)/shard_map/ppermute | solution.py:28
  4.9 0.0 collective-permute-done.when_outer.b1
  4.9 0.0 copy-start
  4.9 0.2 pick.2
  5.1 2.1 %collective-permute-start.1 = (bf16[384,1152]{1,0:T(8,128)(2,1)S(1)}, bf16[384,1152]{1,0:T(8,128)(2,1)S(1)}, u32[]{:S(2)}, u32[]{:S(2)}) collective-permute-start(bf16[384,1152]{1,0:T(8,128)(2,1)S(1)} %pick.2), channel_id=1, source_target_pairs={{0,1},{1,0},{2,3},{3,2},{4,5},{5,4},{6,7},{7,6},{8,9},{9,8},{10,11... | collective-permute-start | bytes 2654216 | tf_op jit(solution)/shard_map/ppermute | solution.py:28
  7.2 18.2 %collective-permute-done.2.when_inner.b2 = bf16[384,1152]{1,0:T(8,128)(2,1)S(1)} collective-permute-done((bf16[384,1152]{1,0:T(8,128)(2,1)S(1)}, bf16[384,1152]{1,0:T(8,128)(2,1)S(1)}, u32[]{:S(2)}, u32[]{:S(2)}) %collective-permute-start.2) | collective-permute-done | bytes 884768 | tf_op jit(solution)/shard_map/ppermute | solution.py:28
  25.4 0.0 copy-start.1
  25.4 0.9 %pick.3 = bf16[384,1152]{1,0:T(8,128)(2,1)} custom-call(bf16[384,1152]{1,0:T(8,128)(2,1)S(1)} %get-tuple-element.24.when_outer, bf16[384,1152]{1,0:T(8,128)(2,1)S(1)} %collective-permute-done.2.when_inner.b2), custom_call_target="tpu_custom_call" | custom-call | flops 1 | bytes 1 | tf_op jit(solution)/shard_map/pick/pallas_call | solution.py:236
  26.3 0.0 copy-done
  26.3 1.8 %collective-permute-start.3 = (bf16[384,1152]{1,0:T(8,128)(2,1)}, bf16[384,1152]{1,0:T(8,128)(2,1)S(1)}, u32[]{:S(2)}, u32[]{:S(2)}) collective-permute-start(bf16[384,1152]{1,0:T(8,128)(2,1)} %pick.3), channel_id=1, source_target_pairs={{0,1},{1,0},{2,3},{3,2},{4,5},{5,4},{6,7},{7,6},{8,9},{9,8},{10,11... | collective-permute-start | bytes 2654216 | tf_op jit(solution)/shard_map/ppermute | solution.py:28
  28.2 0.0 collective-permute-done.1.b3
  28.2 1.8 %collective-permute-start.5 = (bf16[384,1152]{1,0:T(8,128)(2,1)S(1)}, bf16[384,1152]{1,0:T(8,128)(2,1)S(1)}, u32[]{:S(2)}, u32[]{:S(2)}) collective-permute-start(bf16[384,1152]{1,0:T(8,128)(2,1)S(1)} %collective-permute-done.1.b3), channel_id=1, source_target_pairs={{0,30},{1,31},{2,4},{3,5},{4,2},{5,3},{6,8},{7,9},{8,6},{9,7},{10,... | collective-permute-start | bytes 2654216 | tf_op jit(solution)/shard_map/ppermute | solution.py:28
  31.3 0.1 iota.7.scalars
  31.4 0.0 copy-done.1
  31.4 9.0 %near_blocks.1 = (bf16[768,1152]{1,0:T(8,128)(2,1)S(1)}, f32[384,1152]{1,0:T(8,128)S(1)}, f32[384,1152]{1,0:T(8,128)S(1)}, f32[384,1]{1,0:T(8,128)S(1)}, f32[384...) custom-call(f32[8,128]{1,0:T(8,128)S(1)} %iota.7.scalars, ...), custom_call_target="tpu_custom_call" | custom-call | flops 1 | bytes 1 | tf_op jit(solution)/shard_map/near_blocks/pallas_call | solution.py:236
  40.4 5.7 %collective-permute-done.3.b5 = bf16[384,1152]{1,0:T(8,128)(2,1)S(1)} collective-permute-done((bf16[384,1152]{1,0:T(8,128)(2,1)}, bf16[384,1152]{1,0:T(8,128)(2,1)S(1)}, u32[]{:S(2)}, u32[]{:S(2)}) %collective-permute-start.3) | collective-permute-done | bytes 884768 | tf_op jit(solution)/shard_map/ppermute | solution.py:28
  46.1 2.8 %fifth_block.1 = (f32[384,1152]{1,0:T(8,128)S(1)}, f32[384,128]{1,0:T(8,128)S(1)}, bf16[384,1280]{1,0:T(8,128)(2,1)S(1)}) custom-call(f32[8,128]{1,0:T(8,128)S(1)} %iota.7.scalars, bf16[384,1152]{1,0:T(8,128)(2,1)S(1)} %collective-permute-done.3.b5, bf16[768,1152]{1,0:T(8,128)(2,1)S(1)} %get-tuple-element.29.z_pair, ...), custom_call_target="tpu_custom_call" | custom-call | flops 1 | bytes 1 | tf_op jit(solution)/shard_map/fifth_block/pallas_call | solution.py:236
  48.9 0.1 collective-permute-start.4
  49.0 1.2 %collective-permute-done.5.b4 = bf16[384,1152]{1,0:T(8,128)(2,1)S(1)} collective-permute-done((bf16[384,1152]{1,0:T(8,128)(2,1)S(1)}, bf16[384,1152]{1,0:T(8,128)(2,1)S(1)}, u32[]{:S(2)}, u32[]{:S(2)}) %collective-permute-start.5) | collective-permute-done | bytes 884768 | tf_op jit(solution)/shard_map/ppermute | solution.py:28
  50.2 1.8 %finish_u.1 = (bf16[384,1152]{1,0:T(8,128)(2,1)S(1)}, f32[384,128]{1,0:T(8,128)S(1)}) custom-call(f32[8,128]{1,0:T(8,128)S(1)} %iota.7.scalars, bf16[384,1152]{1,0:T(8,128)(2,1)S(1)} %collective-permute-done.5.b4, bf16[768,1152]{1,0:T(8,128)(2,1)S(1)} %get-tuple-element.29.z_pair, f32[384,1152]{1,0:T(8,128)S(1)} %get-tuple-element.36.grad_u, ...), custom_call_target="tpu_custom_call" | custom-call | flops 10000000000 | bytes 1 | tf_op jit(solution)/shard_map/finish_u/pallas_call | solution.py:236
  52.0 0.0 collective-permute-done.4.last
  52.0 1.8 %finish_w.1 = (bf16[384,1152]{1,0:T(8,128)(2,1)}, bf16[384,1152]{1,0:T(8,128)(2,1)}, f32[384]{0:T(512)}) custom-call(bf16[384,1280]{1,0:T(8,128)(2,1)S(1)} %collective-permute-done.4.last, f32[384,1152]{1,0:T(8,128)S(1)} %get-tuple-element.35.part_w, f32[384,128]{1,0:T(8,128)S(1)} %get-tuple-element.40.loss_in, bf16[384,1152]{1,0:T(8,128)(2,1)S(1)} %get-tuple-element.41.done_u), custom_call_target="tpu_custom_call" | custom-call | flops 1 | bytes 1 | tf_op jit(solution)/shard_map/finish_w/pallas_call | solution.py:236
  (1 shorter events, 0.0 us)
Async XLA Ops:
  2.1 2.8 %collective-permute-start = (bf16[384,1152]{1,0:T(8,128)(2,1)S(1)}, bf16[384,1152]{1,0:T(8,128)(2,1)S(1)}, u32[]{:S(2)}, u32[]{:S(2)}) collective-permute-start(bf16[384,1152]{1,0:T(8,128)(2,1)S(1)} %get-tuple-element.24.when_outer), channel_id=1, source_target_pairs={{0,2},{1,3},{2,0},{3,1},{4,6},{5,7},{6,4},{7,5},{8,10},{9,11},{10,... | collective-permute-start | bytes 2654216 | tf_op jit(solution)/shard_map/ppermute | solution.py:28
  2.2 23.2 %collective-permute-start.2 = (bf16[384,1152]{1,0:T(8,128)(2,1)S(1)}, bf16[384,1152]{1,0:T(8,128)(2,1)S(1)}, u32[]{:S(2)}, u32[]{:S(2)}) collective-permute-start(bf16[384,1152]{1,0:T(8,128)(2,1)S(1)} %get-tuple-element.25.when_inner), channel_id=1, source_target_pairs={{0,30},{1,31},{2,4},{3,5},{4,2},{5,3},{6,8},{7,9},{8,6},{9,7},{10,... | collective-permute-start | bytes 2654216 | tf_op jit(solution)/shard_map/ppermute | solution.py:28
  4.9 21.4 %copy-start = (bf16[384,1152]{1,0:T(8,128)(2,1)}, bf16[384,1152]{1,0:T(8,128)(2,1)S(1)}, u32[]{:S(2)}) copy-start(bf16[384,1152]{1,0:T(8,128)(2,1)S(1)} %collective-permute-done.when_outer.b1) | copy-start | bytes 2654212
  5.1 23.1 %collective-permute-start.1 = (bf16[384,1152]{1,0:T(8,128)(2,1)S(1)}, bf16[384,1152]{1,0:T(8,128)(2,1)S(1)}, u32[]{:S(2)}, u32[]{:S(2)}) collective-permute-start(bf16[384,1152]{1,0:T(8,128)(2,1)S(1)} %pick.2), channel_id=1, source_target_pairs={{0,1},{1,0},{2,3},{3,2},{4,5},{5,4},{6,7},{7,6},{8,9},{9,8},{10,11... | collective-permute-start | bytes 2654216 | tf_op jit(solution)/shard_map/ppermute | solution.py:28
  25.4 6.0 %copy-start.1 = (bf16[384,1152]{1,0:T(8,128)(2,1)}, bf16[384,1152]{1,0:T(8,128)(2,1)S(1)}, u32[]{:S(2)}) copy-start(bf16[384,1152]{1,0:T(8,128)(2,1)S(1)} %collective-permute-done.2.when_inner.b2) | copy-start | bytes 2654212
  26.3 19.7 %collective-permute-start.3 = (bf16[384,1152]{1,0:T(8,128)(2,1)}, bf16[384,1152]{1,0:T(8,128)(2,1)S(1)}, u32[]{:S(2)}, u32[]{:S(2)}) collective-permute-start(bf16[384,1152]{1,0:T(8,128)(2,1)} %pick.3), channel_id=1, source_target_pairs={{0,1},{1,0},{2,3},{3,2},{4,5},{5,4},{6,7},{7,6},{8,9},{9,8},{10,11... | collective-permute-start | bytes 2654216 | tf_op jit(solution)/shard_map/ppermute | solution.py:28
  28.2 22.0 %collective-permute-start.5 = (bf16[384,1152]{1,0:T(8,128)(2,1)S(1)}, bf16[384,1152]{1,0:T(8,128)(2,1)S(1)}, u32[]{:S(2)}, u32[]{:S(2)}) collective-permute-start(bf16[384,1152]{1,0:T(8,128)(2,1)S(1)} %collective-permute-done.1.b3), channel_id=1, source_target_pairs={{0,30},{1,31},{2,4},{3,5},{4,2},{5,3},{6,8},{7,9},{8,6},{9,7},{10,... | collective-permute-start | bytes 2654216 | tf_op jit(solution)/shard_map/ppermute | solution.py:28
  48.9 3.1 %collective-permute-start.4 = (bf16[384,1280]{1,0:T(8,128)(2,1)S(1)}, bf16[384,1280]{1,0:T(8,128)(2,1)S(1)}, u32[]{:S(2)}, u32[]{:S(2)}) collective-permute-start(bf16[384,1280]{1,0:T(8,128)(2,1)S(1)} %get-tuple-element.34), channel_id=1, source_target_pairs={{0,2},{1,3},{2,0},{3,1},{4,6},{5,7},{6,4},{7,5},{8,10},{9,11},{10,... | collective-permute-start | bytes 2949128 | tf_op jit(solution)/shard_map/ppermute | solution.py:28

commit v17 on v16

--- a/solution.py
+++ b/solution.py
@@ -278,7 +278,7 @@
     slot2 = send(u, GROUP_SHIFT)
     slot3 = send(pick(slot1, u, block), X_SWAP)
     slot4 = send(slot3, GROUP_SHIFT)
-    slot5 = send(pick(w, slot2, pltpu.HBM((rows, width), BF16)), X_SWAP)
+    slot5 = send(pick(w, slot2, block), X_SWAP)
     slot3, score_scaling, score_shift = lax.optimization_barrier((slot3, score_scaling, score_shift))
     first = lax.broadcasted_iota(jnp.int32, (8, 128), 0) == 0
     scalars = jnp.where(first, score_scaling, score_shift)

time: 54 us -> 54.9 us (1.017)
  starting transfers between devices: 8.61 us -> 9.35 us
    ppermute x6, starting transfers between devices: 8.61 us -> 9.35 us  [send(): return lax.ppermute(value, AXES, pairs)]
  transfers between devices with their start and end apart: 6 -> 6, of which waited for: 3 -> 3; matrix products, arithmetic and copies ran while one was open for 0% -> 0% of each run, Pallas kernels for 27% -> 28%
where the time goes in v17:
time: 54.9 us; the launch traced here: 54.6 us
  waiting for transfers between devices  24.7 us (45%)
  Pallas kernels  18.5 us (34%)
  starting transfers between devices  9.35 us (17%)
  between operations  2.01 us (4%)
    ppermute x6, waiting for transfers between devices, send(): return lax.ppermute(value, AXES, pairs)  24.7 us
    pallas_call x7, Pallas kernels, call(): pl.pallas_call(kernel, out_shape=outs, in_specs=in_specs, out_specs=out_s...  18.5 us
    ppermute x6, starting transfers between devices, send(): return lax.ppermute(value, AXES, pairs)  9.35 us
  transfers between devices with their start and end apart: 6, of which 3 were waited for; matrix products, arithmetic and copies ran while one was open for 0% of the time, Pallas kernels for 28%

profile of v17, /device:TPU:1, one launch (start us, length us, event | category | flops | bytes accessed | tf_op | source)
XLA Modules:
  0.0 54.6 jit_solution(18046149852879221956)
XLA Ops:
  0.6 1.5 %sort.1 = (bf16[384,1152]{1,0:T(8,128)(2,1)S(1)}, bf16[384,1152]{1,0:T(8,128)(2,1)S(1)}) custom-call(bf16[384,1152]{1,0:T(8,128)(2,1)} %image.3, bf16[384,1152]{1,0:T(8,128)(2,1)} %text.3), custom_call_target="tpu_custom_call" | custom-call | flops 1 | bytes 1 | tf_op jit(solution)/shard_map/sort/pallas_call | solution.py:236
  2.1 0.1 collective-permute-start
  2.2 2.7 %collective-permute-start.2 = (bf16[384,1152]{1,0:T(8,128)(2,1)S(1)}, bf16[384,1152]{1,0:T(8,128)(2,1)S(1)}, u32[]{:S(2)}, u32[]{:S(2)}) collective-permute-start(bf16[384,1152]{1,0:T(8,128)(2,1)S(1)} %get-tuple-element.25.when_inner), channel_id=1, source_target_pairs={{0,30},{1,31},{2,4},{3,5},{4,2},{5,3},{6,8},{7,9},{8,6},{9,7},{10,... | collective-permute-start | bytes 2654216 | tf_op jit(solution)/shard_map/ppermute | solution.py:28
  4.9 0.0 collective-permute-done.when_outer.b1
  4.9 0.0 copy-start
  4.9 0.2 pick.2
  5.1 2.1 %collective-permute-start.1 = (bf16[384,1152]{1,0:T(8,128)(2,1)S(1)}, bf16[384,1152]{1,0:T(8,128)(2,1)S(1)}, u32[]{:S(2)}, u32[]{:S(2)}) collective-permute-start(bf16[384,1152]{1,0:T(8,128)(2,1)S(1)} %pick.2), channel_id=1, source_target_pairs={{0,1},{1,0},{2,3},{3,2},{4,5},{5,4},{6,7},{7,6},{8,9},{9,8},{10,11... | collective-permute-start | bytes 2654216 | tf_op jit(solution)/shard_map/ppermute | solution.py:28
  7.2 18.2 %collective-permute-done.2.when_inner.b2 = bf16[384,1152]{1,0:T(8,128)(2,1)S(1)} collective-permute-done((bf16[384,1152]{1,0:T(8,128)(2,1)S(1)}, bf16[384,1152]{1,0:T(8,128)(2,1)S(1)}, u32[]{:S(2)}, u32[]{:S(2)}) %collective-permute-start.2) | collective-permute-done | bytes 884768 | tf_op jit(solution)/shard_map/ppermute | solution.py:28
  25.4 0.0 copy-start.1
  25.4 0.2 pick.3
  25.6 0.0 copy-done
  25.6 1.8 %collective-permute-start.3 = (bf16[384,1152]{1,0:T(8,128)(2,1)S(1)}, bf16[384,1152]{1,0:T(8,128)(2,1)}, u32[]{:S(2)}, u32[]{:S(2)}) collective-permute-start(bf16[384,1152]{1,0:T(8,128)(2,1)S(1)} %pick.3), channel_id=1, source_target_pairs={{0,1},{1,0},{2,3},{3,2},{4,5},{5,4},{6,7},{7,6},{8,9},{9,8},{10,11... | collective-permute-start | bytes 2654216 | tf_op jit(solution)/shard_map/ppermute | solution.py:28
  27.4 0.0 collective-permute-done.1.b3
  27.4 2.6 %collective-permute-start.5 = (bf16[384,1152]{1,0:T(8,128)(2,1)S(1)}, bf16[384,1152]{1,0:T(8,128)(2,1)S(1)}, u32[]{:S(2)}, u32[]{:S(2)}) collective-permute-start(bf16[384,1152]{1,0:T(8,128)(2,1)S(1)} %collective-permute-done.1.b3), channel_id=1, source_target_pairs={{0,30},{1,31},{2,4},{3,5},{4,2},{5,3},{6,8},{7,9},{8,6},{9,7},{10,... | collective-permute-start | bytes 2654216 | tf_op jit(solution)/shard_map/ppermute | solution.py:28
  31.3 0.1 iota.7.scalars
  31.4 0.0 copy-done.1
  31.4 9.0 %near_blocks.1 = (bf16[768,1152]{1,0:T(8,128)(2,1)S(1)}, f32[384,1152]{1,0:T(8,128)S(1)}, f32[384,1152]{1,0:T(8,128)S(1)}, f32[384,1]{1,0:T(8,128)S(1)}, f32[384...) custom-call(f32[8,128]{1,0:T(8,128)S(1)} %iota.7.scalars, ...), custom_call_target="tpu_custom_call" | custom-call | flops 1 | bytes 1 | tf_op jit(solution)/shard_map/near_blocks/pallas_call | solution.py:236
  40.4 5.8 %collective-permute-done.3.b5 = bf16[384,1152]{1,0:T(8,128)(2,1)} collective-permute-done((bf16[384,1152]{1,0:T(8,128)(2,1)S(1)}, bf16[384,1152]{1,0:T(8,128)(2,1)}, u32[]{:S(2)}, u32[]{:S(2)}) %collective-permute-start.3) | collective-permute-done | bytes 884768 | tf_op jit(solution)/shard_map/ppermute | solution.py:28
  46.2 4.0 %fifth_block.1 = (f32[384,1152]{1,0:T(8,128)S(1)}, f32[384,128]{1,0:T(8,128)S(1)}, bf16[384,1280]{1,0:T(8,128)(2,1)S(1)}) custom-call(f32[8,128]{1,0:T(8,128)S(1)} %iota.7.scalars, bf16[384,1152]{1,0:T(8,128)(2,1)} %collective-permute-done.3.b5, bf16[768,1152]{1,0:T(8,128)(2,1)S(1)} %get-tuple-element.29.z_pair, ...), custom_call_target="tpu_custom_call" | custom-call | flops 1 | bytes 1 | tf_op jit(solution)/shard_map/fifth_block/pallas_call | solution.py:236
  50.2 0.1 collective-permute-start.4
  50.3 0.0 collective-permute-done.5.b4
  50.3 1.8 %finish_u.1 = (bf16[384,1152]{1,0:T(8,128)(2,1)S(1)}, f32[384,128]{1,0:T(8,128)S(1)}) custom-call(f32[8,128]{1,0:T(8,128)S(1)} %iota.7.scalars, bf16[384,1152]{1,0:T(8,128)(2,1)S(1)} %collective-permute-done.5.b4, bf16[768,1152]{1,0:T(8,128)(2,1)S(1)} %get-tuple-element.29.z_pair, f32[384,1152]{1,0:T(8,128)S(1)} %get-tuple-element.36.grad_u, ...), custom_call_target="tpu_custom_call" | custom-call | flops 10000000000 | bytes 1 | tf_op jit(solution)/shard_map/finish_u/pallas_call | solution.py:236
  52.1 0.7 %collective-permute-done.4.last = bf16[384,1280]{1,0:T(8,128)(2,1)S(1)} collective-permute-done((bf16[384,1280]{1,0:T(8,128)(2,1)S(1)}, bf16[384,1280]{1,0:T(8,128)(2,1)S(1)}, u32[]{:S(2)}, u32[]{:S(2)}) %collective-permute-start.4) | collective-permute-done | bytes 983072 | tf_op jit(solution)/shard_map/ppermute | solution.py:28
  52.8 1.8 %finish_w.1 = (bf16[384,1152]{1,0:T(8,128)(2,1)}, bf16[384,1152]{1,0:T(8,128)(2,1)}, f32[384]{0:T(512)}) custom-call(bf16[384,1280]{1,0:T(8,128)(2,1)S(1)} %collective-permute-done.4.last, f32[384,1152]{1,0:T(8,128)S(1)} %get-tuple-element.35.part_w, f32[384,128]{1,0:T(8,128)S(1)} %get-tuple-element.40.loss_in, bf16[384,1152]{1,0:T(8,128)(2,1)S(1)} %get-tuple-element.41.done_u), custom_call_target="tpu_custom_call" | custom-call | flops 1 | bytes 1 | tf_op jit(solution)/shard_map/finish_w/pallas_call | solution.py:236
  (1 shorter events, 0.0 us)
Async XLA Ops:
  2.1 2.8 %collective-permute-start = (bf16[384,1152]{1,0:T(8,128)(2,1)S(1)}, bf16[384,1152]{1,0:T(8,128)(2,1)S(1)}, u32[]{:S(2)}, u32[]{:S(2)}) collective-permute-start(bf16[384,1152]{1,0:T(8,128)(2,1)S(1)} %get-tuple-element.24.when_outer), channel_id=1, source_target_pairs={{0,2},{1,3},{2,0},{3,1},{4,6},{5,7},{6,4},{7,5},{8,10},{9,11},{10,... | collective-permute-start | bytes 2654216 | tf_op jit(solution)/shard_map/ppermute | solution.py:28
  2.2 23.2 %collective-permute-start.2 = (bf16[384,1152]{1,0:T(8,128)(2,1)S(1)}, bf16[384,1152]{1,0:T(8,128)(2,1)S(1)}, u32[]{:S(2)}, u32[]{:S(2)}) collective-permute-start(bf16[384,1152]{1,0:T(8,128)(2,1)S(1)} %get-tuple-element.25.when_inner), channel_id=1, source_target_pairs={{0,30},{1,31},{2,4},{3,5},{4,2},{5,3},{6,8},{7,9},{8,6},{9,7},{10,... | collective-permute-start | bytes 2654216 | tf_op jit(solution)/shard_map/ppermute | solution.py:28
  4.9 20.7 %copy-start = (bf16[384,1152]{1,0:T(8,128)(2,1)}, bf16[384,1152]{1,0:T(8,128)(2,1)S(1)}, u32[]{:S(2)}) copy-start(bf16[384,1152]{1,0:T(8,128)(2,1)S(1)} %collective-permute-done.when_outer.b1) | copy-start | bytes 2654212
  5.1 22.3 %collective-permute-start.1 = (bf16[384,1152]{1,0:T(8,128)(2,1)S(1)}, bf16[384,1152]{1,0:T(8,128)(2,1)S(1)}, u32[]{:S(2)}, u32[]{:S(2)}) collective-permute-start(bf16[384,1152]{1,0:T(8,128)(2,1)S(1)} %pick.2), channel_id=1, source_target_pairs={{0,1},{1,0},{2,3},{3,2},{4,5},{5,4},{6,7},{7,6},{8,9},{9,8},{10,11... | collective-permute-start | bytes 2654216 | tf_op jit(solution)/shard_map/ppermute | solution.py:28
  25.4 6.0 %copy-start.1 = (bf16[384,1152]{1,0:T(8,128)(2,1)}, bf16[384,1152]{1,0:T(8,128)(2,1)S(1)}, u32[]{:S(2)}) copy-start(bf16[384,1152]{1,0:T(8,128)(2,1)S(1)} %collective-permute-done.2.when_inner.b2) | copy-start | bytes 2654212
  25.6 20.6 %collective-permute-start.3 = (bf16[384,1152]{1,0:T(8,128)(2,1)S(1)}, bf16[384,1152]{1,0:T(8,128)(2,1)}, u32[]{:S(2)}, u32[]{:S(2)}) collective-permute-start(bf16[384,1152]{1,0:T(8,128)(2,1)S(1)} %pick.3), channel_id=1, source_target_pairs={{0,1},{1,0},{2,3},{3,2},{4,5},{5,4},{6,7},{7,6},{8,9},{9,8},{10,11... | collective-permute-start | bytes 2654216 | tf_op jit(solution)/shard_map/ppermute | solution.py:28
  27.4 22.8 %collective-permute-start.5 = (bf16[384,1152]{1,0:T(8,128)(2,1)S(1)}, bf16[384,1152]{1,0:T(8,128)(2,1)S(1)}, u32[]{:S(2)}, u32[]{:S(2)}) collective-permute-start(bf16[384,1152]{1,0:T(8,128)(2,1)S(1)} %collective-permute-done.1.b3), channel_id=1, source_target_pairs={{0,30},{1,31},{2,4},{3,5},{4,2},{5,3},{6,8},{7,9},{8,6},{9,7},{10,... | collective-permute-start | bytes 2654216 | tf_op jit(solution)/shard_map/ppermute | solution.py:28
  50.2 2.6 %collective-permute-start.4 = (bf16[384,1280]{1,0:T(8,128)(2,1)S(1)}, bf16[384,1280]{1,0:T(8,128)(2,1)S(1)}, u32[]{:S(2)}, u32[]{:S(2)}) collective-permute-start(bf16[384,1280]{1,0:T(8,128)(2,1)S(1)} %get-tuple-element.34), channel_id=1, source_target_pairs={{0,2},{1,3},{2,0},{3,1},{4,6},{5,7},{6,4},{7,5},{8,10},{9,11},{10,... | collective-permute-start | bytes 2949128 | tf_op jit(solution)/shard_map/ppermute | solution.py:28

commit v18 on v16

--- a/solution.py
+++ b/solution.py
@@ -85,6 +85,20 @@
         p = jnp.exp(scale * score + shift)
         coef = (sigmoid_of(p) * scale).astype(BF16)
         products.append(dot_nn(coef, others))
+        losses.append(softplus_lanes(p))
+    return jnp.concatenate(products), jnp.concatenate(losses)
+
+
+def raw_terms(own, raw, scale, shift):
+    values = raw.astype(F32)
+    inverse = 1.0 / jnp.sqrt(jnp.sum(values * values, axis=1, keepdims=True) + 1e-06)
+    factor = scale * jnp.transpose(jnp.broadcast_to(inverse, (raw.shape[0], 128)))[:1]
+    half = own.shape[0] // 2
+    scores = [dot_nt(own[:half], raw), dot_nt(own[half:], raw)]
+    products, losses = [], []
+    for score in scores:
+        p = jnp.exp(factor * score + shift)
+        products.append(dot_nn((sigmoid_of(p) * factor).astype(BF16), raw))
         losses.append(softplus_lanes(p))
     return jnp.concatenate(products), jnp.concatenate(losses)
 
@@ -183,19 +197,19 @@
 
 
 def fifth_kernel(
-    scalars, b5, z_pair, unit_other, inverse_other, grad_in, loss_in, grad_u, loss, for_partner, work
+    scalars, b5, z_pair, unit_other, inverse_other, grad_in, loss_in, grad_u, loss, for_partner
 ):
     rows, width = b5.shape
-    term, row_loss = pair_step(z_pair[...], (b5[...],), *scalar_pair(scalars), work)
+    term, row_loss = raw_terms(z_pair[...], b5[...], *scalar_pair(scalars))
     for_partner[:, :width] = project(unit_other[...], inverse_other[...], term[rows:]).astype(BF16)
     for_partner[:, width:] = row_loss[rows:].astype(BF16)
     grad_u[...] = grad_in[...] + term[:rows]
     loss[...] = loss_in[...] + image_is_u().astype(F32) * row_loss[:rows]
 
 
-def u_kernel(scalars, b4, z_pair, grad_u, loss_in, unit, inverse, done_u, loss, work):
+def u_kernel(scalars, b4, z_pair, grad_u, loss_in, unit, inverse, done_u, loss):
     rows = done_u.shape[0]
-    term, row_loss = pair_step(z_pair[:rows], (b4[...],), *scalar_pair(scalars), work)
+    term, row_loss = raw_terms(z_pair[:rows], b4[...], *scalar_pair(scalars))
     loss[...] = loss_in[...] + image_is_u().astype(F32) * row_loss
     done_u[...] = project(unit[...], inverse[...], grad_u[...] + term).astype(BF16)
 
@@ -294,7 +308,7 @@
         (pltpu.with_memory_space_constraint(slot5, pltpu.VMEM), z_pair, unit_other, inverse_other, grad_u, loss),
         (sums, partial, jax.ShapeDtypeStruct((rows, width + 128), BF16)),
         "fifth_block",
-        (raw,),
+        (),
     )
     last = send(for_partner, CORE_SWAP)
     done_u, loss = compute(
@@ -302,7 +316,7 @@
         (pltpu.with_memory_space_constraint(slot4, pltpu.VMEM), z_pair, grad_u, loss, unit_u, inverse_u),
         (block, partial),
         "finish_u",
-        (raw,),
+        (),
         10**10,
     )
     image_grad, text_grad, loss_rows = call(

time: 54 us -> 53.9 us (level)
  no operation moved by 1% of the time
where the time goes in v18:
time: 53.9 us; the launch traced here: 53.7 us
  waiting for transfers between devices  25.3 us (47%)
  Pallas kernels  17.7 us (33%)
  starting transfers between devices  8.61 us (16%)
  between operations  2.01 us (4%)
    ppermute x6, waiting for transfers between devices, send(): return lax.ppermute(value, AXES, pairs)  25.3 us
    pallas_call x7, Pallas kernels, call(): pl.pallas_call(kernel, out_shape=outs, in_specs=in_specs, out_specs=out_s...  17.7 us
    ppermute x6, starting transfers between devices, send(): return lax.ppermute(value, AXES, pairs)  8.61 us
  transfers between devices with their start and end apart: 6, of which 3 were waited for; matrix products, arithmetic and copies ran while one was open for 0% of the time, Pallas kernels for 27%

profile of v18, /device:TPU:1, one launch (start us, length us, event | category | flops | bytes accessed | tf_op | source)
XLA Modules:
  0.0 53.7 jit_solution(1030246973288484600)
XLA Ops:
  0.6 1.5 %sort.1 = (bf16[384,1152]{1,0:T(8,128)(2,1)S(1)}, bf16[384,1152]{1,0:T(8,128)(2,1)S(1)}) custom-call(bf16[384,1152]{1,0:T(8,128)(2,1)} %image.3, bf16[384,1152]{1,0:T(8,128)(2,1)} %text.3), custom_call_target="tpu_custom_call" | custom-call | flops 1 | bytes 1 | tf_op jit(solution)/shard_map/sort/pallas_call | solution.py:250
  2.1 0.1 collective-permute-start
  2.2 2.7 %collective-permute-start.2 = (bf16[384,1152]{1,0:T(8,128)(2,1)S(1)}, bf16[384,1152]{1,0:T(8,128)(2,1)S(1)}, u32[]{:S(2)}, u32[]{:S(2)}) collective-permute-start(bf16[384,1152]{1,0:T(8,128)(2,1)S(1)} %get-tuple-element.25.when_inner), channel_id=1, source_target_pairs={{0,30},{1,31},{2,4},{3,5},{4,2},{5,3},{6,8},{7,9},{8,6},{9,7},{10,... | collective-permute-start | bytes 2654216 | tf_op jit(solution)/shard_map/ppermute | solution.py:28
  4.9 0.0 collective-permute-done.when_outer.b1
  4.9 0.0 copy-start
  4.9 0.2 pick.2
  5.1 2.1 %collective-permute-start.1 = (bf16[384,1152]{1,0:T(8,128)(2,1)S(1)}, bf16[384,1152]{1,0:T(8,128)(2,1)S(1)}, u32[]{:S(2)}, u32[]{:S(2)}) collective-permute-start(bf16[384,1152]{1,0:T(8,128)(2,1)S(1)} %pick.2), channel_id=1, source_target_pairs={{0,1},{1,0},{2,3},{3,2},{4,5},{5,4},{6,7},{7,6},{8,9},{9,8},{10,11... | collective-permute-start | bytes 2654216 | tf_op jit(solution)/shard_map/ppermute | solution.py:28
  7.2 18.2 %collective-permute-done.2.when_inner.b2 = bf16[384,1152]{1,0:T(8,128)(2,1)S(1)} collective-permute-done((bf16[384,1152]{1,0:T(8,128)(2,1)S(1)}, bf16[384,1152]{1,0:T(8,128)(2,1)S(1)}, u32[]{:S(2)}, u32[]{:S(2)}) %collective-permute-start.2) | collective-permute-done | bytes 884768 | tf_op jit(solution)/shard_map/ppermute | solution.py:28
  25.4 0.0 copy-start.1
  25.4 0.9 %pick.3 = bf16[384,1152]{1,0:T(8,128)(2,1)} custom-call(bf16[384,1152]{1,0:T(8,128)(2,1)S(1)} %get-tuple-element.24.when_outer, bf16[384,1152]{1,0:T(8,128)(2,1)S(1)} %collective-permute-done.2.when_inner.b2), custom_call_target="tpu_custom_call" | custom-call | flops 1 | bytes 1 | tf_op jit(solution)/shard_map/pick/pallas_call | solution.py:250
  26.3 0.0 copy-done
  26.3 1.8 %collective-permute-start.3 = (bf16[384,1152]{1,0:T(8,128)(2,1)}, bf16[384,1152]{1,0:T(8,128)(2,1)S(1)}, u32[]{:S(2)}, u32[]{:S(2)}) collective-permute-start(bf16[384,1152]{1,0:T(8,128)(2,1)} %pick.3), channel_id=1, source_target_pairs={{0,1},{1,0},{2,3},{3,2},{4,5},{5,4},{6,7},{7,6},{8,9},{9,8},{10,11... | collective-permute-start | bytes 2654216 | tf_op jit(solution)/shard_map/ppermute | solution.py:28
  28.2 0.0 collective-permute-done.1.b3
  28.2 1.8 %collective-permute-start.5 = (bf16[384,1152]{1,0:T(8,128)(2,1)S(1)}, bf16[384,1152]{1,0:T(8,128)(2,1)S(1)}, u32[]{:S(2)}, u32[]{:S(2)}) collective-permute-start(bf16[384,1152]{1,0:T(8,128)(2,1)S(1)} %collective-permute-done.1.b3), channel_id=1, source_target_pairs={{0,30},{1,31},{2,4},{3,5},{4,2},{5,3},{6,8},{7,9},{8,6},{9,7},{10,... | collective-permute-start | bytes 2654216 | tf_op jit(solution)/shard_map/ppermute | solution.py:28
  31.3 0.1 iota.7.scalars
  31.4 0.0 copy-done.1
  31.4 9.0 %near_blocks.1 = (bf16[768,1152]{1,0:T(8,128)(2,1)S(1)}, f32[384,1152]{1,0:T(8,128)S(1)}, f32[384,1152]{1,0:T(8,128)S(1)}, f32[384,1]{1,0:T(8,128)S(1)}, f32[384...) custom-call(f32[8,128]{1,0:T(8,128)S(1)} %iota.7.scalars, ...), custom_call_target="tpu_custom_call" | custom-call | flops 1 | bytes 1 | tf_op jit(solution)/shard_map/near_blocks/pallas_call | solution.py:250
  40.4 5.7 %collective-permute-done.3.b5 = bf16[384,1152]{1,0:T(8,128)(2,1)S(1)} collective-permute-done((bf16[384,1152]{1,0:T(8,128)(2,1)}, bf16[384,1152]{1,0:T(8,128)(2,1)S(1)}, u32[]{:S(2)}, u32[]{:S(2)}) %collective-permute-start.3) | collective-permute-done | bytes 884768 | tf_op jit(solution)/shard_map/ppermute | solution.py:28
  46.1 2.6 %fifth_block.1 = (f32[384,1152]{1,0:T(8,128)S(1)}, f32[384,128]{1,0:T(8,128)S(1)}, bf16[384,1280]{1,0:T(8,128)(2,1)S(1)}) custom-call(f32[8,128]{1,0:T(8,128)S(1)} %iota.7.scalars, bf16[384,1152]{1,0:T(8,128)(2,1)S(1)} %collective-permute-done.3.b5, bf16[768,1152]{1,0:T(8,128)(2,1)S(1)} %get-tuple-element.29.z_pair, ...), custom_call_target="tpu_custom_call" | custom-call | flops 1 | bytes 1 | tf_op jit(solution)/shard_map/fifth_block/pallas_call | solution.py:250
  48.7 0.1 collective-permute-start.4
  48.8 1.4 %collective-permute-done.5.b4 = bf16[384,1152]{1,0:T(8,128)(2,1)S(1)} collective-permute-done((bf16[384,1152]{1,0:T(8,128)(2,1)S(1)}, bf16[384,1152]{1,0:T(8,128)(2,1)S(1)}, u32[]{:S(2)}, u32[]{:S(2)}) %collective-permute-start.5) | collective-permute-done | bytes 884768 | tf_op jit(solution)/shard_map/ppermute | solution.py:28
  50.2 1.7 %finish_u.1 = (bf16[384,1152]{1,0:T(8,128)(2,1)S(1)}, f32[384,128]{1,0:T(8,128)S(1)}) custom-call(f32[8,128]{1,0:T(8,128)S(1)} %iota.7.scalars, bf16[384,1152]{1,0:T(8,128)(2,1)S(1)} %collective-permute-done.5.b4, bf16[768,1152]{1,0:T(8,128)(2,1)S(1)} %get-tuple-element.29.z_pair, f32[384,1152]{1,0:T(8,128)S(1)} %get-tuple-element.36.grad_u, ...), custom_call_target="tpu_custom_call" | custom-call | flops 10000000000 | bytes 1 | tf_op jit(solution)/shard_map/finish_u/pallas_call | solution.py:250
  51.9 0.0 collective-permute-done.4.last
  51.9 1.8 %finish_w.1 = (bf16[384,1152]{1,0:T(8,128)(2,1)}, bf16[384,1152]{1,0:T(8,128)(2,1)}, f32[384]{0:T(512)}) custom-call(bf16[384,1280]{1,0:T(8,128)(2,1)S(1)} %collective-permute-done.4.last, f32[384,1152]{1,0:T(8,128)S(1)} %get-tuple-element.35.part_w, f32[384,128]{1,0:T(8,128)S(1)} %get-tuple-element.40.loss_in, bf16[384,1152]{1,0:T(8,128)(2,1)S(1)} %get-tuple-element.41.done_u), custom_call_target="tpu_custom_call" | custom-call | flops 1 | bytes 1 | tf_op jit(solution)/shard_map/finish_w/pallas_call | solution.py:250
  (1 shorter events, 0.0 us)
Async XLA Ops:
  2.1 2.8 %collective-permute-start = (bf16[384,1152]{1,0:T(8,128)(2,1)S(1)}, bf16[384,1152]{1,0:T(8,128)(2,1)S(1)}, u32[]{:S(2)}, u32[]{:S(2)}) collective-permute-start(bf16[384,1152]{1,0:T(8,128)(2,1)S(1)} %get-tuple-element.24.when_outer), channel_id=1, source_target_pairs={{0,2},{1,3},{2,0},{3,1},{4,6},{5,7},{6,4},{7,5},{8,10},{9,11},{10,... | collective-permute-start | bytes 2654216 | tf_op jit(solution)/shard_map/ppermute | solution.py:28
  2.2 23.2 %collective-permute-start.2 = (bf16[384,1152]{1,0:T(8,128)(2,1)S(1)}, bf16[384,1152]{1,0:T(8,128)(2,1)S(1)}, u32[]{:S(2)}, u32[]{:S(2)}) collective-permute-start(bf16[384,1152]{1,0:T(8,128)(2,1)S(1)} %get-tuple-element.25.when_inner), channel_id=1, source_target_pairs={{0,30},{1,31},{2,4},{3,5},{4,2},{5,3},{6,8},{7,9},{8,6},{9,7},{10,... | collective-permute-start | bytes 2654216 | tf_op jit(solution)/shard_map/ppermute | solution.py:28
  4.9 21.4 %copy-start = (bf16[384,1152]{1,0:T(8,128)(2,1)}, bf16[384,1152]{1,0:T(8,128)(2,1)S(1)}, u32[]{:S(2)}) copy-start(bf16[384,1152]{1,0:T(8,128)(2,1)S(1)} %collective-permute-done.when_outer.b1) | copy-start | bytes 2654212
  5.1 23.1 %collective-permute-start.1 = (bf16[384,1152]{1,0:T(8,128)(2,1)S(1)}, bf16[384,1152]{1,0:T(8,128)(2,1)S(1)}, u32[]{:S(2)}, u32[]{:S(2)}) collective-permute-start(bf16[384,1152]{1,0:T(8,128)(2,1)S(1)} %pick.2), channel_id=1, source_target_pairs={{0,1},{1,0},{2,3},{3,2},{4,5},{5,4},{6,7},{7,6},{8,9},{9,8},{10,11... | collective-permute-start | bytes 2654216 | tf_op jit(solution)/shard_map/ppermute | solution.py:28
  25.4 6.0 %copy-start.1 = (bf16[384,1152]{1,0:T(8,128)(2,1)}, bf16[384,1152]{1,0:T(8,128)(2,1)S(1)}, u32[]{:S(2)}) copy-start(bf16[384,1152]{1,0:T(8,128)(2,1)S(1)} %collective-permute-done.2.when_inner.b2) | copy-start | bytes 2654212
  26.3 19.7 %collective-permute-start.3 = (bf16[384,1152]{1,0:T(8,128)(2,1)}, bf16[384,1152]{1,0:T(8,128)(2,1)S(1)}, u32[]{:S(2)}, u32[]{:S(2)}) collective-permute-start(bf16[384,1152]{1,0:T(8,128)(2,1)} %pick.3), channel_id=1, source_target_pairs={{0,1},{1,0},{2,3},{3,2},{4,5},{5,4},{6,7},{7,6},{8,9},{9,8},{10,11... | collective-permute-start | bytes 2654216 | tf_op jit(solution)/shard_map/ppermute | solution.py:28
  28.2 22.0 %collective-permute-start.5 = (bf16[384,1152]{1,0:T(8,128)(2,1)S(1)}, bf16[384,1152]{1,0:T(8,128)(2,1)S(1)}, u32[]{:S(2)}, u32[]{:S(2)}) collective-permute-start(bf16[384,1152]{1,0:T(8,128)(2,1)S(1)} %collective-permute-done.1.b3), channel_id=1, source_target_pairs={{0,30},{1,31},{2,4},{3,5},{4,2},{5,3},{6,8},{7,9},{8,6},{9,7},{10,... | collective-permute-start | bytes 2654216 | tf_op jit(solution)/shard_map/ppermute | solution.py:28
  48.7 3.2 %collective-permute-start.4 = (bf16[384,1280]{1,0:T(8,128)(2,1)S(1)}, bf16[384,1280]{1,0:T(8,128)(2,1)S(1)}, u32[]{:S(2)}, u32[]{:S(2)}) collective-permute-start(bf16[384,1280]{1,0:T(8,128)(2,1)S(1)} %get-tuple-element.34), channel_id=1, source_target_pairs={{0,2},{1,3},{2,0},{3,1},{4,6},{5,7},{6,4},{7,5},{8,10},{9,11},{10,... | collective-permute-start | bytes 2949128 | tf_op jit(solution)/shard_map/ppermute | solution.py:28

commit v19 on v18

--- a/solution.py
+++ b/solution.py
@@ -93,14 +93,14 @@
     values = raw.astype(F32)
     inverse = 1.0 / jnp.sqrt(jnp.sum(values * values, axis=1, keepdims=True) + 1e-06)
     factor = scale * jnp.transpose(jnp.broadcast_to(inverse, (raw.shape[0], 128)))[:1]
-    half = own.shape[0] // 2
-    scores = [dot_nt(own[:half], raw), dot_nt(own[half:], raw)]
-    products, losses = [], []
-    for score in scores:
+    size = raw.shape[0] // 2
+    chunks = [slice(start, start + size) for start in range(0, own.shape[0], size)]
+    score = dot_nt(own[chunks[0]], raw)
+    for place, chunk in enumerate(chunks):
         p = jnp.exp(factor * score + shift)
-        products.append(dot_nn((sigmoid_of(p) * factor).astype(BF16), raw))
-        losses.append(softplus_lanes(p))
-    return jnp.concatenate(products), jnp.concatenate(losses)
+        if place + 1 < len(chunks):
+            score = dot_nt(own[chunks[place + 1]], raw)
+        yield chunk, dot_nn((sigmoid_of(p) * factor).astype(BF16), raw), softplus_lanes(p)
 
 
 def project(unit, inverse, grad):
@@ -200,18 +200,24 @@
     scalars, b5, z_pair, unit_other, inverse_other, grad_in, loss_in, grad_u, loss, for_partner
 ):
     rows, width = b5.shape
-    term, row_loss = raw_terms(z_pair[...], b5[...], *scalar_pair(scalars))
-    for_partner[:, :width] = project(unit_other[...], inverse_other[...], term[rows:]).astype(BF16)
-    for_partner[:, width:] = row_loss[rows:].astype(BF16)
-    grad_u[...] = grad_in[...] + term[:rows]
-    loss[...] = loss_in[...] + image_is_u().astype(F32) * row_loss[:rows]
+    weight = image_is_u().astype(F32)
+    for chunk, term, row_loss in raw_terms(z_pair, b5[...], *scalar_pair(scalars)):
+        if chunk.start < rows:
+            grad_u[chunk] = grad_in[chunk] + term
+            loss[chunk] = loss_in[chunk] + weight * row_loss
+        else:
+            part = slice(chunk.start - rows, chunk.stop - rows)
+            projected = project(unit_other[part], inverse_other[part], term)
+            for_partner[part, :width] = projected.astype(BF16)
+            for_partner[part, width:] = row_loss.astype(BF16)
 
 
 def u_kernel(scalars, b4, z_pair, grad_u, loss_in, unit, inverse, done_u, loss):
-    rows = done_u.shape[0]
-    term, row_loss = raw_terms(z_pair[:rows], b4[...], *scalar_pair(scalars))
-    loss[...] = loss_in[...] + image_is_u().astype(F32) * row_loss
-    done_u[...] = project(unit[...], inverse[...], grad_u[...] + term).astype(BF16)
+    weight = image_is_u().astype(F32)
+    own = z_pair.at[pl.ds(0, done_u.shape[0])]
+    for chunk, term, row_loss in raw_terms(own, b4[...], *scalar_pair(scalars)):
+        loss[chunk] = loss_in[chunk] + weight * row_loss
+        done_u[chunk] = project(unit[chunk], inverse[chunk], grad_u[chunk] + term).astype(BF16)
 
 
 def w_kernel(

time: 53.9 us -> 53.9 us (level)
  no operation moved by 1% of the time
where the time goes in v19:
time: 53.9 us; the launch traced here: 53.7 us
  waiting for transfers between devices  25.2 us (47%)
  Pallas kernels  17.8 us (33%)
  starting transfers between devices  8.61 us (16%)
  between operations  2.01 us (4%)
    ppermute x6, waiting for transfers between devices, send(): return lax.ppermute(value, AXES, pairs)  25.2 us
    pallas_call x7, Pallas kernels, call(): pl.pallas_call(kernel, out_shape=outs, in_specs=in_specs, out_specs=out_s...  17.8 us
    ppermute x6, starting transfers between devices, send(): return lax.ppermute(value, AXES, pairs)  8.61 us
  transfers between devices with their start and end apart: 6, of which 3 were waited for; matrix products, arithmetic and copies ran while one was open for 0% of the time, Pallas kernels for 27%

profile of v19, /device:TPU:1, one launch (start us, length us, event | category | flops | bytes accessed | tf_op | source)
XLA Modules:
  0.0 53.7 jit_solution(908058475354992720)
XLA Ops:
  0.6 1.5 %sort.1 = (bf16[384,1152]{1,0:T(8,128)(2,1)S(1)}, bf16[384,1152]{1,0:T(8,128)(2,1)S(1)}) custom-call(bf16[384,1152]{1,0:T(8,128)(2,1)} %image.3, bf16[384,1152]{1,0:T(8,128)(2,1)} %text.3), custom_call_target="tpu_custom_call" | custom-call | flops 1 | bytes 1 | tf_op jit(solution)/shard_map/sort/pallas_call | solution.py:256
  2.1 0.1 collective-permute-start
  2.2 2.7 %collective-permute-start.2 = (bf16[384,1152]{1,0:T(8,128)(2,1)S(1)}, bf16[384,1152]{1,0:T(8,128)(2,1)S(1)}, u32[]{:S(2)}, u32[]{:S(2)}) collective-permute-start(bf16[384,1152]{1,0:T(8,128)(2,1)S(1)} %get-tuple-element.25.when_inner), channel_id=1, source_target_pairs={{0,30},{1,31},{2,4},{3,5},{4,2},{5,3},{6,8},{7,9},{8,6},{9,7},{10,... | collective-permute-start | bytes 2654216 | tf_op jit(solution)/shard_map/ppermute | solution.py:28
  4.9 0.0 collective-permute-done.when_outer.b1
  4.9 0.0 copy-start
  4.9 0.2 pick.2
  5.1 2.1 %collective-permute-start.1 = (bf16[384,1152]{1,0:T(8,128)(2,1)S(1)}, bf16[384,1152]{1,0:T(8,128)(2,1)S(1)}, u32[]{:S(2)}, u32[]{:S(2)}) collective-permute-start(bf16[384,1152]{1,0:T(8,128)(2,1)S(1)} %pick.2), channel_id=1, source_target_pairs={{0,1},{1,0},{2,3},{3,2},{4,5},{5,4},{6,7},{7,6},{8,9},{9,8},{10,11... | collective-permute-start | bytes 2654216 | tf_op jit(solution)/shard_map/ppermute | solution.py:28
  7.2 18.2 %collective-permute-done.2.when_inner.b2 = bf16[384,1152]{1,0:T(8,128)(2,1)S(1)} collective-permute-done((bf16[384,1152]{1,0:T(8,128)(2,1)S(1)}, bf16[384,1152]{1,0:T(8,128)(2,1)S(1)}, u32[]{:S(2)}, u32[]{:S(2)}) %collective-permute-start.2) | collective-permute-done | bytes 884768 | tf_op jit(solution)/shard_map/ppermute | solution.py:28
  25.4 0.0 copy-start.1
  25.4 0.9 %pick.3 = bf16[384,1152]{1,0:T(8,128)(2,1)} custom-call(bf16[384,1152]{1,0:T(8,128)(2,1)S(1)} %get-tuple-element.24.when_outer, bf16[384,1152]{1,0:T(8,128)(2,1)S(1)} %collective-permute-done.2.when_inner.b2), custom_call_target="tpu_custom_call" | custom-call | flops 1 | bytes 1 | tf_op jit(solution)/shard_map/pick/pallas_call | solution.py:256
  26.3 0.0 copy-done
  26.3 1.8 %collective-permute-start.3 = (bf16[384,1152]{1,0:T(8,128)(2,1)}, bf16[384,1152]{1,0:T(8,128)(2,1)S(1)}, u32[]{:S(2)}, u32[]{:S(2)}) collective-permute-start(bf16[384,1152]{1,0:T(8,128)(2,1)} %pick.3), channel_id=1, source_target_pairs={{0,1},{1,0},{2,3},{3,2},{4,5},{5,4},{6,7},{7,6},{8,9},{9,8},{10,11... | collective-permute-start | bytes 2654216 | tf_op jit(solution)/shard_map/ppermute | solution.py:28
  28.2 0.0 collective-permute-done.1.b3
  28.2 1.8 %collective-permute-start.5 = (bf16[384,1152]{1,0:T(8,128)(2,1)S(1)}, bf16[384,1152]{1,0:T(8,128)(2,1)S(1)}, u32[]{:S(2)}, u32[]{:S(2)}) collective-permute-start(bf16[384,1152]{1,0:T(8,128)(2,1)S(1)} %collective-permute-done.1.b3), channel_id=1, source_target_pairs={{0,30},{1,31},{2,4},{3,5},{4,2},{5,3},{6,8},{7,9},{8,6},{9,7},{10,... | collective-permute-start | bytes 2654216 | tf_op jit(solution)/shard_map/ppermute | solution.py:28
  31.3 0.1 iota.7.scalars
  31.4 0.0 copy-done.1
  31.4 9.0 %near_blocks.1 = (bf16[768,1152]{1,0:T(8,128)(2,1)S(1)}, f32[384,1152]{1,0:T(8,128)S(1)}, f32[384,1152]{1,0:T(8,128)S(1)}, f32[384,1]{1,0:T(8,128)S(1)}, f32[384...) custom-call(f32[8,128]{1,0:T(8,128)S(1)} %iota.7.scalars, ...), custom_call_target="tpu_custom_call" | custom-call | flops 1 | bytes 1 | tf_op jit(solution)/shard_map/near_blocks/pallas_call | solution.py:256
  40.4 5.7 %collective-permute-done.3.b5 = bf16[384,1152]{1,0:T(8,128)(2,1)S(1)} collective-permute-done((bf16[384,1152]{1,0:T(8,128)(2,1)}, bf16[384,1152]{1,0:T(8,128)(2,1)S(1)}, u32[]{:S(2)}, u32[]{:S(2)}) %collective-permute-start.3) | collective-permute-done | bytes 884768 | tf_op jit(solution)/shard_map/ppermute | solution.py:28
  46.1 2.7 %fifth_block.1 = (f32[384,1152]{1,0:T(8,128)S(1)}, f32[384,128]{1,0:T(8,128)S(1)}, bf16[384,1280]{1,0:T(8,128)(2,1)S(1)}) custom-call(f32[8,128]{1,0:T(8,128)S(1)} %iota.7.scalars, bf16[384,1152]{1,0:T(8,128)(2,1)S(1)} %collective-permute-done.3.b5, bf16[768,1152]{1,0:T(8,128)(2,1)S(1)} %get-tuple-element.29.z_pair, ...), custom_call_target="tpu_custom_call" | custom-call | flops 1 | bytes 1 | tf_op jit(solution)/shard_map/fifth_block/pallas_call | solution.py:256
  48.8 0.1 collective-permute-start.4
  48.9 1.3 %collective-permute-done.5.b4 = bf16[384,1152]{1,0:T(8,128)(2,1)S(1)} collective-permute-done((bf16[384,1152]{1,0:T(8,128)(2,1)S(1)}, bf16[384,1152]{1,0:T(8,128)(2,1)S(1)}, u32[]{:S(2)}, u32[]{:S(2)}) %collective-permute-start.5) | collective-permute-done | bytes 884768 | tf_op jit(solution)/shard_map/ppermute | solution.py:28
  50.2 1.7 %finish_u.1 = (bf16[384,1152]{1,0:T(8,128)(2,1)S(1)}, f32[384,128]{1,0:T(8,128)S(1)}) custom-call(f32[8,128]{1,0:T(8,128)S(1)} %iota.7.scalars, bf16[384,1152]{1,0:T(8,128)(2,1)S(1)} %collective-permute-done.5.b4, bf16[768,1152]{1,0:T(8,128)(2,1)S(1)} %get-tuple-element.29.z_pair, f32[384,1152]{1,0:T(8,128)S(1)} %get-tuple-element.36.grad_u, ...), custom_call_target="tpu_custom_call" | custom-call | flops 10000000000 | bytes 1 | tf_op jit(solution)/shard_map/finish_u/pallas_call | solution.py:256
  51.9 0.0 collective-permute-done.4.last
  51.9 1.8 %finish_w.1 = (bf16[384,1152]{1,0:T(8,128)(2,1)}, bf16[384,1152]{1,0:T(8,128)(2,1)}, f32[384]{0:T(512)}) custom-call(bf16[384,1280]{1,0:T(8,128)(2,1)S(1)} %collective-permute-done.4.last, f32[384,1152]{1,0:T(8,128)S(1)} %get-tuple-element.35.part_w, f32[384,128]{1,0:T(8,128)S(1)} %get-tuple-element.40.loss_in, bf16[384,1152]{1,0:T(8,128)(2,1)S(1)} %get-tuple-element.41.done_u), custom_call_target="tpu_custom_call" | custom-call | flops 1 | bytes 1 | tf_op jit(solution)/shard_map/finish_w/pallas_call | solution.py:256
  (1 shorter events, 0.0 us)
Async XLA Ops:
  2.1 2.8 %collective-permute-start = (bf16[384,1152]{1,0:T(8,128)(2,1)S(1)}, bf16[384,1152]{1,0:T(8,128)(2,1)S(1)}, u32[]{:S(2)}, u32[]{:S(2)}) collective-permute-start(bf16[384,1152]{1,0:T(8,128)(2,1)S(1)} %get-tuple-element.24.when_outer), channel_id=1, source_target_pairs={{0,2},{1,3},{2,0},{3,1},{4,6},{5,7},{6,4},{7,5},{8,10},{9,11},{10,... | collective-permute-start | bytes 2654216 | tf_op jit(solution)/shard_map/ppermute | solution.py:28
  2.2 23.2 %collective-permute-start.2 = (bf16[384,1152]{1,0:T(8,128)(2,1)S(1)}, bf16[384,1152]{1,0:T(8,128)(2,1)S(1)}, u32[]{:S(2)}, u32[]{:S(2)}) collective-permute-start(bf16[384,1152]{1,0:T(8,128)(2,1)S(1)} %get-tuple-element.25.when_inner), channel_id=1, source_target_pairs={{0,30},{1,31},{2,4},{3,5},{4,2},{5,3},{6,8},{7,9},{8,6},{9,7},{10,... | collective-permute-start | bytes 2654216 | tf_op jit(solution)/shard_map/ppermute | solution.py:28
  4.9 21.4 %copy-start = (bf16[384,1152]{1,0:T(8,128)(2,1)}, bf16[384,1152]{1,0:T(8,128)(2,1)S(1)}, u32[]{:S(2)}) copy-start(bf16[384,1152]{1,0:T(8,128)(2,1)S(1)} %collective-permute-done.when_outer.b1) | copy-start | bytes 2654212
  5.1 23.1 %collective-permute-start.1 = (bf16[384,1152]{1,0:T(8,128)(2,1)S(1)}, bf16[384,1152]{1,0:T(8,128)(2,1)S(1)}, u32[]{:S(2)}, u32[]{:S(2)}) collective-permute-start(bf16[384,1152]{1,0:T(8,128)(2,1)S(1)} %pick.2), channel_id=1, source_target_pairs={{0,1},{1,0},{2,3},{3,2},{4,5},{5,4},{6,7},{7,6},{8,9},{9,8},{10,11... | collective-permute-start | bytes 2654216 | tf_op jit(solution)/shard_map/ppermute | solution.py:28
  25.4 6.0 %copy-start.1 = (bf16[384,1152]{1,0:T(8,128)(2,1)}, bf16[384,1152]{1,0:T(8,128)(2,1)S(1)}, u32[]{:S(2)}) copy-start(bf16[384,1152]{1,0:T(8,128)(2,1)S(1)} %collective-permute-done.2.when_inner.b2) | copy-start | bytes 2654212
  26.3 19.7 %collective-permute-start.3 = (bf16[384,1152]{1,0:T(8,128)(2,1)}, bf16[384,1152]{1,0:T(8,128)(2,1)S(1)}, u32[]{:S(2)}, u32[]{:S(2)}) collective-permute-start(bf16[384,1152]{1,0:T(8,128)(2,1)} %pick.3), channel_id=1, source_target_pairs={{0,1},{1,0},{2,3},{3,2},{4,5},{5,4},{6,7},{7,6},{8,9},{9,8},{10,11... | collective-permute-start | bytes 2654216 | tf_op jit(solution)/shard_map/ppermute | solution.py:28
  28.2 22.0 %collective-permute-start.5 = (bf16[384,1152]{1,0:T(8,128)(2,1)S(1)}, bf16[384,1152]{1,0:T(8,128)(2,1)S(1)}, u32[]{:S(2)}, u32[]{:S(2)}) collective-permute-start(bf16[384,1152]{1,0:T(8,128)(2,1)S(1)} %collective-permute-done.1.b3), channel_id=1, source_target_pairs={{0,30},{1,31},{2,4},{3,5},{4,2},{5,3},{6,8},{7,9},{8,6},{9,7},{10,... | collective-permute-start | bytes 2654216 | tf_op jit(solution)/shard_map/ppermute | solution.py:28
  48.8 3.1 %collective-permute-start.4 = (bf16[384,1280]{1,0:T(8,128)(2,1)S(1)}, bf16[384,1280]{1,0:T(8,128)(2,1)S(1)}, u32[]{:S(2)}, u32[]{:S(2)}) collective-permute-start(bf16[384,1280]{1,0:T(8,128)(2,1)S(1)} %get-tuple-element.34), channel_id=1, source_target_pairs={{0,2},{1,3},{2,0},{3,1},{4,6},{5,7},{6,4},{7,5},{8,10},{9,11},{10,... | collective-permute-start | bytes 2949128 | tf_op jit(solution)/shard_map/ppermute | solution.py:28

commit v20 on v19

--- a/solution.py
+++ b/solution.py
@@ -93,7 +93,7 @@
     values = raw.astype(F32)
     inverse = 1.0 / jnp.sqrt(jnp.sum(values * values, axis=1, keepdims=True) + 1e-06)
     factor = scale * jnp.transpose(jnp.broadcast_to(inverse, (raw.shape[0], 128)))[:1]
-    size = raw.shape[0] // 2
+    size = raw.shape[0] // (3 if raw.shape[0] % 48 == 0 else 1)
     chunks = [slice(start, start + size) for start in range(0, own.shape[0], size)]
     score = dot_nt(own[chunks[0]], raw)
     for place, chunk in enumerate(chunks):
@@ -235,17 +235,19 @@
         def _():
             action(pltpu.make_async_copy(source.at[part], text_grad.at[part], sem))
 
-    whole = pl.ds(0, done_w.shape[0])
-    output(lambda copy: copy.start(), done_u, whole, u_is_image, sems.at[0])
+    thirds = row_parts(done_w.shape[0], 3)
+    for place, part in enumerate(thirds):
+        output(lambda copy: copy.start(), done_u, part, u_is_image, sems.at[place])
     width = done_w.shape[1]
     for place, part in enumerate(parts):
         done_w[part] = (part_w[part] + last[part, :width].astype(F32)).astype(BF16)
-        output(lambda copy: copy.start(), done_w, part, jnp.logical_not(u_is_image), sems.at[1 + place])
+        output(lambda copy: copy.start(), done_w, part, jnp.logical_not(u_is_image), sems.at[3 + place])
     total = loss_in[...] + (1.0 - u_is_image.astype(F32)) * last[:, width:].astype(F32)
     loss_rows[...] = jnp.sum(jnp.transpose(total), axis=0) / (SPAN * total.shape[0])
-    output(lambda copy: copy.wait(), done_u, whole, u_is_image, sems.at[0])
+    for place, part in enumerate(thirds):
+        output(lambda copy: copy.wait(), done_u, part, u_is_image, sems.at[place])
     for place, part in enumerate(parts):
-        output(lambda copy: copy.wait(), done_w, part, jnp.logical_not(u_is_image), sems.at[1 + place])
+        output(lambda copy: copy.wait(), done_w, part, jnp.logical_not(u_is_image), sems.at[3 + place])
 
 
 VMEM = pl.BlockSpec(memory_space=pltpu.VMEM)
@@ -274,7 +276,7 @@
     partial = jax.ShapeDtypeStruct((rows, 128), F32)
     line = jax.ShapeDtypeStruct((rows,), F32)
     raw = pltpu.VMEM((rows, width), BF16)
-    copies = pltpu.SemaphoreType.DMA((7,))
+    copies = pltpu.SemaphoreType.DMA((9,))
 
     def in_hbm(*arrays):
         return [pltpu.with_memory_space_constraint(x, pltpu.HBM) for x in arrays]

time: 53.9 us -> 54.2 us (level)
  Pallas kernels: 17.8 us -> 18.6 us
    pallas_call x7, Pallas kernels: 17.8 us -> 18.6 us  [call(): pl.pallas_call(kernel, out_shape=outs, in_specs=in_specs, out_specs=out_s...]
  transfers between devices with their start and end apart: 6 -> 6, of which waited for: 3 -> 3; matrix products, arithmetic and copies ran while one was open for 0% -> 0% of each run, Pallas kernels for 27% -> 28%
where the time goes in v20:
time: 54.2 us; the launch traced here: 54.1 us
  waiting for transfers between devices  24.8 us (46%)
  Pallas kernels  18.6 us (34%)
  starting transfers between devices  8.61 us (16%)
  between operations  2.01 us (4%)
    ppermute x6, waiting for transfers between devices, send(): return lax.ppermute(value, AXES, pairs)  24.8 us
    pallas_call x7, Pallas kernels, call(): pl.pallas_call(kernel, out_shape=outs, in_specs=in_specs, out_specs=out_s...  18.6 us
    ppermute x6, starting transfers between devices, send(): return lax.ppermute(value, AXES, pairs)  8.61 us
  transfers between devices with their start and end apart: 6, of which 3 were waited for; matrix products, arithmetic and copies ran while one was open for 0% of the time, Pallas kernels for 28%

profile of v20, /device:TPU:1, one launch (start us, length us, event | category | flops | bytes accessed | tf_op | source)
XLA Modules:
  0.0 54.1 jit_solution(4572004818277463688)
XLA Ops:
  0.6 1.5 %sort.1 = (bf16[384,1152]{1,0:T(8,128)(2,1)S(1)}, bf16[384,1152]{1,0:T(8,128)(2,1)S(1)}) custom-call(bf16[384,1152]{1,0:T(8,128)(2,1)} %image.3, bf16[384,1152]{1,0:T(8,128)(2,1)} %text.3), custom_call_target="tpu_custom_call" | custom-call | flops 1 | bytes 1 | tf_op jit(solution)/shard_map/sort/pallas_call | solution.py:258
  2.1 0.1 collective-permute-start
  2.3 2.7 %collective-permute-start.2 = (bf16[384,1152]{1,0:T(8,128)(2,1)S(1)}, bf16[384,1152]{1,0:T(8,128)(2,1)S(1)}, u32[]{:S(2)}, u32[]{:S(2)}) collective-permute-start(bf16[384,1152]{1,0:T(8,128)(2,1)S(1)} %get-tuple-element.25.when_inner), channel_id=1, source_target_pairs={{0,30},{1,31},{2,4},{3,5},{4,2},{5,3},{6,8},{7,9},{8,6},{9,7},{10,... | collective-permute-start | bytes 2654216 | tf_op jit(solution)/shard_map/ppermute | solution.py:28
  4.9 0.0 collective-permute-done.when_outer.b1
  4.9 0.0 copy-start
  4.9 0.2 pick.2
  5.1 2.1 %collective-permute-start.1 = (bf16[384,1152]{1,0:T(8,128)(2,1)S(1)}, bf16[384,1152]{1,0:T(8,128)(2,1)S(1)}, u32[]{:S(2)}, u32[]{:S(2)}) collective-permute-start(bf16[384,1152]{1,0:T(8,128)(2,1)S(1)} %pick.2), channel_id=1, source_target_pairs={{0,1},{1,0},{2,3},{3,2},{4,5},{5,4},{6,7},{7,6},{8,9},{9,8},{10,11... | collective-permute-start | bytes 2654216 | tf_op jit(solution)/shard_map/ppermute | solution.py:28
  7.2 18.2 %collective-permute-done.2.when_inner.b2 = bf16[384,1152]{1,0:T(8,128)(2,1)S(1)} collective-permute-done((bf16[384,1152]{1,0:T(8,128)(2,1)S(1)}, bf16[384,1152]{1,0:T(8,128)(2,1)S(1)}, u32[]{:S(2)}, u32[]{:S(2)}) %collective-permute-start.2) | collective-permute-done | bytes 884768 | tf_op jit(solution)/shard_map/ppermute | solution.py:28
  25.4 0.0 copy-start.1
  25.4 0.9 %pick.3 = bf16[384,1152]{1,0:T(8,128)(2,1)} custom-call(bf16[384,1152]{1,0:T(8,128)(2,1)S(1)} %get-tuple-element.24.when_outer, bf16[384,1152]{1,0:T(8,128)(2,1)S(1)} %collective-permute-done.2.when_inner.b2), custom_call_target="tpu_custom_call" | custom-call | flops 1 | bytes 1 | tf_op jit(solution)/shard_map/pick/pallas_call | solution.py:258
  26.4 0.0 copy-done
  26.4 1.8 %collective-permute-start.3 = (bf16[384,1152]{1,0:T(8,128)(2,1)}, bf16[384,1152]{1,0:T(8,128)(2,1)S(1)}, u32[]{:S(2)}, u32[]{:S(2)}) collective-permute-start(bf16[384,1152]{1,0:T(8,128)(2,1)} %pick.3), channel_id=1, source_target_pairs={{0,1},{1,0},{2,3},{3,2},{4,5},{5,4},{6,7},{7,6},{8,9},{9,8},{10,11... | collective-permute-start | bytes 2654216 | tf_op jit(solution)/shard_map/ppermute | solution.py:28
  28.2 0.0 collective-permute-done.1.b3
  28.2 1.8 %collective-permute-start.5 = (bf16[384,1152]{1,0:T(8,128)(2,1)S(1)}, bf16[384,1152]{1,0:T(8,128)(2,1)S(1)}, u32[]{:S(2)}, u32[]{:S(2)}) collective-permute-start(bf16[384,1152]{1,0:T(8,128)(2,1)S(1)} %collective-permute-done.1.b3), channel_id=1, source_target_pairs={{0,30},{1,31},{2,4},{3,5},{4,2},{5,3},{6,8},{7,9},{8,6},{9,7},{10,... | collective-permute-start | bytes 2654216 | tf_op jit(solution)/shard_map/ppermute | solution.py:28
  31.3 0.1 iota.7.scalars
  31.4 0.0 copy-done.1
  31.4 9.0 %near_blocks.1 = (bf16[768,1152]{1,0:T(8,128)(2,1)S(1)}, f32[384,1152]{1,0:T(8,128)S(1)}, f32[384,1152]{1,0:T(8,128)S(1)}, f32[384,1]{1,0:T(8,128)S(1)}, f32[384...) custom-call(f32[8,128]{1,0:T(8,128)S(1)} %iota.7.scalars, ...), custom_call_target="tpu_custom_call" | custom-call | flops 1 | bytes 1 | tf_op jit(solution)/shard_map/near_blocks/pallas_call | solution.py:258
  40.4 5.7 %collective-permute-done.3.b5 = bf16[384,1152]{1,0:T(8,128)(2,1)S(1)} collective-permute-done((bf16[384,1152]{1,0:T(8,128)(2,1)}, bf16[384,1152]{1,0:T(8,128)(2,1)S(1)}, u32[]{:S(2)}, u32[]{:S(2)}) %collective-permute-start.3) | collective-permute-done | bytes 884768 | tf_op jit(solution)/shard_map/ppermute | solution.py:28
  46.1 3.1 %fifth_block.1 = (f32[384,1152]{1,0:T(8,128)S(1)}, f32[384,128]{1,0:T(8,128)S(1)}, bf16[384,1280]{1,0:T(8,128)(2,1)S(1)}) custom-call(f32[8,128]{1,0:T(8,128)S(1)} %iota.7.scalars, bf16[384,1152]{1,0:T(8,128)(2,1)S(1)} %collective-permute-done.3.b5, bf16[768,1152]{1,0:T(8,128)(2,1)S(1)} %get-tuple-element.29.z_pair, ...), custom_call_target="tpu_custom_call" | custom-call | flops 1 | bytes 1 | tf_op jit(solution)/shard_map/fifth_block/pallas_call | solution.py:258
  49.2 0.1 collective-permute-start.4
  49.3 0.9 %collective-permute-done.5.b4 = bf16[384,1152]{1,0:T(8,128)(2,1)S(1)} collective-permute-done((bf16[384,1152]{1,0:T(8,128)(2,1)S(1)}, bf16[384,1152]{1,0:T(8,128)(2,1)S(1)}, u32[]{:S(2)}, u32[]{:S(2)}) %collective-permute-start.5) | collective-permute-done | bytes 884768 | tf_op jit(solution)/shard_map/ppermute | solution.py:28
  50.2 1.9 %finish_u.1 = (bf16[384,1152]{1,0:T(8,128)(2,1)S(1)}, f32[384,128]{1,0:T(8,128)S(1)}) custom-call(f32[8,128]{1,0:T(8,128)S(1)} %iota.7.scalars, bf16[384,1152]{1,0:T(8,128)(2,1)S(1)} %collective-permute-done.5.b4, bf16[768,1152]{1,0:T(8,128)(2,1)S(1)} %get-tuple-element.29.z_pair, f32[384,1152]{1,0:T(8,128)S(1)} %get-tuple-element.36.grad_u, ...), custom_call_target="tpu_custom_call" | custom-call | flops 10000000000 | bytes 1 | tf_op jit(solution)/shard_map/finish_u/pallas_call | solution.py:258
  52.2 0.0 collective-permute-done.4.last
  52.2 1.9 %finish_w.1 = (bf16[384,1152]{1,0:T(8,128)(2,1)}, bf16[384,1152]{1,0:T(8,128)(2,1)}, f32[384]{0:T(512)}) custom-call(bf16[384,1280]{1,0:T(8,128)(2,1)S(1)} %collective-permute-done.4.last, f32[384,1152]{1,0:T(8,128)S(1)} %get-tuple-element.35.part_w, f32[384,128]{1,0:T(8,128)S(1)} %get-tuple-element.40.loss_in, bf16[384,1152]{1,0:T(8,128)(2,1)S(1)} %get-tuple-element.41.done_u), custom_call_target="tpu_custom_call" | custom-call | flops 1 | bytes 1 | tf_op jit(solution)/shard_map/finish_w/pallas_call | solution.py:258
  (1 shorter events, 0.0 us)
Async XLA Ops:
  2.1 2.8 %collective-permute-start = (bf16[384,1152]{1,0:T(8,128)(2,1)S(1)}, bf16[384,1152]{1,0:T(8,128)(2,1)S(1)}, u32[]{:S(2)}, u32[]{:S(2)}) collective-permute-start(bf16[384,1152]{1,0:T(8,128)(2,1)S(1)} %get-tuple-element.24.when_outer), channel_id=1, source_target_pairs={{0,2},{1,3},{2,0},{3,1},{4,6},{5,7},{6,4},{7,5},{8,10},{9,11},{10,... | collective-permute-start | bytes 2654216 | tf_op jit(solution)/shard_map/ppermute | solution.py:28
  2.3 23.2 %collective-permute-start.2 = (bf16[384,1152]{1,0:T(8,128)(2,1)S(1)}, bf16[384,1152]{1,0:T(8,128)(2,1)S(1)}, u32[]{:S(2)}, u32[]{:S(2)}) collective-permute-start(bf16[384,1152]{1,0:T(8,128)(2,1)S(1)} %get-tuple-element.25.when_inner), channel_id=1, source_target_pairs={{0,30},{1,31},{2,4},{3,5},{4,2},{5,3},{6,8},{7,9},{8,6},{9,7},{10,... | collective-permute-start | bytes 2654216 | tf_op jit(solution)/shard_map/ppermute | solution.py:28
  4.9 21.4 %copy-start = (bf16[384,1152]{1,0:T(8,128)(2,1)}, bf16[384,1152]{1,0:T(8,128)(2,1)S(1)}, u32[]{:S(2)}) copy-start(bf16[384,1152]{1,0:T(8,128)(2,1)S(1)} %collective-permute-done.when_outer.b1) | copy-start | bytes 2654212
  5.1 23.1 %collective-permute-start.1 = (bf16[384,1152]{1,0:T(8,128)(2,1)S(1)}, bf16[384,1152]{1,0:T(8,128)(2,1)S(1)}, u32[]{:S(2)}, u32[]{:S(2)}) collective-permute-start(bf16[384,1152]{1,0:T(8,128)(2,1)S(1)} %pick.2), channel_id=1, source_target_pairs={{0,1},{1,0},{2,3},{3,2},{4,5},{5,4},{6,7},{7,6},{8,9},{9,8},{10,11... | collective-permute-start | bytes 2654216 | tf_op jit(solution)/shard_map/ppermute | solution.py:28
  25.4 6.0 %copy-start.1 = (bf16[384,1152]{1,0:T(8,128)(2,1)}, bf16[384,1152]{1,0:T(8,128)(2,1)S(1)}, u32[]{:S(2)}) copy-start(bf16[384,1152]{1,0:T(8,128)(2,1)S(1)} %collective-permute-done.2.when_inner.b2) | copy-start | bytes 2654212
  26.4 19.7 %collective-permute-start.3 = (bf16[384,1152]{1,0:T(8,128)(2,1)}, bf16[384,1152]{1,0:T(8,128)(2,1)S(1)}, u32[]{:S(2)}, u32[]{:S(2)}) collective-permute-start(bf16[384,1152]{1,0:T(8,128)(2,1)} %pick.3), channel_id=1, source_target_pairs={{0,1},{1,0},{2,3},{3,2},{4,5},{5,4},{6,7},{7,6},{8,9},{9,8},{10,11... | collective-permute-start | bytes 2654216 | tf_op jit(solution)/shard_map/ppermute | solution.py:28
  28.2 22.0 %collective-permute-start.5 = (bf16[384,1152]{1,0:T(8,128)(2,1)S(1)}, bf16[384,1152]{1,0:T(8,128)(2,1)S(1)}, u32[]{:S(2)}, u32[]{:S(2)}) collective-permute-start(bf16[384,1152]{1,0:T(8,128)(2,1)S(1)} %collective-permute-done.1.b3), channel_id=1, source_target_pairs={{0,30},{1,31},{2,4},{3,5},{4,2},{5,3},{6,8},{7,9},{8,6},{9,7},{10,... | collective-permute-start | bytes 2654216 | tf_op jit(solution)/shard_map/ppermute | solution.py:28
  49.2 2.9 %collective-permute-start.4 = (bf16[384,1280]{1,0:T(8,128)(2,1)S(1)}, bf16[384,1280]{1,0:T(8,128)(2,1)S(1)}, u32[]{:S(2)}, u32[]{:S(2)}) collective-permute-start(bf16[384,1280]{1,0:T(8,128)(2,1)S(1)} %get-tuple-element.34), channel_id=1, source_target_pairs={{0,2},{1,3},{2,0},{3,1},{4,6},{5,7},{6,4},{7,5},{8,10},{9,11},{10,... | collective-permute-start | bytes 2949128 | tf_op jit(solution)/shard_map/ppermute | solution.py:28

commit v21 on v19

--- a/solution.py
+++ b/solution.py
@@ -93,7 +93,7 @@
     values = raw.astype(F32)
     inverse = 1.0 / jnp.sqrt(jnp.sum(values * values, axis=1, keepdims=True) + 1e-06)
     factor = scale * jnp.transpose(jnp.broadcast_to(inverse, (raw.shape[0], 128)))[:1]
-    size = raw.shape[0] // 2
+    size = own.shape[0] // 2
     chunks = [slice(start, start + size) for start in range(0, own.shape[0], size)]
     score = dot_nt(own[chunks[0]], raw)
     for place, chunk in enumerate(chunks):

time: 53.9 us -> 53.9 us (level)
  no operation moved by 1% of the time
where the time goes in v21:
time: 53.9 us; the launch traced here: 53.7 us
  waiting for transfers between devices  25.3 us (47%)
  Pallas kernels  17.7 us (33%)
  starting transfers between devices  8.61 us (16%)
  between operations  2.01 us (4%)
    ppermute x6, waiting for transfers between devices, send(): return lax.ppermute(value, AXES, pairs)  25.3 us
    pallas_call x7, Pallas kernels, call(): pl.pallas_call(kernel, out_shape=outs, in_specs=in_specs, out_specs=out_s...  17.7 us
    ppermute x6, starting transfers between devices, send(): return lax.ppermute(value, AXES, pairs)  8.61 us
  transfers between devices with their start and end apart: 6, of which 3 were waited for; matrix products, arithmetic and copies ran while one was open for 0% of the time, Pallas kernels for 27%

profile of v21, /device:TPU:1, one launch (start us, length us, event | category | flops | bytes accessed | tf_op | source)
XLA Modules:
  0.0 53.7 jit_solution(15203791577473857972)
XLA Ops:
  0.6 1.5 %sort.1 = (bf16[384,1152]{1,0:T(8,128)(2,1)S(1)}, bf16[384,1152]{1,0:T(8,128)(2,1)S(1)}) custom-call(bf16[384,1152]{1,0:T(8,128)(2,1)} %image.3, bf16[384,1152]{1,0:T(8,128)(2,1)} %text.3), custom_call_target="tpu_custom_call" | custom-call | flops 1 | bytes 1 | tf_op jit(solution)/shard_map/sort/pallas_call | solution.py:256
  2.1 0.1 collective-permute-start
  2.2 2.7 %collective-permute-start.2 = (bf16[384,1152]{1,0:T(8,128)(2,1)S(1)}, bf16[384,1152]{1,0:T(8,128)(2,1)S(1)}, u32[]{:S(2)}, u32[]{:S(2)}) collective-permute-start(bf16[384,1152]{1,0:T(8,128)(2,1)S(1)} %get-tuple-element.25.when_inner), channel_id=1, source_target_pairs={{0,30},{1,31},{2,4},{3,5},{4,2},{5,3},{6,8},{7,9},{8,6},{9,7},{10,... | collective-permute-start | bytes 2654216 | tf_op jit(solution)/shard_map/ppermute | solution.py:28
  4.9 0.0 collective-permute-done.when_outer.b1
  4.9 0.0 copy-start
  4.9 0.2 pick.2
  5.1 2.1 %collective-permute-start.1 = (bf16[384,1152]{1,0:T(8,128)(2,1)S(1)}, bf16[384,1152]{1,0:T(8,128)(2,1)S(1)}, u32[]{:S(2)}, u32[]{:S(2)}) collective-permute-start(bf16[384,1152]{1,0:T(8,128)(2,1)S(1)} %pick.2), channel_id=1, source_target_pairs={{0,1},{1,0},{2,3},{3,2},{4,5},{5,4},{6,7},{7,6},{8,9},{9,8},{10,11... | collective-permute-start | bytes 2654216 | tf_op jit(solution)/shard_map/ppermute | solution.py:28
  7.2 18.2 %collective-permute-done.2.when_inner.b2 = bf16[384,1152]{1,0:T(8,128)(2,1)S(1)} collective-permute-done((bf16[384,1152]{1,0:T(8,128)(2,1)S(1)}, bf16[384,1152]{1,0:T(8,128)(2,1)S(1)}, u32[]{:S(2)}, u32[]{:S(2)}) %collective-permute-start.2) | collective-permute-done | bytes 884768 | tf_op jit(solution)/shard_map/ppermute | solution.py:28
  25.4 0.0 copy-start.1
  25.4 0.9 %pick.3 = bf16[384,1152]{1,0:T(8,128)(2,1)} custom-call(bf16[384,1152]{1,0:T(8,128)(2,1)S(1)} %get-tuple-element.24.when_outer, bf16[384,1152]{1,0:T(8,128)(2,1)S(1)} %collective-permute-done.2.when_inner.b2), custom_call_target="tpu_custom_call" | custom-call | flops 1 | bytes 1 | tf_op jit(solution)/shard_map/pick/pallas_call | solution.py:256
  26.3 0.0 copy-done
  26.3 1.8 %collective-permute-start.3 = (bf16[384,1152]{1,0:T(8,128)(2,1)}, bf16[384,1152]{1,0:T(8,128)(2,1)S(1)}, u32[]{:S(2)}, u32[]{:S(2)}) collective-permute-start(bf16[384,1152]{1,0:T(8,128)(2,1)} %pick.3), channel_id=1, source_target_pairs={{0,1},{1,0},{2,3},{3,2},{4,5},{5,4},{6,7},{7,6},{8,9},{9,8},{10,11... | collective-permute-start | bytes 2654216 | tf_op jit(solution)/shard_map/ppermute | solution.py:28
  28.2 0.0 collective-permute-done.1.b3
  28.2 1.8 %collective-permute-start.5 = (bf16[384,1152]{1,0:T(8,128)(2,1)S(1)}, bf16[384,1152]{1,0:T(8,128)(2,1)S(1)}, u32[]{:S(2)}, u32[]{:S(2)}) collective-permute-start(bf16[384,1152]{1,0:T(8,128)(2,1)S(1)} %collective-permute-done.1.b3), channel_id=1, source_target_pairs={{0,30},{1,31},{2,4},{3,5},{4,2},{5,3},{6,8},{7,9},{8,6},{9,7},{10,... | collective-permute-start | bytes 2654216 | tf_op jit(solution)/shard_map/ppermute | solution.py:28
  31.3 0.1 iota.7.scalars
  31.4 0.0 copy-done.1
  31.4 9.0 %near_blocks.1 = (bf16[768,1152]{1,0:T(8,128)(2,1)S(1)}, f32[384,1152]{1,0:T(8,128)S(1)}, f32[384,1152]{1,0:T(8,128)S(1)}, f32[384,1]{1,0:T(8,128)S(1)}, f32[384...) custom-call(f32[8,128]{1,0:T(8,128)S(1)} %iota.7.scalars, ...), custom_call_target="tpu_custom_call" | custom-call | flops 1 | bytes 1 | tf_op jit(solution)/shard_map/near_blocks/pallas_call | solution.py:256
  40.4 5.7 %collective-permute-done.3.b5 = bf16[384,1152]{1,0:T(8,128)(2,1)S(1)} collective-permute-done((bf16[384,1152]{1,0:T(8,128)(2,1)}, bf16[384,1152]{1,0:T(8,128)(2,1)S(1)}, u32[]{:S(2)}, u32[]{:S(2)}) %collective-permute-start.3) | collective-permute-done | bytes 884768 | tf_op jit(solution)/shard_map/ppermute | solution.py:28
  46.1 2.6 %fifth_block.1 = (f32[384,1152]{1,0:T(8,128)S(1)}, f32[384,128]{1,0:T(8,128)S(1)}, bf16[384,1280]{1,0:T(8,128)(2,1)S(1)}) custom-call(f32[8,128]{1,0:T(8,128)S(1)} %iota.7.scalars, bf16[384,1152]{1,0:T(8,128)(2,1)S(1)} %collective-permute-done.3.b5, bf16[768,1152]{1,0:T(8,128)(2,1)S(1)} %get-tuple-element.29.z_pair, ...), custom_call_target="tpu_custom_call" | custom-call | flops 1 | bytes 1 | tf_op jit(solution)/shard_map/fifth_block/pallas_call | solution.py:256
  48.7 0.1 collective-permute-start.4
  48.8 1.5 %collective-permute-done.5.b4 = bf16[384,1152]{1,0:T(8,128)(2,1)S(1)} collective-permute-done((bf16[384,1152]{1,0:T(8,128)(2,1)S(1)}, bf16[384,1152]{1,0:T(8,128)(2,1)S(1)}, u32[]{:S(2)}, u32[]{:S(2)}) %collective-permute-start.5) | collective-permute-done | bytes 884768 | tf_op jit(solution)/shard_map/ppermute | solution.py:28
  50.2 1.7 %finish_u.1 = (bf16[384,1152]{1,0:T(8,128)(2,1)S(1)}, f32[384,128]{1,0:T(8,128)S(1)}) custom-call(f32[8,128]{1,0:T(8,128)S(1)} %iota.7.scalars, bf16[384,1152]{1,0:T(8,128)(2,1)S(1)} %collective-permute-done.5.b4, bf16[768,1152]{1,0:T(8,128)(2,1)S(1)} %get-tuple-element.29.z_pair, f32[384,1152]{1,0:T(8,128)S(1)} %get-tuple-element.36.grad_u, ...), custom_call_target="tpu_custom_call" | custom-call | flops 10000000000 | bytes 1 | tf_op jit(solution)/shard_map/finish_u/pallas_call | solution.py:256
  51.9 0.0 collective-permute-done.4.last
  51.9 1.8 %finish_w.1 = (bf16[384,1152]{1,0:T(8,128)(2,1)}, bf16[384,1152]{1,0:T(8,128)(2,1)}, f32[384]{0:T(512)}) custom-call(bf16[384,1280]{1,0:T(8,128)(2,1)S(1)} %collective-permute-done.4.last, f32[384,1152]{1,0:T(8,128)S(1)} %get-tuple-element.35.part_w, f32[384,128]{1,0:T(8,128)S(1)} %get-tuple-element.40.loss_in, bf16[384,1152]{1,0:T(8,128)(2,1)S(1)} %get-tuple-element.41.done_u), custom_call_target="tpu_custom_call" | custom-call | flops 1 | bytes 1 | tf_op jit(solution)/shard_map/finish_w/pallas_call | solution.py:256
  (1 shorter events, 0.0 us)
Async XLA Ops:
  2.1 2.8 %collective-permute-start = (bf16[384,1152]{1,0:T(8,128)(2,1)S(1)}, bf16[384,1152]{1,0:T(8,128)(2,1)S(1)}, u32[]{:S(2)}, u32[]{:S(2)}) collective-permute-start(bf16[384,1152]{1,0:T(8,128)(2,1)S(1)} %get-tuple-element.24.when_outer), channel_id=1, source_target_pairs={{0,2},{1,3},{2,0},{3,1},{4,6},{5,7},{6,4},{7,5},{8,10},{9,11},{10,... | collective-permute-start | bytes 2654216 | tf_op jit(solution)/shard_map/ppermute | solution.py:28
  2.2 23.2 %collective-permute-start.2 = (bf16[384,1152]{1,0:T(8,128)(2,1)S(1)}, bf16[384,1152]{1,0:T(8,128)(2,1)S(1)}, u32[]{:S(2)}, u32[]{:S(2)}) collective-permute-start(bf16[384,1152]{1,0:T(8,128)(2,1)S(1)} %get-tuple-element.25.when_inner), channel_id=1, source_target_pairs={{0,30},{1,31},{2,4},{3,5},{4,2},{5,3},{6,8},{7,9},{8,6},{9,7},{10,... | collective-permute-start | bytes 2654216 | tf_op jit(solution)/shard_map/ppermute | solution.py:28
  4.9 21.4 %copy-start = (bf16[384,1152]{1,0:T(8,128)(2,1)}, bf16[384,1152]{1,0:T(8,128)(2,1)S(1)}, u32[]{:S(2)}) copy-start(bf16[384,1152]{1,0:T(8,128)(2,1)S(1)} %collective-permute-done.when_outer.b1) | copy-start | bytes 2654212
  5.1 23.1 %collective-permute-start.1 = (bf16[384,1152]{1,0:T(8,128)(2,1)S(1)}, bf16[384,1152]{1,0:T(8,128)(2,1)S(1)}, u32[]{:S(2)}, u32[]{:S(2)}) collective-permute-start(bf16[384,1152]{1,0:T(8,128)(2,1)S(1)} %pick.2), channel_id=1, source_target_pairs={{0,1},{1,0},{2,3},{3,2},{4,5},{5,4},{6,7},{7,6},{8,9},{9,8},{10,11... | collective-permute-start | bytes 2654216 | tf_op jit(solution)/shard_map/ppermute | solution.py:28
  25.4 6.0 %copy-start.1 = (bf16[384,1152]{1,0:T(8,128)(2,1)}, bf16[384,1152]{1,0:T(8,128)(2,1)S(1)}, u32[]{:S(2)}) copy-start(bf16[384,1152]{1,0:T(8,128)(2,1)S(1)} %collective-permute-done.2.when_inner.b2) | copy-start | bytes 2654212
  26.3 19.7 %collective-permute-start.3 = (bf16[384,1152]{1,0:T(8,128)(2,1)}, bf16[384,1152]{1,0:T(8,128)(2,1)S(1)}, u32[]{:S(2)}, u32[]{:S(2)}) collective-permute-start(bf16[384,1152]{1,0:T(8,128)(2,1)} %pick.3), channel_id=1, source_target_pairs={{0,1},{1,0},{2,3},{3,2},{4,5},{5,4},{6,7},{7,6},{8,9},{9,8},{10,11... | collective-permute-start | bytes 2654216 | tf_op jit(solution)/shard_map/ppermute | solution.py:28
  28.2 22.0 %collective-permute-start.5 = (bf16[384,1152]{1,0:T(8,128)(2,1)S(1)}, bf16[384,1152]{1,0:T(8,128)(2,1)S(1)}, u32[]{:S(2)}, u32[]{:S(2)}) collective-permute-start(bf16[384,1152]{1,0:T(8,128)(2,1)S(1)} %collective-permute-done.1.b3), channel_id=1, source_target_pairs={{0,30},{1,31},{2,4},{3,5},{4,2},{5,3},{6,8},{7,9},{8,6},{9,7},{10,... | collective-permute-start | bytes 2654216 | tf_op jit(solution)/shard_map/ppermute | solution.py:28
  48.7 3.2 %collective-permute-start.4 = (bf16[384,1280]{1,0:T(8,128)(2,1)S(1)}, bf16[384,1280]{1,0:T(8,128)(2,1)S(1)}, u32[]{:S(2)}, u32[]{:S(2)}) collective-permute-start(bf16[384,1280]{1,0:T(8,128)(2,1)S(1)} %get-tuple-element.34), channel_id=1, source_target_pairs={{0,2},{1,3},{2,0},{3,1},{4,6},{5,7},{6,4},{7,5},{8,10},{9,11},{10,... | collective-permute-start | bytes 2949128 | tf_op jit(solution)/shard_map/ppermute | solution.py:28
